TPU v7x, 128 devices: a whole 4x4x4 slice. The times are simulated.
128 devices in a mesh: section: 4 (over z), sky: 32 (over y, x, core).
Axes of the slice: x: 4, y: 4, z: 4, core: 2. Of those that a mesh axis runs over, the one named last changes fastest.
Arguments:
- exposures: bfloat16 [256, 256, 1024], P('sky', 'section'), may hold values from -6 to 6
- coef_code: int32 [256, 27], P('sky'), may hold values from 0 to 63
- coef_table: float32 [27, 64], replicated, may hold values from -1.25 to 1.25
- basis_rows: float32 [27, 23], replicated, may hold values from -1.25 to 1.25
- basis_cols: float32 [27, 23], replicated, may hold values from -1.25 to 1.25
- exposure_weight: int32 [256], P('sky'), may hold values from 1 to 8
- intersection_patch: int32 [256, 8], P('sky'), may hold values from 0 to 31, all different within a row; in each aligned block of 8 rows (0 to 7, 8 to 15, ...) at most 4 rows name the same one
- intersection_shift: int32 [256, 8], P('sky'), may hold values from 0 to 128
- psf_kernels: bfloat16 [3, 41, 41], replicated, may hold values from -0.15625 to 0.15625
Outputs:
- coadd: float32 [32, 256, 1024], P('sky', 'section')
- detect: float32 [32, 3, 256, 1024], P('sky', None, 'section')
Inputs may be any that keep to these rules, and one draw needn't show every extreme that they name: `intersection_patch`: no exposure names a patch twice. Within the exposures of one device (aligned blocks of 8 exposures) no patch is named by more than 4 entries, a bound that some block reaches. Every patch is named by some exposure.
All inputs are finite; a program needn't handle non-finite values.
Results may differ from a plain program's by a relative error of at most 0.005.
Values may be sent and summed in bfloat16 or wider, within the bound.
No kernel may reach another device: no remote copies, remote signals or barrier semaphores. Data moves between devices by JAX's collectives and lax.ppermute only.
A program may use at most 192 MiB of HBM per device.

v0:
```python
import jax
import jax.numpy as jnp
from jax import lax
from jax.sharding import PartitionSpec as P

lane_block = 128


def with_halo(block, sides, width):
    for axis, dim in sides:
        count = lax.axis_size(axis)
        forward = [(i, i + 1) for i in range(count - 1)]
        backward = [(target, source) for source, target in forward]
        low = lax.ppermute(
            lax.slice_in_dim(block, block.shape[dim] - width, None, axis=dim), axis, forward
        )
        high = lax.ppermute(lax.slice_in_dim(block, 0, width, axis=dim), axis, backward)
        block = jnp.concatenate([low, block, high], axis=dim)
    return block


def band_matrix(kernel):
    tap_count = kernel.shape[-1]
    span = lane_block + tap_count - 1
    tap_index = jnp.arange(tap_count)[:, None, None]
    col_in = jnp.arange(span)[None, :, None]
    col_out = jnp.arange(lane_block)[None, None, :]
    onehot = (col_in - col_out == tap_index).astype(jnp.bfloat16)
    banded = jnp.einsum("...ij,jwc->...iwc", kernel, onehot, preferred_element_type=jnp.float32)
    return banded.astype(jnp.bfloat16)


def column_windows(widened, block_count, span, axis_pos):
    pieces = [
        lax.slice_in_dim(widened, block * lane_block, block * lane_block + span, axis=axis_pos)
        for block in range(block_count)
    ]
    return jnp.stack(pieces, axis=0)


def match_exposures(framed, kernel):
    exp_count, tall_rows, col_count = framed.shape
    tap_count = kernel.shape[-1]
    row_count = tall_rows - tap_count + 1
    half_taps = tap_count // 2
    span = lane_block + tap_count - 1
    block_count = col_count // lane_block
    banded = band_matrix(kernel)
    widened = jnp.pad(framed, ((0, 0), (0, 0), (half_taps, half_taps)))
    windows = column_windows(widened, block_count, span, 2)
    total = jnp.zeros((block_count, exp_count, row_count, lane_block), jnp.float32)
    for lag in range(tap_count):
        total = total + jnp.einsum(
            "berw,ewc->berc",
            windows[:, :, lag : lag + row_count, :],
            banded[:, lag],
            preferred_element_type=jnp.float32,
        )
    blocks = total.astype(jnp.bfloat16)
    return jnp.moveaxis(blocks, 0, 2).reshape(exp_count, row_count, col_count)


def detect_sources(framed, psf_kernels):
    tall_rows, col_count = framed.shape
    scale_count, tap_count = (psf_kernels.shape[0], psf_kernels.shape[-1])
    row_count = tall_rows - tap_count + 1
    half_taps = tap_count // 2
    span = lane_block + tap_count - 1
    block_count = col_count // lane_block
    banded = band_matrix(psf_kernels)
    widened = jnp.pad(framed, ((0, 0), (half_taps, half_taps)))
    windows = column_windows(widened, block_count, span, 1)
    total = jnp.zeros((block_count, scale_count, row_count, lane_block), jnp.float32)
    for lag in range(tap_count):
        total = total + jnp.einsum(
            "brw,swc->bsrc",
            windows[:, lag : lag + row_count, :],
            banded[:, lag],
            preferred_element_type=jnp.float32,
        )
    return jnp.moveaxis(total, 0, 2).reshape(scale_count, row_count, col_count)


def shift_right(plane, offset, col_reach):
    widened = jnp.pad(plane, ((0, 0), (col_reach, 0)))
    return lax.dynamic_slice_in_dim(widened, col_reach - offset, plane.shape[1], 1)


def on_device(
    exposures,
    coef_code,
    coef_table,
    basis_rows,
    basis_cols,
    exposure_weight,
    intersection_patch,
    intersection_shift,
    psf_kernels,
):
    exp_count, row_count, col_count = exposures.shape
    owners = lax.axis_size("sky")
    col_reach = col_count // 8
    levels = coef_table.shape[1]
    picked = coef_code[:, :, None] == jnp.arange(levels)[None, None, :]
    coefficient = jnp.sum(jnp.where(picked, coef_table[None], 0.0), axis=2)
    kernel = jnp.einsum(
        "eb,bi,bj->eij", coefficient, basis_rows, basis_cols, precision=lax.Precision.HIGHEST
    ).astype(jnp.bfloat16)
    framed = with_halo(exposures, (("section", 1),), basis_rows.shape[1] // 2)
    matched = match_exposures(framed, kernel)
    intersections = intersection_patch.shape[1]
    entries = exp_count * intersections
    target = intersection_patch.reshape(-1)
    offset = intersection_shift.reshape(-1)
    source = jnp.repeat(jnp.arange(exp_count), intersections)
    weight = jnp.repeat(exposure_weight, intersections)
    column = jnp.arange(col_count)
    capacity = 2 + (entries + owners - 1) // owners
    entry_ids = jnp.arange(entries)
    earlier = (target[:, None] == target[None, :]) & (entry_ids[None, :] < entry_ids[:, None])
    slot_rank = jnp.sum(earlier.astype(jnp.int32), axis=1)
    slot_hit = (target[:, None, None] == jnp.arange(owners)[None, :, None]) & (
        slot_rank[:, None, None] == jnp.arange(capacity)[None, None, :]
    )
    is_live = jnp.any(slot_hit, axis=0)
    slot_source = jnp.sum(jnp.where(slot_hit, source[:, None, None], 0), axis=0)
    slot_weight = jnp.sum(jnp.where(slot_hit, weight[:, None, None], 0), axis=0)
    slot_offset = jnp.sum(jnp.where(slot_hit, offset[:, None, None], 0), axis=0)
    outgoing = jnp.where(
        is_live[:, :, None, None],
        jnp.take(matched, slot_source, axis=0),
        jnp.zeros((), jnp.bfloat16),
    )
    labels = jnp.stack([slot_weight, slot_offset], axis=2)
    got_slots, got_labels = (
        lax.all_to_all(outgoing, "sky", split_axis=0, concat_axis=0, tiled=True),
        lax.all_to_all(labels, "sky", split_axis=0, concat_axis=0, tiled=True),
    )
    flattened = got_slots.reshape(-1, row_count, col_count)
    got_weight = got_labels[:, :, 0].reshape(-1)
    got_offset = got_labels[:, :, 1].reshape(-1)
    pieces = jax.vmap(lambda plane, shift_by: shift_right(plane, shift_by, col_reach))(
        flattened, got_offset
    )
    numerator = jnp.einsum(
        "k,krc->rc", got_weight.astype(jnp.bfloat16), pieces, preferred_element_type=jnp.float32
    )
    coverage = (column[None, :] >= got_offset[:, None]).astype(jnp.float32)
    denominator = jnp.dot(got_weight.astype(jnp.float32), coverage, precision=lax.Precision.HIGHEST)
    coadd = numerator / jnp.maximum(denominator, 1.0)[None, :]
    framed_coadd = with_halo(
        coadd.astype(jnp.bfloat16), (("section", 0),), psf_kernels.shape[-1] // 2
    )
    detect = detect_sources(framed_coadd, psf_kernels)
    return (coadd[None], detect[None])


def solution(mesh):
    return jax.shard_map(
        on_device,
        mesh=mesh,
        in_specs=(
            P("sky", "section", None),
            P("sky", None),
            P(),
            P(),
            P(),
            P("sky"),
            P("sky", None),
            P("sky", None),
            P(),
        ),
        out_specs=(P("sky", "section", None), P("sky", None, "section", None)),
        check_vma=False,
    )
```

profile of v0, /device:TPU:32, one launch (start us, length us, event | category | flops | bytes accessed | tf_op | source)
XLA Modules:
  0.0 857.1 jit_solution(1500923180678460957)
XLA Ops:
  4.3 7.4 all-to-all-start
  14.9 3.8 collective-permute-start
  23.5 11.0 %fusion.253 = (bf16[8,1,150,128]{3,1,2,0:T(2,128)(2,1)S(1)}, bf16[8,1,150,128]{3,1,2,0:T(2,128)(2,1)}, bf16[8,1,150,128]{3,1,2,0:T(2,128)(2,1)}, bf16[8,1,150,12...) fusion(bf16[8,23,150,128]{3,1,2,0:T(8,128)(2,1)S(1)} %convoluti, ...), kind=kLoop, calls=%fused_computation.387 | loop fusion | bytes 11673600 | tf_op jit(solution)/shard_map/slice | solution.py:56
  34.6 3.4 fusion.254
  86.8 16.6 %fusion.59 = bf16[8,8,8,8,128]{4,3,2,1,0:T(8,128)(2,1)} fusion(f32[8,128,8,64]{1,3,2,0:T(8,128)} %fusion.7, f32[8,128,8,64]{1,3,2,0:T(8,128)} %fusion.9, f32[8,128,8,64]{1,3,2,0:T(8,128)} %fusion.11, f32[8,128,8,64]{1,3,2,0:T(8,128)} %fusion.13, f32[8,128,8,64]{1,3,2,0:T(8,128)} %fusion.15, f32[8,128,8,64]{1,3,2,0:T(8,128)} %fusion.17, ...), kind=kOutput, calls=%fused_computation.70 | convolution fusion | flops 169345024 | bytes 49897472 | tf_op jit(solution)/shard_map/berw,ewc->berc/dot_general | solution.py:53
  104.9 8.0 gather_fusion
  112.9 14.3 %select_select_fusion = bf16[32,4,64,1024]{3,2,1,0:T(8,128)(2,1)} fusion(bf16[32,4,64,1024]{3,2,1,0:T(8,128)(2,1)} %bitcast.808, pred[32,4]{1,0:T(8,128)(4,1)S(1)} %copy.274, pred[32,4]{1,0:T(8,128)(4,1)S(1)} %copy.273), kind=kLoop, calls=%fused_computation.5 | loop fusion | flops 16777216 | bytes 33554688 | tf_op jit(solution)/shard_map/jit(_where)/select_n | solution.py:129
  127.1 7.5 all-to-all-start.1
  136.4 5.0 fusion.256
  141.5 5.6 fusion.255
  150.5 197.3 %all-to-all-done.1 = bf16[32,4,64,1024]{3,2,1,0:T(8,128)(2,1)} async-done(((bf16[32,4,64,1024]{3,2,1,0:T(8,128)(2,1)}), bf16[32,4,64,1024]{3,2,1,0:T(8,128)(2,1)}, u32[]{:S(2)}, u32[]{:S(2)}) %all-to-all-start.1) | async-done | bytes 16777248 | tf_op jit(solution)/shard_map/all_to_all | solution.py:136
  347.8 14.5 %pad.14 = bf16[128,64,1152]{2,1,0:T(8,128)(2,1)} pad(bf16[128,64,1024]{2,1,0:T(8,128)(2,1)} %bitcast.125, bf16[]{:T(256)} %constant.8.clone.1), padding=0_0x0_0x128_0 | pad | bytes 35651584 | tf_op jit(solution)/shard_map/vmap(jit(_pad))/pad | solution.py:85
  362.3 443.9 %while.1 = (s32[]{:T(128)}, bf16[128,64,1152]{2,1,0:T(8,128)(2,1)}, s32[128,3]{0,1:T(4,128)S(1)}, bf16[128,64,1024]{2,1,0:T(8,128)(2,1)}, s32[]{:T(128)}) while((s32[]{:T(128)}, bf16[128,64,1152]{2,1,0:T(8,128)(2,1)}, s32[128,3]{0,1:T(4,128)S(1)}, bf16[128,64,1024]{2,1,0:T(8,128)(2,1)}, s32[]{:T(128)}) %tuple.89), condition=%wide.while_cond, body=%wide.while_body.sunk | while | flops 2 | bytes 263285 | solution.py:86
  363.0 2.9 dynamic-slice_dynamic-update-slice_fusion.2
  390.7 2.9 dynamic-slice_dynamic-update-slice_fusion.2
  414.9 2.9 dynamic-slice_dynamic-update-slice_fusion.2
  421.9 2.9 dynamic-slice_dynamic-update-slice_fusion.2
  428.8 2.9 dynamic-slice_dynamic-update-slice_fusion.2
  435.8 2.9 dynamic-slice_dynamic-update-slice_fusion.2
  446.2 2.9 dynamic-slice_dynamic-update-slice_fusion.2
  473.9 2.9 dynamic-slice_dynamic-update-slice_fusion.2
  491.2 2.9 dynamic-slice_dynamic-update-slice_fusion.2
  501.6 2.9 dynamic-slice_dynamic-update-slice_fusion.2
  508.6 2.9 dynamic-slice_dynamic-update-slice_fusion.2
  512.1 2.9 dynamic-slice_dynamic-update-slice_fusion.2
  532.9 2.9 dynamic-slice_dynamic-update-slice_fusion.2
  543.3 2.9 dynamic-slice_dynamic-update-slice_fusion.2
  560.6 2.9 dynamic-slice_dynamic-update-slice_fusion.2
  571.0 2.9 dynamic-slice_dynamic-update-slice_fusion.2
  612.6 2.9 dynamic-slice_dynamic-update-slice_fusion.2
  616.0 2.9 dynamic-slice_dynamic-update-slice_fusion.2
  619.5 2.9 dynamic-slice_dynamic-update-slice_fusion.2
  636.9 2.9 dynamic-slice_dynamic-update-slice_fusion.2
  643.8 2.9 dynamic-slice_dynamic-update-slice_fusion.2
  681.9 2.9 dynamic-slice_dynamic-update-slice_fusion.2
  685.4 2.9 dynamic-slice_dynamic-update-slice_fusion.2
  709.6 2.9 dynamic-slice_dynamic-update-slice_fusion.2
  723.5 2.9 dynamic-slice_dynamic-update-slice_fusion.2
  727.0 2.9 dynamic-slice_dynamic-update-slice_fusion.2
  754.7 2.9 dynamic-slice_dynamic-update-slice_fusion.2
  761.6 2.9 dynamic-slice_dynamic-update-slice_fusion.2
  765.1 2.9 dynamic-slice_dynamic-update-slice_fusion.2
  768.6 2.9 dynamic-slice_dynamic-update-slice_fusion.2
  792.8 2.9 dynamic-slice_dynamic-update-slice_fusion.2
  799.8 2.9 dynamic-slice_dynamic-update-slice_fusion.2
  806.3 23.5 %fusion = f32[1,64,1024]{2,0,1:T(1,128)S(1)} fusion(bf16[128,1,1]{0,1,2:T(2,128)(2,1)S(1)} %reshape.208, bf16[128,64,1024]{2,1,0:T(8,128)(2,1)} %get-tuple-element.9), kind=kOutput, calls=%fused_computation.3 | convolution fusion | flops 16777216 | bytes 17039616 | tf_op jit(solution)/shard_map/k,krc->rc/dot_general | solution.py:145
  832.6 3.9 collective-permute-start.2
  836.6 3.3 fusion.257
  (588 shorter events, 438.0 us)
Async XLA Ops:
  0.6 134.0 %copy-start = (bf16[3,41,41]{2,1,0:T(8,128)(2,1)S(1)}, bf16[3,41,41]{2,1,0:T(8,128)(2,1)}, u32[]{:S(2)}) copy-start(bf16[3,41,41]{2,1,0:T(8,128)(2,1)} %param.17) | copy-start | bytes 30262
  4.3 122.8 %all-to-all-start = ((s32[32,4,2]{1,2,0:T(2,128)}), s32[32,4,2]{1,2,0:T(2,128)}, u32[]{:S(2)}, u32[]{:S(2)}) async-start(s32[32,4,2]{1,2,0:T(2,128)} %copy.272), calls=%async_computation | async-start | bytes 65536 | tf_op jit(solution)/shard_map/all_to_all | solution.py:137
  12.9 25.7 %collective-permute-start.1 = (bf16[8,11,1024]{2,1,0:T(8,128)(2,1)S(1)}, bf16[8,11,1024]{2,1,0:T(8,128)(2,1)S(1)}, u32[]{:S(2)}, u32[]{:S(2)}) collective-permute-start(bf16[8,11,1024]{2,1,0:T(8,128)(2,1)S(1)} %get-tuple-element.91), channel_id=1, source_target_pairs={{32,0},{64,32},{96,64},{33,1},{65,33},{97,65},{34,2},{66,34},{98,6... | collective-permute-start | bytes 540680 | tf_op jit(solution)/shard_map/ppermute | solution.py:17
  14.9 23.7 %collective-permute-start = (bf16[8,11,1024]{2,1,0:T(8,128)(2,1)S(1)}, bf16[8,11,1024]{2,1,0:T(8,128)(2,1)S(1)}, u32[]{:S(2)}, u32[]{:S(2)}) collective-permute-start(bf16[8,11,1024]{2,1,0:T(8,128)(2,1)S(1)} %get-tuple-element.90), channel_id=1, source_target_pairs={{0,32},{32,64},{64,96},{1,33},{33,65},{65,97},{2,34},{34,66},{66,9... | collective-permute-start | bytes 540680 | tf_op jit(solution)/shard_map/ppermute | solution.py:14
  34.6 4.1 copy-start.2
  39.9 1.1 copy-start.21
  41.0 2.1 copy-start.20
  43.0 2.0 copy-start.19
  45.1 2.1 copy-start.18
  47.2 2.1 copy-start.17
  49.3 2.1 copy-start.6
  51.4 2.1 copy-start.5
  53.4 2.0 copy-start.16
  55.5 2.0 copy-start.15
  57.5 2.1 copy-start.14
  59.5 2.0 copy-start.13
  61.6 2.1 copy-start.12
  63.7 2.1 copy-start.11
  65.8 2.1 copy-start.4
  67.9 2.1 copy-start.3
  70.0 2.5 copy-start.10
  72.5 2.0 copy-start.9
  74.5 2.0 copy-start.8
  76.5 2.0 copy-start.24
  78.6 2.0 copy-start.23
  80.6 2.1 copy-start.22
  82.7 2.1 copy-start.7
  127.1 220.7 %all-to-all-start.1 = ((bf16[32,4,64,1024]{3,2,1,0:T(8,128)(2,1)}), bf16[32,4,64,1024]{3,2,1,0:T(8,128)(2,1)}, u32[]{:S(2)}, u32[]{:S(2)}) async-start(bf16[32,4,64,1024]{3,2,1,0:T(8,128)(2,1)} %select_select_fusion), calls=%async_computation.1 | async-start | bytes 33554432 | tf_op jit(solution)/shard_map/all_to_all | solution.py:136
  136.4 5.0 copy-start.1
  829.8 11.0 %copy-start.39 = (bf16[3,1,168,128]{3,1,0,2:T(2,128)(2,1)S(1)}, bf16[3,1,168,128]{3,1,0,2:T(2,128)(2,1)}, u32[]{:S(2)}) copy-start(bf16[3,1,168,128]{3,1,0,2:T(2,128)(2,1)} %get-tuple-element.50) | copy-start | bytes 387076
  830.6 9.4 %collective-permute-start.3 = (bf16[20,1024]{1,0:T(8,128)(2,1)S(1)}, bf16[20,1024]{1,0:T(8,128)(2,1)S(1)}, u32[]{:S(2)}, u32[]{:S(2)}) collective-permute-start(bf16[20,1024]{1,0:T(8,128)(2,1)S(1)} %get-tuple-element.95), channel_id=1, source_target_pairs={{32,0},{64,32},{96,64},{33,1},{65,33},{97,65},{34,2},{66,34},{98,6... | collective-permute-start | bytes 122888 | tf_op jit(solution)/shard_map/ppermute | solution.py:17
  832.6 8.5 copy-start.49
  832.6 7.3 collective-permute-start.2
  839.9 1.5 copy-start.48
  840.6 1.1 copy-start.47
  841.4 1.0 copy-start.37
  841.7 1.0 copy-start.36
  841.7 1.3 copy-start.35
  842.0 1.3 copy-start.34
  842.4 1.3 copy-start.46
  843.3 1.0 copy-start.33
  843.6 1.0 copy-start.32
  843.9 1.0 copy-start.31
  844.3 1.0 copy-start.30
  844.3 1.3 copy-start.29
  844.6 1.3 copy-start.44
  846.2 1.0 copy-start.27
  846.5 1.0 copy-start.26
  (8 other events, 7.8 us)
where the time goes:
time: 868 us; the launch traced here: 857 us
  local copies, waits for them, and re-layouts  507 us (58%)
  waiting for transfers between devices  197 us (23%)
  matrix products  104 us (12%)
  starting transfers between devices  26.7 us (3%)
  other arithmetic  19.6 us (2%)
    gather x384, local copies, waits for them, and re-layouts  444 us
    all_to_all x1, waiting for transfers between devices, on_device(): lax.all_to_all(outgoing, 'sky', split_axis=0, concat_axis=0, tiled=True)  197 us
    dot_general x23, matrix products, match_exposures(): jnp.einsum('berw,ewc->berc', windows[:, :, lag:lag + row_count, :], bande...  62.3 us
    dot_general x1, matrix products, on_device(): jnp.einsum('k,krc->rc', got_weight.astype(jnp.bfloat16), pieces, preferre...  23.5 us
  transfers between devices with their start and end apart: 6, of which 1 were waited for; matrix products, arithmetic and copies ran while one was open for 15% of the time, Pallas kernels for 0%

commit v1 on v0

v1 whole, which is shorter than its diff:
```python
import functools

import jax
import jax.numpy as jnp
from jax import lax
from jax.experimental import pallas as pl
from jax.experimental.pallas import tpu as pltpu
from jax.sharding import Mesh, PartitionSpec as P

f32 = jnp.float32
bf16 = jnp.bfloat16

lanes = 128
half = 64
group = 4
vmem_bytes = 56 * 1024 * 1024


def neighbours(count):
    up = [(i, i + 1) for i in range(count - 1)]
    return up, [(b, a) for a, b in up]


def profile_rows(profile, taps):
    lead = profile.shape[:-1]
    zeros = lambda n: jnp.zeros(lead + (n,), profile.dtype)
    first = jnp.concatenate(
        [profile[..., :1], zeros(lanes - taps), profile[..., :0:-1]], axis=-1
    )
    second = jnp.concatenate(
        [zeros(half - taps + 1), profile[..., ::-1], zeros(lanes - half - 1)], axis=-1
    )
    return first, second


def pad_rows(rows, low, high):
    return jnp.pad(rows, [(0, 0)] * (rows.ndim - 2) + [(low, high), (0, 0)])


def lane_ids(rows):
    return lax.broadcasted_iota(jnp.int32, (rows, lanes), 1)


def band_mask(depth, taps):
    k = lax.broadcasted_iota(jnp.int32, (depth, lanes), 0)
    gap = k - lane_ids(depth) % half
    return (gap >= 0) & (gap < taps)


def band_tile(row, mask):
    depth = mask.shape[0]
    wide = jnp.broadcast_to(row, (depth, lanes))
    turned = pltpu.roll(wide, 0, 1, stride=1, stride_axis=0)
    return jnp.where(mask, turned, 0.0).astype(bf16)


def put_frame(frame, tiles, row, reach):
    count = len(tiles)
    rows = tiles[0].shape[0]
    lane = lane_ids(rows)
    zero = jnp.zeros((rows, lanes), f32)
    right = [pltpu.roll(t, reach, 1) for t in tiles]
    left = [pltpu.roll(t, half + reach, 1) for t in tiles]
    for m in range(count):
        before = right[m - 1] if m else zero
        frame[0, m, row : row + rows, :] = jnp.where(lane < reach, before, right[m])
        after = left[m + 1] if m + 1 < count else zero
        frame[1, m, row : row + rows, :] = jnp.where(lane < half + reach, left[m], after)


def put_lhs(lhs, frame, spans, row):
    tiles = frame.shape[1]
    for t in range(spans):
        for par in range(2):
            for m in range(tiles):
                at = (par * tiles + m) * 16
                piece = frame[par, m, pl.ds(row + t, 16, stride=group), :]
                lhs[at : at + 16, t * lanes : (t + 1) * lanes] = piece.astype(bf16)


def split_rows(even, odd, lane):
    first = jnp.where(lane < half, even, pltpu.roll(odd, half, 1))
    second = jnp.where(lane < half, pltpu.roll(even, half, 1), odd)
    return first, second


def match_body(taps, code, table, g, x, lo, hi, out, frame, lhs, w):
    e = pl.program_id(0)
    reach = taps // 2
    count = x.shape[2] // lanes
    depth = 96

    @pl.when(e == 0)
    def _():
        w[...] = jnp.zeros_like(w)

    total = jnp.zeros(g.shape[1:], f32)
    for b in range(g.shape[0]):
        total = total + table[b, code[e, b]] * g[b]
    total = total.astype(bf16).astype(f32)
    mask = band_mask(depth, taps)
    for u in range(taps + 1):
        tile = band_tile(total[u : u + 1, :], mask)
        w[u * lanes : u * lanes + depth, 0:lanes] = tile
        w[(u + 2) * lanes : (u + 2) * lanes + depth, lanes : 2 * lanes] = tile

    for ref, row in ((lo, 16 - reach), (x, 16), (hi, 80)):
        rows = ref[0].astype(f32)
        put_frame(frame, [rows[:, m * lanes : (m + 1) * lanes] for m in range(count)], row, reach)
    put_lhs(lhs, frame, taps + 3, 16 - reach)
    acc = jnp.dot(lhs[...], w[...], preferred_element_type=f32)
    lane = lane_ids(16)
    for m in range(count):
        for h in range(2):
            even = acc[m * 16 : m * 16 + 16, h * lanes : (h + 1) * lanes]
            odd = acc[(count + m) * 16 : (count + m) * 16 + 16, h * lanes : (h + 1) * lanes]
            for b, part in enumerate(split_rows(even, odd, lane)):
                at = (2 * h + b) * 16
                out[0, at : at + 16, m * lanes : (m + 1) * lanes] = part.astype(bf16)


def match(code, table, g, x, lo, hi, taps):
    number, rows, cols = x.shape
    smem = pl.BlockSpec(memory_space=pltpu.SMEM)
    one = lambda n: pl.BlockSpec((1, n, cols), lambda e: (e, 0, 0))
    spans = taps + 3
    return pl.pallas_call(
        functools.partial(match_body, taps),
        grid=(number,),
        in_specs=[smem, smem, pl.BlockSpec(g.shape, lambda e: (0, 0, 0)),
                  one(rows), one(lo.shape[1]), one(hi.shape[1])],
        out_specs=one(rows),
        out_shape=jax.ShapeDtypeStruct((number, rows, cols), bf16),
        scratch_shapes=[
            pltpu.VMEM((2, cols // lanes, 96, lanes), f32),
            pltpu.VMEM((256, spans * lanes), bf16),
            pltpu.VMEM((spans * lanes, 256), bf16),
        ],
        compiler_params=pltpu.CompilerParams(vmem_limit_bytes=vmem_bytes),
        cost_estimate=pl.CostEstimate(
            flops=number * 2 * 256 * 256 * spans * lanes, bytes_accessed=4 * x.size, transcendentals=0
        ),
        name="match",
    )(code, table, g, x, lo, hi)


def pile_body(core, weight, patch, shift, mine, other, out, planes, counts, source, offset):
    i = pl.program_id(0)
    number, rows, cols = mine.shape
    tiles = cols // lanes
    per = patch.shape[1]
    slots = 8
    patches = counts.shape[0]

    @pl.when(i == 0)
    def _():
        for e in range(2 * number):
            ref = mine if e < number else other
            scale = weight[e].astype(f32)
            value = ref[e % number].astype(f32) * scale
            for m in range(tiles):
                planes[e, m] = value[:, m * lanes : (m + 1) * lanes]
        planes[2 * number] = jnp.zeros((tiles, rows, lanes), f32)

        def clear(p, _):
            counts[p] = 0
            for s in range(slots):
                source[p * slots + s] = 2 * number
                offset[p * slots + s] = 0
            return 0

        lax.fori_loop(0, patches, clear, 0)

        def enter(e, _):
            for k in range(per):
                p = patch[e, k]
                at = counts[p]
                source[p * slots + at] = e
                offset[p * slots + at] = shift[e, k]
                counts[p] = at + 1
            return 0

        lax.fori_loop(0, 2 * number, enter, 0)

    p = 2 * i + core[0]
    lane = lane_ids(16)
    for c in range(rows // 16):
        total = [None] * tiles
        for s in range(slots):
            e = source[p * slots + s]
            o = offset[p * slots + s]
            keep = lane < o
            before = jnp.zeros((16, lanes), f32)
            for m in range(tiles):
                turned = pltpu.roll(planes[e, m, c * 16 : c * 16 + 16, :], o, 1)
                part = jnp.where(keep, before, turned)
                before = turned
                total[m] = part if s == 0 else total[m] + part
        for m in range(tiles):
            out[0, c * 16 : c * 16 + 16, m * lanes : (m + 1) * lanes] = total[m].astype(bf16)


def pile(core, weight, patch, shift, mine, other, patches):
    number, rows, cols = mine.shape
    smem = pl.BlockSpec(memory_space=pltpu.SMEM)
    whole = pl.BlockSpec(mine.shape, lambda i: (0, 0, 0))
    return pl.pallas_call(
        pile_body,
        grid=(patches // 2,),
        in_specs=[smem] * 4 + [whole] * 2,
        out_specs=pl.BlockSpec((1, rows, cols), lambda i: (i, 0, 0)),
        out_shape=jax.ShapeDtypeStruct((patches // 2, rows, cols), bf16),
        scratch_shapes=[
            pltpu.VMEM((2 * number + 1, cols // lanes, rows, lanes), f32),
            pltpu.SMEM((patches,), jnp.int32),
            pltpu.SMEM((patches * 8,), jnp.int32),
            pltpu.SMEM((patches * 8,), jnp.int32),
        ],
        compiler_params=pltpu.CompilerParams(vmem_limit_bytes=vmem_bytes),
        name="pile",
    )(core, weight, patch, shift, mine, other)


def coadd_body(reach, parts, cover, coadd, low, high, stage):
    count, rows, cols = parts.shape
    tiles = cols // lanes
    for m in range(tiles):
        scale = jnp.maximum(cover[0:1, m * lanes : (m + 1) * lanes], 1.0)
        for b in range(group):
            total = jnp.zeros((16, lanes), f32)
            for n in range(count):
                total = total + parts[n, b * 16 : b * 16 + 16, m * lanes : (m + 1) * lanes].astype(f32)
            stage[m, pl.ds(b, 16, stride=group), :] = total / scale
    for m in range(tiles):
        cut = slice(m * lanes, (m + 1) * lanes)
        coadd[:, cut] = stage[m]
        low[:, cut] = stage[m, 0:reach, :].astype(bf16)
        high[:, cut] = stage[m, rows - reach : rows, :].astype(bf16)


def coadd_of(parts, cover, reach):
    count, rows, cols = parts.shape
    edge = jax.ShapeDtypeStruct((reach, cols), bf16)
    return pl.pallas_call(
        functools.partial(coadd_body, reach),
        out_shape=(jax.ShapeDtypeStruct((rows, cols), f32), edge, edge),
        scratch_shapes=[pltpu.VMEM((cols // lanes, rows, lanes), f32)],
        compiler_params=pltpu.CompilerParams(vmem_limit_bytes=vmem_bytes),
        name="coadd",
    )(parts, cover)


def detect_body(taps, profile, x, lo, hi, out, frame, lhs, w, stage):
    reach = taps // 2
    rows, cols = x.shape
    count = cols // lanes
    scales = profile.shape[0]
    depth = 112
    mask = band_mask(depth, taps)
    w[...] = jnp.zeros_like(w)
    for s in range(scales):
        for u in range(taps + 1):
            tile = band_tile(profile[s, u : u + 1, :], mask)
            w[u * lanes : u * lanes + depth, 2 * s * lanes : (2 * s + 1) * lanes] = tile
            w[(u + 2) * lanes : (u + 2) * lanes + depth, (2 * s + 1) * lanes : (2 * s + 2) * lanes] = tile
    for ref, row in ((lo, 24 - reach), (x, 24), (hi, 24 + rows)):
        value = ref[...].astype(bf16).astype(f32)
        put_frame(frame, [value[:, m * lanes : (m + 1) * lanes] for m in range(count)], row, reach)
    put_lhs(lhs, frame, taps + 3, 24 - reach)
    lane = lane_ids(16)
    for s in range(scales):
        acc = jnp.dot(
            lhs[...], w[:, 2 * s * lanes : (2 * s + 2) * lanes], preferred_element_type=f32
        )
        for m in range(count):
            for h in range(2):
                even = acc[m * 16 : m * 16 + 16, h * lanes : (h + 1) * lanes]
                odd = acc[(count + m) * 16 : (count + m) * 16 + 16, h * lanes : (h + 1) * lanes]
                for b, part in enumerate(split_rows(even, odd, lane)):
                    stage[m, pl.ds(2 * h + b, 16, stride=group), :] = part
            out[s, :, m * lanes : (m + 1) * lanes] = stage[m]


def detect_of(profile, x, lo, hi, taps):
    rows, cols = x.shape
    scales = profile.shape[0]
    spans = taps + 3
    return pl.pallas_call(
        functools.partial(detect_body, taps),
        out_shape=jax.ShapeDtypeStruct((scales, rows, cols), f32),
        scratch_shapes=[
            pltpu.VMEM((2, cols // lanes, 24 + rows + 24, lanes), f32),
            pltpu.VMEM((256, spans * lanes), bf16),
            pltpu.VMEM((spans * lanes, scales * 256), bf16),
            pltpu.VMEM((cols // lanes, rows, lanes), f32),
        ],
        compiler_params=pltpu.CompilerParams(vmem_limit_bytes=vmem_bytes),
        name="detect",
    )(profile, x, lo, hi)


def on_device(
    exposures,
    coef_code,
    coef_table,
    basis_rows,
    basis_cols,
    exposure_weight,
    intersection_patch,
    intersection_shift,
    psf_kernels,
):
    number, rows, cols = exposures.shape
    taps = basis_rows.shape[1]
    reach = taps // 2
    wide = psf_kernels.shape[-1]
    wide_reach = wide // 2
    sections = lax.axis_size("section")
    across = ("sy", "sx")
    patches = lax.axis_size("sy") * lax.axis_size("sx") * 2
    core = lax.axis_index("core")
    up, down = neighbours(sections)

    lo = lax.ppermute(exposures[:, rows - reach :, :], "section", up)
    hi = lax.ppermute(exposures[:, :reach, :], "section", down)

    labels = jnp.concatenate(
        [exposure_weight[:, None], intersection_patch, intersection_shift], axis=1
    )
    everyone = lax.all_gather(labels, ("sy", "sx", "core"), axis=0)
    me = lax.axis_index(across) * 2 + core
    partner = lax.dynamic_index_in_dim(everyone, me + 1 - 2 * core, 0, keepdims=False)
    per = intersection_patch.shape[1]
    both = jnp.concatenate([labels, partner], axis=0)
    flat = everyone.reshape(-1, 1 + 2 * per)
    strength = jnp.where(flat[:, 1 : 1 + per] == me, flat[:, :1], 0).astype(f32)
    column = jnp.arange(lanes)
    cover = jnp.sum(
        jnp.where(column[:, None, None] >= flat[None, :, 1 + per :], strength[None], 0.0), axis=(1, 2)
    )
    cover = jnp.concatenate([cover, jnp.broadcast_to(jnp.sum(strength), (cols - lanes,))])[None]

    cols_a, cols_b = profile_rows(basis_cols, taps)
    rows_a = jnp.pad(basis_rows, ((0, 0), (0, 1)))
    rows_b = jnp.pad(basis_rows, ((0, 0), (1, 0)))
    g = rows_a[:, :, None] * cols_a[:, None, :] + rows_b[:, :, None] * cols_b[:, None, :]
    psf_a, psf_b = profile_rows(psf_kernels.astype(f32), wide)
    profile = pad_rows(psf_a, 0, 1) + pad_rows(psf_b, 1, 0)

    matched = match(coef_code, coef_table, g, exposures, lo, hi, taps)
    other = lax.ppermute(matched, "core", [(0, 1), (1, 0)])
    partial = pile(
        core[None], both[:, 0], both[:, 1 : 1 + per], both[:, 1 + per :], matched, other, patches
    )
    parts = lax.all_to_all(partial, across, split_axis=0, concat_axis=0, tiled=True)
    coadd, low, high = coadd_of(parts, cover, wide_reach)
    lo = lax.ppermute(high, "section", up)
    hi = lax.ppermute(low, "section", down)
    detect = detect_of(profile, coadd, lo, hi, wide)
    return (coadd[None], detect[None])


def solution(mesh):
    sections, sky = mesh.devices.shape
    grid = Mesh(mesh.devices.reshape(sections, 4, sky // 8, 2), ("section", "sy", "sx", "core"))
    sky = ("sy", "sx", "core")
    return jax.shard_map(
        on_device,
        mesh=grid,
        in_specs=(
            P(sky, "section", None),
            P(sky, None),
            P(),
            P(),
            P(),
            P(sky),
            P(sky, None),
            P(sky, None),
            P(),
        ),
        out_specs=(P(sky, "section", None), P(sky, None, "section", None)),
        check_vma=False,
    )
```

time: 868 us -> 126 us (0.15); the launches traced: 857 us -> 125 us
  local copies, waits for them, and re-layouts: 507 us -> 11.6 us
  waiting for transfers between devices: 197 us -> 34.8 us
  matrix products: 104 us -> 0 us
  Pallas kernels: 0 us -> 33 us
  blocking collectives: 0 us -> 24.9 us
  other arithmetic: 19.6 us -> 3.73 us
  starting transfers between devices: 26.7 us -> 16.5 us
    gather x385 -> x0, local copies, waits for them, and re-layouts: 452 us -> none
    all_to_all x2 -> x1, waiting for transfers between devices: 197 us -> 29.8 us  [on_device(): lax.all_to_all(partial, across, split_axis=0, concat_axis=0, tiled=True)]
    dot_general x69 -> x0, matrix products: 104 us -> none  [the longest x23 62.3 us: match_exposures(): jnp.einsum('berw,ewc->berc', windows[:, :, lag:lag + row_count, :], bande...]
    pallas_call x0 -> x4, Pallas kernels: none -> 33 us  [the longest x1 14.2 us: pile(): pl.pallas_call(pile_body, grid=(patches // 2,), in_specs=[smem] * 4 + [wh...]
    slice x7 -> x11, local copies, waits for them, and re-layouts: 29.5 us -> 4.35 us  [the longest x1 1.12 us: on_device(): hi = lax.ppermute(exposures[:, :reach, :], 'section', down)]
    all_gather x0 -> x1, blocking collectives: none -> 24.9 us  [on_device(): everyone = lax.all_gather(labels, ('sy', 'sx', 'core'), axis=0)]
    pad x1, local copies, waits for them, and re-layouts: 14.5 us -> 0.08 us  [on_device(): rows_a = jnp.pad(basis_rows, ((0, 0), (0, 1)))]
    select_n x3 -> x0, other arithmetic: 14.3 us -> none  [the longest x1 14.3 us: on_device(): jnp.where(is_live[:, :, None, None], jnp.take(matched, slot_source, axis=...]
  transfers between devices with their start and end apart: 6 -> 6, of which waited for: 1 -> 3; matrix products, arithmetic and copies ran while one was open for 15% -> 8% of each run, Pallas kernels for 0% -> 0%
where the time goes in v1:
time: 126 us; the launch traced here: 125 us
  waiting for transfers between devices  34.8 us (28%)
  Pallas kernels  33 us (26%)
  blocking collectives  24.9 us (20%)
  starting transfers between devices  16.5 us (13%)
  local copies, waits for them, and re-layouts  11.6 us (9%)
  other arithmetic  3.73 us (3%)
    all_to_all x1, waiting for transfers between devices, on_device(): lax.all_to_all(partial, across, split_axis=0, concat_axis=0, tiled=True)  29.8 us
    all_gather x1, blocking collectives, on_device(): everyone = lax.all_gather(labels, ('sy', 'sx', 'core'), axis=0)  24.9 us
    pallas_call x1, Pallas kernels, pile(): pl.pallas_call(pile_body, grid=(patches // 2,), in_specs=[smem] * 4 + [wh...  14.2 us
    pallas_call x1, Pallas kernels, match(): pl.pallas_call(functools.partial(match_body, taps), grid=(number,), in_sp...  10.5 us
    pallas_call x1, Pallas kernels, detect_of(): pl.pallas_call(functools.partial(detect_body, taps), out_shape=jax.ShapeD...  5.56 us
    all_to_all x1, starting transfers between devices, on_device(): lax.all_to_all(partial, across, split_axis=0, concat_axis=0, tiled=True)  4.82 us
    unnamed x21, local copies, waits for them, and re-layouts  4.45 us
    ppermute x1, starting transfers between devices, on_device(): lo = lax.ppermute(exposures[:, rows - reach:, :], 'section', up)  3.91 us
  transfers between devices with their start and end apart: 6, of which 3 were waited for; matrix products, arithmetic and copies ran while one was open for 8% of the time, Pallas kernels for 0%

profile of v1, /device:TPU:32, one launch (start us, length us, event | category | flops | bytes accessed | tf_op | source)
XLA Modules:
  0.0 125.3 jit_solution(5820462642190368932)
XLA Ops:
  0.6 1.1 fusion.1
  1.8 1.9 %collective-permute-start.1 = (bf16[8,11,1024]{2,1,0:T(8,128)(2,1)S(1)}, bf16[8,11,1024]{2,1,0:T(8,128)(2,1)S(1)}, u32[]{:S(2)}, u32[]{:S(2)}) collective-permute-start(bf16[8,11,1024]{2,1,0:T(8,128)(2,1)S(1)} %get-tuple-element.10), channel_id=1, source_target_pairs={{32,0},{64,32},{96,64},{33,1},{65,33},{97,65},{34,2},{66,34},{98,6... | collective-permute-start | bytes 540680 | tf_op jit(solution)/shard_map/ppermute | solution.py:325
  3.7 3.9 %collective-permute-start = (bf16[8,11,1024]{2,1,0:T(8,128)(2,1)S(1)}, bf16[8,11,1024]{2,1,0:T(8,128)(2,1)S(1)}, u32[]{:S(2)}, u32[]{:S(2)}) collective-permute-start(bf16[8,11,1024]{2,1,0:T(8,128)(2,1)S(1)} %get-tuple-element.11), channel_id=1, source_target_pairs={{0,32},{32,64},{64,96},{1,33},{33,65},{65,97},{2,34},{34,66},{66,9... | collective-permute-start | bytes 540680 | tf_op jit(solution)/shard_map/ppermute | solution.py:324
  7.6 0.7 slice.39
  8.3 0.7 rev.13
  9.0 0.7 slice.40
  9.7 0.1 pad.29.clone
  9.8 0.1 pad.31.clone
  9.9 0.1 copy.28
  10.0 0.1 copy.26
  10.1 0.1 copy.25
  10.2 0.8 copy.31
  11.0 0.1 fusion.2
  11.1 0.1 pad_maximum_fusion.1
  11.2 1.0 multiply_add_fusion.g
  12.1 1.5 %collective-permute-done.lo = bf16[8,11,1024]{2,1,0:T(8,128)(2,1)S(1)} collective-permute-done((bf16[8,11,1024]{2,1,0:T(8,128)(2,1)S(1)}, bf16[8,11,1024]{2,1,0:T(8,128)(2,1)S(1)}, u32[]{:S(2)}, u32[]{:S(2)}) %collective-permute-start) | collective-permute-done | bytes 180256 | tf_op jit(solution)/shard_map/ppermute | solution.py:324
  13.6 0.7 copy-done.9
  14.3 10.5 %match.1.mine = bf16[8,64,1024]{2,1,0:T(8,128)(2,1)} custom-call(s32[8,27]{1,0:T(8,128)} %code.1, f32[27,64]{1,0:T(8,128)} %table.1, f32[27,24,128]{2,1,0:T(8,128)} %multiply_add_fusion.g, bf16[8,64,1024]{2,1,0:T(8,128)(2,1)} %x.11, bf16[8,11,1024]{2,1,0:T(8,128)(2,1)} %copy-done.9, bf16[8,11,1024]{2,1,0:T(8,128)(2,1)} %copy-done.8), custom_call_target="tpu_custom_call" | custom-call | flops 3489660928 | bytes 2097152 | tf_op jit(solution)/shard_map/match/pallas_call | solution.py:127
  24.8 0.1 copy.23
  24.9 0.1 pad_add_fusion.2
  25.0 24.9 %all-gather = s32[256,17]{1,0:T(8,128)S(1)} all-gather(s32[8,17]{1,0:T(8,128)S(1)} %pad_add_fusion.2), channel_id=2, replica_groups=mesh['section'=4,'sy'=4,'sx'=4,'core'=2] {'sy','sx','core'}, dimensions={0}, use_global_device_ids=true | all-gather | bytes 17952 | tf_op jit(solution)/shard_map/all_gather | solution.py:330
  49.9 0.1 pad_add_fusion.1
  50.0 0.7 slice_reduce_fusion.1.weight
  50.7 0.7 fusion.3
  51.3 1.0 copy-done.1
  52.3 14.2 %pile.1 = bf16[16,64,1024]{2,1,0:T(8,128)(2,1)} custom-call(s32[1]{0:T(128)} %bitcast.core, s32[16]{0:T(128)} %slice_reduce_fusion.1.weight, s32[16,8]{1,0:T(8,128)} %get-tuple-element.15.patch, s32[16,8]{1,0:T(8,128)} %get-tuple-element.14.shift, bf16[8,64,1024]{2,1,0:T(8,128)(2,1)} %match.1.mine, bf16[8,64,1024]{2,1,0:T(8,128)(2,1)} %copy-done.1), custom_call_target="tpu_custom_call" | custom-call | tf_op jit(solution)/shard_map/pile/pallas_call | solution.py:207
  66.6 4.8 %all-to-all-start = ((bf16[16,64,1024]{2,1,0:T(8,128)(2,1)}), bf16[16,64,1024]{2,1,0:T(8,128)(2,1)S(1)}, u32[]{:S(2)}, u32[]{:S(2)}) async-start(bf16[16,64,1024]{2,1,0:T(8,128)(2,1)} %pile.1), calls=%async_computation | async-start | bytes 4194304 | tf_op jit(solution)/shard_map/all_to_all | solution.py:355
  71.4 0.1 slice.55
  71.5 0.1 rev.15
  71.6 0.1 slice.51
  71.7 0.1 pad.25.clone
  71.8 0.1 rev.14
  71.9 0.1 slice_reduce_fusion
  72.0 0.7 fusion
  72.7 0.1 copy.30
  72.8 0.1 copy.29
  72.8 1.0 select_reduce_fusion
  73.9 1.2 concatenate.25
  75.1 0.1 pad_maximum_fusion
  75.2 29.8 %all-to-all-done.parts = bf16[16,64,1024]{2,1,0:T(8,128)(2,1)S(1)} async-done(((bf16[16,64,1024]{2,1,0:T(8,128)(2,1)}), bf16[16,64,1024]{2,1,0:T(8,128)(2,1)S(1)}, u32[]{:S(2)}, u32[]{:S(2)}) %all-to-all-start) | async-done | bytes 2097184 | tf_op jit(solution)/shard_map/all_to_all | solution.py:355
  105.1 1.3 %copy-done = bf16[16,64,1024]{2,1,0:T(8,128)(2,1)} copy-done((bf16[16,64,1024]{2,1,0:T(8,128)(2,1)}, bf16[16,64,1024]{2,1,0:T(8,128)(2,1)S(1)}, u32[]{:S(2)}) %copy-start) | copy-done | bytes 2097176
  106.4 2.7 %coadd.1 = (f32[64,1024]{1,0:T(8,128)}, bf16[20,1024]{1,0:T(8,128)(2,1)}, bf16[20,1024]{1,0:T(8,128)(2,1)}) custom-call(bf16[16,64,1024]{2,1,0:T(8,128)(2,1)} %copy-done, f32[1,1024]{1,0:T(1,128)} %bitcast.11), custom_call_target="tpu_custom_call" | custom-call | tf_op jit(solution)/shard_map/coadd/pallas_call | solution.py:244
  109.1 3.8 %collective-permute-start.3 = (bf16[20,1024]{1,0:T(8,128)(2,1)}, bf16[20,1024]{1,0:T(8,128)(2,1)S(1)}, u32[]{:S(2)}, u32[]{:S(2)}) collective-permute-start(bf16[20,1024]{1,0:T(8,128)(2,1)} %get-tuple-element.6), channel_id=1, source_target_pairs={{0,32},{32,64},{64,96},{1,33},{33,65},{65,97},{2,34},{34,66},{66,9... | collective-permute-start | bytes 122888 | tf_op jit(solution)/shard_map/ppermute | solution.py:357
  112.9 2.0 %collective-permute-start.4 = (bf16[20,1024]{1,0:T(8,128)(2,1)}, bf16[20,1024]{1,0:T(8,128)(2,1)S(1)}, u32[]{:S(2)}, u32[]{:S(2)}) collective-permute-start(bf16[20,1024]{1,0:T(8,128)(2,1)} %get-tuple-element.7), channel_id=1, source_target_pairs={{32,0},{64,32},{96,64},{33,1},{65,33},{97,65},{34,2},{66,34},{98,6... | collective-permute-start | bytes 122888 | tf_op jit(solution)/shard_map/ppermute | solution.py:358
  114.9 0.6 pad_add_fusion.profile
  115.6 3.5 %collective-permute-done.4.hi = bf16[20,1024]{1,0:T(8,128)(2,1)S(1)} collective-permute-done((bf16[20,1024]{1,0:T(8,128)(2,1)}, bf16[20,1024]{1,0:T(8,128)(2,1)S(1)}, u32[]{:S(2)}, u32[]{:S(2)}) %collective-permute-start.4) | collective-permute-done | bytes 40992 | tf_op jit(solution)/shard_map/ppermute | solution.py:358
  119.1 0.6 copy-done.4
  119.7 5.6 %detect.1 = f32[3,64,1024]{2,1,0:T(8,128)} custom-call(f32[3,42,128]{2,1,0:T(8,128)} %pad_add_fusion.profile, f32[64,1024]{1,0:T(8,128)} %get-tuple-element.5.x, bf16[20,1024]{1,0:T(8,128)(2,1)} %copy-done.3, bf16[20,1024]{1,0:T(8,128)(2,1)} %copy-done.4), custom_call_target="tpu_custom_call" | custom-call | tf_op jit(solution)/shard_map/detect/pallas_call | solution.py:288
  (30 shorter events, 0.1 us)
Async XLA Ops:
  1.8 10.4 %collective-permute-start.1 = (bf16[8,11,1024]{2,1,0:T(8,128)(2,1)S(1)}, bf16[8,11,1024]{2,1,0:T(8,128)(2,1)S(1)}, u32[]{:S(2)}, u32[]{:S(2)}) collective-permute-start(bf16[8,11,1024]{2,1,0:T(8,128)(2,1)S(1)} %get-tuple-element.10), channel_id=1, source_target_pairs={{32,0},{64,32},{96,64},{33,1},{65,33},{97,65},{34,2},{66,34},{98,6... | collective-permute-start | bytes 540680 | tf_op jit(solution)/shard_map/ppermute | solution.py:325
  3.7 9.9 %collective-permute-start = (bf16[8,11,1024]{2,1,0:T(8,128)(2,1)S(1)}, bf16[8,11,1024]{2,1,0:T(8,128)(2,1)S(1)}, u32[]{:S(2)}, u32[]{:S(2)}) collective-permute-start(bf16[8,11,1024]{2,1,0:T(8,128)(2,1)S(1)} %get-tuple-element.11), channel_id=1, source_target_pairs={{0,32},{32,64},{64,96},{1,33},{33,65},{65,97},{2,34},{34,66},{66,9... | collective-permute-start | bytes 540680 | tf_op jit(solution)/shard_map/ppermute | solution.py:324
  12.1 12.7 %copy-start.7 = (s32[8]{0:T(128)S(1)}, s32[8]{0:T(128)}, u32[]{:S(2)}) copy-start(s32[8]{0:T(128)} %param.14) | copy-start | bytes 100
  12.1 12.8 %copy-start.5 = (s32[8,8]{1,0:T(8,128)S(1)}, s32[8,8]{1,0:T(8,128)}, u32[]{:S(2)}) copy-start(s32[8,8]{1,0:T(8,128)} %param.16) | copy-start | bytes 772
  12.1 12.8 %copy-start.6 = (s32[8,8]{1,0:T(8,128)S(1)}, s32[8,8]{1,0:T(8,128)}, u32[]{:S(2)}) copy-start(s32[8,8]{1,0:T(8,128)} %param.15) | copy-start | bytes 772
  12.1 1.5 %copy-start.8 = (bf16[8,11,1024]{2,1,0:T(8,128)(2,1)}, bf16[8,11,1024]{2,1,0:T(8,128)(2,1)S(1)}, u32[]{:S(2)}) copy-start(bf16[8,11,1024]{2,1,0:T(8,128)(2,1)S(1)} %collective-permute-done.1.hi) | copy-start | bytes 540676
  13.6 0.7 copy-start.9
  24.8 26.5 %collective-permute-start.2 = (bf16[8,64,1024]{2,1,0:T(8,128)(2,1)}, bf16[8,64,1024]{2,1,0:T(8,128)(2,1)S(1)}, u32[]{:S(2)}, u32[]{:S(2)}) collective-permute-start(bf16[8,64,1024]{2,1,0:T(8,128)(2,1)} %match.1.mine), channel_id=1, source_target_pairs={{0,1},{1,0},{2,3},{3,2},{4,5},{5,4},{6,7},{7,6},{8,9},{9,8},{10,11... | collective-permute-start | bytes 3145736 | tf_op jit(solution)/shard_map/ppermute | solution.py:351
  51.3 1.0 copy-start.1
  66.6 4.8 %copy-start.2 = (bf16[3,41,41]{2,1,0:T(8,128)(2,1)S(1)}, bf16[3,41,41]{2,1,0:T(8,128)(2,1)}, u32[]{:S(2)}) copy-start(bf16[3,41,41]{2,1,0:T(8,128)(2,1)} %param.17) | copy-start | bytes 30262
  66.6 38.5 %all-to-all-start = ((bf16[16,64,1024]{2,1,0:T(8,128)(2,1)}), bf16[16,64,1024]{2,1,0:T(8,128)(2,1)S(1)}, u32[]{:S(2)}, u32[]{:S(2)}) async-start(bf16[16,64,1024]{2,1,0:T(8,128)(2,1)} %pile.1), calls=%async_computation | async-start | bytes 4194304 | tf_op jit(solution)/shard_map/all_to_all | solution.py:355
  105.1 1.3 %copy-start = (bf16[16,64,1024]{2,1,0:T(8,128)(2,1)}, bf16[16,64,1024]{2,1,0:T(8,128)(2,1)S(1)}, u32[]{:S(2)}) copy-start(bf16[16,64,1024]{2,1,0:T(8,128)(2,1)S(1)} %all-to-all-done.parts) | copy-start | bytes 6291460
  109.1 6.5 %collective-permute-start.3 = (bf16[20,1024]{1,0:T(8,128)(2,1)}, bf16[20,1024]{1,0:T(8,128)(2,1)S(1)}, u32[]{:S(2)}, u32[]{:S(2)}) collective-permute-start(bf16[20,1024]{1,0:T(8,128)(2,1)} %get-tuple-element.6), channel_id=1, source_target_pairs={{0,32},{32,64},{64,96},{1,33},{33,65},{65,97},{2,34},{34,66},{66,9... | collective-permute-start | bytes 122888 | tf_op jit(solution)/shard_map/ppermute | solution.py:357
  112.9 6.2 %collective-permute-start.4 = (bf16[20,1024]{1,0:T(8,128)(2,1)}, bf16[20,1024]{1,0:T(8,128)(2,1)S(1)}, u32[]{:S(2)}, u32[]{:S(2)}) collective-permute-start(bf16[20,1024]{1,0:T(8,128)(2,1)} %get-tuple-element.7), channel_id=1, source_target_pairs={{32,0},{64,32},{96,64},{33,1},{65,33},{97,65},{34,2},{66,34},{98,6... | collective-permute-start | bytes 122888 | tf_op jit(solution)/shard_map/ppermute | solution.py:358
  115.6 3.5 %copy-start.3 = (bf16[20,1024]{1,0:T(8,128)(2,1)}, bf16[20,1024]{1,0:T(8,128)(2,1)S(1)}, u32[]{:S(2)}) copy-start(bf16[20,1024]{1,0:T(8,128)(2,1)S(1)} %collective-permute-done.3.lo) | copy-start | bytes 122884
  119.1 0.6 copy-start.4

commit v2 on v1

v2 whole, which is shorter than its diff:
```python
import functools

import jax
import jax.numpy as jnp
from jax import lax
from jax.experimental import pallas as pl
from jax.experimental.pallas import tpu as pltpu
from jax.sharding import Mesh, PartitionSpec as P

f32 = jnp.float32
bf16 = jnp.bfloat16

lanes = 128
half = 64
group = 4
vmem_bytes = 56 * 1024 * 1024


def neighbours(count):
    up = [(i, i + 1) for i in range(count - 1)]
    return up, [(b, a) for a, b in up]


def profile_rows(profile, taps):
    lead = profile.shape[:-1]
    zeros = lambda n: jnp.zeros(lead + (n,), profile.dtype)
    first = jnp.concatenate(
        [profile[..., :1], zeros(lanes - taps), profile[..., :0:-1]], axis=-1
    )
    second = jnp.concatenate(
        [zeros(half - taps + 1), profile[..., ::-1], zeros(lanes - half - 1)], axis=-1
    )
    return first, second


def pad_rows(rows, low, high):
    return jnp.pad(rows, [(0, 0)] * (rows.ndim - 2) + [(low, high), (0, 0)])


def lane_ids(rows):
    return lax.broadcasted_iota(jnp.int32, (rows, lanes), 1)


def band_mask(depth, taps):
    k = lax.broadcasted_iota(jnp.int32, (depth, lanes), 0)
    gap = k - lane_ids(depth) % half
    return (gap >= 0) & (gap < taps)


def band_tile(row, mask):
    depth = mask.shape[0]
    wide = jnp.broadcast_to(row, (depth, lanes))
    turned = pltpu.roll(wide, 0, 1, stride=1, stride_axis=0)
    return jnp.where(mask, turned, 0.0).astype(bf16)


def put_frame(frame, tiles, row, reach):
    count = len(tiles)
    rows = tiles[0].shape[0]
    lane = lane_ids(rows)
    zero = jnp.zeros((rows, lanes), f32)
    right = [pltpu.roll(t, reach, 1).astype(f32) for t in tiles]
    left = [pltpu.roll(t, half + reach, 1).astype(f32) for t in tiles]
    for m in range(count):
        before = right[m - 1] if m else zero
        frame[0, m, row : row + rows, :] = jnp.where(lane < reach, before, right[m])
        after = left[m + 1] if m + 1 < count else zero
        frame[1, m, row : row + rows, :] = jnp.where(lane < half + reach, left[m], after)


def put_lhs(lhs, frame, spans, row):
    tiles = frame.shape[1]
    for t in range(spans):
        for par in range(2):
            for m in range(tiles):
                at = (par * tiles + m) * 16
                piece = frame[par, m, pl.ds(row + t, 16, stride=group), :]
                lhs[at : at + 16, t * lanes : (t + 1) * lanes] = piece.astype(bf16)


def split_rows(even, odd, lane):
    first = jnp.where(lane < half, even, pltpu.roll(odd, half, 1))
    second = jnp.where(lane < half, pltpu.roll(even, half, 1), odd)
    return first, second


def match_body(taps, code, table, g, x, lo, hi, out, frame, lhs, w):
    reach = taps // 2
    number, _, cols = x.shape
    count = cols // lanes
    depth = 96
    w[...] = jnp.zeros_like(w)
    mask = band_mask(depth, taps)
    lane = lane_ids(16)

    def one(e, _):
        total = jnp.zeros(g.shape[1:], f32)
        for b in range(g.shape[0]):
            total = total + table[b, code[e, b]] * g[b]
        total = total.astype(bf16).astype(f32)
        for u in range(taps + 1):
            tile = band_tile(total[u : u + 1, :], mask)
            w[u * lanes : u * lanes + depth, 0:lanes] = tile
            w[(u + 2) * lanes : (u + 2) * lanes + depth, lanes : 2 * lanes] = tile
        for ref, row in ((lo, 16 - reach), (x, 16), (hi, 80)):
            rows = ref[e]
            put_frame(frame, [rows[:, m * lanes : (m + 1) * lanes] for m in range(count)], row, reach)
        put_lhs(lhs, frame, taps + 3, 16 - reach)
        acc = jnp.dot(lhs[...], w[...], preferred_element_type=f32)
        for m in range(count):
            for h in range(2):
                cut = slice(h * lanes, (h + 1) * lanes)
                even = acc[m * 16 : m * 16 + 16, cut]
                odd = acc[(count + m) * 16 : (count + m) * 16 + 16, cut]
                for b, part in enumerate(split_rows(even, odd, lane)):
                    at = (2 * h + b) * 16
                    out[e, at : at + 16, m * lanes : (m + 1) * lanes] = part.astype(bf16)
        return 0

    lax.fori_loop(0, number, one, 0)


def match(code, table, g, x, lo, hi, taps):
    number, rows, cols = x.shape
    smem = pl.BlockSpec(memory_space=pltpu.SMEM)
    vmem = pl.BlockSpec(memory_space=pltpu.VMEM)
    spans = taps + 3
    return pl.pallas_call(
        functools.partial(match_body, taps),
        in_specs=[smem, smem, vmem, vmem, vmem, vmem],
        out_specs=vmem,
        out_shape=jax.ShapeDtypeStruct((number, rows, cols), bf16),
        scratch_shapes=[
            pltpu.VMEM((2, cols // lanes, 96, lanes), f32),
            pltpu.VMEM((256, spans * lanes), bf16),
            pltpu.VMEM((spans * lanes, 256), bf16),
        ],
        compiler_params=pltpu.CompilerParams(vmem_limit_bytes=vmem_bytes),
        cost_estimate=pl.CostEstimate(
            flops=number * 2 * 256 * 256 * spans * lanes, bytes_accessed=4 * x.size, transcendentals=0
        ),
        name="match",
    )(code, table, g, x, lo, hi)


def pile_body(core, mine_labels, other_labels, mine, other, out, counts, source, offset, scale, planes):
    number, rows, cols = mine.shape
    tiles = cols // lanes
    per = (mine_labels.shape[1] - 1) // 2
    patches = counts.shape[0]
    slots = 8

    def clear(p, _):
        counts[p] = 0
        for s in range(slots):
            source[p * slots + s] = 0
            offset[p * slots + s] = 0
            scale[p * slots + s] = 0.0
        return 0

    lax.fori_loop(0, patches, clear, 0)

    def enter(base, labels):
        def one(e, _):
            weight = labels[e, 0].astype(f32)
            for k in range(per):
                p = labels[e, 1 + k]
                at = counts[p]
                source[p * slots + at] = base + e
                offset[p * slots + at] = labels[e, 1 + per + k]
                scale[p * slots + at] = weight
                counts[p] = at + 1
            return 0

        lax.fori_loop(0, number, one, 0)

    enter(0, mine_labels)
    enter(number, other_labels)
    planes[0:number] = mine[...]
    planes[number:] = other[...]
    lane = lane_ids(16)

    def patch(i, _):
        p = 2 * i + core[0]

        def some(used):
            entries = [
                (source[p * slots + s], offset[p * slots + s], scale[p * slots + s])
                for s in range(used)
            ]
            for c in range(rows // 16):
                total = [jnp.zeros((16, lanes), f32)] * tiles
                for e, o, weight in entries:
                    keep = lane < o
                    before = jnp.zeros((16, lanes), f32)
                    for m in range(tiles):
                        piece = planes[e, c * 16 : c * 16 + 16, m * lanes : (m + 1) * lanes]
                        turned = pltpu.roll(piece, o, 1).astype(f32)
                        total[m] = total[m] + weight * jnp.where(keep, before, turned)
                        before = turned
                for m in range(tiles):
                    at = m * rows + c * 16
                    out[i, at : at + 16, :] = total[m].astype(bf16)
            cover = jnp.zeros((16, lanes), f32)
            whole = jnp.zeros((16, lanes), f32)
            for e, o, weight in entries:
                cover = cover + jnp.where(lane < o, 0.0, weight)
                whole = whole + weight
            row = lax.broadcasted_iota(jnp.int32, (16, lanes), 0)
            out[i, tiles * rows : tiles * rows + 16, :] = jnp.where(row == 0, cover, whole).astype(bf16)

        used = counts[p]
        for top in range(2, slots + 1, 2):
            low = top - 2 if top > 2 else -1

            @pl.when((used > low) & (used <= top))
            def _():
                some(top)

        return 0

    lax.fori_loop(0, patches // 2, patch, 0)


def pile(core, mine_labels, other_labels, mine, other, patches):
    number, rows, cols = mine.shape
    smem = pl.BlockSpec(memory_space=pltpu.SMEM)
    vmem = pl.BlockSpec(memory_space=pltpu.VMEM)
    length = cols // lanes * rows + 16
    return pl.pallas_call(
        pile_body,
        in_specs=[smem] * 3 + [vmem] * 2,
        out_specs=vmem,
        out_shape=jax.ShapeDtypeStruct((patches // 2, length, lanes), bf16),
        scratch_shapes=[
            pltpu.SMEM((patches,), jnp.int32),
            pltpu.SMEM((patches * 8,), jnp.int32),
            pltpu.SMEM((patches * 8,), jnp.int32),
            pltpu.SMEM((patches * 8,), f32),
            pltpu.VMEM((2 * number, rows, cols), bf16),
        ],
        compiler_params=pltpu.CompilerParams(vmem_limit_bytes=vmem_bytes),
        name="pile",
    )(core, mine_labels, other_labels, mine, other)


def coadd_body(reach, parts, coadd, low, high, stage):
    count = parts.shape[0]
    rows, cols = coadd.shape
    tiles = cols // lanes

    def add(at):
        total = parts[0, at : at + 16, :].astype(f32)
        for n in range(1, count):
            total = total + parts[n, at : at + 16, :].astype(f32)
        return total

    cover = add(tiles * rows)
    scales = [1.0 / jnp.maximum(cover[r : r + 1, :], 1.0) for r in (0, 1)]
    for m in range(tiles):
        for b in range(group):
            value = add(m * rows + b * 16) * scales[min(m, 1)]
            stage[m, pl.ds(b, 16, stride=group), :] = value
    for m in range(tiles):
        cut = slice(m * lanes, (m + 1) * lanes)
        coadd[:, cut] = stage[m]
        low[:, cut] = stage[m, 0:reach, :].astype(bf16)
        high[:, cut] = stage[m, rows - reach : rows, :].astype(bf16)


def coadd_of(parts, rows, cols, reach):
    edge = jax.ShapeDtypeStruct((reach, cols), bf16)
    return pl.pallas_call(
        functools.partial(coadd_body, reach),
        out_shape=(jax.ShapeDtypeStruct((rows, cols), f32), edge, edge),
        scratch_shapes=[pltpu.VMEM((cols // lanes, rows, lanes), f32)],
        compiler_params=pltpu.CompilerParams(vmem_limit_bytes=vmem_bytes),
        name="coadd",
    )(parts)


def detect_body(taps, profile, x, lo, hi, out, frame, lhs, w, stage):
    reach = taps // 2
    rows, cols = x.shape
    count = cols // lanes
    scales = profile.shape[0]
    depth = 112
    mask = band_mask(depth, taps)
    w[...] = jnp.zeros_like(w)
    for s in range(scales):
        for u in range(taps + 1):
            tile = band_tile(profile[s, u : u + 1, :], mask)
            w[u * lanes : u * lanes + depth, 2 * s * lanes : (2 * s + 1) * lanes] = tile
            w[(u + 2) * lanes : (u + 2) * lanes + depth, (2 * s + 1) * lanes : (2 * s + 2) * lanes] = tile
    for ref, row in ((lo, 24 - reach), (x, 24), (hi, 24 + rows)):
        value = ref[...].astype(bf16)
        put_frame(frame, [value[:, m * lanes : (m + 1) * lanes] for m in range(count)], row, reach)
    put_lhs(lhs, frame, taps + 3, 24 - reach)
    lane = lane_ids(16)
    for s in range(scales):
        acc = jnp.dot(
            lhs[...], w[:, 2 * s * lanes : (2 * s + 2) * lanes], preferred_element_type=f32
        )
        for m in range(count):
            for h in range(2):
                even = acc[m * 16 : m * 16 + 16, h * lanes : (h + 1) * lanes]
                odd = acc[(count + m) * 16 : (count + m) * 16 + 16, h * lanes : (h + 1) * lanes]
                for b, part in enumerate(split_rows(even, odd, lane)):
                    stage[m, pl.ds(2 * h + b, 16, stride=group), :] = part
            out[s, :, m * lanes : (m + 1) * lanes] = stage[m]


def detect_of(profile, x, lo, hi, taps):
    rows, cols = x.shape
    scales = profile.shape[0]
    spans = taps + 3
    return pl.pallas_call(
        functools.partial(detect_body, taps),
        out_shape=jax.ShapeDtypeStruct((scales, rows, cols), f32),
        scratch_shapes=[
            pltpu.VMEM((2, cols // lanes, 24 + rows + 24, lanes), f32),
            pltpu.VMEM((256, spans * lanes), bf16),
            pltpu.VMEM((spans * lanes, scales * 256), bf16),
            pltpu.VMEM((cols // lanes, rows, lanes), f32),
        ],
        compiler_params=pltpu.CompilerParams(vmem_limit_bytes=vmem_bytes),
        name="detect",
    )(profile, x, lo, hi)


def on_device(
    exposures,
    coef_code,
    coef_table,
    basis_rows,
    basis_cols,
    exposure_weight,
    intersection_patch,
    intersection_shift,
    psf_kernels,
):
    number, rows, cols = exposures.shape
    taps = basis_rows.shape[1]
    reach = taps // 2
    wide = psf_kernels.shape[-1]
    wide_reach = wide // 2
    sections = lax.axis_size("section")
    across = ("sy", "sx")
    patches = lax.axis_size("sy") * lax.axis_size("sx") * 2
    core = lax.axis_index("core")
    up, down = neighbours(sections)

    lo = lax.ppermute(exposures[:, rows - reach :, :], "section", up)
    hi = lax.ppermute(exposures[:, :reach, :], "section", down)

    labels = jnp.concatenate(
        [exposure_weight[:, None], intersection_patch, intersection_shift], axis=1
    )
    swap = [(0, 1), (1, 0)]
    other_labels = lax.ppermute(labels, "core", swap)

    cols_a, cols_b = profile_rows(basis_cols, taps)
    rows_a = jnp.pad(basis_rows, ((0, 0), (0, 1)))
    rows_b = jnp.pad(basis_rows, ((0, 0), (1, 0)))
    g = rows_a[:, :, None] * cols_a[:, None, :] + rows_b[:, :, None] * cols_b[:, None, :]
    psf_a, psf_b = profile_rows(psf_kernels.astype(f32), wide)
    profile = pad_rows(psf_a, 0, 1) + pad_rows(psf_b, 1, 0)

    matched = match(coef_code, coef_table, g, exposures, lo, hi, taps)
    other = lax.ppermute(matched, "core", swap)
    partial = pile(core[None], labels, other_labels, matched, other, patches)
    parts = lax.all_to_all(partial, across, split_axis=0, concat_axis=0, tiled=True)
    coadd, low, high = coadd_of(parts, rows, cols, wide_reach)
    lo = lax.ppermute(high, "section", up)
    hi = lax.ppermute(low, "section", down)
    detect = detect_of(profile, coadd, lo, hi, wide)
    return (coadd[None], detect[None])


def solution(mesh):
    sections, sky = mesh.devices.shape
    grid = Mesh(mesh.devices.reshape(sections, 4, sky // 8, 2), ("section", "sy", "sx", "core"))
    sky = ("sy", "sx", "core")
    return jax.shard_map(
        on_device,
        mesh=grid,
        in_specs=(
            P(sky, "section", None),
            P(sky, None),
            P(),
            P(),
            P(),
            P(sky),
            P(sky, None),
            P(sky, None),
            P(),
        ),
        out_specs=(P(sky, "section", None), P(sky, None, "section", None)),
        check_vma=False,
    )
```

time: 126 us -> 102 us (0.81)
  blocking collectives: 24.9 us -> 0 us
  waiting for transfers between devices: 34.8 us -> 43.2 us
  Pallas kernels: 33 us -> 27.3 us
  local copies, waits for them, and re-layouts: 11.6 us -> 8.67 us
  starting transfers between devices: 16.5 us -> 19.4 us
  other arithmetic: 3.73 us -> 1.86 us
    all_gather x1 -> x0, blocking collectives: 24.9 us -> none  [on_device(): everyone = lax.all_gather(labels, ('sy', 'sx', 'core'), axis=0)]
    pallas_call x2, Pallas kernels: 24.7 us -> 19.1 us  [the longest x1 10.8 us: match(): pl.pallas_call(functools.partial(match_body, taps), in_specs=[smem, smem,...]
    all_to_all x1, waiting for transfers between devices: 29.8 us -> 34.7 us  [on_device(): lax.all_to_all(partial, across, split_axis=0, concat_axis=0, tiled=True)]
    ppermute x1, waiting for transfers between devices: 0.01 us -> 3.08 us  [on_device(): hi = lax.ppermute(exposures[:, :reach, :], 'section', down)]
    all_to_all x1, starting transfers between devices: 4.82 us -> 7.17 us  [on_device(): lax.all_to_all(partial, across, split_axis=0, concat_axis=0, tiled=True)]
    ppermute x1 -> x2, waiting for transfers between devices: 0.01 us -> 2.16 us  [the longest x1 1.96 us: on_device(): other_labels = lax.ppermute(labels, 'core', swap)]
    reduce_sum x2 -> x0, other arithmetic: 1.79 us -> none  [the longest x1 1.04 us: on_device(): jnp.sum(jnp.where(column[:, None, None] >= flat[None, :, 1 + per:], stren...]
    slice x5 -> x0, local copies, waits for them, and re-layouts: 1.64 us -> none  [the longest x1 0.7 us: on_device(): both[:, 0]]
  transfers between devices with their start and end apart: 6 -> 7, of which waited for: 3 -> 5; matrix products, arithmetic and copies ran while one was open for 8% -> 6% of each run, Pallas kernels for 0% -> 0%
where the time goes in v2:
time: 102 us; the launch traced here: 101 us
  waiting for transfers between devices  43.2 us (42%)
  Pallas kernels  27.3 us (27%)
  starting transfers between devices  19.4 us (19%)
  local copies, waits for them, and re-layouts  8.67 us (8%)
  other arithmetic  1.86 us (2%)
    all_to_all x1, waiting for transfers between devices, on_device(): lax.all_to_all(partial, across, split_axis=0, concat_axis=0, tiled=True)  34.7 us
    pallas_call x1, Pallas kernels, match(): pl.pallas_call(functools.partial(match_body, taps), in_specs=[smem, smem,...  10.8 us
    pallas_call x1, Pallas kernels, pile(): pl.pallas_call(pile_body, in_specs=[smem] * 3 + [vmem] * 2, out_specs=vme...  8.34 us
    all_to_all x1, starting transfers between devices, on_device(): lax.all_to_all(partial, across, split_axis=0, concat_axis=0, tiled=True)  7.17 us
    pallas_call x1, Pallas kernels, detect_of(): pl.pallas_call(functools.partial(detect_body, taps), out_shape=jax.ShapeD...  5.57 us
    unnamed x25, local copies, waits for them, and re-layouts  4.48 us
    ppermute x1, starting transfers between devices, on_device(): lo = lax.ppermute(exposures[:, rows - reach:, :], 'section', up)  3.83 us
    ppermute x1, starting transfers between devices, on_device(): lo = lax.ppermute(high, 'section', up)  3.52 us
  transfers between devices with their start and end apart: 7, of which 5 were waited for; matrix products, arithmetic and copies ran while one was open for 6% of the time, Pallas kernels for 0%

profile of v2, /device:TPU:32, one launch (start us, length us, event | category | flops | bytes accessed | tf_op | source)
XLA Modules:
  0.0 101.3 jit_solution(3104225141179514359)
XLA Ops:
  0.6 1.1 %fusion = (bf16[8,11,1024]{2,1,0:T(8,128)(2,1)S(1)}, bf16[8,11,1024]{2,1,0:T(8,128)(2,1)S(1)}) fusion(bf16[8,64,1024]{2,1,0:T(8,128)(2,1)} %x.9), kind=kLoop, calls=%fused_computation.7 | loop fusion | bytes 720896 | tf_op jit(solution)/shard_map/slice | solution.py:354
  1.8 3.8 %collective-permute-start.1 = (bf16[8,11,1024]{2,1,0:T(8,128)(2,1)S(1)}, bf16[8,11,1024]{2,1,0:T(8,128)(2,1)S(1)}, u32[]{:S(2)}, u32[]{:S(2)}) collective-permute-start(bf16[8,11,1024]{2,1,0:T(8,128)(2,1)S(1)} %get-tuple-element.9), channel_id=1, source_target_pairs={{0,32},{32,64},{64,96},{1,33},{33,65},{65,97},{2,34},{34,66},{66,9... | collective-permute-start | bytes 540680 | tf_op jit(solution)/shard_map/ppermute | solution.py:353
  5.6 2.0 %collective-permute-start.2 = (bf16[8,11,1024]{2,1,0:T(8,128)(2,1)S(1)}, bf16[8,11,1024]{2,1,0:T(8,128)(2,1)S(1)}, u32[]{:S(2)}, u32[]{:S(2)}) collective-permute-start(bf16[8,11,1024]{2,1,0:T(8,128)(2,1)S(1)} %get-tuple-element.8), channel_id=1, source_target_pairs={{32,0},{64,32},{96,64},{33,1},{65,33},{97,65},{34,2},{66,34},{98,6... | collective-permute-start | bytes 540680 | tf_op jit(solution)/shard_map/ppermute | solution.py:354
  7.6 0.7 slice.19
  8.3 0.7 rev.13
  9.1 0.7 slice.18
  9.8 0.1 copy.14
  9.9 0.1 copy.16
  10.0 0.1 copy.13
  10.1 0.1 pad.28.clone
  10.1 0.1 pad.30.clone
  10.2 0.8 copy.17
  11.0 0.1 fusion.1
  11.1 0.1 pad_maximum_fusion.1
  11.2 1.0 multiply_add_fusion.g
  12.1 0.0 collective-permute-done.1.lo
  12.2 0.0 copy-start.10
  12.2 3.1 %collective-permute-done.2.hi = bf16[8,11,1024]{2,1,0:T(8,128)(2,1)S(1)} collective-permute-done((bf16[8,11,1024]{2,1,0:T(8,128)(2,1)S(1)}, bf16[8,11,1024]{2,1,0:T(8,128)(2,1)S(1)}, u32[]{:S(2)}, u32[]{:S(2)}) %collective-permute-start.2) | collective-permute-done | bytes 180256 | tf_op jit(solution)/shard_map/ppermute | solution.py:354
  15.2 0.0 copy-done.10
  15.3 0.7 copy-done.11
  16.0 10.8 %match.1.mine = bf16[8,64,1024]{2,1,0:T(8,128)(2,1)} custom-call(s32[8,27]{1,0:T(8,128)} %code.1, f32[27,64]{1,0:T(8,128)} %table.1, f32[27,24,128]{2,1,0:T(8,128)} %multiply_add_fusion.g, bf16[8,64,1024]{2,1,0:T(8,128)(2,1)} %x.9, bf16[8,11,1024]{2,1,0:T(8,128)(2,1)} %copy-done.10, bf16[8,11,1024]{2,1,0:T(8,128)(2,1)} %copy-done.11), custom_call_target="tpu_custom_call" | custom-call | flops 3489660928 | bytes 2097152 | tf_op jit(solution)/shard_map/match/pallas_call | solution.py:128
  26.8 0.0 collective-permute-start.3
  26.8 0.1 copy.11
  26.9 0.1 pad_add_fusion.1.mine_labels
  26.9 0.5 collective-permute-start
  27.5 2.0 %collective-permute-done.other_labels = s32[8,17]{1,0:T(8,128)S(1)} collective-permute-done((s32[8,17]{1,0:T(8,128)S(1)}, s32[8,17]{1,0:T(8,128)S(1)}, u32[]{:S(2)}, u32[]{:S(2)}) %collective-permute-start) | collective-permute-done | bytes 576 | tf_op jit(solution)/shard_map/ppermute | solution.py:360
  29.4 0.2 collective-permute-done.3.other
  29.7 0.4 copy-done.6
  30.0 0.6 copy-done.1
  30.6 8.3 %pile.1 = bf16[16,528,128]{2,1,0:T(8,128)(2,1)} custom-call(s32[1]{0:T(128)} %bitcast.core, s32[8,17]{1,0:T(8,128)} %copy-done.5, s32[8,17]{1,0:T(8,128)} %copy-done.6, bf16[8,64,1024]{2,1,0:T(8,128)(2,1)} %match.1.mine, bf16[8,64,1024]{2,1,0:T(8,128)(2,1)} %copy-done.1), custom_call_target="tpu_custom_call" | custom-call | tf_op jit(solution)/shard_map/pile/pallas_call | solution.py:230
  38.9 7.2 %all-to-all-start = ((bf16[16,528,128]{2,1,0:T(8,128)(2,1)}), bf16[16,528,128]{2,1,0:T(8,128)(2,1)S(1)}, u32[]{:S(2)}, u32[]{:S(2)}) async-start(bf16[16,528,128]{2,1,0:T(8,128)(2,1)} %pile.1), calls=%async_computation | async-start | bytes 4325376 | tf_op jit(solution)/shard_map/all_to_all | solution.py:372
  46.1 0.0 copy-done.2
  46.1 0.1 slice.25
  46.2 0.1 rev.15
  46.3 0.1 rev.14
  46.4 0.1 pad.24.clone
  46.5 0.1 pad_maximum_fusion
  46.6 34.7 %all-to-all-done.parts = bf16[16,528,128]{2,1,0:T(8,128)(2,1)S(1)} async-done(((bf16[16,528,128]{2,1,0:T(8,128)(2,1)}), bf16[16,528,128]{2,1,0:T(8,128)(2,1)S(1)}, u32[]{:S(2)}, u32[]{:S(2)}) %all-to-all-start) | async-done | bytes 2162720 | tf_op jit(solution)/shard_map/all_to_all | solution.py:372
  81.4 1.4 %copy-done = bf16[16,528,128]{2,1,0:T(8,128)(2,1)} copy-done((bf16[16,528,128]{2,1,0:T(8,128)(2,1)}, bf16[16,528,128]{2,1,0:T(8,128)(2,1)S(1)}, u32[]{:S(2)}) %copy-start) | copy-done | bytes 2162712
  82.7 2.6 %coadd.1 = (f32[64,1024]{1,0:T(8,128)}, bf16[20,1024]{1,0:T(8,128)(2,1)}, bf16[20,1024]{1,0:T(8,128)(2,1)}) custom-call(bf16[16,528,128]{2,1,0:T(8,128)(2,1)} %copy-done), custom_call_target="tpu_custom_call" | custom-call | tf_op jit(solution)/shard_map/coadd/pallas_call | solution.py:273
  85.3 3.5 %collective-permute-start.4 = (bf16[20,1024]{1,0:T(8,128)(2,1)}, bf16[20,1024]{1,0:T(8,128)(2,1)S(1)}, u32[]{:S(2)}, u32[]{:S(2)}) collective-permute-start(bf16[20,1024]{1,0:T(8,128)(2,1)} %get-tuple-element.6), channel_id=1, source_target_pairs={{0,32},{32,64},{64,96},{1,33},{33,65},{65,97},{2,34},{34,66},{66,9... | collective-permute-start | bytes 122888 | tf_op jit(solution)/shard_map/ppermute | solution.py:374
  88.9 2.3 %collective-permute-start.5 = (bf16[20,1024]{1,0:T(8,128)(2,1)}, bf16[20,1024]{1,0:T(8,128)(2,1)S(1)}, u32[]{:S(2)}, u32[]{:S(2)}) collective-permute-start(bf16[20,1024]{1,0:T(8,128)(2,1)} %get-tuple-element.7), channel_id=1, source_target_pairs={{32,0},{64,32},{96,64},{33,1},{65,33},{97,65},{34,2},{66,34},{98,6... | collective-permute-start | bytes 122888 | tf_op jit(solution)/shard_map/ppermute | solution.py:375
  91.2 0.6 pad_add_fusion.profile
  91.8 0.0 collective-permute-done.4.lo
  91.8 3.2 %collective-permute-done.5.hi = bf16[20,1024]{1,0:T(8,128)(2,1)S(1)} collective-permute-done((bf16[20,1024]{1,0:T(8,128)(2,1)}, bf16[20,1024]{1,0:T(8,128)(2,1)S(1)}, u32[]{:S(2)}, u32[]{:S(2)}) %collective-permute-start.5) | collective-permute-done | bytes 40992 | tf_op jit(solution)/shard_map/ppermute | solution.py:375
  95.1 0.0 copy-done.3
  95.1 0.6 copy-done.4
  95.7 5.6 %detect.1 = f32[3,64,1024]{2,1,0:T(8,128)} custom-call(f32[3,42,128]{2,1,0:T(8,128)} %pad_add_fusion.profile, f32[64,1024]{1,0:T(8,128)} %get-tuple-element.5.x, bf16[20,1024]{1,0:T(8,128)(2,1)} %copy-done.3, bf16[20,1024]{1,0:T(8,128)(2,1)} %copy-done.4), custom_call_target="tpu_custom_call" | custom-call | tf_op jit(solution)/shard_map/detect/pallas_call | solution.py:317
  (24 shorter events, 0.1 us)
Async XLA Ops:
  1.8 10.4 %collective-permute-start.1 = (bf16[8,11,1024]{2,1,0:T(8,128)(2,1)S(1)}, bf16[8,11,1024]{2,1,0:T(8,128)(2,1)S(1)}, u32[]{:S(2)}, u32[]{:S(2)}) collective-permute-start(bf16[8,11,1024]{2,1,0:T(8,128)(2,1)S(1)} %get-tuple-element.9), channel_id=1, source_target_pairs={{0,32},{32,64},{64,96},{1,33},{33,65},{65,97},{2,34},{34,66},{66,9... | collective-permute-start | bytes 540680 | tf_op jit(solution)/shard_map/ppermute | solution.py:353
  5.6 9.7 %collective-permute-start.2 = (bf16[8,11,1024]{2,1,0:T(8,128)(2,1)S(1)}, bf16[8,11,1024]{2,1,0:T(8,128)(2,1)S(1)}, u32[]{:S(2)}, u32[]{:S(2)}) collective-permute-start(bf16[8,11,1024]{2,1,0:T(8,128)(2,1)S(1)} %get-tuple-element.8), channel_id=1, source_target_pairs={{32,0},{64,32},{96,64},{33,1},{65,33},{97,65},{34,2},{66,34},{98,6... | collective-permute-start | bytes 540680 | tf_op jit(solution)/shard_map/ppermute | solution.py:354
  12.1 14.6 %copy-start.9 = (s32[8]{0:T(128)S(1)}, s32[8]{0:T(128)}, u32[]{:S(2)}) copy-start(s32[8]{0:T(128)} %param.14) | copy-start | bytes 100
  12.1 14.7 %copy-start.7 = (s32[8,8]{1,0:T(8,128)S(1)}, s32[8,8]{1,0:T(8,128)}, u32[]{:S(2)}) copy-start(s32[8,8]{1,0:T(8,128)} %param.16) | copy-start | bytes 772
  12.1 14.7 %copy-start.8 = (s32[8,8]{1,0:T(8,128)S(1)}, s32[8,8]{1,0:T(8,128)}, u32[]{:S(2)}) copy-start(s32[8,8]{1,0:T(8,128)} %param.15) | copy-start | bytes 772
  12.2 3.1 %copy-start.10 = (bf16[8,11,1024]{2,1,0:T(8,128)(2,1)}, bf16[8,11,1024]{2,1,0:T(8,128)(2,1)S(1)}, u32[]{:S(2)}) copy-start(bf16[8,11,1024]{2,1,0:T(8,128)(2,1)S(1)} %collective-permute-done.1.lo) | copy-start | bytes 540676
  15.2 0.7 copy-start.11
  26.8 2.9 %collective-permute-start.3 = (bf16[8,64,1024]{2,1,0:T(8,128)(2,1)}, bf16[8,64,1024]{2,1,0:T(8,128)(2,1)S(1)}, u32[]{:S(2)}, u32[]{:S(2)}) collective-permute-start(bf16[8,64,1024]{2,1,0:T(8,128)(2,1)} %match.1.mine), channel_id=1, source_target_pairs={{0,1},{1,0},{2,3},{3,2},{4,5},{5,4},{6,7},{7,6},{8,9},{9,8},{10,11... | collective-permute-start | bytes 3145736 | tf_op jit(solution)/shard_map/ppermute | solution.py:370
  26.9 2.7 %copy-start.5 = (s32[8,17]{1,0:T(8,128)}, s32[8,17]{1,0:T(8,128)S(1)}, u32[]{:S(2)}) copy-start(s32[8,17]{1,0:T(8,128)S(1)} %pad_add_fusion.1.mine_labels) | copy-start | bytes 1636
  26.9 2.5 %collective-permute-start = (s32[8,17]{1,0:T(8,128)S(1)}, s32[8,17]{1,0:T(8,128)S(1)}, u32[]{:S(2)}, u32[]{:S(2)}) collective-permute-start(s32[8,17]{1,0:T(8,128)S(1)} %pad_add_fusion.1.mine_labels), channel_id=1, source_target_pairs={{0,1},{1,0},{2,3},{3,2},{4,5},{5,4},{6,7},{7,6},{8,9},{9,8},{10,11... | collective-permute-start | bytes 1640 | tf_op jit(solution)/shard_map/ppermute | solution.py:360
  29.4 0.6 copy-start.6
  29.6 1.0 copy-start.1
  38.9 7.2 %copy-start.2 = (bf16[3,41,41]{2,1,0:T(8,128)(2,1)S(1)}, bf16[3,41,41]{2,1,0:T(8,128)(2,1)}, u32[]{:S(2)}) copy-start(bf16[3,41,41]{2,1,0:T(8,128)(2,1)} %param.17) | copy-start | bytes 30262
  38.9 42.4 %all-to-all-start = ((bf16[16,528,128]{2,1,0:T(8,128)(2,1)}), bf16[16,528,128]{2,1,0:T(8,128)(2,1)S(1)}, u32[]{:S(2)}, u32[]{:S(2)}) async-start(bf16[16,528,128]{2,1,0:T(8,128)(2,1)} %pile.1), calls=%async_computation | async-start | bytes 4325376 | tf_op jit(solution)/shard_map/all_to_all | solution.py:372
  81.4 1.4 %copy-start = (bf16[16,528,128]{2,1,0:T(8,128)(2,1)}, bf16[16,528,128]{2,1,0:T(8,128)(2,1)S(1)}, u32[]{:S(2)}) copy-start(bf16[16,528,128]{2,1,0:T(8,128)(2,1)S(1)} %all-to-all-done.parts) | copy-start | bytes 6488068
  85.3 6.5 %collective-permute-start.4 = (bf16[20,1024]{1,0:T(8,128)(2,1)}, bf16[20,1024]{1,0:T(8,128)(2,1)S(1)}, u32[]{:S(2)}, u32[]{:S(2)}) collective-permute-start(bf16[20,1024]{1,0:T(8,128)(2,1)} %get-tuple-element.6), channel_id=1, source_target_pairs={{0,32},{32,64},{64,96},{1,33},{33,65},{65,97},{2,34},{34,66},{66,9... | collective-permute-start | bytes 122888 | tf_op jit(solution)/shard_map/ppermute | solution.py:374
  88.9 6.2 %collective-permute-start.5 = (bf16[20,1024]{1,0:T(8,128)(2,1)}, bf16[20,1024]{1,0:T(8,128)(2,1)S(1)}, u32[]{:S(2)}, u32[]{:S(2)}) collective-permute-start(bf16[20,1024]{1,0:T(8,128)(2,1)} %get-tuple-element.7), channel_id=1, source_target_pairs={{32,0},{64,32},{96,64},{33,1},{65,33},{97,65},{34,2},{66,34},{98,6... | collective-permute-start | bytes 122888 | tf_op jit(solution)/shard_map/ppermute | solution.py:375
  91.8 3.2 %copy-start.3 = (bf16[20,1024]{1,0:T(8,128)(2,1)}, bf16[20,1024]{1,0:T(8,128)(2,1)S(1)}, u32[]{:S(2)}) copy-start(bf16[20,1024]{1,0:T(8,128)(2,1)S(1)} %collective-permute-done.4.lo) | copy-start | bytes 122884
  95.1 0.6 copy-start.4

commit v3 on v2

--- a/solution.py
+++ b/solution.py
@@ -16,25 +16,20 @@
 vmem_bytes = 56 * 1024 * 1024
 
 
-def neighbours(count):
-    up = [(i, i + 1) for i in range(count - 1)]
-    return up, [(b, a) for a, b in up]
-
-
-def profile_rows(profile, taps):
-    lead = profile.shape[:-1]
-    zeros = lambda n: jnp.zeros(lead + (n,), profile.dtype)
-    first = jnp.concatenate(
-        [profile[..., :1], zeros(lanes - taps), profile[..., :0:-1]], axis=-1
-    )
-    second = jnp.concatenate(
-        [zeros(half - taps + 1), profile[..., ::-1], zeros(lanes - half - 1)], axis=-1
-    )
+def one_hot(rows, cols, at):
+    row = lax.broadcasted_iota(jnp.int32, (rows, cols), 0)
+    col = lax.broadcasted_iota(jnp.int32, (rows, cols), 1)
+    return (col == at(row)).astype(f32)
+
+
+def lane_places(taps):
+    first = one_hot(taps, lanes, lambda j: (lanes - j) % lanes)
+    second = one_hot(taps, lanes, lambda j: half - j)
     return first, second
 
 
-def pad_rows(rows, low, high):
-    return jnp.pad(rows, [(0, 0)] * (rows.ndim - 2) + [(low, high), (0, 0)])
+def row_places(rows, taps):
+    return one_hot(rows, taps, lambda t: t), one_hot(rows, taps, lambda t: t - 1)
 
 
 def lane_ids(rows):
@@ -84,63 +79,181 @@
     return first, second
 
 
-def match_body(taps, code, table, g, x, lo, hi, out, frame, lhs, w):
+def columns(rows):
+    return [rows[:, m * lanes : (m + 1) * lanes] for m in range(rows.shape[1] // lanes)]
+
+
+def put_band(w, profile, taps, mask, first, last, at):
+    depth = mask.shape[0]
+    for u in range(max(first - 2, 0), min(last, taps + 1)):
+        tile = band_tile(profile[u : u + 1, :], mask)
+        if u >= first:
+            row = (u - first) * lanes
+            w[row : row + depth, at : at + lanes] = tile
+        if first <= u + 2 < last:
+            row = (u + 2 - first) * lanes
+            w[row : row + depth, at + lanes : at + 2 * lanes] = tile
+
+
+def edge_spans(taps):
+    return (taps // 2 + 1) // 2 * 2
+
+
+def put_edge_lhs(lhs, frame, spans):
+    tiles = frame.shape[1]
+    for t in range(spans):
+        for par in range(2):
+            for m in range(0, tiles, 2):
+                pair = [frame[par, m + i, pl.ds(t, 8, stride=group), :] for i in range(2)]
+                at = (par * tiles + m) * 8
+                lhs[at : at + 16, t * lanes : (t + 1) * lanes] = jnp.concatenate(pair, axis=0).astype(bf16)
+
+
+def edge_scratch(taps, tiles, width):
+    spans = edge_spans(taps)
+    return [
+        pltpu.VMEM((2, 2, tiles, 48, lanes), f32),
+        pltpu.VMEM((2, 128, spans * lanes), bf16),
+        pltpu.VMEM((2, spans * lanes, width), bf16),
+    ]
+
+
+def put_edges(taps, frame, lhs, lo, hi):
     reach = taps // 2
-    number, _, cols = x.shape
-    count = cols // lanes
-    depth = 96
+    spans = edge_spans(taps)
+    put_frame(frame.at[0], columns(lo), 0, reach)
+    put_frame(frame.at[1], columns(hi), 28 - reach + spans, reach)
+    for side in range(2):
+        put_edge_lhs(lhs.at[side], frame.at[side], spans)
+
+
+def halo_pair(odd, first, second):
+    return jnp.where(odd, first, second), jnp.where(odd, second, first)
+
+
+def own_body(taps, code, table, base_rows, base_cols, x, acc, profile, g, frame, lhs, w):
+    number, rows, _ = x.shape
+    basis = base_rows.shape[0]
+    reach = taps // 2
+    spans = taps + 3
+    exact = lax.Precision.HIGHEST
+    cols_ab = [
+        jnp.dot(base_cols[...], places, precision=exact, preferred_element_type=f32)
+        for places in lane_places(taps)
+    ]
+    rows_ab = [
+        lax.dot_general(
+            places, base_rows[...], (((1,), (1,)), ((), ())), precision=exact, preferred_element_type=f32
+        )
+        for places in row_places(taps + 1, taps)
+    ]
+    for b in range(basis):
+        g[b] = sum(r[:, b : b + 1] * c[b : b + 1, :] for r, c in zip(rows_ab, cols_ab))
+    frame[...] = jnp.zeros_like(frame)
     w[...] = jnp.zeros_like(w)
-    mask = band_mask(depth, taps)
-    lane = lane_ids(16)
-
-    def one(e, _):
+    mask = band_mask(96, taps)
+
+    def one(e, way):
         total = jnp.zeros(g.shape[1:], f32)
-        for b in range(g.shape[0]):
+        for b in range(basis):
             total = total + table[b, code[e, b]] * g[b]
         total = total.astype(bf16).astype(f32)
-        for u in range(taps + 1):
-            tile = band_tile(total[u : u + 1, :], mask)
-            w[u * lanes : u * lanes + depth, 0:lanes] = tile
-            w[(u + 2) * lanes : (u + 2) * lanes + depth, lanes : 2 * lanes] = tile
-        for ref, row in ((lo, 16 - reach), (x, 16), (hi, 80)):
-            rows = ref[e]
-            put_frame(frame, [rows[:, m * lanes : (m + 1) * lanes] for m in range(count)], row, reach)
-        put_lhs(lhs, frame, taps + 3, 16 - reach)
-        acc = jnp.dot(lhs[...], w[...], preferred_element_type=f32)
-        for m in range(count):
-            for h in range(2):
-                cut = slice(h * lanes, (h + 1) * lanes)
-                even = acc[m * 16 : m * 16 + 16, cut]
-                odd = acc[(count + m) * 16 : (count + m) * 16 + 16, cut]
-                for b, part in enumerate(split_rows(even, odd, lane)):
-                    at = (2 * h + b) * 16
-                    out[e, at : at + 16, m * lanes : (m + 1) * lanes] = part.astype(bf16)
+        profile[e] = total
+        put_band(w.at[way], total, taps, mask, 0, spans, 0)
+        put_frame(frame.at[way], columns(x[e]), 16, reach)
+        put_lhs(lhs.at[way], frame.at[way], spans, 16 - reach)
+        acc[e] = jnp.dot(lhs[way], w[way], preferred_element_type=f32)
+
+    def some(i, _):
+        for way in range(ways):
+            one(ways * i + way, way)
         return 0
 
-    lax.fori_loop(0, number, one, 0)
-
-
-def match(code, table, g, x, lo, hi, taps):
+    lax.fori_loop(0, number // ways, some, 0)
+
+
+ways = 2
+
+
+def match_own(code, table, base_rows, base_cols, x):
     number, rows, cols = x.shape
+    basis, taps = base_rows.shape
     smem = pl.BlockSpec(memory_space=pltpu.SMEM)
     vmem = pl.BlockSpec(memory_space=pltpu.VMEM)
     spans = taps + 3
     return pl.pallas_call(
-        functools.partial(match_body, taps),
-        in_specs=[smem, smem, vmem, vmem, vmem, vmem],
-        out_specs=vmem,
-        out_shape=jax.ShapeDtypeStruct((number, rows, cols), bf16),
+        functools.partial(own_body, taps),
+        in_specs=[smem, smem, vmem, vmem, vmem],
+        out_specs=(vmem, vmem),
+        out_shape=(
+            jax.ShapeDtypeStruct((number, 256, 256), f32),
+            jax.ShapeDtypeStruct((number, taps + 1, lanes), f32),
+        ),
         scratch_shapes=[
-            pltpu.VMEM((2, cols // lanes, 96, lanes), f32),
-            pltpu.VMEM((256, spans * lanes), bf16),
-            pltpu.VMEM((spans * lanes, 256), bf16),
+            pltpu.VMEM((basis, taps + 1, lanes), f32),
+            pltpu.VMEM((ways, 2, cols // lanes, 96, lanes), f32),
+            pltpu.VMEM((ways, 256, spans * lanes), bf16),
+            pltpu.VMEM((ways, spans * lanes, 256), bf16),
         ],
         compiler_params=pltpu.CompilerParams(vmem_limit_bytes=vmem_bytes),
         cost_estimate=pl.CostEstimate(
             flops=number * 2 * 256 * 256 * spans * lanes, bytes_accessed=4 * x.size, transcendentals=0
         ),
-        name="match",
-    )(code, table, g, x, lo, hi)
+        name="match_own",
+    )(code, table, base_rows, base_cols, x)
+
+
+def halo_body(taps, odd, profile, first, second, acc, out, frame, lhs, w):
+    number, _, cols = out.shape
+    count = cols // lanes
+    spans = edge_spans(taps)
+    frame[...] = jnp.zeros_like(frame)
+    w[...] = jnp.zeros_like(w)
+    mask = band_mask(96, taps)
+    lane = lane_ids(16)
+
+    def one(e, way):
+        band = profile[e]
+        put_band(w.at[way, 0], band, taps, mask, 0, spans, 0)
+        put_band(w.at[way, 1], band, taps, mask, taps + 3 - spans, taps + 3, 0)
+        lo, hi = halo_pair(odd[0] == 1, first[e], second[e])
+        put_edges(taps, frame.at[way], lhs.at[way], lo, hi)
+        ends = [
+            jnp.dot(lhs[way, side], w[way, side], preferred_element_type=f32) for side in range(2)
+        ]
+        for m in range(count):
+            for h in range(2):
+                cut = slice(h * lanes, (h + 1) * lanes)
+                blocks = []
+                for n in (m, count + m):
+                    more = jnp.concatenate([end[n * 8 : n * 8 + 8, cut] for end in ends], axis=0)
+                    blocks.append(acc[e, n * 16 : n * 16 + 16, cut] + more)
+                for b, part in enumerate(split_rows(*blocks, lane)):
+                    at = (2 * h + b) * 16
+                    out[e, at : at + 16, m * lanes : (m + 1) * lanes] = part.astype(bf16)
+
+    def some(i, _):
+        for way in range(ways):
+            one(ways * i + way, way)
+        return 0
+
+    lax.fori_loop(0, number // ways, some, 0)
+
+
+def match_halo(odd, profile, first, second, acc, rows, taps):
+    number, _, cols = first.shape
+    smem = pl.BlockSpec(memory_space=pltpu.SMEM)
+    vmem = pl.BlockSpec(memory_space=pltpu.VMEM)
+    scratch = edge_scratch(taps, cols // lanes, 256)
+    return pl.pallas_call(
+        functools.partial(halo_body, taps),
+        in_specs=[smem, vmem, vmem, vmem, vmem],
+        out_specs=vmem,
+        out_shape=jax.ShapeDtypeStruct((number, rows, cols), bf16),
+        scratch_shapes=[pltpu.VMEM((ways,) + each.shape, each.dtype) for each in scratch],
+        compiler_params=pltpu.CompilerParams(vmem_limit_bytes=vmem_bytes),
+        name="match_halo",
+    )(odd, profile, first, second, acc)
 
 
 def pile_body(core, mine_labels, other_labels, mine, other, out, counts, source, offset, scale, planes):
@@ -244,7 +357,7 @@
     )(core, mine_labels, other_labels, mine, other)
 
 
-def coadd_body(reach, parts, coadd, low, high, stage):
+def coadd_body(reach, odd, parts, coadd, first, second, stage):
     count = parts.shape[0]
     rows, cols = coadd.shape
     tiles = cols // lanes
@@ -264,68 +377,127 @@
     for m in range(tiles):
         cut = slice(m * lanes, (m + 1) * lanes)
         coadd[:, cut] = stage[m]
-        low[:, cut] = stage[m, 0:reach, :].astype(bf16)
-        high[:, cut] = stage[m, rows - reach : rows, :].astype(bf16)
-
-
-def coadd_of(parts, rows, cols, reach):
+        low = stage[m, 0:reach, :]
+        high = stage[m, rows - reach : rows, :]
+        first[:, cut] = jnp.where(odd[0] == 1, low, high).astype(bf16)
+        second[:, cut] = jnp.where(odd[0] == 1, high, low).astype(bf16)
+
+
+def coadd_of(odd, parts, rows, cols, reach):
     edge = jax.ShapeDtypeStruct((reach, cols), bf16)
+    smem = pl.BlockSpec(memory_space=pltpu.SMEM)
+    vmem = pl.BlockSpec(memory_space=pltpu.VMEM)
     return pl.pallas_call(
         functools.partial(coadd_body, reach),
+        in_specs=[smem, vmem],
+        out_specs=(vmem, vmem, vmem),
         out_shape=(jax.ShapeDtypeStruct((rows, cols), f32), edge, edge),
         scratch_shapes=[pltpu.VMEM((cols // lanes, rows, lanes), f32)],
         compiler_params=pltpu.CompilerParams(vmem_limit_bytes=vmem_bytes),
         name="coadd",
-    )(parts)
-
-
-def detect_body(taps, profile, x, lo, hi, out, frame, lhs, w, stage):
+    )(odd, parts)
+
+
+def detect_own_body(taps, psf, x, acc, profile, frame, lhs, w):
     reach = taps // 2
     rows, cols = x.shape
-    count = cols // lanes
-    scales = profile.shape[0]
-    depth = 112
-    mask = band_mask(depth, taps)
+    spans = taps + 3
+    mask = band_mask(112, taps)
+    frame[...] = jnp.zeros_like(frame)
+    put_frame(frame, columns(x[...].astype(bf16)), 24, reach)
+    put_lhs(lhs, frame, spans, 24 - reach)
     w[...] = jnp.zeros_like(w)
-    for s in range(scales):
-        for u in range(taps + 1):
-            tile = band_tile(profile[s, u : u + 1, :], mask)
-            w[u * lanes : u * lanes + depth, 2 * s * lanes : (2 * s + 1) * lanes] = tile
-            w[(u + 2) * lanes : (u + 2) * lanes + depth, (2 * s + 1) * lanes : (2 * s + 2) * lanes] = tile
-    for ref, row in ((lo, 24 - reach), (x, 24), (hi, 24 + rows)):
-        value = ref[...].astype(bf16)
-        put_frame(frame, [value[:, m * lanes : (m + 1) * lanes] for m in range(count)], row, reach)
-    put_lhs(lhs, frame, taps + 3, 24 - reach)
-    lane = lane_ids(16)
-    for s in range(scales):
-        acc = jnp.dot(
-            lhs[...], w[:, 2 * s * lanes : (2 * s + 2) * lanes], preferred_element_type=f32
-        )
-        for m in range(count):
-            for h in range(2):
-                even = acc[m * 16 : m * 16 + 16, h * lanes : (h + 1) * lanes]
-                odd = acc[(count + m) * 16 : (count + m) * 16 + 16, h * lanes : (h + 1) * lanes]
-                for b, part in enumerate(split_rows(even, odd, lane)):
-                    stage[m, pl.ds(2 * h + b, 16, stride=group), :] = part
-            out[s, :, m * lanes : (m + 1) * lanes] = stage[m]
-
-
-def detect_of(profile, x, lo, hi, taps):
+    for s in range(psf.shape[0]):
+        total = 0.0
+        for rows_at, cols_at in zip(row_places(profile.shape[1], taps), lane_places(taps)):
+            moved = jnp.dot(rows_at.astype(bf16), psf[s], preferred_element_type=f32)
+            total = total + jnp.dot(
+                moved.astype(bf16), cols_at.astype(bf16), preferred_element_type=f32
+            )
+        profile[s] = total
+        put_band(w, total, taps, mask, 0, spans, 256 * s)
+        cut = slice(256 * s, 256 * s + 256)
+        acc[:, cut] = jnp.dot(lhs[...], w[:, cut], preferred_element_type=f32)
+
+
+def detect_own(psf, x):
     rows, cols = x.shape
-    scales = profile.shape[0]
+    scales, _, taps = psf.shape
     spans = taps + 3
     return pl.pallas_call(
-        functools.partial(detect_body, taps),
-        out_shape=jax.ShapeDtypeStruct((scales, rows, cols), f32),
+        functools.partial(detect_own_body, taps),
+        out_shape=(
+            jax.ShapeDtypeStruct((256, scales * 256), f32),
+            jax.ShapeDtypeStruct((scales, 48, lanes), f32),
+        ),
         scratch_shapes=[
             pltpu.VMEM((2, cols // lanes, 24 + rows + 24, lanes), f32),
             pltpu.VMEM((256, spans * lanes), bf16),
             pltpu.VMEM((spans * lanes, scales * 256), bf16),
-            pltpu.VMEM((cols // lanes, rows, lanes), f32),
         ],
         compiler_params=pltpu.CompilerParams(vmem_limit_bytes=vmem_bytes),
-        name="detect",
-    )(profile, x, lo, hi)
+        cost_estimate=pl.CostEstimate(
+            flops=scales * 2 * 256 * 256 * spans * lanes, bytes_accessed=4 * x.size, transcendentals=0
+        ),
+        name="detect_own",
+    )(psf, x)
+
+
+def detect_halo_body(taps, odd, profile, first, second, acc, out, frame, lhs, w, stage):
+    scales, rows, cols = out.shape
+    count = cols // lanes
+    spans = edge_spans(taps)
+    frame[...] = jnp.zeros_like(frame)
+    w[...] = jnp.zeros_like(w)
+    mask = band_mask(112, taps)
+    lane = lane_ids(16)
+    lo, hi = halo_pair(odd[0] == 1, first[...], second[...])
+    put_edges(taps, frame, lhs, lo, hi)
+    for s in range(scales):
+        at = 256 * s
+        put_band(w.at[0], profile[s], taps, mask, 0, spans, at)
+        put_band(w.at[1], profile[s], taps, mask, taps + 3 - spans, taps + 3, at)
+        ends = [
+            jnp.dot(lhs[side], w[side, :, at : at + 256], preferred_element_type=f32)
+            for side in range(2)
+        ]
+        for m in range(count):
+            for h in range(2):
+                cut = slice(h * lanes, (h + 1) * lanes)
+                blocks = []
+                for n in (m, count + m):
+                    more = jnp.concatenate([end[n * 8 : n * 8 + 8, cut] for end in ends], axis=0)
+                    own = acc[n * 16 : n * 16 + 16, at + h * lanes : at + (h + 1) * lanes]
+                    blocks.append(own + more)
+                for b, part in enumerate(split_rows(*blocks, lane)):
+                    stage[s, m, pl.ds(2 * h + b, 16, stride=group), :] = part
+            out[s, :, m * lanes : (m + 1) * lanes] = stage[s, m]
+
+
+def detect_halo(odd, profile, first, second, acc, rows, taps):
+    cols = first.shape[1]
+    scales = profile.shape[0]
+    smem = pl.BlockSpec(memory_space=pltpu.SMEM)
+    vmem = pl.BlockSpec(memory_space=pltpu.VMEM)
+    return pl.pallas_call(
+        functools.partial(detect_halo_body, taps),
+        in_specs=[smem, vmem, vmem, vmem, vmem],
+        out_specs=vmem,
+        out_shape=jax.ShapeDtypeStruct((scales, rows, cols), f32),
+        scratch_shapes=edge_scratch(taps, cols // lanes, scales * 256)
+        + [pltpu.VMEM((scales, cols // lanes, rows, lanes), f32)],
+        compiler_params=pltpu.CompilerParams(vmem_limit_bytes=vmem_bytes),
+        name="detect_halo",
+    )(odd, profile, first, second, acc)
+
+
+def trade(first, second):
+    count = lax.axis_size("section")
+    out = []
+    for start, rows in ((0, first), (1, second)):
+        pairs = [(i, i + 1) for i in range(start, count - 1, 2)]
+        out.append(lax.ppermute(rows, "section", pairs + [(b, a) for a, b in pairs]))
+    return out
 
 
 def on_device(
@@ -344,14 +516,14 @@
     reach = taps // 2
     wide = psf_kernels.shape[-1]
     wide_reach = wide // 2
-    sections = lax.axis_size("section")
     across = ("sy", "sx")
     patches = lax.axis_size("sy") * lax.axis_size("sx") * 2
     core = lax.axis_index("core")
-    up, down = neighbours(sections)
-
-    lo = lax.ppermute(exposures[:, rows - reach :, :], "section", up)
-    hi = lax.ppermute(exposures[:, :reach, :], "section", down)
+    odd = lax.axis_index("section") % 2
+
+    low, high = exposures[:, :reach, :], exposures[:, rows - reach :, :]
+    first, second = trade(jnp.where(odd == 1, low, high), jnp.where(odd == 1, high, low))
+    odd = odd[None]
 
     labels = jnp.concatenate(
         [exposure_weight[:, None], intersection_patch, intersection_shift], axis=1
@@ -359,21 +531,15 @@
     swap = [(0, 1), (1, 0)]
     other_labels = lax.ppermute(labels, "core", swap)
 
-    cols_a, cols_b = profile_rows(basis_cols, taps)
-    rows_a = jnp.pad(basis_rows, ((0, 0), (0, 1)))
-    rows_b = jnp.pad(basis_rows, ((0, 0), (1, 0)))
-    g = rows_a[:, :, None] * cols_a[:, None, :] + rows_b[:, :, None] * cols_b[:, None, :]
-    psf_a, psf_b = profile_rows(psf_kernels.astype(f32), wide)
-    profile = pad_rows(psf_a, 0, 1) + pad_rows(psf_b, 1, 0)
-
-    matched = match(coef_code, coef_table, g, exposures, lo, hi, taps)
+    acc, profile = match_own(coef_code, coef_table, basis_rows, basis_cols, exposures)
+    matched = match_halo(odd, profile, first, second, acc, rows, taps)
     other = lax.ppermute(matched, "core", swap)
     partial = pile(core[None], labels, other_labels, matched, other, patches)
     parts = lax.all_to_all(partial, across, split_axis=0, concat_axis=0, tiled=True)
-    coadd, low, high = coadd_of(parts, rows, cols, wide_reach)
-    lo = lax.ppermute(high, "section", up)
-    hi = lax.ppermute(low, "section", down)
-    detect = detect_of(profile, coadd, lo, hi, wide)
+    coadd, first, second = coadd_of(odd, parts, rows, cols, wide_reach)
+    first, second = trade(first, second)
+    acc, profile = detect_own(psf_kernels, coadd)
+    detect = detect_halo(odd, profile, first, second, acc, rows, wide)
     return (coadd[None], detect[None])
 
 

time: 102 us -> 94.1 us (0.923)
  waiting for transfers between devices: 43.2 us -> 2.17 us
  blocking collectives: 0 us -> 37.1 us
  Pallas kernels: 27.3 us -> 38.9 us
  starting transfers between devices: 19.4 us -> 8.64 us
  local copies, waits for them, and re-layouts: 8.67 us -> 5.24 us
    all_to_all x0 -> x1, blocking collectives: none -> 37.1 us  [on_device(): lax.all_to_all(partial, across, split_axis=0, concat_axis=0, tiled=True)]
    all_to_all x1 -> x0, waiting for transfers between devices: 34.7 us -> none  [on_device(): lax.all_to_all(partial, across, split_axis=0, concat_axis=0, tiled=True)]
    pallas_call x3 -> x5, Pallas kernels: 19 us -> 30.7 us  [the longest x1 9.7 us: match_own(): pl.pallas_call(functools.partial(own_body, taps), in_specs=[smem, smem, v...]
    all_to_all x1 -> x0, starting transfers between devices: 7.17 us -> none  [on_device(): lax.all_to_all(partial, across, split_axis=0, concat_axis=0, tiled=True)]
    ppermute x4, waiting for transfers between devices: 6.32 us -> 0.01 us  [trade(): lax.ppermute(rows, 'section', pairs + [(b, a) for a, b in pairs])]
    ppermute x4, starting transfers between devices: 11.7 us -> 8.11 us  [trade(): lax.ppermute(rows, 'section', pairs + [(b, a) for a, b in pairs])]
    slice x6 -> x0, local copies, waits for them, and re-layouts: 2.7 us -> none  [the longest x1 1.12 us: on_device(): hi = lax.ppermute(exposures[:, :reach, :], 'section', down)]
    add x2 -> x0, other arithmetic: 1.61 us -> none  [the longest x1 0.97 us: on_device(): rows_a[:, :, None] * cols_a[:, None, :]]
  transfers between devices with their start and end apart: 7 -> 6, of which waited for: 5 -> 2; matrix products, arithmetic and copies ran while one was open for 6% -> 3% of each run, Pallas kernels for 0% -> 17%
where the time goes in v3:
time: 94.1 us; the launch traced here: 94 us
  Pallas kernels  38.9 us (41%)
  blocking collectives  37.1 us (39%)
  starting transfers between devices  8.64 us (9%)
  local copies, waits for them, and re-layouts  5.24 us (6%)
  waiting for transfers between devices  2.17 us (2%)
  other arithmetic  1.19 us (1%)
    all_to_all x1, blocking collectives, on_device(): lax.all_to_all(partial, across, split_axis=0, concat_axis=0, tiled=True)  37.1 us
    pallas_call x1, Pallas kernels, match_own(): pl.pallas_call(functools.partial(own_body, taps), in_specs=[smem, smem, v...  9.7 us
    pallas_call x1, Pallas kernels, pile(): pl.pallas_call(pile_body, in_specs=[smem] * 3 + [vmem] * 2, out_specs=vme...  8.25 us
    ppermute x4, starting transfers between devices, trade(): lax.ppermute(rows, 'section', pairs + [(b, a) for a, b in pairs])  8.11 us
    pallas_call x1, Pallas kernels, match_halo(): pl.pallas_call(functools.partial(halo_body, taps), in_specs=[smem, vmem,...  7.57 us
    pallas_call x1, Pallas kernels, detect_own(): pl.pallas_call(functools.partial(detect_own_body, taps), out_shape=(jax.S...  5.84 us
    unnamed x22, local copies, waits for them, and re-layouts  5.16 us
    pallas_call x1, Pallas kernels, detect_halo(): pl.pallas_call(functools.partial(detect_halo_body, taps), in_specs=[smem,...  4.92 us
  transfers between devices with their start and end apart: 6, of which 2 were waited for; matrix products, arithmetic and copies ran while one was open for 3% of the time, Pallas kernels for 17%

profile of v3, /device:TPU:32, one launch (start us, length us, event | category | flops | bytes accessed | tf_op | source)
XLA Modules:
  0.0 94.0 jit_solution(17146472797560979418)
XLA Ops:
  0.6 1.1 %broadcast_select_fusion = (bf16[8,11,1024]{2,1,0:T(8,128)(2,1)S(1)}, bf16[8,11,1024]{2,1,0:T(8,128)(2,1)S(1)}) fusion(pred[]{:T(512)S(6)} %eq.6, bf16[8,64,1024]{2,1,0:T(8,128)(2,1)} %x.1), kind=kLoop, calls=%fused_computation | loop fusion | flops 180224 | bytes 720897 | tf_op jit(solution)/shard_map/jit(_where)/select_n | solution.py:525
  1.8 3.8 %collective-permute-start.2 = (bf16[8,11,1024]{2,1,0:T(8,128)(2,1)S(1)}, bf16[8,11,1024]{2,1,0:T(8,128)(2,1)S(1)}, u32[]{:S(2)}, u32[]{:S(2)}) collective-permute-start(bf16[8,11,1024]{2,1,0:T(8,128)(2,1)S(1)} %get-tuple-element.16), channel_id=1, source_target_pairs={{32,64},{64,32},{33,65},{65,33},{34,66},{66,34},{35,67},{67,35},{3... | collective-permute-start | bytes 540680 | tf_op jit(solution)/shard_map/ppermute | solution.py:499
  5.6 0.1 collective-permute-start.1
  5.7 1.4 %copy.12.base_rows = f32[27,23]{1,0:T(8,128)} copy(f32[27,23]{0,1:T(8,128)} %param.12) | data formatting | bytes 4968 | tf_op args[3]
  7.1 1.4 %copy.13.base_cols = f32[27,23]{1,0:T(8,128)} copy(f32[27,23]{0,1:T(8,128)} %param.13) | data formatting | bytes 4968 | tf_op args[4]
  8.5 9.7 %match_own.1 = (f32[8,256,256]{2,1,0:T(8,128)}, f32[8,24,128]{2,1,0:T(8,128)}) custom-call(s32[8,27]{1,0:T(8,128)} %code.1, f32[27,64]{1,0:T(8,128)} %table.1, f32[27,23]{1,0:T(8,128)} %copy.12.base_rows, f32[27,23]{1,0:T(8,128)} %copy.13.base_cols, bf16[8,64,1024]{2,1,0:T(8,128)(2,1)} %x.1), custom_call_target="tpu_custom_call" | custom-call | flops 3489660928 | bytes 2097152 | tf_op jit(solution)/shard_map/match_own/pallas_call | solution.py:184
  18.2 0.0 copy-start.9
  18.2 0.0 copy-start.7
  18.2 0.0 copy-start.8
  18.2 0.0 collective-permute-done.2.second
  18.2 0.0 copy-start.1
  18.2 0.0 collective-permute-done.1.first
  18.2 0.0 copy-start.2
  18.2 0.7 copy-done.1
  18.9 0.1 copy-done.2
  19.0 7.6 %match_halo.1.mine = bf16[8,64,1024]{2,1,0:T(8,128)(2,1)} custom-call(s32[1]{0:T(128)} %bitcast.odd, f32[8,24,128]{2,1,0:T(8,128)} %get-tuple-element.9.profile, bf16[8,11,1024]{2,1,0:T(8,128)(2,1)} %copy-done.2, bf16[8,11,1024]{2,1,0:T(8,128)(2,1)} %copy-done.1, f32[8,256,256]{2,1,0:T(8,128)} %get-tuple-element.10.acc), custom_call_target="tpu_custom_call" | custom-call | tf_op jit(solution)/shard_map/match_halo/pallas_call | solution.py:248
  26.6 0.0 collective-permute-start.3
  26.6 0.0 copy-done.9
  26.6 0.1 copy.11
  26.7 0.0 copy-done.7
  26.7 0.0 copy-done.8
  26.7 0.1 pad_add_fusion.mine_labels
  26.7 0.0 copy-start.5
  26.7 0.5 collective-permute-start
  27.3 2.0 %collective-permute-done.other_labels = s32[8,17]{1,0:T(8,128)S(1)} collective-permute-done((s32[8,17]{1,0:T(8,128)S(1)}, s32[8,17]{1,0:T(8,128)S(1)}, u32[]{:S(2)}, u32[]{:S(2)}) %collective-permute-start) | collective-permute-done | bytes 576 | tf_op jit(solution)/shard_map/ppermute | solution.py:532
  29.2 0.0 copy-start.6
  29.2 0.2 collective-permute-done.3.other
  29.4 0.0 copy-start
  29.4 0.0 copy-done.5
  29.4 0.4 copy-done.6
  29.8 0.6 copy-done
  30.4 8.2 %pile.1 = bf16[16,528,128]{2,1,0:T(8,128)(2,1)} custom-call(s32[1]{0:T(128)} %bitcast.1.core, s32[8,17]{1,0:T(8,128)} %copy-done.5, s32[8,17]{1,0:T(8,128)} %copy-done.6, bf16[8,64,1024]{2,1,0:T(8,128)(2,1)} %match_halo.1.mine, bf16[8,64,1024]{2,1,0:T(8,128)(2,1)} %copy-done), custom_call_target="tpu_custom_call" | custom-call | tf_op jit(solution)/shard_map/pile/pallas_call | solution.py:343
  38.6 37.1 %all_to_all.5.parts = bf16[16,528,128]{2,1,0:T(8,128)(2,1)} all-to-all(bf16[16,528,128]{2,1,0:T(8,128)(2,1)} %pile.1), channel_id=1, replica_groups=mesh['section'=4,'sy'=4,'sx'=4,'core'=2] {'sy','sx'}, dimensions={0} | all-to-all | bytes 4325376 | tf_op jit(solution)/shard_map/all_to_all | solution.py:538
  75.8 2.6 %coadd.1 = (f32[64,1024]{1,0:T(8,128)}, bf16[20,1024]{1,0:T(8,128)(2,1)}, bf16[20,1024]{1,0:T(8,128)(2,1)}) custom-call(s32[1]{0:T(128)} %bitcast.odd, bf16[16,528,128]{2,1,0:T(8,128)(2,1)} %all_to_all.5.parts), custom_call_target="tpu_custom_call" | custom-call | tf_op jit(solution)/shard_map/coadd/pallas_call | solution.py:390
  78.4 2.0 %collective-permute-start.4 = (bf16[20,1024]{1,0:T(8,128)(2,1)}, bf16[20,1024]{1,0:T(8,128)(2,1)S(1)}, u32[]{:S(2)}, u32[]{:S(2)}) collective-permute-start(bf16[20,1024]{1,0:T(8,128)(2,1)} %get-tuple-element.13), channel_id=1, source_target_pairs={{0,32},{64,96},{32,0},{96,64},{1,33},{65,97},{33,1},{97,65},{2,34}... | collective-permute-start | bytes 122888 | tf_op jit(solution)/shard_map/ppermute | solution.py:499
  80.4 2.2 %collective-permute-start.5 = (bf16[20,1024]{1,0:T(8,128)(2,1)}, bf16[20,1024]{1,0:T(8,128)(2,1)S(1)}, u32[]{:S(2)}, u32[]{:S(2)}) collective-permute-start(bf16[20,1024]{1,0:T(8,128)(2,1)} %get-tuple-element.14), channel_id=1, source_target_pairs={{32,64},{64,32},{33,65},{65,33},{34,66},{66,34},{35,67},{67,35},{3... | collective-permute-start | bytes 122888 | tf_op jit(solution)/shard_map/ppermute | solution.py:499
  82.6 5.8 %detect_own.1 = (f32[256,768]{1,0:T(8,128)}, f32[3,48,128]{2,1,0:T(8,128)}) custom-call(bf16[3,41,41]{2,1,0:T(8,128)(2,1)} %psf.1, f32[64,1024]{1,0:T(8,128)} %get-tuple-element.11.x), custom_call_target="tpu_custom_call" | custom-call | flops 2214592512 | bytes 262144 | tf_op jit(solution)/shard_map/detect_own/pallas_call | solution.py:427
  88.5 0.0 collective-permute-done.4.first
  88.5 0.0 copy-start.3
  88.5 0.0 collective-permute-done.5.second
  88.5 0.0 copy-start.4
  88.5 0.6 copy-done.3
  89.1 0.0 copy-done.4
  89.1 4.9 %detect_halo.1 = f32[3,64,1024]{2,1,0:T(8,128)} custom-call(s32[1]{0:T(128)} %bitcast.odd, f32[3,48,128]{2,1,0:T(8,128)} %get-tuple-element.12.profile, bf16[20,1024]{1,0:T(8,128)(2,1)} %copy-done.3, bf16[20,1024]{1,0:T(8,128)(2,1)} %copy-done.4, f32[256,768]{1,0:T(8,128)} %get-tuple-element.15.acc), custom_call_target="tpu_custom_call" | custom-call | tf_op jit(solution)/shard_map/detect_halo/pallas_call | solution.py:482
Async XLA Ops:
  1.8 16.4 %collective-permute-start.2 = (bf16[8,11,1024]{2,1,0:T(8,128)(2,1)S(1)}, bf16[8,11,1024]{2,1,0:T(8,128)(2,1)S(1)}, u32[]{:S(2)}, u32[]{:S(2)}) collective-permute-start(bf16[8,11,1024]{2,1,0:T(8,128)(2,1)S(1)} %get-tuple-element.16), channel_id=1, source_target_pairs={{32,64},{64,32},{33,65},{65,33},{34,66},{66,34},{35,67},{67,35},{3... | collective-permute-start | bytes 540680 | tf_op jit(solution)/shard_map/ppermute | solution.py:499
  5.6 12.6 %collective-permute-start.1 = (bf16[8,11,1024]{2,1,0:T(8,128)(2,1)S(1)}, bf16[8,11,1024]{2,1,0:T(8,128)(2,1)S(1)}, u32[]{:S(2)}, u32[]{:S(2)}) collective-permute-start(bf16[8,11,1024]{2,1,0:T(8,128)(2,1)S(1)} %get-tuple-element.17), channel_id=1, source_target_pairs={{0,32},{64,96},{32,0},{96,64},{1,33},{65,97},{33,1},{97,65},{2,34}... | collective-permute-start | bytes 540680 | tf_op jit(solution)/shard_map/ppermute | solution.py:499
  18.2 8.4 %copy-start.9 = (s32[8]{0:T(128)S(1)}, s32[8]{0:T(128)}, u32[]{:S(2)}) copy-start(s32[8]{0:T(128)} %param.14) | copy-start | bytes 100
  18.2 8.5 %copy-start.7 = (s32[8,8]{1,0:T(8,128)S(1)}, s32[8,8]{1,0:T(8,128)}, u32[]{:S(2)}) copy-start(s32[8,8]{1,0:T(8,128)} %param.16) | copy-start | bytes 772
  18.2 8.5 %copy-start.8 = (s32[8,8]{1,0:T(8,128)S(1)}, s32[8,8]{1,0:T(8,128)}, u32[]{:S(2)}) copy-start(s32[8,8]{1,0:T(8,128)} %param.15) | copy-start | bytes 772
  18.2 0.7 copy-start.1
  18.2 0.8 copy-start.2
  26.6 2.9 %collective-permute-start.3 = (bf16[8,64,1024]{2,1,0:T(8,128)(2,1)}, bf16[8,64,1024]{2,1,0:T(8,128)(2,1)S(1)}, u32[]{:S(2)}, u32[]{:S(2)}) collective-permute-start(bf16[8,64,1024]{2,1,0:T(8,128)(2,1)} %match_halo.1.mine), channel_id=1, source_target_pairs={{0,1},{1,0},{2,3},{3,2},{4,5},{5,4},{6,7},{7,6},{8,9},{9,8},{10,11... | collective-permute-start | bytes 3145736 | tf_op jit(solution)/shard_map/ppermute | solution.py:536
  26.7 2.7 %copy-start.5 = (s32[8,17]{1,0:T(8,128)}, s32[8,17]{1,0:T(8,128)S(1)}, u32[]{:S(2)}) copy-start(s32[8,17]{1,0:T(8,128)S(1)} %pad_add_fusion.mine_labels) | copy-start | bytes 1636
  26.7 2.5 %collective-permute-start = (s32[8,17]{1,0:T(8,128)S(1)}, s32[8,17]{1,0:T(8,128)S(1)}, u32[]{:S(2)}, u32[]{:S(2)}) collective-permute-start(s32[8,17]{1,0:T(8,128)S(1)} %pad_add_fusion.mine_labels), channel_id=1, source_target_pairs={{0,1},{1,0},{2,3},{3,2},{4,5},{5,4},{6,7},{7,6},{8,9},{9,8},{10,11... | collective-permute-start | bytes 1640 | tf_op jit(solution)/shard_map/ppermute | solution.py:532
  29.2 0.6 copy-start.6
  29.4 1.0 %copy-start = (bf16[8,64,1024]{2,1,0:T(8,128)(2,1)}, bf16[8,64,1024]{2,1,0:T(8,128)(2,1)S(1)}, u32[]{:S(2)}) copy-start(bf16[8,64,1024]{2,1,0:T(8,128)(2,1)S(1)} %collective-permute-done.3.other) | copy-start | bytes 3145732
  78.4 10.1 %collective-permute-start.4 = (bf16[20,1024]{1,0:T(8,128)(2,1)}, bf16[20,1024]{1,0:T(8,128)(2,1)S(1)}, u32[]{:S(2)}, u32[]{:S(2)}) collective-permute-start(bf16[20,1024]{1,0:T(8,128)(2,1)} %get-tuple-element.13), channel_id=1, source_target_pairs={{0,32},{64,96},{32,0},{96,64},{1,33},{65,97},{33,1},{97,65},{2,34}... | collective-permute-start | bytes 122888 | tf_op jit(solution)/shard_map/ppermute | solution.py:499
  80.4 8.0 %collective-permute-start.5 = (bf16[20,1024]{1,0:T(8,128)(2,1)}, bf16[20,1024]{1,0:T(8,128)(2,1)S(1)}, u32[]{:S(2)}, u32[]{:S(2)}) collective-permute-start(bf16[20,1024]{1,0:T(8,128)(2,1)} %get-tuple-element.14), channel_id=1, source_target_pairs={{32,64},{64,32},{33,65},{65,33},{34,66},{66,34},{35,67},{67,35},{3... | collective-permute-start | bytes 122888 | tf_op jit(solution)/shard_map/ppermute | solution.py:499
  88.5 0.6 copy-start.3
  88.5 0.6 copy-start.4

commit v4 on v3

--- a/solution.py
+++ b/solution.py
@@ -14,6 +14,18 @@
 half = 64
 group = 4
 vmem_bytes = 56 * 1024 * 1024
+
+
+def profile_rows(profile, taps):
+    lead = profile.shape[:-1]
+    zeros = lambda n: jnp.zeros(lead + (n,), profile.dtype)
+    first = jnp.concatenate(
+        [profile[..., :1], zeros(lanes - taps), profile[..., :0:-1]], axis=-1
+    )
+    second = jnp.concatenate(
+        [zeros(half - taps + 1), profile[..., ::-1], zeros(lanes - half - 1)], axis=-1
+    )
+    return first, second
 
 
 def one_hot(rows, cols, at):
@@ -95,6 +107,17 @@
             w[row : row + depth, at + lanes : at + 2 * lanes] = tile
 
 
+def clear_band(w, taps, depth, first, last):
+    width = w.shape[1]
+    for t in range(first, last):
+        row = (t - first) * lanes
+        w[row + depth : row + lanes, :] = jnp.zeros((lanes - depth, width), bf16)
+        for u, at in ((t, 0), (t - 2, lanes)):
+            if not 0 <= u <= taps:
+                for n in range(at, width, 2 * lanes):
+                    w[row : row + depth, n : n + lanes] = jnp.zeros((depth, lanes), bf16)
+
+
 def edge_spans(taps):
     return (taps // 2 + 1) // 2 * 2
 
@@ -131,38 +154,38 @@
     return jnp.where(odd, first, second), jnp.where(odd, second, first)
 
 
-def own_body(taps, code, table, base_rows, base_cols, x, acc, profile, g, frame, lhs, w):
-    number, rows, _ = x.shape
-    basis = base_rows.shape[0]
+ways = 4
+
+
+def match_body(taps, odd, code, table, g, x, first, second, out, frame, lhs, w):
+    number, _, cols = x.shape
     reach = taps // 2
     spans = taps + 3
-    exact = lax.Precision.HIGHEST
-    cols_ab = [
-        jnp.dot(base_cols[...], places, precision=exact, preferred_element_type=f32)
-        for places in lane_places(taps)
-    ]
-    rows_ab = [
-        lax.dot_general(
-            places, base_rows[...], (((1,), (1,)), ((), ())), precision=exact, preferred_element_type=f32
-        )
-        for places in row_places(taps + 1, taps)
-    ]
-    for b in range(basis):
-        g[b] = sum(r[:, b : b + 1] * c[b : b + 1, :] for r, c in zip(rows_ab, cols_ab))
-    frame[...] = jnp.zeros_like(frame)
-    w[...] = jnp.zeros_like(w)
-    mask = band_mask(96, taps)
+    count = cols // lanes
+    depth = 96
+    mask = band_mask(depth, taps)
+    lane = lane_ids(16)
+    for way in range(ways):
+        clear_band(w.at[way], taps, depth, 0, spans)
 
     def one(e, way):
         total = jnp.zeros(g.shape[1:], f32)
-        for b in range(basis):
+        for b in range(g.shape[0]):
             total = total + table[b, code[e, b]] * g[b]
         total = total.astype(bf16).astype(f32)
-        profile[e] = total
         put_band(w.at[way], total, taps, mask, 0, spans, 0)
-        put_frame(frame.at[way], columns(x[e]), 16, reach)
+        lo, hi = halo_pair(odd[0] == 1, first[e], second[e])
+        for piece, row in ((lo, 16 - reach), (x[e], 16), (hi, 80)):
+            put_frame(frame.at[way], columns(piece), row, reach)
         put_lhs(lhs.at[way], frame.at[way], spans, 16 - reach)
-        acc[e] = jnp.dot(lhs[way], w[way], preferred_element_type=f32)
+        acc = jnp.dot(lhs[way], w[way], preferred_element_type=f32)
+        for m in range(count):
+            for h in range(2):
+                cut = slice(h * lanes, (h + 1) * lanes)
+                blocks = [acc[n * 16 : n * 16 + 16, cut] for n in (m, count + m)]
+                for b, part in enumerate(split_rows(*blocks, lane)):
+                    at = (2 * h + b) * 16
+                    out[e, at : at + 16, m * lanes : (m + 1) * lanes] = part.astype(bf16)
 
     def some(i, _):
         for way in range(ways):
@@ -172,25 +195,17 @@
     lax.fori_loop(0, number // ways, some, 0)
 
 
-ways = 2
-
-
-def match_own(code, table, base_rows, base_cols, x):
+def match(odd, code, table, g, x, first, second, taps):
     number, rows, cols = x.shape
-    basis, taps = base_rows.shape
     smem = pl.BlockSpec(memory_space=pltpu.SMEM)
     vmem = pl.BlockSpec(memory_space=pltpu.VMEM)
     spans = taps + 3
     return pl.pallas_call(
-        functools.partial(own_body, taps),
-        in_specs=[smem, smem, vmem, vmem, vmem],
-        out_specs=(vmem, vmem),
-        out_shape=(
-            jax.ShapeDtypeStruct((number, 256, 256), f32),
-            jax.ShapeDtypeStruct((number, taps + 1, lanes), f32),
-        ),
+        functools.partial(match_body, taps),
+        in_specs=[smem, smem, smem, vmem, vmem, vmem, vmem],
+        out_specs=vmem,
+        out_shape=jax.ShapeDtypeStruct((number, rows, cols), bf16),
         scratch_shapes=[
-            pltpu.VMEM((basis, taps + 1, lanes), f32),
             pltpu.VMEM((ways, 2, cols // lanes, 96, lanes), f32),
             pltpu.VMEM((ways, 256, spans * lanes), bf16),
             pltpu.VMEM((ways, spans * lanes, 256), bf16),
@@ -199,108 +214,75 @@
         cost_estimate=pl.CostEstimate(
             flops=number * 2 * 256 * 256 * spans * lanes, bytes_accessed=4 * x.size, transcendentals=0
         ),
-        name="match_own",
-    )(code, table, base_rows, base_cols, x)
-
-
-def halo_body(taps, odd, profile, first, second, acc, out, frame, lhs, w):
-    number, _, cols = out.shape
-    count = cols // lanes
-    spans = edge_spans(taps)
-    frame[...] = jnp.zeros_like(frame)
-    w[...] = jnp.zeros_like(w)
-    mask = band_mask(96, taps)
-    lane = lane_ids(16)
-
-    def one(e, way):
-        band = profile[e]
-        put_band(w.at[way, 0], band, taps, mask, 0, spans, 0)
-        put_band(w.at[way, 1], band, taps, mask, taps + 3 - spans, taps + 3, 0)
-        lo, hi = halo_pair(odd[0] == 1, first[e], second[e])
-        put_edges(taps, frame.at[way], lhs.at[way], lo, hi)
-        ends = [
-            jnp.dot(lhs[way, side], w[way, side], preferred_element_type=f32) for side in range(2)
-        ]
-        for m in range(count):
-            for h in range(2):
-                cut = slice(h * lanes, (h + 1) * lanes)
-                blocks = []
-                for n in (m, count + m):
-                    more = jnp.concatenate([end[n * 8 : n * 8 + 8, cut] for end in ends], axis=0)
-                    blocks.append(acc[e, n * 16 : n * 16 + 16, cut] + more)
-                for b, part in enumerate(split_rows(*blocks, lane)):
-                    at = (2 * h + b) * 16
-                    out[e, at : at + 16, m * lanes : (m + 1) * lanes] = part.astype(bf16)
-
-    def some(i, _):
-        for way in range(ways):
-            one(ways * i + way, way)
+        name="match",
+    )(odd, code, table, g, x, first, second)
+
+
+slots = 8
+
+
+def slot_body(mine, other, out):
+    number = mine.shape[0]
+    per = (mine.shape[1] - 1) // 2
+    patches = out.shape[0] // (slots + 1)
+
+    def clear(p, _):
+        out[p] = 0
+        for s in range(slots):
+            out[patches + p * slots + s] = 0
         return 0
 
-    lax.fori_loop(0, number // ways, some, 0)
-
-
-def match_halo(odd, profile, first, second, acc, rows, taps):
-    number, _, cols = first.shape
+    lax.fori_loop(0, patches, clear, 0)
+    for base, labels in ((0, mine), (number, other)):
+
+        def one(e, _):
+            plane = (labels[e, 0] * 2 * number + base + e) * 256
+            for k in range(per):
+                p = labels[e, 1 + k]
+                at = out[p]
+                out[patches + p * slots + at] = plane + labels[e, 1 + per + k]
+                out[p] = at + 1
+            return 0
+
+        lax.fori_loop(0, number, one, 0)
+
+
+def slot_table(mine, other, patches):
     smem = pl.BlockSpec(memory_space=pltpu.SMEM)
-    vmem = pl.BlockSpec(memory_space=pltpu.VMEM)
-    scratch = edge_scratch(taps, cols // lanes, 256)
     return pl.pallas_call(
-        functools.partial(halo_body, taps),
-        in_specs=[smem, vmem, vmem, vmem, vmem],
-        out_specs=vmem,
-        out_shape=jax.ShapeDtypeStruct((number, rows, cols), bf16),
-        scratch_shapes=[pltpu.VMEM((ways,) + each.shape, each.dtype) for each in scratch],
-        compiler_params=pltpu.CompilerParams(vmem_limit_bytes=vmem_bytes),
-        name="match_halo",
-    )(odd, profile, first, second, acc)
-
-
-def pile_body(core, mine_labels, other_labels, mine, other, out, counts, source, offset, scale, planes):
+        slot_body,
+        in_specs=[smem, smem],
+        out_specs=smem,
+        out_shape=jax.ShapeDtypeStruct((patches * (slots + 1),), jnp.int32),
+        name="slot_table",
+    )(mine, other)
+
+
+def pile_body(core, table, mine, other, out, planes, done, arrive, leave):
     number, rows, cols = mine.shape
     tiles = cols // lanes
-    per = (mine_labels.shape[1] - 1) // 2
-    patches = counts.shape[0]
-    slots = 8
-
-    def clear(p, _):
-        counts[p] = 0
-        for s in range(slots):
-            source[p * slots + s] = 0
-            offset[p * slots + s] = 0
-            scale[p * slots + s] = 0.0
-        return 0
-
-    lax.fori_loop(0, patches, clear, 0)
-
-    def enter(base, labels):
-        def one(e, _):
-            weight = labels[e, 0].astype(f32)
-            for k in range(per):
-                p = labels[e, 1 + k]
-                at = counts[p]
-                source[p * slots + at] = base + e
-                offset[p * slots + at] = labels[e, 1 + per + k]
-                scale[p * slots + at] = weight
-                counts[p] = at + 1
-            return 0
-
-        lax.fori_loop(0, number, one, 0)
-
-    enter(0, mine_labels)
-    enter(number, other_labels)
-    planes[0:number] = mine[...]
-    planes[number:] = other[...]
+    patches = table.shape[0] // (slots + 1)
+    come = [
+        pltpu.make_async_copy(ref, planes.at[pl.ds(i * number, number)], arrive.at[i])
+        for i, ref in enumerate((mine, other))
+    ]
+    for copy in come:
+        copy.start()
+    for copy in come:
+        copy.wait()
     lane = lane_ids(16)
 
     def patch(i, _):
         p = 2 * i + core[0]
 
         def some(used):
-            entries = [
-                (source[p * slots + s], offset[p * slots + s], scale[p * slots + s])
-                for s in range(used)
-            ]
+            entries = []
+            for s in range(used):
+                word = table[patches + p * slots + s]
+                plane = word // 256
+                entries.append(
+                    (plane % (2 * number), word % 256, (plane // (2 * number)).astype(f32))
+                )
             for c in range(rows // 16):
                 total = [jnp.zeros((16, lanes), f32)] * tiles
                 for e, o, weight in entries:
@@ -313,16 +295,16 @@
                         before = turned
                 for m in range(tiles):
                     at = m * rows + c * 16
-                    out[i, at : at + 16, :] = total[m].astype(bf16)
+                    done[i, at : at + 16, :] = total[m].astype(bf16)
             cover = jnp.zeros((16, lanes), f32)
             whole = jnp.zeros((16, lanes), f32)
             for e, o, weight in entries:
                 cover = cover + jnp.where(lane < o, 0.0, weight)
                 whole = whole + weight
             row = lax.broadcasted_iota(jnp.int32, (16, lanes), 0)
-            out[i, tiles * rows : tiles * rows + 16, :] = jnp.where(row == 0, cover, whole).astype(bf16)
-
-        used = counts[p]
+            done[i, tiles * rows : tiles * rows + 16, :] = jnp.where(row == 0, cover, whole).astype(bf16)
+
+        used = table[p]
         for top in range(2, slots + 1, 2):
             low = top - 2 if top > 2 else -1
 
@@ -330,37 +312,51 @@
             def _():
                 some(top)
 
+        pltpu.make_async_copy(done.at[i], out.at[i], leave.at[i]).start()
         return 0
 
     lax.fori_loop(0, patches // 2, patch, 0)
 
-
-def pile(core, mine_labels, other_labels, mine, other, patches):
+    def wait(i, _):
+        pltpu.make_async_copy(done.at[i], out.at[i], leave.at[i]).wait()
+        return 0
+
+    lax.fori_loop(0, patches // 2, wait, 0)
+
+
+def pile(core, table, mine, other):
     number, rows, cols = mine.shape
+    patches = table.shape[0] // (slots + 1)
     smem = pl.BlockSpec(memory_space=pltpu.SMEM)
-    vmem = pl.BlockSpec(memory_space=pltpu.VMEM)
-    length = cols // lanes * rows + 16
+    far = pl.BlockSpec(memory_space=pl.ANY)
+    shape = (patches // 2, cols // lanes * rows + 16, lanes)
     return pl.pallas_call(
         pile_body,
-        in_specs=[smem] * 3 + [vmem] * 2,
-        out_specs=vmem,
-        out_shape=jax.ShapeDtypeStruct((patches // 2, length, lanes), bf16),
+        in_specs=[smem, smem, far, far],
+        out_specs=far,
+        out_shape=jax.ShapeDtypeStruct(shape, bf16),
         scratch_shapes=[
-            pltpu.SMEM((patches,), jnp.int32),
-            pltpu.SMEM((patches * 8,), jnp.int32),
-            pltpu.SMEM((patches * 8,), jnp.int32),
-            pltpu.SMEM((patches * 8,), f32),
             pltpu.VMEM((2 * number, rows, cols), bf16),
+            pltpu.VMEM(shape, bf16),
+            pltpu.SemaphoreType.DMA((2,)),
+            pltpu.SemaphoreType.DMA((patches // 2,)),
         ],
         compiler_params=pltpu.CompilerParams(vmem_limit_bytes=vmem_bytes),
         name="pile",
-    )(core, mine_labels, other_labels, mine, other)
-
-
-def coadd_body(reach, odd, parts, coadd, first, second, stage):
+    )(core, table, mine, other)
+
+
+def coadd_body(reach, odd, far, coadd, first, second, parts, stage, arrive):
     count = parts.shape[0]
     rows, cols = coadd.shape
     tiles = cols // lanes
+    starts = [tiles * rows] + [m * rows for m in range(tiles)]
+    ends = [tiles * rows + 16] + [m * rows + rows for m in range(tiles)]
+    come = []
+    for i, (start, end) in enumerate(zip(starts, ends)):
+        span = pl.ds(start, end - start)
+        come.append(pltpu.make_async_copy(far.at[:, span, :], parts.at[:, span, :], arrive.at[i]))
+        come[i].start()
 
     def add(at):
         total = parts[0, at : at + 16, :].astype(f32)
@@ -368,13 +364,14 @@
             total = total + parts[n, at : at + 16, :].astype(f32)
         return total
 
+    come[0].wait()
     cover = add(tiles * rows)
     scales = [1.0 / jnp.maximum(cover[r : r + 1, :], 1.0) for r in (0, 1)]
     for m in range(tiles):
+        come[m + 1].wait()
         for b in range(group):
             value = add(m * rows + b * 16) * scales[min(m, 1)]
             stage[m, pl.ds(b, 16, stride=group), :] = value
-    for m in range(tiles):
         cut = slice(m * lanes, (m + 1) * lanes)
         coadd[:, cut] = stage[m]
         low = stage[m, 0:reach, :]
@@ -389,10 +386,14 @@
     vmem = pl.BlockSpec(memory_space=pltpu.VMEM)
     return pl.pallas_call(
         functools.partial(coadd_body, reach),
-        in_specs=[smem, vmem],
+        in_specs=[smem, pl.BlockSpec(memory_space=pl.ANY)],
         out_specs=(vmem, vmem, vmem),
         out_shape=(jax.ShapeDtypeStruct((rows, cols), f32), edge, edge),
-        scratch_shapes=[pltpu.VMEM((cols // lanes, rows, lanes), f32)],
+        scratch_shapes=[
+            pltpu.VMEM(parts.shape, bf16),
+            pltpu.VMEM((cols // lanes, rows, lanes), f32),
+            pltpu.SemaphoreType.DMA((cols // lanes + 1,)),
+        ],
         compiler_params=pltpu.CompilerParams(vmem_limit_bytes=vmem_bytes),
         name="coadd",
     )(odd, parts)
@@ -403,10 +404,11 @@
     rows, cols = x.shape
     spans = taps + 3
     mask = band_mask(112, taps)
-    frame[...] = jnp.zeros_like(frame)
+    for row in (0, 24 + rows):
+        frame[:, :, row : row + 24, :] = jnp.zeros((2, cols // lanes, 24, lanes), f32)
     put_frame(frame, columns(x[...].astype(bf16)), 24, reach)
     put_lhs(lhs, frame, spans, 24 - reach)
-    w[...] = jnp.zeros_like(w)
+    clear_band(w, taps, 112, 0, spans)
     for s in range(psf.shape[0]):
         total = 0.0
         for rows_at, cols_at in zip(row_places(profile.shape[1], taps), lane_places(taps)):
@@ -448,7 +450,8 @@
     count = cols // lanes
     spans = edge_spans(taps)
     frame[...] = jnp.zeros_like(frame)
-    w[...] = jnp.zeros_like(w)
+    clear_band(w.at[0], taps, 112, 0, spans)
+    clear_band(w.at[1], taps, 112, taps + 3 - spans, taps + 3)
     mask = band_mask(112, taps)
     lane = lane_ids(16)
     lo, hi = halo_pair(odd[0] == 1, first[...], second[...])
@@ -531,10 +534,14 @@
     swap = [(0, 1), (1, 0)]
     other_labels = lax.ppermute(labels, "core", swap)
 
-    acc, profile = match_own(coef_code, coef_table, basis_rows, basis_cols, exposures)
-    matched = match_halo(odd, profile, first, second, acc, rows, taps)
+    table = slot_table(labels, other_labels, patches)
+    cols_a, cols_b = profile_rows(basis_cols, taps)
+    rows_a = jnp.pad(basis_rows, ((0, 0), (0, 1)))
+    rows_b = jnp.pad(basis_rows, ((0, 0), (1, 0)))
+    g = rows_a[:, :, None] * cols_a[:, None, :] + rows_b[:, :, None] * cols_b[:, None, :]
+    matched = match(odd, coef_code, coef_table, g, exposures, first, second, taps)
     other = lax.ppermute(matched, "core", swap)
-    partial = pile(core[None], labels, other_labels, matched, other, patches)
+    partial = pile(core[None], table, matched, other)
     parts = lax.all_to_all(partial, across, split_axis=0, concat_axis=0, tiled=True)
     coadd, first, second = coadd_of(odd, parts, rows, cols, wide_reach)
     first, second = trade(first, second)

time: 94.1 us -> 90.2 us (0.959)
  Pallas kernels: 38.9 us -> 31.3 us
  waiting for transfers between devices: 2.17 us -> 5.2 us
  starting transfers between devices: 8.64 us -> 7.27 us
  local copies, waits for them, and re-layouts: 5.24 us -> 6.44 us
  other arithmetic: 1.19 us -> 2.24 us
    pallas_call x4, Pallas kernels: 28.1 us -> 21.4 us  [the longest x1 8.97 us: match(): pl.pallas_call(functools.partial(match_body, taps), in_specs=[smem, smem,...]
    ppermute x4, waiting for transfers between devices: 0.01 us -> 3.24 us  [trade(): lax.ppermute(rows, 'section', pairs + [(b, a) for a, b in pairs])]
    slice x0 -> x3, local copies, waits for them, and re-layouts: none -> 1.5 us  [the longest x2 0.79 us: profile_rows(): profile[..., :1]]
    unnamed x22 -> x21, local copies, waits for them, and re-layouts: 5.16 us -> 3.69 us
    ppermute x4, starting transfers between devices: 8.11 us -> 6.74 us  [trade(): lax.ppermute(rows, 'section', pairs + [(b, a) for a, b in pairs])]
    add x0 -> x1, other arithmetic: none -> 0.97 us  [on_device(): rows_a[:, :, None] * cols_a[:, None, :]]
  transfers between devices with their start and end apart: 6 -> 6, of which waited for: 2 -> 3; matrix products, arithmetic and copies ran while one was open for 3% -> 5% of each run, Pallas kernels for 17% -> 9%
where the time goes in v4:
time: 90.2 us; the launch traced here: 89.7 us
  blocking collectives  36.5 us (40%)
  Pallas kernels  31.3 us (35%)
  starting transfers between devices  7.27 us (8%)
  local copies, waits for them, and re-layouts  6.44 us (7%)
  waiting for transfers between devices  5.2 us (6%)
  other arithmetic  2.24 us (2%)
    all_to_all x1, blocking collectives, on_device(): lax.all_to_all(partial, across, split_axis=0, concat_axis=0, tiled=True)  36.5 us
    pallas_call x1, Pallas kernels, match(): pl.pallas_call(functools.partial(match_body, taps), in_specs=[smem, smem,...  8.97 us
    pallas_call x1, Pallas kernels, pile(): pl.pallas_call(pile_body, in_specs=[smem, smem, far, far], out_specs=far,...  7.5 us
    ppermute x4, starting transfers between devices, trade(): lax.ppermute(rows, 'section', pairs + [(b, a) for a, b in pairs])  6.74 us
    pallas_call x1, Pallas kernels, detect_own(): pl.pallas_call(functools.partial(detect_own_body, taps), out_shape=(jax.S...  5.42 us
    pallas_call x1, Pallas kernels, detect_halo(): pl.pallas_call(functools.partial(detect_halo_body, taps), in_specs=[smem,...  4.5 us
    unnamed x21, local copies, waits for them, and re-layouts  3.69 us
    ppermute x4, waiting for transfers between devices, trade(): lax.ppermute(rows, 'section', pairs + [(b, a) for a, b in pairs])  3.24 us
  transfers between devices with their start and end apart: 6, of which 3 were waited for; matrix products, arithmetic and copies ran while one was open for 5% of the time, Pallas kernels for 9%

profile of v4, /device:TPU:32, one launch (start us, length us, event | category | flops | bytes accessed | tf_op | source)
XLA Modules:
  0.0 89.7 jit_solution(12002041090042545101)
XLA Ops:
  0.6 1.1 %broadcast_select_fusion = (bf16[8,11,1024]{2,1,0:T(8,128)(2,1)S(1)}, bf16[8,11,1024]{2,1,0:T(8,128)(2,1)S(1)}) fusion(pred[]{:T(512)S(6)} %eq.6, bf16[8,64,1024]{2,1,0:T(8,128)(2,1)} %x.5), kind=kLoop, calls=%fused_computation.1 | loop fusion | flops 180224 | bytes 720897 | tf_op jit(solution)/shard_map/jit(_where)/select_n | solution.py:528
  1.8 3.8 %collective-permute-start.2 = (bf16[8,11,1024]{2,1,0:T(8,128)(2,1)S(1)}, bf16[8,11,1024]{2,1,0:T(8,128)(2,1)S(1)}, u32[]{:S(2)}, u32[]{:S(2)}) collective-permute-start(bf16[8,11,1024]{2,1,0:T(8,128)(2,1)S(1)} %get-tuple-element.12), channel_id=1, source_target_pairs={{32,64},{64,32},{33,65},{65,33},{34,66},{66,34},{35,67},{67,35},{3... | collective-permute-start | bytes 540680 | tf_op jit(solution)/shard_map/ppermute | solution.py:502
  5.6 0.1 collective-permute-start.1
  5.7 0.7 slice.12
  6.4 0.7 rev.7
  7.1 0.7 slice.13
  7.8 0.1 pad.12.clone
  7.9 0.1 pad.14.clone
  8.0 0.1 copy.16
  8.1 0.1 copy.14
  8.2 0.1 copy.13
  8.3 0.8 copy.17
  9.1 0.1 fusion
  9.2 0.1 pad_maximum_fusion
  9.2 1.0 %multiply_add_fusion.g = f32[27,24,128]{2,1,0:T(8,128)} fusion(f32[27,128]{1,0:T(8,128)S(1)} %get-tuple-element.17, f32[27,24]{1,0:T(8,128)S(1)} %get-tuple-element.15, f32[27,128]{1,0:T(8,128)S(1)} %get-tuple-element.16, f32[27,24]{1,0:T(8,128)S(1)} %get-tuple-element.14), kind=kLoop, calls=%fused_computation | loop fusion | flops 248832 | bytes 364608 | tf_op jit(solution)/shard_map/add | solution.py:541
  10.2 1.7 %collective-permute-done.2.second = bf16[8,11,1024]{2,1,0:T(8,128)(2,1)S(1)} collective-permute-done((bf16[8,11,1024]{2,1,0:T(8,128)(2,1)S(1)}, bf16[8,11,1024]{2,1,0:T(8,128)(2,1)S(1)}, u32[]{:S(2)}, u32[]{:S(2)}) %collective-permute-start.2) | collective-permute-done | bytes 180256 | tf_op jit(solution)/shard_map/ppermute | solution.py:502
  11.9 0.0 copy-start.8
  11.9 1.6 %collective-permute-done.1.first = bf16[8,11,1024]{2,1,0:T(8,128)(2,1)S(1)} collective-permute-done((bf16[8,11,1024]{2,1,0:T(8,128)(2,1)S(1)}, bf16[8,11,1024]{2,1,0:T(8,128)(2,1)S(1)}, u32[]{:S(2)}, u32[]{:S(2)}) %collective-permute-start.1) | collective-permute-done | bytes 180256 | tf_op jit(solution)/shard_map/ppermute | solution.py:502
  13.4 0.0 copy-start.9
  13.4 0.0 copy-done.8
  13.4 0.7 copy-done.9
  14.2 9.0 %match.1.mine = bf16[8,64,1024]{2,1,0:T(8,128)(2,1)} custom-call(s32[1]{0:T(128)} %bitcast.odd, s32[8,27]{1,0:T(8,128)} %code.1, f32[27,64]{1,0:T(8,128)} %table.1, f32[27,24,128]{2,1,0:T(8,128)} %multiply_add_fusion.g, bf16[8,64,1024]{2,1,0:T(8,128)(2,1)} %x.5, bf16[8,11,1024]{2,1,0:T(8,128)(2,1)} %copy-done.9, bf16[8,11,1024]{2,1,0:T(8,128)(2,1)} %copy-done.8), custom_call_target="tpu_custom_call" | custom-call | flops 3489660928 | bytes 2097152 | tf_op jit(solution)/shard_map/match/pallas_call | solution.py:203
  23.1 0.0 collective-permute-start.3
  23.1 0.0 copy-done.7
  23.1 0.1 copy.11
  23.2 0.0 copy-done.5
  23.2 0.0 copy-done.6
  23.2 0.1 pad_add_fusion.mine
  23.3 0.5 collective-permute-start
  23.8 2.0 %collective-permute-done.other = s32[8,17]{1,0:T(8,128)S(1)} collective-permute-done((s32[8,17]{1,0:T(8,128)S(1)}, s32[8,17]{1,0:T(8,128)S(1)}, u32[]{:S(2)}, u32[]{:S(2)}) %collective-permute-start) | collective-permute-done | bytes 576 | tf_op jit(solution)/shard_map/ppermute | solution.py:535
  25.8 0.0 copy-done.3
  25.8 0.6 copy-done.4
  26.4 2.5 %slot_table.1.table = s32[288]{0:T(512)} custom-call(s32[8,17]{1,0:T(8,128)} %copy-done.3, s32[8,17]{1,0:T(8,128)} %copy-done.4), custom_call_target="tpu_custom_call" | custom-call | tf_op jit(solution)/shard_map/slot_table/pallas_call | solution.py:252
  28.9 0.0 collective-permute-done.3.other
  28.9 0.0 copy-start
  28.9 1.0 %copy-done = bf16[8,64,1024]{2,1,0:T(8,128)(2,1)} copy-done((bf16[8,64,1024]{2,1,0:T(8,128)(2,1)}, bf16[8,64,1024]{2,1,0:T(8,128)(2,1)S(1)}, u32[]{:S(2)}) %copy-start) | copy-done | bytes 1048600
  29.9 7.5 %pile.1 = bf16[16,528,128]{2,1,0:T(8,128)(2,1)} custom-call(s32[1]{0:T(128)} %bitcast.1.core, s32[288]{0:T(512)} %slot_table.1.table, bf16[8,64,1024]{2,1,0:T(8,128)(2,1)} %match.1.mine, bf16[8,64,1024]{2,1,0:T(8,128)(2,1)} %copy-done), custom_call_target="tpu_custom_call" | custom-call | tf_op jit(solution)/shard_map/pile/pallas_call | solution.py:333
  37.4 36.5 %all_to_all.5.far = bf16[16,528,128]{2,1,0:T(8,128)(2,1)} all-to-all(bf16[16,528,128]{2,1,0:T(8,128)(2,1)} %pile.1), channel_id=1, replica_groups=mesh['section'=4,'sy'=4,'sx'=4,'core'=2] {'sy','sx'}, dimensions={0} | all-to-all | bytes 4325376 | tf_op jit(solution)/shard_map/all_to_all | solution.py:545
  73.9 2.4 %coadd.1 = (f32[64,1024]{1,0:T(8,128)}, bf16[20,1024]{1,0:T(8,128)(2,1)}, bf16[20,1024]{1,0:T(8,128)(2,1)}) custom-call(s32[1]{0:T(128)} %bitcast.odd, bf16[16,528,128]{2,1,0:T(8,128)(2,1)} %all_to_all.5.far), custom_call_target="tpu_custom_call" | custom-call | tf_op jit(solution)/shard_map/coadd/pallas_call | solution.py:387
  76.3 0.4 collective-permute-start.4
  76.6 2.5 %collective-permute-start.5 = (bf16[20,1024]{1,0:T(8,128)(2,1)}, bf16[20,1024]{1,0:T(8,128)(2,1)S(1)}, u32[]{:S(2)}, u32[]{:S(2)}) collective-permute-start(bf16[20,1024]{1,0:T(8,128)(2,1)} %get-tuple-element.10), channel_id=1, source_target_pairs={{32,64},{64,32},{33,65},{65,33},{34,66},{66,34},{35,67},{67,35},{3... | collective-permute-start | bytes 122888 | tf_op jit(solution)/shard_map/ppermute | solution.py:502
  79.1 5.4 %detect_own.1 = (f32[256,768]{1,0:T(8,128)}, f32[3,48,128]{2,1,0:T(8,128)}) custom-call(bf16[3,41,41]{2,1,0:T(8,128)(2,1)} %psf.1, f32[64,1024]{1,0:T(8,128)} %get-tuple-element.7.x), custom_call_target="tpu_custom_call" | custom-call | flops 2214592512 | bytes 262144 | tf_op jit(solution)/shard_map/detect_own/pallas_call | solution.py:429
  84.5 0.0 collective-permute-done.4.first
  84.5 0.0 collective-permute-done.5.second
  84.5 0.0 copy-start.2
  84.5 0.6 copy-done.1
  85.1 0.0 copy-done.2
  85.2 4.5 %detect_halo.1 = f32[3,64,1024]{2,1,0:T(8,128)} custom-call(s32[1]{0:T(128)} %bitcast.odd, f32[3,48,128]{2,1,0:T(8,128)} %get-tuple-element.8.profile, bf16[20,1024]{1,0:T(8,128)(2,1)} %copy-done.1, bf16[20,1024]{1,0:T(8,128)(2,1)} %copy-done.2, f32[256,768]{1,0:T(8,128)} %get-tuple-element.11.acc), custom_call_target="tpu_custom_call" | custom-call | tf_op jit(solution)/shard_map/detect_halo/pallas_call | solution.py:485
  (11 shorter events, 0.0 us)
Async XLA Ops:
  1.8 10.1 %collective-permute-start.2 = (bf16[8,11,1024]{2,1,0:T(8,128)(2,1)S(1)}, bf16[8,11,1024]{2,1,0:T(8,128)(2,1)S(1)}, u32[]{:S(2)}, u32[]{:S(2)}) collective-permute-start(bf16[8,11,1024]{2,1,0:T(8,128)(2,1)S(1)} %get-tuple-element.12), channel_id=1, source_target_pairs={{32,64},{64,32},{33,65},{65,33},{34,66},{66,34},{35,67},{67,35},{3... | collective-permute-start | bytes 540680 | tf_op jit(solution)/shard_map/ppermute | solution.py:502
  5.6 7.8 %collective-permute-start.1 = (bf16[8,11,1024]{2,1,0:T(8,128)(2,1)S(1)}, bf16[8,11,1024]{2,1,0:T(8,128)(2,1)S(1)}, u32[]{:S(2)}, u32[]{:S(2)}) collective-permute-start(bf16[8,11,1024]{2,1,0:T(8,128)(2,1)S(1)} %get-tuple-element.13), channel_id=1, source_target_pairs={{0,32},{64,96},{32,0},{96,64},{1,33},{65,97},{33,1},{97,65},{2,34}... | collective-permute-start | bytes 540680 | tf_op jit(solution)/shard_map/ppermute | solution.py:502
  11.9 1.6 %copy-start.8 = (bf16[8,11,1024]{2,1,0:T(8,128)(2,1)}, bf16[8,11,1024]{2,1,0:T(8,128)(2,1)S(1)}, u32[]{:S(2)}) copy-start(bf16[8,11,1024]{2,1,0:T(8,128)(2,1)S(1)} %collective-permute-done.2.second) | copy-start | bytes 540676
  13.4 0.7 copy-start.9
  14.1 9.0 %copy-start.7 = (s32[8]{0:T(128)S(1)}, s32[8]{0:T(128)}, u32[]{:S(2)}) copy-start(s32[8]{0:T(128)} %param.14) | copy-start | bytes 100
  14.1 9.1 %copy-start.5 = (s32[8,8]{1,0:T(8,128)S(1)}, s32[8,8]{1,0:T(8,128)}, u32[]{:S(2)}) copy-start(s32[8,8]{1,0:T(8,128)} %param.16) | copy-start | bytes 772
  14.2 9.1 %copy-start.6 = (s32[8,8]{1,0:T(8,128)S(1)}, s32[8,8]{1,0:T(8,128)}, u32[]{:S(2)}) copy-start(s32[8,8]{1,0:T(8,128)} %param.15) | copy-start | bytes 772
  23.1 5.8 %collective-permute-start.3 = (bf16[8,64,1024]{2,1,0:T(8,128)(2,1)}, bf16[8,64,1024]{2,1,0:T(8,128)(2,1)S(1)}, u32[]{:S(2)}, u32[]{:S(2)}) collective-permute-start(bf16[8,64,1024]{2,1,0:T(8,128)(2,1)} %match.1.mine), channel_id=1, source_target_pairs={{0,1},{1,0},{2,3},{3,2},{4,5},{5,4},{6,7},{7,6},{8,9},{9,8},{10,11... | collective-permute-start | bytes 3145736 | tf_op jit(solution)/shard_map/ppermute | solution.py:543
  23.3 2.5 %copy-start.3 = (s32[8,17]{1,0:T(8,128)}, s32[8,17]{1,0:T(8,128)S(1)}, u32[]{:S(2)}) copy-start(s32[8,17]{1,0:T(8,128)S(1)} %pad_add_fusion.mine) | copy-start | bytes 1636
  23.3 2.5 %collective-permute-start = (s32[8,17]{1,0:T(8,128)S(1)}, s32[8,17]{1,0:T(8,128)S(1)}, u32[]{:S(2)}, u32[]{:S(2)}) collective-permute-start(s32[8,17]{1,0:T(8,128)S(1)} %pad_add_fusion.mine), channel_id=1, source_target_pairs={{0,1},{1,0},{2,3},{3,2},{4,5},{5,4},{6,7},{7,6},{8,9},{9,8},{10,11... | collective-permute-start | bytes 1640 | tf_op jit(solution)/shard_map/ppermute | solution.py:535
  25.8 0.6 copy-start.4
  28.9 1.0 %copy-start = (bf16[8,64,1024]{2,1,0:T(8,128)(2,1)}, bf16[8,64,1024]{2,1,0:T(8,128)(2,1)S(1)}, u32[]{:S(2)}) copy-start(bf16[8,64,1024]{2,1,0:T(8,128)(2,1)S(1)} %collective-permute-done.3.other) | copy-start | bytes 3145732
  76.3 8.3 %collective-permute-start.4 = (bf16[20,1024]{1,0:T(8,128)(2,1)}, bf16[20,1024]{1,0:T(8,128)(2,1)S(1)}, u32[]{:S(2)}, u32[]{:S(2)}) collective-permute-start(bf16[20,1024]{1,0:T(8,128)(2,1)} %get-tuple-element.9), channel_id=1, source_target_pairs={{0,32},{64,96},{32,0},{96,64},{1,33},{65,97},{33,1},{97,65},{2,34}... | collective-permute-start | bytes 122888 | tf_op jit(solution)/shard_map/ppermute | solution.py:502
  76.6 7.9 %collective-permute-start.5 = (bf16[20,1024]{1,0:T(8,128)(2,1)}, bf16[20,1024]{1,0:T(8,128)(2,1)S(1)}, u32[]{:S(2)}, u32[]{:S(2)}) collective-permute-start(bf16[20,1024]{1,0:T(8,128)(2,1)} %get-tuple-element.10), channel_id=1, source_target_pairs={{32,64},{64,32},{33,65},{65,33},{34,66},{66,34},{35,67},{67,35},{3... | collective-permute-start | bytes 122888 | tf_op jit(solution)/shard_map/ppermute | solution.py:502
  84.5 0.6 copy-start.1
  84.5 0.6 copy-start.2

commit v5 on v4

--- a/solution.py
+++ b/solution.py
@@ -13,19 +13,7 @@
 lanes = 128
 half = 64
 group = 4
-vmem_bytes = 56 * 1024 * 1024
-
-
-def profile_rows(profile, taps):
-    lead = profile.shape[:-1]
-    zeros = lambda n: jnp.zeros(lead + (n,), profile.dtype)
-    first = jnp.concatenate(
-        [profile[..., :1], zeros(lanes - taps), profile[..., :0:-1]], axis=-1
-    )
-    second = jnp.concatenate(
-        [zeros(half - taps + 1), profile[..., ::-1], zeros(lanes - half - 1)], axis=-1
-    )
-    return first, second
+mib = 1024 * 1024
 
 
 def one_hot(rows, cols, at):
@@ -157,9 +145,22 @@
 ways = 4
 
 
-def match_body(taps, odd, code, table, g, x, first, second, out, frame, lhs, w):
+def match_body(taps, odd, code, table, base_rows, base_cols, x, first, second, out, g, frame, lhs, w):
     number, _, cols = x.shape
     reach = taps // 2
+    exact = lax.Precision.HIGHEST
+    rows_ab = [
+        jnp.dot(places, base_rows[...], precision=exact, preferred_element_type=f32)
+        for places in row_places(taps + 1, taps)
+    ]
+    cols_ab = [
+        lax.dot_general(
+            base_cols[...], places, (((0,), (0,)), ((), ())), precision=exact, preferred_element_type=f32
+        )
+        for places in lane_places(taps)
+    ]
+    for b in range(g.shape[0]):
+        g[b] = sum(r[:, b : b + 1] * c[b : b + 1, :] for r, c in zip(rows_ab, cols_ab))
     spans = taps + 3
     count = cols // lanes
     depth = 96
@@ -195,27 +196,29 @@
     lax.fori_loop(0, number // ways, some, 0)
 
 
-def match(odd, code, table, g, x, first, second, taps):
+def match(odd, code, table, base_rows, base_cols, x, first, second):
     number, rows, cols = x.shape
+    taps, basis = base_rows.shape
     smem = pl.BlockSpec(memory_space=pltpu.SMEM)
     vmem = pl.BlockSpec(memory_space=pltpu.VMEM)
     spans = taps + 3
     return pl.pallas_call(
         functools.partial(match_body, taps),
-        in_specs=[smem, smem, smem, vmem, vmem, vmem, vmem],
+        in_specs=[smem, smem, smem] + [vmem] * 5,
         out_specs=vmem,
         out_shape=jax.ShapeDtypeStruct((number, rows, cols), bf16),
         scratch_shapes=[
+            pltpu.VMEM((basis, taps + 1, lanes), f32),
             pltpu.VMEM((ways, 2, cols // lanes, 96, lanes), f32),
             pltpu.VMEM((ways, 256, spans * lanes), bf16),
             pltpu.VMEM((ways, spans * lanes, 256), bf16),
         ],
-        compiler_params=pltpu.CompilerParams(vmem_limit_bytes=vmem_bytes),
+        compiler_params=pltpu.CompilerParams(vmem_limit_bytes=24 * mib),
         cost_estimate=pl.CostEstimate(
             flops=number * 2 * 256 * 256 * spans * lanes, bytes_accessed=4 * x.size, transcendentals=0
         ),
         name="match",
-    )(odd, code, table, g, x, first, second)
+    )(odd, code, table, base_rows, base_cols, x, first, second)
 
 
 slots = 8
@@ -341,7 +344,7 @@
             pltpu.SemaphoreType.DMA((2,)),
             pltpu.SemaphoreType.DMA((patches // 2,)),
         ],
-        compiler_params=pltpu.CompilerParams(vmem_limit_bytes=vmem_bytes),
+        compiler_params=pltpu.CompilerParams(vmem_limit_bytes=8 * mib),
         name="pile",
     )(core, table, mine, other)
 
@@ -394,7 +397,7 @@
             pltpu.VMEM((cols // lanes, rows, lanes), f32),
             pltpu.SemaphoreType.DMA((cols // lanes + 1,)),
         ],
-        compiler_params=pltpu.CompilerParams(vmem_limit_bytes=vmem_bytes),
+        compiler_params=pltpu.CompilerParams(vmem_limit_bytes=8 * mib),
         name="coadd",
     )(odd, parts)
 
@@ -437,7 +440,7 @@
             pltpu.VMEM((256, spans * lanes), bf16),
             pltpu.VMEM((spans * lanes, scales * 256), bf16),
         ],
-        compiler_params=pltpu.CompilerParams(vmem_limit_bytes=vmem_bytes),
+        compiler_params=pltpu.CompilerParams(vmem_limit_bytes=20 * mib),
         cost_estimate=pl.CostEstimate(
             flops=scales * 2 * 256 * 256 * spans * lanes, bytes_accessed=4 * x.size, transcendentals=0
         ),
@@ -489,7 +492,7 @@
         out_shape=jax.ShapeDtypeStruct((scales, rows, cols), f32),
         scratch_shapes=edge_scratch(taps, cols // lanes, scales * 256)
         + [pltpu.VMEM((scales, cols // lanes, rows, lanes), f32)],
-        compiler_params=pltpu.CompilerParams(vmem_limit_bytes=vmem_bytes),
+        compiler_params=pltpu.CompilerParams(vmem_limit_bytes=20 * mib),
         name="detect_halo",
     )(odd, profile, first, second, acc)
 
@@ -535,11 +538,8 @@
     other_labels = lax.ppermute(labels, "core", swap)
 
     table = slot_table(labels, other_labels, patches)
-    cols_a, cols_b = profile_rows(basis_cols, taps)
-    rows_a = jnp.pad(basis_rows, ((0, 0), (0, 1)))
-    rows_b = jnp.pad(basis_rows, ((0, 0), (1, 0)))
-    g = rows_a[:, :, None] * cols_a[:, None, :] + rows_b[:, :, None] * cols_b[:, None, :]
-    matched = match(odd, coef_code, coef_table, g, exposures, first, second, taps)
+    table, coef_code = lax.optimization_barrier((table, coef_code))
+    matched = match(odd, coef_code, coef_table, basis_rows.T, basis_cols.T, exposures, first, second)
     other = lax.ppermute(matched, "core", swap)
     partial = pile(core[None], table, matched, other)
     parts = lax.all_to_all(partial, across, split_axis=0, concat_axis=0, tiled=True)

time: 90.2 us -> 85.3 us (0.946)
  Pallas kernels: 31.3 us -> 27.1 us
    ppermute x1, waiting for transfers between devices: 0.01 us -> 2.64 us  [on_device(): other = lax.ppermute(matched, 'core', swap)]
    unnamed x21 -> x20, local copies, waits for them, and re-layouts: 3.69 us -> 5.59 us
    pallas_call x1, Pallas kernels: 5.42 us -> 3.56 us  [detect_own(): pl.pallas_call(functools.partial(detect_own_body, taps), out_shape=(jax.S...]
    slice x3 -> x0, local copies, waits for them, and re-layouts: 1.5 us -> none  [the longest x2 0.79 us: profile_rows(): profile[..., :1]]
    ppermute x4, waiting for transfers between devices: 3.24 us -> 1.94 us  [trade(): lax.ppermute(rows, 'section', pairs + [(b, a) for a, b in pairs])]
    pallas_call x1, Pallas kernels: 4.5 us -> 3.31 us  [detect_halo(): pl.pallas_call(functools.partial(detect_halo_body, taps), in_specs=[smem,...]
    pallas_call x1, Pallas kernels: 8.97 us -> 7.78 us  [match(): pl.pallas_call(functools.partial(match_body, taps), in_specs=[smem, smem,...]
    pallas_call x1, Pallas kernels: 7.5 us -> 8.51 us  [pile(): pl.pallas_call(pile_body, in_specs=[smem, smem, far, far], out_specs=far,...]
  transfers between devices with their start and end apart: 6 -> 6, of which waited for: 3 -> 4; matrix products, arithmetic and copies ran while one was open for 5% -> 2% of each run, Pallas kernels for 9% -> 7%
where the time goes in v5:
time: 85.3 us; the launch traced here: 84.3 us
  blocking collectives  35.7 us (42%)
  Pallas kernels  27.1 us (32%)
  starting transfers between devices  6.85 us (8%)
  local copies, waits for them, and re-layouts  6.32 us (7%)
  waiting for transfers between devices  5.73 us (7%)
  other arithmetic  1.9 us (2%)
    all_to_all x1, blocking collectives, on_device(): lax.all_to_all(partial, across, split_axis=0, concat_axis=0, tiled=True)  35.7 us
    pallas_call x1, Pallas kernels, pile(): pl.pallas_call(pile_body, in_specs=[smem, smem, far, far], out_specs=far,...  8.51 us
    pallas_call x1, Pallas kernels, match(): pl.pallas_call(functools.partial(match_body, taps), in_specs=[smem, smem,...  7.78 us
    ppermute x4, starting transfers between devices, trade(): lax.ppermute(rows, 'section', pairs + [(b, a) for a, b in pairs])  6.74 us
    unnamed x20, local copies, waits for them, and re-layouts  5.59 us
    pallas_call x1, Pallas kernels, detect_own(): pl.pallas_call(functools.partial(detect_own_body, taps), out_shape=(jax.S...  3.56 us
    pallas_call x1, Pallas kernels, detect_halo(): pl.pallas_call(functools.partial(detect_halo_body, taps), in_specs=[smem,...  3.31 us
    ppermute x1, waiting for transfers between devices, on_device(): other = lax.ppermute(matched, 'core', swap)  2.64 us
  transfers between devices with their start and end apart: 6, of which 4 were waited for; matrix products, arithmetic and copies ran while one was open for 2% of the time, Pallas kernels for 7%

profile of v5, /device:TPU:32, one launch (start us, length us, event | category | flops | bytes accessed | tf_op | source)
XLA Modules:
  0.0 84.3 jit_solution(2225066850758502904)
XLA Ops:
  0.6 1.1 %broadcast_select_fusion = (bf16[8,11,1024]{2,1,0:T(8,128)(2,1)S(1)}, bf16[8,11,1024]{2,1,0:T(8,128)(2,1)S(1)}) fusion(pred[]{:T(512)S(6)} %eq.6, bf16[8,64,1024]{2,1,0:T(8,128)(2,1)} %x.1), kind=kLoop, calls=%fused_computation | loop fusion | flops 180224 | bytes 720897 | tf_op jit(solution)/shard_map/jit(_where)/select_n | solution.py:531
  1.8 3.8 %collective-permute-start.2 = (bf16[8,11,1024]{2,1,0:T(8,128)(2,1)S(1)}, bf16[8,11,1024]{2,1,0:T(8,128)(2,1)S(1)}, u32[]{:S(2)}, u32[]{:S(2)}) collective-permute-start(bf16[8,11,1024]{2,1,0:T(8,128)(2,1)S(1)} %get-tuple-element.16), channel_id=1, source_target_pairs={{32,64},{64,32},{33,65},{65,33},{34,66},{66,34},{35,67},{67,35},{3... | collective-permute-start | bytes 540680 | tf_op jit(solution)/shard_map/ppermute | solution.py:505
  5.6 0.1 collective-permute-start.1
  5.7 0.7 copy.11
  6.4 0.8 pad_add_fusion.mine
  7.2 0.0 copy-start.8
  7.2 0.0 collective-permute-start
  7.2 1.2 %collective-permute-done.other = s32[8,17]{1,0:T(8,128)S(1)} collective-permute-done((s32[8,17]{1,0:T(8,128)S(1)}, s32[8,17]{1,0:T(8,128)S(1)}, u32[]{:S(2)}, u32[]{:S(2)}) %collective-permute-start) | collective-permute-done | bytes 576 | tf_op jit(solution)/shard_map/ppermute | solution.py:538
  8.4 0.0 copy-done.8
  8.4 0.0 copy-start.9
  8.4 0.6 copy-done.9
  9.0 2.5 %slot_table.1.table = s32[288]{0:T(512)} custom-call(s32[8,17]{1,0:T(8,128)} %copy-done.8, s32[8,17]{1,0:T(8,128)} %copy-done.9), custom_call_target="tpu_custom_call" | custom-call | tf_op jit(solution)/shard_map/slot_table/pallas_call | solution.py:255
  11.5 0.4 collective-permute-done.2.second
  11.9 1.6 %collective-permute-done.1.first = bf16[8,11,1024]{2,1,0:T(8,128)(2,1)S(1)} collective-permute-done((bf16[8,11,1024]{2,1,0:T(8,128)(2,1)S(1)}, bf16[8,11,1024]{2,1,0:T(8,128)(2,1)S(1)}, u32[]{:S(2)}, u32[]{:S(2)}) %collective-permute-start.1) | collective-permute-done | bytes 180256 | tf_op jit(solution)/shard_map/ppermute | solution.py:505
  13.4 0.0 copy-start
  13.4 1.2 %copy-done = bf16[8,64,1024]{2,1,0:T(8,128)(2,1)S(1)} copy-done((bf16[8,64,1024]{2,1,0:T(8,128)(2,1)S(1)}, bf16[8,64,1024]{2,1,0:T(8,128)(2,1)}, u32[]{:S(2)}) %copy-start) | copy-done | bytes 1048600
  14.7 0.0 copy-start.4
  14.7 0.7 copy-done.4
  15.4 0.0 copy-start.5
  15.4 0.7 copy-done.5
  16.1 0.0 copy-start.6
  16.1 0.7 copy-done.6
  16.8 0.0 copy-start.7
  16.8 0.7 copy-done.7
  17.5 0.0 copy-start.1
  17.5 7.8 %match.1.mine = bf16[8,64,1024]{2,1,0:T(8,128)(2,1)S(1)} custom-call(s32[1]{0:T(128)} %bitcast.odd, s32[8,27]{1,0:T(8,128)S(1)} %copy-done.7, f32[27,64]{1,0:T(8,128)S(1)} %copy-done.4, f32[23,27]{1,0:T(8,128)S(1)} %bitcast.8, f32[23,27]{1,0:T(8,128)S(1)} %bitcast.9, bf16[8,64,1024]{2,1,0:T(8,128)(2,1)S(1)} %copy-done, ...), custom_call_target="tpu_custom_call" | custom-call | flops 3489660928 | bytes 2097152 | tf_op jit(solution)/shard_map/match/pallas_call | solution.py:205
  25.3 0.1 collective-permute-start.3
  25.4 2.6 %collective-permute-done.3.other = bf16[8,64,1024]{2,1,0:T(8,128)(2,1)S(1)} collective-permute-done((bf16[8,64,1024]{2,1,0:T(8,128)(2,1)S(1)}, bf16[8,64,1024]{2,1,0:T(8,128)(2,1)S(1)}, u32[]{:S(2)}, u32[]{:S(2)}) %collective-permute-start.3) | collective-permute-done | bytes 1048608 | tf_op jit(solution)/shard_map/ppermute | solution.py:543
  28.0 0.0 copy-done.1
  28.0 8.5 %pile.1 = bf16[16,528,128]{2,1,0:T(8,128)(2,1)S(1)} custom-call(s32[1]{0:T(128)} %bitcast.1.core, s32[288]{0:T(512)S(1)} %copy-done.1, bf16[8,64,1024]{2,1,0:T(8,128)(2,1)S(1)} %match.1.mine, bf16[8,64,1024]{2,1,0:T(8,128)(2,1)S(1)} %collective-permute-done.3.other), custom_call_target="tpu_custom_call" | custom-call | tf_op jit(solution)/shard_map/pile/pallas_call | solution.py:336
  36.5 35.7 %all_to_all.5.far = bf16[16,528,128]{2,1,0:T(8,128)(2,1)S(1)} all-to-all(bf16[16,528,128]{2,1,0:T(8,128)(2,1)S(1)} %pile.1), channel_id=1, replica_groups=mesh['section'=4,'sy'=4,'sx'=4,'core'=2] {'sy','sx'}, dimensions={0} | all-to-all | bytes 4325376 | tf_op jit(solution)/shard_map/all_to_all | solution.py:545
  72.2 0.0 copy-start.3
  72.2 1.4 %coadd.1 = (f32[64,1024]{1,0:T(8,128)}, bf16[20,1024]{1,0:T(8,128)(2,1)S(1)}, bf16[20,1024]{1,0:T(8,128)(2,1)S(1)}) custom-call(s32[1]{0:T(128)} %bitcast.odd, bf16[16,528,128]{2,1,0:T(8,128)(2,1)S(1)} %all_to_all.5.far), custom_call_target="tpu_custom_call" | custom-call | tf_op jit(solution)/shard_map/coadd/pallas_call | solution.py:390
  73.6 0.4 collective-permute-start.4
  74.0 2.5 %collective-permute-start.5 = (bf16[20,1024]{1,0:T(8,128)(2,1)S(1)}, bf16[20,1024]{1,0:T(8,128)(2,1)S(1)}, u32[]{:S(2)}, u32[]{:S(2)}) collective-permute-start(bf16[20,1024]{1,0:T(8,128)(2,1)S(1)} %get-tuple-element.14), channel_id=1, source_target_pairs={{32,64},{64,32},{33,65},{65,33},{34,66},{66,34},{35,67},{67,35},{3... | collective-permute-start | bytes 122888 | tf_op jit(solution)/shard_map/ppermute | solution.py:505
  76.5 0.0 copy-done.3
  76.5 0.0 copy-start.2
  76.5 0.9 %copy-done.2 = f32[64,1024]{1,0:T(8,128)S(1)} copy-done((f32[64,1024]{1,0:T(8,128)S(1)}, f32[64,1024]{1,0:T(8,128)}, u32[]{:S(2)}) %copy-start.2) | copy-done | bytes 262168
  77.4 3.6 %detect_own.1 = (f32[256,768]{1,0:T(8,128)S(1)}, f32[3,48,128]{2,1,0:T(8,128)S(1)}) custom-call(bf16[3,41,41]{2,1,0:T(8,128)(2,1)S(1)} %copy-done.3, f32[64,1024]{1,0:T(8,128)S(1)} %copy-done.2), custom_call_target="tpu_custom_call" | custom-call | flops 2214592512 | bytes 262144 | tf_op jit(solution)/shard_map/detect_own/pallas_call | solution.py:432
  81.0 0.0 collective-permute-done.4.first
  81.0 0.0 collective-permute-done.5.second
  81.0 3.3 %detect_halo.1 = f32[3,64,1024]{2,1,0:T(8,128)} custom-call(s32[1]{0:T(128)} %bitcast.odd, f32[3,48,128]{2,1,0:T(8,128)S(1)} %get-tuple-element.12.profile, bf16[20,1024]{1,0:T(8,128)(2,1)S(1)} %collective-permute-done.4.first, bf16[20,1024]{1,0:T(8,128)(2,1)S(1)} %collective-permute-done.5.second, f32[256,768]{1,0:T(8,128)S(1)} %get-tuple-element.15.acc), custom_call_target="tpu_custom_call" | custom-call | tf_op jit(solution)/shard_map/detect_halo/pallas_call | solution.py:488
Async XLA Ops:
  1.8 10.1 %collective-permute-start.2 = (bf16[8,11,1024]{2,1,0:T(8,128)(2,1)S(1)}, bf16[8,11,1024]{2,1,0:T(8,128)(2,1)S(1)}, u32[]{:S(2)}, u32[]{:S(2)}) collective-permute-start(bf16[8,11,1024]{2,1,0:T(8,128)(2,1)S(1)} %get-tuple-element.16), channel_id=1, source_target_pairs={{32,64},{64,32},{33,65},{65,33},{34,66},{66,34},{35,67},{67,35},{3... | collective-permute-start | bytes 540680 | tf_op jit(solution)/shard_map/ppermute | solution.py:505
  5.6 7.8 %collective-permute-start.1 = (bf16[8,11,1024]{2,1,0:T(8,128)(2,1)S(1)}, bf16[8,11,1024]{2,1,0:T(8,128)(2,1)S(1)}, u32[]{:S(2)}, u32[]{:S(2)}) collective-permute-start(bf16[8,11,1024]{2,1,0:T(8,128)(2,1)S(1)} %get-tuple-element.17), channel_id=1, source_target_pairs={{0,32},{64,96},{32,0},{96,64},{1,33},{65,97},{33,1},{97,65},{2,34}... | collective-permute-start | bytes 540680 | tf_op jit(solution)/shard_map/ppermute | solution.py:505
  7.2 1.2 %copy-start.8 = (s32[8,17]{1,0:T(8,128)}, s32[8,17]{1,0:T(8,128)S(1)}, u32[]{:S(2)}) copy-start(s32[8,17]{1,0:T(8,128)S(1)} %pad_add_fusion.mine) | copy-start | bytes 1636
  7.2 1.2 %collective-permute-start = (s32[8,17]{1,0:T(8,128)S(1)}, s32[8,17]{1,0:T(8,128)S(1)}, u32[]{:S(2)}, u32[]{:S(2)}) collective-permute-start(s32[8,17]{1,0:T(8,128)S(1)} %pad_add_fusion.mine), channel_id=1, source_target_pairs={{0,1},{1,0},{2,3},{3,2},{4,5},{5,4},{6,7},{7,6},{8,9},{9,8},{10,11... | collective-permute-start | bytes 1640 | tf_op jit(solution)/shard_map/ppermute | solution.py:538
  8.4 0.6 copy-start.9
  13.4 1.2 %copy-start = (bf16[8,64,1024]{2,1,0:T(8,128)(2,1)S(1)}, bf16[8,64,1024]{2,1,0:T(8,128)(2,1)}, u32[]{:S(2)}) copy-start(bf16[8,64,1024]{2,1,0:T(8,128)(2,1)} %x.1) | copy-start | bytes 3145732
  14.7 0.7 copy-start.4
  15.4 0.7 copy-start.5
  16.1 0.7 copy-start.6
  16.8 0.7 copy-start.7
  17.5 10.5 %copy-start.1 = (s32[288]{0:T(512)S(1)}, s32[288]{0:T(512)}, u32[]{:S(2)}) copy-start(s32[288]{0:T(512)} %slot_table.1.table) | copy-start | bytes 3460
  25.3 2.7 %collective-permute-start.3 = (bf16[8,64,1024]{2,1,0:T(8,128)(2,1)S(1)}, bf16[8,64,1024]{2,1,0:T(8,128)(2,1)S(1)}, u32[]{:S(2)}, u32[]{:S(2)}) collective-permute-start(bf16[8,64,1024]{2,1,0:T(8,128)(2,1)S(1)} %match.1.mine), channel_id=1, source_target_pairs={{0,1},{1,0},{2,3},{3,2},{4,5},{5,4},{6,7},{7,6},{8,9},{9,8},{10,11... | collective-permute-start | bytes 3145736 | tf_op jit(solution)/shard_map/ppermute | solution.py:543
  72.2 4.2 %copy-start.3 = (bf16[3,41,41]{2,1,0:T(8,128)(2,1)S(1)}, bf16[3,41,41]{2,1,0:T(8,128)(2,1)}, u32[]{:S(2)}) copy-start(bf16[3,41,41]{2,1,0:T(8,128)(2,1)} %psf.1) | copy-start | bytes 30262
  73.6 7.4 %collective-permute-start.4 = (bf16[20,1024]{1,0:T(8,128)(2,1)S(1)}, bf16[20,1024]{1,0:T(8,128)(2,1)S(1)}, u32[]{:S(2)}, u32[]{:S(2)}) collective-permute-start(bf16[20,1024]{1,0:T(8,128)(2,1)S(1)} %get-tuple-element.13), channel_id=1, source_target_pairs={{0,32},{64,96},{32,0},{96,64},{1,33},{65,97},{33,1},{97,65},{2,34}... | collective-permute-start | bytes 122888 | tf_op jit(solution)/shard_map/ppermute | solution.py:505
  74.0 7.0 %collective-permute-start.5 = (bf16[20,1024]{1,0:T(8,128)(2,1)S(1)}, bf16[20,1024]{1,0:T(8,128)(2,1)S(1)}, u32[]{:S(2)}, u32[]{:S(2)}) collective-permute-start(bf16[20,1024]{1,0:T(8,128)(2,1)S(1)} %get-tuple-element.14), channel_id=1, source_target_pairs={{32,64},{64,32},{33,65},{65,33},{34,66},{66,34},{35,67},{67,35},{3... | collective-permute-start | bytes 122888 | tf_op jit(solution)/shard_map/ppermute | solution.py:505
  76.5 1.0 %copy-start.2 = (f32[64,1024]{1,0:T(8,128)S(1)}, f32[64,1024]{1,0:T(8,128)}, u32[]{:S(2)}) copy-start(f32[64,1024]{1,0:T(8,128)} %get-tuple-element.11.x) | copy-start | bytes 786436

commit v6 on v5

--- a/solution.py
+++ b/solution.py
@@ -145,13 +145,13 @@
 ways = 4
 
 
-def match_body(taps, odd, code, table, base_rows, base_cols, x, first, second, out, g, frame, lhs, w):
-    number, _, cols = x.shape
-    reach = taps // 2
+def profile_body(code, table, base_rows, base_cols, out, g):
+    number, spans, _ = out.shape
+    taps = base_rows.shape[0]
     exact = lax.Precision.HIGHEST
     rows_ab = [
         jnp.dot(places, base_rows[...], precision=exact, preferred_element_type=f32)
-        for places in row_places(taps + 1, taps)
+        for places in row_places(spans, taps)
     ]
     cols_ab = [
         lax.dot_general(
@@ -161,20 +161,49 @@
     ]
     for b in range(g.shape[0]):
         g[b] = sum(r[:, b : b + 1] * c[b : b + 1, :] for r, c in zip(rows_ab, cols_ab))
+
+    def one(e, _):
+        total = jnp.zeros((spans, lanes), f32)
+        for b in range(g.shape[0]):
+            total = total + table[b, code[e, b]] * g[b]
+        out[e] = total.astype(bf16).astype(f32)
+        return 0
+
+    lax.fori_loop(0, number, one, 0)
+
+
+def profiles(code, table, base_rows, base_cols):
+    number, basis = code.shape
+    taps = base_rows.shape[0]
+    smem = pl.BlockSpec(memory_space=pltpu.SMEM)
+    vmem = pl.BlockSpec(memory_space=pltpu.VMEM)
+    return pl.pallas_call(
+        profile_body,
+        in_specs=[smem, smem, vmem, vmem],
+        out_specs=vmem,
+        out_shape=jax.ShapeDtypeStruct((number, taps + 1, lanes), f32),
+        scratch_shapes=[pltpu.VMEM((basis, taps + 1, lanes), f32)],
+        compiler_params=pltpu.CompilerParams(vmem_limit_bytes=56 * mib),
+        name="profiles",
+    )(code, table, base_rows, base_cols)
+
+
+def match_body(taps, odd, profile, far, first, second, out, x, frame, lhs, w, arrive):
+    number, _, cols = x.shape
+    reach = taps // 2
     spans = taps + 3
     count = cols // lanes
     depth = 96
+    come = [pltpu.make_async_copy(far.at[e], x.at[e], arrive.at[e]) for e in range(number)]
+    for copy in come:
+        copy.start()
     mask = band_mask(depth, taps)
     lane = lane_ids(16)
     for way in range(ways):
         clear_band(w.at[way], taps, depth, 0, spans)
 
     def one(e, way):
-        total = jnp.zeros(g.shape[1:], f32)
-        for b in range(g.shape[0]):
-            total = total + table[b, code[e, b]] * g[b]
-        total = total.astype(bf16).astype(f32)
-        put_band(w.at[way], total, taps, mask, 0, spans, 0)
+        put_band(w.at[way], profile[e], taps, mask, 0, spans, 0)
         lo, hi = halo_pair(odd[0] == 1, first[e], second[e])
         for piece, row in ((lo, 16 - reach), (x[e], 16), (hi, 80)):
             put_frame(frame.at[way], columns(piece), row, reach)
@@ -188,6 +217,9 @@
                     at = (2 * h + b) * 16
                     out[e, at : at + 16, m * lanes : (m + 1) * lanes] = part.astype(bf16)
 
+    for copy in come:
+        copy.wait()
+
     def some(i, _):
         for way in range(ways):
             one(ways * i + way, way)
@@ -196,29 +228,31 @@
     lax.fori_loop(0, number // ways, some, 0)
 
 
-def match(odd, code, table, base_rows, base_cols, x, first, second):
+def match(odd, profile, x, first, second):
     number, rows, cols = x.shape
-    taps, basis = base_rows.shape
+    taps = profile.shape[1] - 1
     smem = pl.BlockSpec(memory_space=pltpu.SMEM)
     vmem = pl.BlockSpec(memory_space=pltpu.VMEM)
+    far = pl.BlockSpec(memory_space=pltpu.HBM)
     spans = taps + 3
     return pl.pallas_call(
         functools.partial(match_body, taps),
-        in_specs=[smem, smem, smem] + [vmem] * 5,
+        in_specs=[smem, vmem, far, vmem, vmem],
         out_specs=vmem,
         out_shape=jax.ShapeDtypeStruct((number, rows, cols), bf16),
         scratch_shapes=[
-            pltpu.VMEM((basis, taps + 1, lanes), f32),
+            pltpu.VMEM(x.shape, bf16),
             pltpu.VMEM((ways, 2, cols // lanes, 96, lanes), f32),
             pltpu.VMEM((ways, 256, spans * lanes), bf16),
             pltpu.VMEM((ways, spans * lanes, 256), bf16),
+            pltpu.SemaphoreType.DMA((number,)),
         ],
         compiler_params=pltpu.CompilerParams(vmem_limit_bytes=24 * mib),
         cost_estimate=pl.CostEstimate(
             flops=number * 2 * 256 * 256 * spans * lanes, bytes_accessed=4 * x.size, transcendentals=0
         ),
         name="match",
-    )(odd, code, table, base_rows, base_cols, x, first, second)
+    )(odd, profile, x, first, second)
 
 
 slots = 8
@@ -261,18 +295,12 @@
     )(mine, other)
 
 
-def pile_body(core, table, mine, other, out, planes, done, arrive, leave):
+def pile_body(core, table, mine, other, out, planes):
     number, rows, cols = mine.shape
     tiles = cols // lanes
     patches = table.shape[0] // (slots + 1)
-    come = [
-        pltpu.make_async_copy(ref, planes.at[pl.ds(i * number, number)], arrive.at[i])
-        for i, ref in enumerate((mine, other))
-    ]
-    for copy in come:
-        copy.start()
-    for copy in come:
-        copy.wait()
+    planes[0:number] = mine[...]
+    planes[number:] = other[...]
     lane = lane_ids(16)
 
     def patch(i, _):
@@ -298,14 +326,14 @@
                         before = turned
                 for m in range(tiles):
                     at = m * rows + c * 16
-                    done[i, at : at + 16, :] = total[m].astype(bf16)
+                    out[i, at : at + 16, :] = total[m].astype(bf16)
             cover = jnp.zeros((16, lanes), f32)
             whole = jnp.zeros((16, lanes), f32)
             for e, o, weight in entries:
                 cover = cover + jnp.where(lane < o, 0.0, weight)
                 whole = whole + weight
             row = lax.broadcasted_iota(jnp.int32, (16, lanes), 0)
-            done[i, tiles * rows : tiles * rows + 16, :] = jnp.where(row == 0, cover, whole).astype(bf16)
+            out[i, tiles * rows : tiles * rows + 16, :] = jnp.where(row == 0, cover, whole).astype(bf16)
 
         used = table[p]
         for top in range(2, slots + 1, 2):
@@ -315,63 +343,41 @@
             def _():
                 some(top)
 
-        pltpu.make_async_copy(done.at[i], out.at[i], leave.at[i]).start()
         return 0
 
     lax.fori_loop(0, patches // 2, patch, 0)
-
-    def wait(i, _):
-        pltpu.make_async_copy(done.at[i], out.at[i], leave.at[i]).wait()
-        return 0
-
-    lax.fori_loop(0, patches // 2, wait, 0)
 
 
 def pile(core, table, mine, other):
     number, rows, cols = mine.shape
     patches = table.shape[0] // (slots + 1)
     smem = pl.BlockSpec(memory_space=pltpu.SMEM)
-    far = pl.BlockSpec(memory_space=pl.ANY)
+    vmem = pl.BlockSpec(memory_space=pltpu.VMEM)
     shape = (patches // 2, cols // lanes * rows + 16, lanes)
     return pl.pallas_call(
         pile_body,
-        in_specs=[smem, smem, far, far],
-        out_specs=far,
+        in_specs=[smem, smem, vmem, vmem],
+        out_specs=vmem,
         out_shape=jax.ShapeDtypeStruct(shape, bf16),
-        scratch_shapes=[
-            pltpu.VMEM((2 * number, rows, cols), bf16),
-            pltpu.VMEM(shape, bf16),
-            pltpu.SemaphoreType.DMA((2,)),
-            pltpu.SemaphoreType.DMA((patches // 2,)),
-        ],
-        compiler_params=pltpu.CompilerParams(vmem_limit_bytes=8 * mib),
+        scratch_shapes=[pltpu.VMEM((2 * number, rows, cols), bf16)],
+        compiler_params=pltpu.CompilerParams(vmem_limit_bytes=12 * mib),
         name="pile",
     )(core, table, mine, other)
 
 
-def coadd_body(reach, odd, far, coadd, first, second, parts, stage, arrive):
+def coadd_body(reach, odd, parts, coadd, first, second, stage):
     count = parts.shape[0]
     rows, cols = coadd.shape
     tiles = cols // lanes
-    starts = [tiles * rows] + [m * rows for m in range(tiles)]
-    ends = [tiles * rows + 16] + [m * rows + rows for m in range(tiles)]
-    come = []
-    for i, (start, end) in enumerate(zip(starts, ends)):
-        span = pl.ds(start, end - start)
-        come.append(pltpu.make_async_copy(far.at[:, span, :], parts.at[:, span, :], arrive.at[i]))
-        come[i].start()
-
     def add(at):
         total = parts[0, at : at + 16, :].astype(f32)
         for n in range(1, count):
             total = total + parts[n, at : at + 16, :].astype(f32)
         return total
 
-    come[0].wait()
     cover = add(tiles * rows)
     scales = [1.0 / jnp.maximum(cover[r : r + 1, :], 1.0) for r in (0, 1)]
     for m in range(tiles):
-        come[m + 1].wait()
         for b in range(group):
             value = add(m * rows + b * 16) * scales[min(m, 1)]
             stage[m, pl.ds(b, 16, stride=group), :] = value
@@ -389,13 +395,11 @@
     vmem = pl.BlockSpec(memory_space=pltpu.VMEM)
     return pl.pallas_call(
         functools.partial(coadd_body, reach),
-        in_specs=[smem, pl.BlockSpec(memory_space=pl.ANY)],
+        in_specs=[smem, vmem],
         out_specs=(vmem, vmem, vmem),
         out_shape=(jax.ShapeDtypeStruct((rows, cols), f32), edge, edge),
         scratch_shapes=[
-            pltpu.VMEM(parts.shape, bf16),
             pltpu.VMEM((cols // lanes, rows, lanes), f32),
-            pltpu.SemaphoreType.DMA((cols // lanes + 1,)),
         ],
         compiler_params=pltpu.CompilerParams(vmem_limit_bytes=8 * mib),
         name="coadd",
@@ -537,9 +541,10 @@
     swap = [(0, 1), (1, 0)]
     other_labels = lax.ppermute(labels, "core", swap)
 
+    profile = profiles(coef_code, coef_table, basis_rows.T, basis_cols.T)
     table = slot_table(labels, other_labels, patches)
-    table, coef_code = lax.optimization_barrier((table, coef_code))
-    matched = match(odd, coef_code, coef_table, basis_rows.T, basis_cols.T, exposures, first, second)
+    table, profile = lax.optimization_barrier((table, profile))
+    matched = match(odd, profile, exposures, first, second)
     other = lax.ppermute(matched, "core", swap)
     partial = pile(core[None], table, matched, other)
     parts = lax.all_to_all(partial, across, split_axis=0, concat_axis=0, tiled=True)

time: 85.3 us -> 80.7 us (0.946)
  waiting for transfers between devices: 5.73 us -> 3.03 us
  local copies, waits for them, and re-layouts: 6.32 us -> 4.39 us
  Pallas kernels: 27.1 us -> 25.6 us
  starting transfers between devices: 6.85 us -> 8.23 us
    unnamed x20 -> x14, local copies, waits for them, and re-layouts: 5.59 us -> 3.66 us
    ppermute x4, waiting for transfers between devices: 1.94 us -> 0.43 us  [trade(): lax.ppermute(rows, 'section', pairs + [(b, a) for a, b in pairs])]
    pallas_call x3 -> x4, Pallas kernels: 17.7 us -> 16.2 us  [the longest x1 7.44 us: match(): pl.pallas_call(functools.partial(match_body, taps), in_specs=[smem, vmem,...]
    ppermute x4, starting transfers between devices: 6.74 us -> 8.05 us  [trade(): lax.ppermute(rows, 'section', pairs + [(b, a) for a, b in pairs])]
    ppermute x1, waiting for transfers between devices: 1.15 us -> 0.01 us  [on_device(): other_labels = lax.ppermute(labels, 'core', swap)]
  transfers between devices with their start and end apart: 6 -> 6, of which waited for: 4 -> 2; matrix products, arithmetic and copies ran while one was open for 2% -> 2% of each run, Pallas kernels for 7% -> 11%
where the time goes in v6:
time: 80.7 us; the launch traced here: 80.1 us
  blocking collectives  36.3 us (45%)
  Pallas kernels  25.6 us (32%)
  starting transfers between devices  8.23 us (10%)
  local copies, waits for them, and re-layouts  4.39 us (5%)
  waiting for transfers between devices  3.03 us (4%)
  other arithmetic  1.9 us (2%)
    all_to_all x1, blocking collectives, on_device(): lax.all_to_all(partial, across, split_axis=0, concat_axis=0, tiled=True)  36.3 us
    ppermute x4, starting transfers between devices, trade(): lax.ppermute(rows, 'section', pairs + [(b, a) for a, b in pairs])  8.05 us
    pallas_call x1, Pallas kernels, match(): pl.pallas_call(functools.partial(match_body, taps), in_specs=[smem, vmem,...  7.44 us
    pallas_call x1, Pallas kernels, pile(): pl.pallas_call(pile_body, in_specs=[smem, smem, vmem, vmem], out_specs=vm...  5.07 us
    unnamed x14, local copies, waits for them, and re-layouts  3.66 us
    pallas_call x1, Pallas kernels, detect_own(): pl.pallas_call(functools.partial(detect_own_body, taps), out_shape=(jax.S...  3.57 us
    pallas_call x1, Pallas kernels, detect_halo(): pl.pallas_call(functools.partial(detect_halo_body, taps), in_specs=[smem,...  3.31 us
    pallas_call x1, Pallas kernels, profiles(): pl.pallas_call(profile_body, in_specs=[smem, smem, vmem, vmem], out_specs...  2.65 us
  transfers between devices with their start and end apart: 6, of which 2 were waited for; matrix products, arithmetic and copies ran while one was open for 2% of the time, Pallas kernels for 11%

profile of v6, /device:TPU:32, one launch (start us, length us, event | category | flops | bytes accessed | tf_op | source)
XLA Modules:
  0.0 80.1 jit_solution(10900744651448441407)
XLA Ops:
  0.6 1.1 %broadcast_select_fusion = (bf16[8,11,1024]{2,1,0:T(8,128)(2,1)S(1)}, bf16[8,11,1024]{2,1,0:T(8,128)(2,1)S(1)}) fusion(pred[]{:T(512)S(6)} %eq.6, bf16[8,64,1024]{2,1,0:T(8,128)(2,1)} %far.1), kind=kLoop, calls=%fused_computation | loop fusion | flops 180224 | bytes 720897 | tf_op jit(solution)/shard_map/jit(_where)/select_n | solution.py:535
  1.8 3.8 %collective-permute-start.2 = (bf16[8,11,1024]{2,1,0:T(8,128)(2,1)S(1)}, bf16[8,11,1024]{2,1,0:T(8,128)(2,1)S(1)}, u32[]{:S(2)}, u32[]{:S(2)}) collective-permute-start(bf16[8,11,1024]{2,1,0:T(8,128)(2,1)S(1)} %get-tuple-element.16), channel_id=1, source_target_pairs={{32,64},{64,32},{33,65},{65,33},{34,66},{66,34},{35,67},{67,35},{3... | collective-permute-start | bytes 540680 | tf_op jit(solution)/shard_map/ppermute | solution.py:509
  5.6 0.1 collective-permute-start.1
  5.7 0.7 copy.11
  6.4 0.8 pad_add_fusion.mine
  7.2 0.0 copy-start.5
  7.2 0.0 collective-permute-start
  7.2 2.6 %profiles.1.profile = f32[8,24,128]{2,1,0:T(8,128)} custom-call(s32[8,27]{1,0:T(8,128)} %code.1, f32[27,64]{1,0:T(8,128)} %table.1, f32[23,27]{1,0:T(8,128)} %bitcast.9, f32[23,27]{1,0:T(8,128)} %bitcast.10), custom_call_target="tpu_custom_call" | custom-call | tf_op jit(solution)/shard_map/profiles/pallas_call | solution.py:180
  9.9 0.0 collective-permute-done.other
  9.9 0.0 copy-done.5
  9.9 0.0 copy-start.6
  9.9 0.6 copy-done.6
  10.5 2.5 %slot_table.1.table = s32[288]{0:T(512)} custom-call(s32[8,17]{1,0:T(8,128)} %copy-done.5, s32[8,17]{1,0:T(8,128)} %copy-done.6), custom_call_target="tpu_custom_call" | custom-call | tf_op jit(solution)/shard_map/slot_table/pallas_call | solution.py:289
  13.0 0.0 collective-permute-done.2.second
  13.0 0.4 collective-permute-done.1.first
  13.4 0.0 copy-start
  13.4 1.2 %copy-done = bf16[8,64,1024]{2,1,0:T(8,128)(2,1)S(1)} copy-done((bf16[8,64,1024]{2,1,0:T(8,128)(2,1)S(1)}, bf16[8,64,1024]{2,1,0:T(8,128)(2,1)}, u32[]{:S(2)}) %copy-start) | copy-done | bytes 1048600
  14.7 0.0 copy-start.1
  14.7 0.9 %copy-done.1 = f32[8,24,128]{2,1,0:T(8,128)S(1)} copy-done((f32[8,24,128]{2,1,0:T(8,128)S(1)}, f32[8,24,128]{2,1,0:T(8,128)}, u32[]{:S(2)}) %copy-start.1) | copy-done | bytes 98328
  15.6 0.0 copy-start.2
  15.6 7.4 %match.1.mine = bf16[8,64,1024]{2,1,0:T(8,128)(2,1)S(1)} custom-call(s32[1]{0:T(128)} %bitcast.odd, f32[8,24,128]{2,1,0:T(8,128)S(1)} %copy-done.1, bf16[8,64,1024]{2,1,0:T(8,128)(2,1)S(1)} %copy-done, bf16[8,11,1024]{2,1,0:T(8,128)(2,1)S(1)} %collective-permute-done.1.first, bf16[8,11,1024]{2,1,0:T(8,128)(2,1)S(1)} %collective-permute-done.2.second), custom_call_target="tpu_custom_call" | custom-call | flops 3489660928 | bytes 2097152 | tf_op jit(solution)/shard_map/match/pallas_call | solution.py:238
  23.0 0.2 collective-permute-start.3
  23.2 2.6 %collective-permute-done.3.other = bf16[8,64,1024]{2,1,0:T(8,128)(2,1)S(1)} collective-permute-done((bf16[8,64,1024]{2,1,0:T(8,128)(2,1)S(1)}, bf16[8,64,1024]{2,1,0:T(8,128)(2,1)S(1)}, u32[]{:S(2)}, u32[]{:S(2)}) %collective-permute-start.3) | collective-permute-done | bytes 1048608 | tf_op jit(solution)/shard_map/ppermute | solution.py:548
  25.8 0.0 copy-done.2
  25.8 5.1 %pile.1 = bf16[16,528,128]{2,1,0:T(8,128)(2,1)S(1)} custom-call(s32[1]{0:T(128)} %bitcast.1.core, s32[288]{0:T(512)S(1)} %copy-done.2, bf16[8,64,1024]{2,1,0:T(8,128)(2,1)S(1)} %match.1.mine, bf16[8,64,1024]{2,1,0:T(8,128)(2,1)S(1)} %collective-permute-done.3.other), custom_call_target="tpu_custom_call" | custom-call | tf_op jit(solution)/shard_map/pile/pallas_call | solution.py:357
  30.8 36.3 %all_to_all.5.parts = bf16[16,528,128]{2,1,0:T(8,128)(2,1)S(1)} all-to-all(bf16[16,528,128]{2,1,0:T(8,128)(2,1)S(1)} %pile.1), channel_id=1, replica_groups=mesh['section'=4,'sy'=4,'sx'=4,'core'=2] {'sy','sx'}, dimensions={0} | all-to-all | bytes 4325376 | tf_op jit(solution)/shard_map/all_to_all | solution.py:550
  67.1 0.0 copy-start.4
  67.1 1.0 %coadd.1 = (f32[64,1024]{1,0:T(8,128)}, bf16[20,1024]{1,0:T(8,128)(2,1)S(1)}, bf16[20,1024]{1,0:T(8,128)(2,1)S(1)}) custom-call(s32[1]{0:T(128)} %bitcast.odd, bf16[16,528,128]{2,1,0:T(8,128)(2,1)S(1)} %all_to_all.5.parts), custom_call_target="tpu_custom_call" | custom-call | tf_op jit(solution)/shard_map/coadd/pallas_call | solution.py:396
  68.1 2.0 %collective-permute-start.4 = (bf16[20,1024]{1,0:T(8,128)(2,1)S(1)}, bf16[20,1024]{1,0:T(8,128)(2,1)S(1)}, u32[]{:S(2)}, u32[]{:S(2)}) collective-permute-start(bf16[20,1024]{1,0:T(8,128)(2,1)S(1)} %get-tuple-element.13), channel_id=1, source_target_pairs={{0,32},{64,96},{32,0},{96,64},{1,33},{65,97},{33,1},{97,65},{2,34}... | collective-permute-start | bytes 122888 | tf_op jit(solution)/shard_map/ppermute | solution.py:509
  70.1 2.2 %collective-permute-start.5 = (bf16[20,1024]{1,0:T(8,128)(2,1)S(1)}, bf16[20,1024]{1,0:T(8,128)(2,1)S(1)}, u32[]{:S(2)}, u32[]{:S(2)}) collective-permute-start(bf16[20,1024]{1,0:T(8,128)(2,1)S(1)} %get-tuple-element.14), channel_id=1, source_target_pairs={{32,64},{64,32},{33,65},{65,33},{34,66},{66,34},{35,67},{67,35},{3... | collective-permute-start | bytes 122888 | tf_op jit(solution)/shard_map/ppermute | solution.py:509
  72.3 0.0 copy-done.4
  72.3 0.0 copy-start.3
  72.3 0.9 %copy-done.3 = f32[64,1024]{1,0:T(8,128)S(1)} copy-done((f32[64,1024]{1,0:T(8,128)S(1)}, f32[64,1024]{1,0:T(8,128)}, u32[]{:S(2)}) %copy-start.3) | copy-done | bytes 262168
  73.2 3.6 %detect_own.1 = (f32[256,768]{1,0:T(8,128)S(1)}, f32[3,48,128]{2,1,0:T(8,128)S(1)}) custom-call(bf16[3,41,41]{2,1,0:T(8,128)(2,1)S(1)} %copy-done.4, f32[64,1024]{1,0:T(8,128)S(1)} %copy-done.3), custom_call_target="tpu_custom_call" | custom-call | flops 2214592512 | bytes 262144 | tf_op jit(solution)/shard_map/detect_own/pallas_call | solution.py:436
  76.8 0.0 collective-permute-done.4.first
  76.8 0.0 collective-permute-done.5.second
  76.8 3.3 %detect_halo.1 = f32[3,64,1024]{2,1,0:T(8,128)} custom-call(s32[1]{0:T(128)} %bitcast.odd, f32[3,48,128]{2,1,0:T(8,128)S(1)} %get-tuple-element.12.profile, bf16[20,1024]{1,0:T(8,128)(2,1)S(1)} %collective-permute-done.4.first, bf16[20,1024]{1,0:T(8,128)(2,1)S(1)} %collective-permute-done.5.second, f32[256,768]{1,0:T(8,128)S(1)} %get-tuple-element.15.acc), custom_call_target="tpu_custom_call" | custom-call | tf_op jit(solution)/shard_map/detect_halo/pallas_call | solution.py:492
Async XLA Ops:
  1.8 11.2 %collective-permute-start.2 = (bf16[8,11,1024]{2,1,0:T(8,128)(2,1)S(1)}, bf16[8,11,1024]{2,1,0:T(8,128)(2,1)S(1)}, u32[]{:S(2)}, u32[]{:S(2)}) collective-permute-start(bf16[8,11,1024]{2,1,0:T(8,128)(2,1)S(1)} %get-tuple-element.16), channel_id=1, source_target_pairs={{32,64},{64,32},{33,65},{65,33},{34,66},{66,34},{35,67},{67,35},{3... | collective-permute-start | bytes 540680 | tf_op jit(solution)/shard_map/ppermute | solution.py:509
  5.6 7.8 %collective-permute-start.1 = (bf16[8,11,1024]{2,1,0:T(8,128)(2,1)S(1)}, bf16[8,11,1024]{2,1,0:T(8,128)(2,1)S(1)}, u32[]{:S(2)}, u32[]{:S(2)}) collective-permute-start(bf16[8,11,1024]{2,1,0:T(8,128)(2,1)S(1)} %get-tuple-element.17), channel_id=1, source_target_pairs={{0,32},{64,96},{32,0},{96,64},{1,33},{65,97},{33,1},{97,65},{2,34}... | collective-permute-start | bytes 540680 | tf_op jit(solution)/shard_map/ppermute | solution.py:509
  7.2 2.7 %copy-start.5 = (s32[8,17]{1,0:T(8,128)}, s32[8,17]{1,0:T(8,128)S(1)}, u32[]{:S(2)}) copy-start(s32[8,17]{1,0:T(8,128)S(1)} %pad_add_fusion.mine) | copy-start | bytes 1636
  7.2 2.7 %collective-permute-start = (s32[8,17]{1,0:T(8,128)S(1)}, s32[8,17]{1,0:T(8,128)S(1)}, u32[]{:S(2)}, u32[]{:S(2)}) collective-permute-start(s32[8,17]{1,0:T(8,128)S(1)} %pad_add_fusion.mine), channel_id=1, source_target_pairs={{0,1},{1,0},{2,3},{3,2},{4,5},{5,4},{6,7},{7,6},{8,9},{9,8},{10,11... | collective-permute-start | bytes 1640 | tf_op jit(solution)/shard_map/ppermute | solution.py:542
  9.9 0.6 copy-start.6
  13.4 1.2 %copy-start = (bf16[8,64,1024]{2,1,0:T(8,128)(2,1)S(1)}, bf16[8,64,1024]{2,1,0:T(8,128)(2,1)}, u32[]{:S(2)}) copy-start(bf16[8,64,1024]{2,1,0:T(8,128)(2,1)} %far.1) | copy-start | bytes 3145732
  14.7 0.9 %copy-start.1 = (f32[8,24,128]{2,1,0:T(8,128)S(1)}, f32[8,24,128]{2,1,0:T(8,128)}, u32[]{:S(2)}) copy-start(f32[8,24,128]{2,1,0:T(8,128)} %profiles.1.profile) | copy-start | bytes 294916
  15.6 10.2 %copy-start.2 = (s32[288]{0:T(512)S(1)}, s32[288]{0:T(512)}, u32[]{:S(2)}) copy-start(s32[288]{0:T(512)} %slot_table.1.table) | copy-start | bytes 3460
  23.0 2.7 %collective-permute-start.3 = (bf16[8,64,1024]{2,1,0:T(8,128)(2,1)S(1)}, bf16[8,64,1024]{2,1,0:T(8,128)(2,1)S(1)}, u32[]{:S(2)}, u32[]{:S(2)}) collective-permute-start(bf16[8,64,1024]{2,1,0:T(8,128)(2,1)S(1)} %match.1.mine), channel_id=1, source_target_pairs={{0,1},{1,0},{2,3},{3,2},{4,5},{5,4},{6,7},{7,6},{8,9},{9,8},{10,11... | collective-permute-start | bytes 3145736 | tf_op jit(solution)/shard_map/ppermute | solution.py:548
  67.1 5.2 %copy-start.4 = (bf16[3,41,41]{2,1,0:T(8,128)(2,1)S(1)}, bf16[3,41,41]{2,1,0:T(8,128)(2,1)}, u32[]{:S(2)}) copy-start(bf16[3,41,41]{2,1,0:T(8,128)(2,1)} %psf.1) | copy-start | bytes 30262
  68.1 8.7 %collective-permute-start.4 = (bf16[20,1024]{1,0:T(8,128)(2,1)S(1)}, bf16[20,1024]{1,0:T(8,128)(2,1)S(1)}, u32[]{:S(2)}, u32[]{:S(2)}) collective-permute-start(bf16[20,1024]{1,0:T(8,128)(2,1)S(1)} %get-tuple-element.13), channel_id=1, source_target_pairs={{0,32},{64,96},{32,0},{96,64},{1,33},{65,97},{33,1},{97,65},{2,34}... | collective-permute-start | bytes 122888 | tf_op jit(solution)/shard_map/ppermute | solution.py:509
  70.1 6.8 %collective-permute-start.5 = (bf16[20,1024]{1,0:T(8,128)(2,1)S(1)}, bf16[20,1024]{1,0:T(8,128)(2,1)S(1)}, u32[]{:S(2)}, u32[]{:S(2)}) collective-permute-start(bf16[20,1024]{1,0:T(8,128)(2,1)S(1)} %get-tuple-element.14), channel_id=1, source_target_pairs={{32,64},{64,32},{33,65},{65,33},{34,66},{66,34},{35,67},{67,35},{3... | collective-permute-start | bytes 122888 | tf_op jit(solution)/shard_map/ppermute | solution.py:509
  72.3 1.0 %copy-start.3 = (f32[64,1024]{1,0:T(8,128)S(1)}, f32[64,1024]{1,0:T(8,128)}, u32[]{:S(2)}) copy-start(f32[64,1024]{1,0:T(8,128)} %get-tuple-element.11.x) | copy-start | bytes 786436

commit v7 on v6

--- a/solution.py
+++ b/solution.py
@@ -183,12 +183,12 @@
         out_specs=vmem,
         out_shape=jax.ShapeDtypeStruct((number, taps + 1, lanes), f32),
         scratch_shapes=[pltpu.VMEM((basis, taps + 1, lanes), f32)],
-        compiler_params=pltpu.CompilerParams(vmem_limit_bytes=56 * mib),
+        compiler_params=pltpu.CompilerParams(vmem_limit_bytes=4 * mib),
         name="profiles",
     )(code, table, base_rows, base_cols)
 
 
-def match_body(taps, odd, profile, far, first, second, out, x, frame, lhs, w, arrive):
+def match_body(taps, odd, place, profile, far, first, second, keep, send, x, frame, lhs, w, arrive):
     number, _, cols = x.shape
     reach = taps // 2
     spans = taps + 3
@@ -209,13 +209,21 @@
             put_frame(frame.at[way], columns(piece), row, reach)
         put_lhs(lhs.at[way], frame.at[way], spans, 16 - reach)
         acc = jnp.dot(lhs[way], w[way], preferred_element_type=f32)
-        for m in range(count):
-            for h in range(2):
-                cut = slice(h * lanes, (h + 1) * lanes)
+        for h in range(2):
+            cut = slice(h * lanes, (h + 1) * lanes)
+            parts = []
+            for m in range(count):
                 blocks = [acc[n * 16 : n * 16 + 16, cut] for n in (m, count + m)]
-                for b, part in enumerate(split_rows(*blocks, lane)):
-                    at = (2 * h + b) * 16
-                    out[e, at : at + 16, m * lanes : (m + 1) * lanes] = part.astype(bf16)
+                parts.append([part.astype(bf16) for part in split_rows(*blocks, lane)])
+            for b in range(2):
+                rows = slice((2 * h + b) * 16, (2 * h + b) * 16 + 16)
+                tiles = [part[b] for part in parts]
+                low = [jnp.zeros((16, lanes), bf16)] + tiles[: count // 2]
+                high = tiles[count // 2 - 1 :]
+                for k in range(count // 2 + 1):
+                    at = slice(k * lanes, (k + 1) * lanes)
+                    keep[e, rows, at] = jnp.where(place[0] == 0, low[k], high[k])
+                    send[e, rows, at] = jnp.where(place[0] == 0, high[k], low[k])
 
     for copy in come:
         copy.wait()
@@ -228,7 +236,7 @@
     lax.fori_loop(0, number // ways, some, 0)
 
 
-def match(odd, profile, x, first, second):
+def match(odd, place, profile, x, first, second):
     number, rows, cols = x.shape
     taps = profile.shape[1] - 1
     smem = pl.BlockSpec(memory_space=pltpu.SMEM)
@@ -237,9 +245,9 @@
     spans = taps + 3
     return pl.pallas_call(
         functools.partial(match_body, taps),
-        in_specs=[smem, vmem, far, vmem, vmem],
-        out_specs=vmem,
-        out_shape=jax.ShapeDtypeStruct((number, rows, cols), bf16),
+        in_specs=[smem, smem, vmem, far, vmem, vmem],
+        out_specs=(vmem, vmem),
+        out_shape=(jax.ShapeDtypeStruct((number, rows, cols // 2 + lanes), bf16),) * 2,
         scratch_shapes=[
             pltpu.VMEM(x.shape, bf16),
             pltpu.VMEM((ways, 2, cols // lanes, 96, lanes), f32),
@@ -252,7 +260,7 @@
             flops=number * 2 * 256 * 256 * spans * lanes, bytes_accessed=4 * x.size, transcendentals=0
         ),
         name="match",
-    )(odd, profile, x, first, second)
+    )(odd, place, profile, x, first, second)
 
 
 slots = 8
@@ -291,119 +299,195 @@
         in_specs=[smem, smem],
         out_specs=smem,
         out_shape=jax.ShapeDtypeStruct((patches * (slots + 1),), jnp.int32),
+        compiler_params=pltpu.CompilerParams(vmem_limit_bytes=mib),
         name="slot_table",
     )(mine, other)
 
 
-def pile_body(core, table, mine, other, out, planes):
+def role_pairs(step, size, shift):
+    index = lambda y, x, core: ((y % size) * size + x % size) * 2 + core
+    pairs = []
+    for y in range(size):
+        for x in range(size):
+            for core in range(2):
+                to = (y, x + shift) if core == step else (y + shift, x)
+                pairs.append((index(y, x, core), index(*to, core)))
+    return pairs
+
+
+def pile_body(chunks, size, place, table, mine, other, *rest):
+    outs, planes = rest[:-1], rest[-1]
     number, rows, cols = mine.shape
-    tiles = cols // lanes
+    tiles = cols // lanes - 1
     patches = table.shape[0] // (slots + 1)
+    core = place[0]
     planes[0:number] = mine[...]
     planes[number:] = other[...]
     lane = lane_ids(16)
-
-    def patch(i, _):
-        p = 2 * i + core[0]
-
-        def some(used):
-            entries = []
-            for s in range(used):
-                word = table[patches + p * slots + s]
-                plane = word // 256
-                entries.append(
-                    (plane % (2 * number), word % 256, (plane // (2 * number)).astype(f32))
-                )
-            for c in range(rows // 16):
-                total = [jnp.zeros((16, lanes), f32)] * tiles
+    tail = lax.broadcasted_iota(jnp.int32, (16, lanes), 0)
+
+    for chunk, out in zip(chunks, outs):
+
+        def patch(i, _):
+            u = (place[1] + chunk) % size
+            v = (place[2] + i // 2) % size
+            p = jnp.where(core == 0, v * size + u, u * size + v) * 2 + i % 2
+
+            def some(used):
+                entries = []
+                for s in range(used):
+                    word = table[patches + p * slots + s]
+                    plane = word // 256
+                    entries.append(
+                        (plane % (2 * number), word % 256, (plane // (2 * number)).astype(f32))
+                    )
+                for c in range(rows // 16):
+                    total = [jnp.zeros((16, lanes), f32)] * tiles
+                    for e, o, weight in entries:
+                        early = lane < o
+                        before = None
+                        for k in range(tiles + 1):
+                            piece = planes[e, c * 16 : c * 16 + 16, k * lanes : (k + 1) * lanes]
+                            turned = pltpu.roll(piece, o, 1).astype(f32)
+                            if k:
+                                part = jnp.where(early, before, turned)
+                                total[k - 1] = total[k - 1] + weight * part
+                            before = turned
+                    for k in range(tiles):
+                        at = k * rows + c * 16
+                        out[i, at : at + 16, :] = total[k].astype(out.dtype)
+                cover = jnp.zeros((16, lanes), f32)
+                whole = jnp.zeros((16, lanes), f32)
                 for e, o, weight in entries:
-                    keep = lane < o
-                    before = jnp.zeros((16, lanes), f32)
-                    for m in range(tiles):
-                        piece = planes[e, c * 16 : c * 16 + 16, m * lanes : (m + 1) * lanes]
-                        turned = pltpu.roll(piece, o, 1).astype(f32)
-                        total[m] = total[m] + weight * jnp.where(keep, before, turned)
-                        before = turned
-                for m in range(tiles):
-                    at = m * rows + c * 16
-                    out[i, at : at + 16, :] = total[m].astype(bf16)
-            cover = jnp.zeros((16, lanes), f32)
-            whole = jnp.zeros((16, lanes), f32)
-            for e, o, weight in entries:
-                cover = cover + jnp.where(lane < o, 0.0, weight)
-                whole = whole + weight
-            row = lax.broadcasted_iota(jnp.int32, (16, lanes), 0)
-            out[i, tiles * rows : tiles * rows + 16, :] = jnp.where(row == 0, cover, whole).astype(bf16)
-
-        used = table[p]
-        for top in range(2, slots + 1, 2):
-            low = top - 2 if top > 2 else -1
-
-            @pl.when((used > low) & (used <= top))
-            def _():
-                some(top)
-
-        return 0
-
-    lax.fori_loop(0, patches // 2, patch, 0)
-
-
-def pile(core, table, mine, other):
+                    cover = cover + jnp.where(lane < o, 0.0, weight)
+                    whole = whole + weight
+                out[i, tiles * rows :, :] = jnp.where(tail == 0, cover, whole).astype(out.dtype)
+
+            used = table[p]
+            for top in range(2, slots + 1, 2):
+                low = top - 2 if top > 2 else -1
+
+                @pl.when((used > low) & (used <= top))
+                def _():
+                    some(top)
+
+            return 0
+
+        lax.fori_loop(0, 2 * size, patch, 0)
+
+
+def pile(chunks, kinds, size, place, table, mine, other):
     number, rows, cols = mine.shape
-    patches = table.shape[0] // (slots + 1)
     smem = pl.BlockSpec(memory_space=pltpu.SMEM)
     vmem = pl.BlockSpec(memory_space=pltpu.VMEM)
-    shape = (patches // 2, cols // lanes * rows + 16, lanes)
-    return pl.pallas_call(
-        pile_body,
+    shape = (2 * size, (cols // lanes - 1) * rows + 16, lanes)
+    return pl.pallas_call(
+        functools.partial(pile_body, chunks, size),
         in_specs=[smem, smem, vmem, vmem],
-        out_specs=vmem,
-        out_shape=jax.ShapeDtypeStruct(shape, bf16),
+        out_specs=[vmem] * len(chunks),
+        out_shape=[jax.ShapeDtypeStruct(shape, kind) for kind in kinds],
         scratch_shapes=[pltpu.VMEM((2 * number, rows, cols), bf16)],
-        compiler_params=pltpu.CompilerParams(vmem_limit_bytes=12 * mib),
-        name="pile",
-    )(core, table, mine, other)
-
-
-def coadd_body(reach, odd, parts, coadd, first, second, stage):
-    count = parts.shape[0]
+        compiler_params=pltpu.CompilerParams(vmem_limit_bytes=8 * mib),
+        cost_estimate=pl.CostEstimate(
+            flops=len(chunks) * 1000000000, bytes_accessed=4 * mine.size, transcendentals=0
+        ),
+        name="pile_" + "_".join(str(chunk) for chunk in chunks),
+    )(place, table, mine, other)
+
+
+def fold_body(own, *rest):
+    came, keep, sends = rest[: len(rest) // 2], rest[len(rest) // 2], rest[len(rest) // 2 + 1 :]
+    rows = own.shape[1]
+    for i in range(own.shape[0]):
+        for at in range(0, rows, 16):
+            total = own[i, at : at + 16, :]
+            for ref in came:
+                total = total + ref[i, at : at + 16, :].astype(f32)
+            if i < 2:
+                keep[i, at : at + 16, :] = total
+            else:
+                sends[i // 2 - 1][i % 2, at : at + 16, :] = total.astype(bf16)
+
+
+def fold(own, came):
+    vmem = pl.BlockSpec(memory_space=pltpu.VMEM)
+    shape = (2,) + own.shape[1:]
+    return pl.pallas_call(
+        fold_body,
+        in_specs=[vmem] * (1 + len(came)),
+        out_specs=[vmem] * (1 + len(came)),
+        out_shape=[jax.ShapeDtypeStruct(shape, f32)] + [jax.ShapeDtypeStruct(shape, bf16)] * len(came),
+        compiler_params=pltpu.CompilerParams(vmem_limit_bytes=4 * mib),
+        name="fold",
+    )(own, *came)
+
+
+def meet_body(place, own, *rest):
+    came, mine, send = rest[:-2], rest[-2], rest[-1]
+    core = place[0]
+    for at in range(0, own.shape[1], 16):
+        for out, i in ((mine, core), (send, 1 - core)):
+            total = own[i, at : at + 16, :]
+            for ref in came:
+                total = total + ref[i, at : at + 16, :].astype(f32)
+            out[at : at + 16, :] = total
+
+
+def meet(place, own, came):
+    smem = pl.BlockSpec(memory_space=pltpu.SMEM)
+    vmem = pl.BlockSpec(memory_space=pltpu.VMEM)
+    return pl.pallas_call(
+        meet_body,
+        in_specs=[smem] + [vmem] * (1 + len(came)),
+        out_specs=[vmem] * 2,
+        out_shape=[jax.ShapeDtypeStruct(own.shape[1:], f32)] * 2,
+        compiler_params=pltpu.CompilerParams(vmem_limit_bytes=4 * mib),
+        name="meet",
+    )(place, own, *came)
+
+
+def coadd_body(reach, odd, place, mine, other, coadd, rounded, first, second, stage):
     rows, cols = coadd.shape
     tiles = cols // lanes
-    def add(at):
-        total = parts[0, at : at + 16, :].astype(f32)
-        for n in range(1, count):
-            total = total + parts[n, at : at + 16, :].astype(f32)
-        return total
-
-    cover = add(tiles * rows)
+    near = place[0] == 0
+
+    def pick(low, at):
+        a, b = mine[at : at + 16, :], other[at : at + 16, :]
+        return jnp.where(near, a, b) if low else jnp.where(near, b, a)
+
+    cover = pick(True, tiles // 2 * rows)
     scales = [1.0 / jnp.maximum(cover[r : r + 1, :], 1.0) for r in (0, 1)]
     for m in range(tiles):
         for b in range(group):
-            value = add(m * rows + b * 16) * scales[min(m, 1)]
-            stage[m, pl.ds(b, 16, stride=group), :] = value
+            at = m % (tiles // 2) * rows + b * 16
+            stage[m, pl.ds(b, 16, stride=group), :] = pick(m < tiles // 2, at) * scales[min(m, 1)]
         cut = slice(m * lanes, (m + 1) * lanes)
         coadd[:, cut] = stage[m]
+        rounded[:, cut] = stage[m].astype(bf16)
         low = stage[m, 0:reach, :]
         high = stage[m, rows - reach : rows, :]
         first[:, cut] = jnp.where(odd[0] == 1, low, high).astype(bf16)
         second[:, cut] = jnp.where(odd[0] == 1, high, low).astype(bf16)
 
 
-def coadd_of(odd, parts, rows, cols, reach):
+def coadd_of(odd, place, mine, other, rows, cols, reach):
     edge = jax.ShapeDtypeStruct((reach, cols), bf16)
     smem = pl.BlockSpec(memory_space=pltpu.SMEM)
     vmem = pl.BlockSpec(memory_space=pltpu.VMEM)
     return pl.pallas_call(
         functools.partial(coadd_body, reach),
-        in_specs=[smem, vmem],
-        out_specs=(vmem, vmem, vmem),
-        out_shape=(jax.ShapeDtypeStruct((rows, cols), f32), edge, edge),
-        scratch_shapes=[
-            pltpu.VMEM((cols // lanes, rows, lanes), f32),
-        ],
+        in_specs=[smem, smem, vmem, vmem],
+        out_specs=(vmem,) * 4,
+        out_shape=(
+            jax.ShapeDtypeStruct((rows, cols), f32),
+            jax.ShapeDtypeStruct((rows, cols), bf16),
+            edge,
+            edge,
+        ),
+        scratch_shapes=[pltpu.VMEM((cols // lanes, rows, lanes), f32)],
         compiler_params=pltpu.CompilerParams(vmem_limit_bytes=8 * mib),
         name="coadd",
-    )(odd, parts)
+    )(odd, place, mine, other)
 
 
 def detect_own_body(taps, psf, x, acc, profile, frame, lhs, w):
@@ -413,7 +497,7 @@
     mask = band_mask(112, taps)
     for row in (0, 24 + rows):
         frame[:, :, row : row + 24, :] = jnp.zeros((2, cols // lanes, 24, lanes), f32)
-    put_frame(frame, columns(x[...].astype(bf16)), 24, reach)
+    put_frame(frame, columns(x[...]), 24, reach)
     put_lhs(lhs, frame, spans, 24 - reach)
     clear_band(w, taps, 112, 0, spans)
     for s in range(psf.shape[0]):
@@ -526,9 +610,11 @@
     reach = taps // 2
     wide = psf_kernels.shape[-1]
     wide_reach = wide // 2
-    across = ("sy", "sx")
-    patches = lax.axis_size("sy") * lax.axis_size("sx") * 2
-    core = lax.axis_index("core")
+    sky = ("sy", "sx", "core")
+    size = lax.axis_size("sx")
+    patches = size * size * 2
+    core, at_x, at_y = (lax.axis_index(name) for name in ("core", "sx", "sy"))
+    place = jnp.stack([core, jnp.where(core == 0, at_x, at_y), jnp.where(core == 0, at_y, at_x)])
     odd = lax.axis_index("section") % 2
 
     low, high = exposures[:, :reach, :], exposures[:, rows - reach :, :]
@@ -544,13 +630,23 @@
     profile = profiles(coef_code, coef_table, basis_rows.T, basis_cols.T)
     table = slot_table(labels, other_labels, patches)
     table, profile = lax.optimization_barrier((table, profile))
-    matched = match(odd, profile, exposures, first, second)
-    other = lax.ppermute(matched, "core", swap)
-    partial = pile(core[None], table, matched, other)
-    parts = lax.all_to_all(partial, across, split_axis=0, concat_axis=0, tiled=True)
-    coadd, first, second = coadd_of(odd, parts, rows, cols, wide_reach)
+    mine, send = match(odd, place, profile, exposures, first, second)
+    other = lax.ppermute(send, "core", swap)
+
+    steps = (2, 1, 3)
+    move = lambda rows, step, by: lax.ppermute(rows, sky, role_pairs(step, size, by))
+    (far,) = pile((2,), (bf16,), size, place, table, mine, other)
+    came = [move(far, 0, 2)]
+    far, table = lax.optimization_barrier((far, table))
+    ahead, behind, own = pile((1, 3, 0), (bf16, bf16, f32), size, place, table, mine, other)
+    came += [move(ahead, 0, 1), move(behind, 0, 3)]
+    keep, *sends = fold(own, came)
+    came = [move(sends[by - 1], 1, by) for by in steps]
+    mine, send = meet(place, keep, came)
+    other = lax.ppermute(send, "core", swap)
+    coadd, rounded, first, second = coadd_of(odd, place, mine, other, rows, cols, wide_reach)
     first, second = trade(first, second)
-    acc, profile = detect_own(psf_kernels, coadd)
+    acc, profile = detect_own(psf_kernels, rounded)
     detect = detect_halo(odd, profile, first, second, acc, rows, wide)
     return (coadd[None], detect[None])
 

time: 80.7 us -> 70.5 us (0.87)
  blocking collectives: 36.3 us -> 0 us
  waiting for transfers between devices: 3.03 us -> 15.8 us
  starting transfers between devices: 8.23 us -> 19.7 us
  Pallas kernels: 25.6 us -> 30.2 us
  local copies, waits for them, and re-layouts: 4.39 us -> 0.76 us
    all_to_all x1 -> x0, blocking collectives: 36.3 us -> none  [on_device(): lax.all_to_all(partial, across, split_axis=0, concat_axis=0, tiled=True)]
    ppermute x1 -> x8, starting transfers between devices: 0.15 us -> 13 us  [the longest x6 12.9 us: on_device(): lax.ppermute(rows, sky, role_pairs(step, size, by))]
    ppermute x1 -> x8, waiting for transfers between devices: 2.59 us -> 14 us  [the longest x6 10.5 us: on_device(): lax.ppermute(rows, sky, role_pairs(step, size, by))]
    pallas_call x3 -> x6, Pallas kernels: 13.5 us -> 19.1 us  [the longest x2 8.79 us: pile(): pl.pallas_call(functools.partial(pile_body, chunks, size), in_specs=[smem...]
    unnamed x14 -> x12, local copies, waits for them, and re-layouts: 3.66 us -> 0.02 us
    ppermute x4, starting transfers between devices: 8.05 us -> 6.66 us  [trade(): lax.ppermute(rows, 'section', pairs + [(b, a) for a, b in pairs])]
    ppermute x4, waiting for transfers between devices: 0.43 us -> 1.79 us  [trade(): lax.ppermute(rows, 'section', pairs + [(b, a) for a, b in pairs])]
  transfers between devices with their start and end apart: 6 -> 13, of which waited for: 2 -> 6; matrix products, arithmetic and copies ran while one was open for 2% -> 2% of each run, Pallas kernels for 11% -> 20%
where the time goes in v7:
time: 70.5 us; the launch traced here: 69.4 us
  Pallas kernels  30.2 us (43%)
  starting transfers between devices  19.7 us (28%)
  waiting for transfers between devices  15.8 us (22%)
  other arithmetic  2.05 us (3%)
  between operations  0.86 us (1%)
  local copies, waits for them, and re-layouts  0.76 us (1%)
    ppermute x6, starting transfers between devices, on_device(): lax.ppermute(rows, sky, role_pairs(step, size, by))  12.9 us
    ppermute x6, waiting for transfers between devices, on_device(): lax.ppermute(rows, sky, role_pairs(step, size, by))  10.5 us
    pallas_call x2, Pallas kernels, pile(): pl.pallas_call(functools.partial(pile_body, chunks, size), in_specs=[smem...  8.79 us
    pallas_call x1, Pallas kernels, match(): pl.pallas_call(functools.partial(match_body, taps), in_specs=[smem, smem,...  8.09 us
    ppermute x4, starting transfers between devices, trade(): lax.ppermute(rows, 'section', pairs + [(b, a) for a, b in pairs])  6.66 us
    pallas_call x1, Pallas kernels, detect_own(): pl.pallas_call(functools.partial(detect_own_body, taps), out_shape=(jax.S...  3.57 us
    ppermute x2, waiting for transfers between devices, on_device(): other = lax.ppermute(send, 'core', swap)  3.43 us
    pallas_call x1, Pallas kernels, detect_halo(): pl.pallas_call(functools.partial(detect_halo_body, taps), in_specs=[smem,...  3.31 us
  transfers between devices with their start and end apart: 13, of which 6 were waited for; matrix products, arithmetic and copies ran while one was open for 2% of the time, Pallas kernels for 20%

profile of v7, /device:TPU:32, one launch (start us, length us, event | category | flops | bytes accessed | tf_op | source)
XLA Modules:
  0.0 69.4 jit_solution(9283352985638269741)
XLA Ops:
  0.6 0.0 copy-start
  0.6 0.0 copy-start.3
  0.7 0.0 copy-start.2
  0.7 0.0 copy-start.1
  0.7 0.0 copy-start.4
  0.7 1.2 %broadcast_select_fusion = (bf16[8,11,1024]{2,1,0:T(8,128)(2,1)S(1)}, bf16[8,11,1024]{2,1,0:T(8,128)(2,1)S(1)}) fusion(pred[]{:T(512)S(6)} %eq.11, bf16[8,64,1024]{2,1,0:T(8,128)(2,1)} %far.1), kind=kLoop, calls=%fused_computation | loop fusion | flops 180224 | bytes 720897 | tf_op jit(solution)/shard_map/jit(_where)/select_n | solution.py:621
  1.9 3.8 %collective-permute-start.2 = (bf16[8,11,1024]{2,1,0:T(8,128)(2,1)S(1)}, bf16[8,11,1024]{2,1,0:T(8,128)(2,1)S(1)}, u32[]{:S(2)}, u32[]{:S(2)}) collective-permute-start(bf16[8,11,1024]{2,1,0:T(8,128)(2,1)S(1)} %get-tuple-element.42), channel_id=1, source_target_pairs={{32,64},{64,32},{33,65},{65,33},{34,66},{66,34},{35,67},{67,35},{3... | collective-permute-start | bytes 540680 | tf_op jit(solution)/shard_map/ppermute | solution.py:593
  5.7 0.1 collective-permute-start.1
  5.8 0.7 %copy.11 = s32[8,1]{1,0:T(8,128)S(1)} copy(s32[8,1]{0,1:T(1,128)} %bitcast.12) | data formatting | bytes 64 | tf_op jit(solution)/shard_map/broadcast_in_dim | solution.py:625
  6.5 0.8 %pad_add_fusion.mine = s32[8,17]{1,0:T(8,128)S(1)} fusion(s32[8,8]{1,0:T(8,128)} %param.16, s32[8,8]{1,0:T(8,128)} %param.15, s32[8,1]{1,0:T(8,128)S(1)} %copy.11), kind=kLoop, calls=%fused_computation.2 | loop fusion | flops 272 | bytes 1088 | tf_op jit(solution)/shard_map/concatenate | solution.py:624
  7.3 0.0 collective-permute-start
  7.4 0.1 pad_add_fusion.1.place
  7.4 0.0 copy-done.2
  7.5 0.0 copy-done.4
  7.5 1.9 %profiles.1.profile = f32[8,24,128]{2,1,0:T(8,128)S(1)} custom-call(s32[8,27]{1,0:T(8,128)S(1)} %copy-done.4, f32[27,64]{1,0:T(8,128)S(1)} %copy-done.1, f32[23,27]{1,0:T(8,128)S(1)} %bitcast.9, f32[23,27]{1,0:T(8,128)S(1)} %bitcast.10), custom_call_target="tpu_custom_call" | custom-call | tf_op jit(solution)/shard_map/profiles/pallas_call | solution.py:180
  9.3 0.0 collective-permute-done.other
  9.3 2.4 %slot_table.1.table = s32[288]{0:T(512)S(1)} custom-call(s32[8,17]{1,0:T(8,128)S(1)} %pad_add_fusion.mine, s32[8,17]{1,0:T(8,128)S(1)} %collective-permute-done.other), custom_call_target="tpu_custom_call" | custom-call | tf_op jit(solution)/shard_map/slot_table/pallas_call | solution.py:297
  11.8 0.2 collective-permute-done.2.second
  12.0 1.6 %collective-permute-done.1.first = bf16[8,11,1024]{2,1,0:T(8,128)(2,1)S(1)} collective-permute-done((bf16[8,11,1024]{2,1,0:T(8,128)(2,1)S(1)}, bf16[8,11,1024]{2,1,0:T(8,128)(2,1)S(1)}, u32[]{:S(2)}, u32[]{:S(2)}) %collective-permute-start.1) | collective-permute-done | bytes 180256 | tf_op jit(solution)/shard_map/ppermute | solution.py:593
  13.6 8.1 %match.1 = (bf16[8,64,640]{2,1,0:T(8,128)(2,1)S(1)}, bf16[8,64,640]{2,1,0:T(8,128)(2,1)S(1)}) custom-call(s32[1]{0:T(128)} %bitcast.odd, s32[3]{0:T(128)S(1)} %pad_add_fusion.1.place, f32[8,24,128]{2,1,0:T(8,128)S(1)} %profiles.1.profile, bf16[8,64,1024]{2,1,0:T(8,128)(2,1)S(1)} %copy-done, bf16[8,11,1024]{2,1,0:T(8,128)(2,1)S(1)} %collective-permute-done.1.first, ...), custom_call_target="tpu_custom_call" | custom-call | flops 3489660928 | bytes 2097152 | tf_op jit(solution)/shard_map/match/pallas_call | solution.py:246
  21.7 0.1 collective-permute-start.3
  21.8 2.1 %collective-permute-done.3.other = bf16[8,64,640]{2,1,0:T(8,128)(2,1)S(1)} collective-permute-done((bf16[8,64,640]{2,1,0:T(8,128)(2,1)S(1)}, bf16[8,64,640]{2,1,0:T(8,128)(2,1)S(1)}, u32[]{:S(2)}, u32[]{:S(2)}) %collective-permute-start.3) | collective-permute-done | bytes 655392 | tf_op jit(solution)/shard_map/ppermute | solution.py:634
  23.8 2.7 %pile_2.1 = bf16[8,272,128]{2,1,0:T(8,128)(2,1)S(1)} custom-call(s32[3]{0:T(128)S(1)} %pad_add_fusion.1.place, s32[288]{0:T(512)S(1)} %slot_table.1.table, bf16[8,64,640]{2,1,0:T(8,128)(2,1)S(1)} %get-tuple-element.24.mine, bf16[8,64,640]{2,1,0:T(8,128)(2,1)S(1)} %collective-permute-done.3.other), custom_call_target="tpu_custom_call" | custom-call | flops 1000000000 | bytes 1310720 | tf_op jit(solution)/shard_map/pile_2/pallas_call | solution.py:384
  26.5 2.9 %collective-permute-start.4 = (bf16[8,272,128]{2,1,0:T(8,128)(2,1)S(1)}, bf16[8,272,128]{2,1,0:T(8,128)(2,1)S(1)}, u32[]{:S(2)}, u32[]{:S(2)}) collective-permute-start(bf16[8,272,128]{2,1,0:T(8,128)(2,1)S(1)} %pile_2.1), channel_id=1, source_target_pairs={{0,4},{1,17},{2,6},{3,19},{4,0},{5,21},{6,2},{7,23},{8,12},{9,25},... | collective-permute-start | bytes 1671176 | tf_op jit(solution)/shard_map/ppermute | solution.py:637
  29.5 6.1 %pile_1_3_0.1 = (bf16[8,272,128]{2,1,0:T(8,128)(2,1)S(1)}, bf16[8,272,128]{2,1,0:T(8,128)(2,1)S(1)}, f32[8,272,128]{2,1,0:T(8,128)S(1)}) custom-call(s32[3]{0:T(128)S(1)} %pad_add_fusion.1.place, s32[288]{0:T(512)S(1)} %slot_table.1.table, bf16[8,64,640]{2,1,0:T(8,128)(2,1)S(1)} %get-tuple-element.24.mine, bf16[8,64,640]{2,1,0:T(8,128)(2,1)S(1)} %collective-permute-done.3.other), custom_call_target="tpu_custom_call" | custom-call | flops 3000000000 | bytes 1310720 | tf_op jit(solution)/shard_map/pile_1_3_0/pallas_call | solution.py:384
  35.6 1.1 %collective-permute-start.5 = (bf16[8,272,128]{2,1,0:T(8,128)(2,1)S(1)}, bf16[8,272,128]{2,1,0:T(8,128)(2,1)S(1)}, u32[]{:S(2)}, u32[]{:S(2)}) collective-permute-start(bf16[8,272,128]{2,1,0:T(8,128)(2,1)S(1)} %get-tuple-element.28), channel_id=1, source_target_pairs={{0,2},{1,9},{2,4},{3,11},{4,6},{5,13},{6,0},{7,15},{8,10},{9,17},{... | collective-permute-start | bytes 1671176 | tf_op jit(solution)/shard_map/ppermute | solution.py:637
  36.7 2.2 %collective-permute-start.6 = (bf16[8,272,128]{2,1,0:T(8,128)(2,1)S(1)}, bf16[8,272,128]{2,1,0:T(8,128)(2,1)S(1)}, u32[]{:S(2)}, u32[]{:S(2)}) collective-permute-start(bf16[8,272,128]{2,1,0:T(8,128)(2,1)S(1)} %get-tuple-element.29), channel_id=1, source_target_pairs={{0,6},{1,25},{2,0},{3,27},{4,2},{5,29},{6,4},{7,31},{8,14},{9,1},{... | collective-permute-start | bytes 1671176 | tf_op jit(solution)/shard_map/ppermute | solution.py:637
  38.9 0.0 collective-permute-done.4.rest_0_
  38.9 7.5 %collective-permute-done.5.rest_1_ = bf16[8,272,128]{2,1,0:T(8,128)(2,1)S(1)} collective-permute-done((bf16[8,272,128]{2,1,0:T(8,128)(2,1)S(1)}, bf16[8,272,128]{2,1,0:T(8,128)(2,1)S(1)}, u32[]{:S(2)}, u32[]{:S(2)}) %collective-permute-start.5) | collective-permute-done | bytes 557088 | tf_op jit(solution)/shard_map/ppermute | solution.py:637
  46.4 0.0 collective-permute-done.6.rest_2_
  46.4 0.2 fold.1
  46.6 3.4 %collective-permute-start.7 = (bf16[2,272,128]{2,1,0:T(8,128)(2,1)S(1)}, bf16[2,272,128]{2,1,0:T(8,128)(2,1)S(1)}, u32[]{:S(2)}, u32[]{:S(2)}) collective-permute-start(bf16[2,272,128]{2,1,0:T(8,128)(2,1)S(1)} %get-tuple-element.31), channel_id=1, source_target_pairs={{0,16},{1,5},{2,18},{3,7},{4,20},{5,1},{6,22},{7,3},{8,24},{9,13},... | collective-permute-start | bytes 417800 | tf_op jit(solution)/shard_map/ppermute | solution.py:637
  50.0 0.6 collective-permute-start.8
  50.6 2.6 %collective-permute-start.9 = (bf16[2,272,128]{2,1,0:T(8,128)(2,1)S(1)}, bf16[2,272,128]{2,1,0:T(8,128)(2,1)S(1)}, u32[]{:S(2)}, u32[]{:S(2)}) collective-permute-start(bf16[2,272,128]{2,1,0:T(8,128)(2,1)S(1)} %get-tuple-element.33), channel_id=1, source_target_pairs={{0,24},{1,7},{2,26},{3,1},{4,28},{5,3},{6,30},{7,5},{8,0},{9,15},{... | collective-permute-start | bytes 417800 | tf_op jit(solution)/shard_map/ppermute | solution.py:637
  53.3 0.0 collective-permute-done.7.rest_0_
  53.3 3.0 %collective-permute-done.8.rest_1_ = bf16[2,272,128]{2,1,0:T(8,128)(2,1)S(1)} collective-permute-done((bf16[2,272,128]{2,1,0:T(8,128)(2,1)S(1)}, bf16[2,272,128]{2,1,0:T(8,128)(2,1)S(1)}, u32[]{:S(2)}, u32[]{:S(2)}) %collective-permute-start.8) | collective-permute-done | bytes 139296 | tf_op jit(solution)/shard_map/ppermute | solution.py:637
  56.3 0.0 collective-permute-done.9.rest_2_
  56.3 0.6 meet.1
  56.9 0.1 collective-permute-start.10
  57.0 1.3 %collective-permute-done.10.other = f32[272,128]{1,0:T(8,128)S(1)} collective-permute-done((f32[272,128]{1,0:T(8,128)S(1)}, f32[272,128]{1,0:T(8,128)S(1)}, u32[]{:S(2)}, u32[]{:S(2)}) %collective-permute-start.10) | collective-permute-done | bytes 139296 | tf_op jit(solution)/shard_map/ppermute | solution.py:646
  58.4 1.3 %coadd.1 = (f32[64,1024]{1,0:T(8,128)}, bf16[64,1024]{1,0:T(8,128)(2,1)S(1)}, bf16[20,1024]{1,0:T(8,128)(2,1)S(1)}, bf16[20,1024]{1,0:T(8,128)(2,1)S(1)}) custom-call(s32[1]{0:T(128)} %bitcast.odd, s32[3]{0:T(128)S(1)} %pad_add_fusion.1.place, f32[272,128]{1,0:T(8,128)S(1)} %get-tuple-element.34.mine, f32[272,128]{1,0:T(8,128)S(1)} %collective-permute-done.10.other), custom_call_target="tpu_custom_call" | custom-call | tf_op jit(solution)/shard_map/coadd/pallas_call | solution.py:477
  59.7 0.4 collective-permute-start.11
  60.1 2.4 %collective-permute-start.12 = (bf16[20,1024]{1,0:T(8,128)(2,1)S(1)}, bf16[20,1024]{1,0:T(8,128)(2,1)S(1)}, u32[]{:S(2)}, u32[]{:S(2)}) collective-permute-start(bf16[20,1024]{1,0:T(8,128)(2,1)S(1)} %get-tuple-element.40), channel_id=1, source_target_pairs={{32,64},{64,32},{33,65},{65,33},{34,66},{66,34},{35,67},{67,35},{3... | collective-permute-start | bytes 122888 | tf_op jit(solution)/shard_map/ppermute | solution.py:593
  62.4 0.0 copy-done.5
  62.5 3.6 %detect_own.1 = (f32[256,768]{1,0:T(8,128)S(1)}, f32[3,48,128]{2,1,0:T(8,128)S(1)}) custom-call(bf16[3,41,41]{2,1,0:T(8,128)(2,1)S(1)} %copy-done.5, bf16[64,1024]{1,0:T(8,128)(2,1)S(1)} %get-tuple-element.37.x), custom_call_target="tpu_custom_call" | custom-call | flops 2214592512 | bytes 262144 | tf_op jit(solution)/shard_map/detect_own/pallas_call | solution.py:520
  66.0 0.0 collective-permute-done.11.first
  66.0 0.0 collective-permute-done.12.second
  66.0 3.3 %detect_halo.1 = f32[3,64,1024]{2,1,0:T(8,128)} custom-call(s32[1]{0:T(128)} %bitcast.odd, f32[3,48,128]{2,1,0:T(8,128)S(1)} %get-tuple-element.38.profile, bf16[20,1024]{1,0:T(8,128)(2,1)S(1)} %collective-permute-done.11.first, bf16[20,1024]{1,0:T(8,128)(2,1)S(1)} %collective-permute-done.12.second, f32[256,768]{1,0:T(8,128)S(1)} %get-tuple-element.41.acc), custom_call_target="tpu_custom_call" | custom-call | tf_op jit(solution)/shard_map/detect_halo/pallas_call | solution.py:576
  (4 shorter events, 0.0 us)
Async XLA Ops:
  0.6 12.9 %copy-start = (bf16[8,64,1024]{2,1,0:T(8,128)(2,1)S(1)}, bf16[8,64,1024]{2,1,0:T(8,128)(2,1)}, u32[]{:S(2)}) copy-start(bf16[8,64,1024]{2,1,0:T(8,128)(2,1)} %far.1) | copy-start | bytes 3145732
  0.6 6.8 %copy-start.3 = (f32[27,23]{0,1:T(8,128)S(1)}, f32[27,23]{0,1:T(8,128)}, u32[]{:S(2)}) copy-start(f32[27,23]{0,1:T(8,128)} %param.13) | copy-start | bytes 7456
  0.7 6.8 %copy-start.2 = (f32[27,23]{0,1:T(8,128)S(1)}, f32[27,23]{0,1:T(8,128)}, u32[]{:S(2)}) copy-start(f32[27,23]{0,1:T(8,128)} %param.12) | copy-start | bytes 7456
  0.7 6.8 %copy-start.1 = (f32[27,64]{1,0:T(8,128)S(1)}, f32[27,64]{1,0:T(8,128)}, u32[]{:S(2)}) copy-start(f32[27,64]{1,0:T(8,128)} %table.1) | copy-start | bytes 20740
  0.7 6.8 %copy-start.4 = (s32[8,27]{1,0:T(8,128)S(1)}, s32[8,27]{1,0:T(8,128)}, u32[]{:S(2)}) copy-start(s32[8,27]{1,0:T(8,128)} %code.1) | copy-start | bytes 2596
  1.9 10.1 %collective-permute-start.2 = (bf16[8,11,1024]{2,1,0:T(8,128)(2,1)S(1)}, bf16[8,11,1024]{2,1,0:T(8,128)(2,1)S(1)}, u32[]{:S(2)}, u32[]{:S(2)}) collective-permute-start(bf16[8,11,1024]{2,1,0:T(8,128)(2,1)S(1)} %get-tuple-element.42), channel_id=1, source_target_pairs={{32,64},{64,32},{33,65},{65,33},{34,66},{66,34},{35,67},{67,35},{3... | collective-permute-start | bytes 540680 | tf_op jit(solution)/shard_map/ppermute | solution.py:593
  5.7 7.8 %collective-permute-start.1 = (bf16[8,11,1024]{2,1,0:T(8,128)(2,1)S(1)}, bf16[8,11,1024]{2,1,0:T(8,128)(2,1)S(1)}, u32[]{:S(2)}, u32[]{:S(2)}) collective-permute-start(bf16[8,11,1024]{2,1,0:T(8,128)(2,1)S(1)} %get-tuple-element.43), channel_id=1, source_target_pairs={{0,32},{64,96},{32,0},{96,64},{1,33},{65,97},{33,1},{97,65},{2,34}... | collective-permute-start | bytes 540680 | tf_op jit(solution)/shard_map/ppermute | solution.py:593
  7.3 2.0 %collective-permute-start = (s32[8,17]{1,0:T(8,128)S(1)}, s32[8,17]{1,0:T(8,128)S(1)}, u32[]{:S(2)}, u32[]{:S(2)}) collective-permute-start(s32[8,17]{1,0:T(8,128)S(1)} %pad_add_fusion.mine), channel_id=1, source_target_pairs={{0,1},{1,0},{2,3},{3,2},{4,5},{5,4},{6,7},{7,6},{8,9},{9,8},{10,11... | collective-permute-start | bytes 1640 | tf_op jit(solution)/shard_map/ppermute | solution.py:628
  21.7 2.2 %collective-permute-start.3 = (bf16[8,64,640]{2,1,0:T(8,128)(2,1)S(1)}, bf16[8,64,640]{2,1,0:T(8,128)(2,1)S(1)}, u32[]{:S(2)}, u32[]{:S(2)}) collective-permute-start(bf16[8,64,640]{2,1,0:T(8,128)(2,1)S(1)} %get-tuple-element.25), channel_id=1, source_target_pairs={{0,1},{1,0},{2,3},{3,2},{4,5},{5,4},{6,7},{7,6},{8,9},{9,8},{10,11... | collective-permute-start | bytes 1966088 | tf_op jit(solution)/shard_map/ppermute | solution.py:634
  26.5 12.4 %collective-permute-start.4 = (bf16[8,272,128]{2,1,0:T(8,128)(2,1)S(1)}, bf16[8,272,128]{2,1,0:T(8,128)(2,1)S(1)}, u32[]{:S(2)}, u32[]{:S(2)}) collective-permute-start(bf16[8,272,128]{2,1,0:T(8,128)(2,1)S(1)} %pile_2.1), channel_id=1, source_target_pairs={{0,4},{1,17},{2,6},{3,19},{4,0},{5,21},{6,2},{7,23},{8,12},{9,25},... | collective-permute-start | bytes 1671176 | tf_op jit(solution)/shard_map/ppermute | solution.py:637
  35.6 10.8 %collective-permute-start.5 = (bf16[8,272,128]{2,1,0:T(8,128)(2,1)S(1)}, bf16[8,272,128]{2,1,0:T(8,128)(2,1)S(1)}, u32[]{:S(2)}, u32[]{:S(2)}) collective-permute-start(bf16[8,272,128]{2,1,0:T(8,128)(2,1)S(1)} %get-tuple-element.28), channel_id=1, source_target_pairs={{0,2},{1,9},{2,4},{3,11},{4,6},{5,13},{6,0},{7,15},{8,10},{9,17},{... | collective-permute-start | bytes 1671176 | tf_op jit(solution)/shard_map/ppermute | solution.py:637
  36.7 9.7 %collective-permute-start.6 = (bf16[8,272,128]{2,1,0:T(8,128)(2,1)S(1)}, bf16[8,272,128]{2,1,0:T(8,128)(2,1)S(1)}, u32[]{:S(2)}, u32[]{:S(2)}) collective-permute-start(bf16[8,272,128]{2,1,0:T(8,128)(2,1)S(1)} %get-tuple-element.29), channel_id=1, source_target_pairs={{0,6},{1,25},{2,0},{3,27},{4,2},{5,29},{6,4},{7,31},{8,14},{9,1},{... | collective-permute-start | bytes 1671176 | tf_op jit(solution)/shard_map/ppermute | solution.py:637
  46.4 16.1 %copy-start.5 = (bf16[3,41,41]{2,1,0:T(8,128)(2,1)S(1)}, bf16[3,41,41]{2,1,0:T(8,128)(2,1)}, u32[]{:S(2)}) copy-start(bf16[3,41,41]{2,1,0:T(8,128)(2,1)} %psf.1) | copy-start | bytes 30262
  46.6 6.6 %collective-permute-start.7 = (bf16[2,272,128]{2,1,0:T(8,128)(2,1)S(1)}, bf16[2,272,128]{2,1,0:T(8,128)(2,1)S(1)}, u32[]{:S(2)}, u32[]{:S(2)}) collective-permute-start(bf16[2,272,128]{2,1,0:T(8,128)(2,1)S(1)} %get-tuple-element.31), channel_id=1, source_target_pairs={{0,16},{1,5},{2,18},{3,7},{4,20},{5,1},{6,22},{7,3},{8,24},{9,13},... | collective-permute-start | bytes 417800 | tf_op jit(solution)/shard_map/ppermute | solution.py:637
  50.0 6.3 %collective-permute-start.8 = (bf16[2,272,128]{2,1,0:T(8,128)(2,1)S(1)}, bf16[2,272,128]{2,1,0:T(8,128)(2,1)S(1)}, u32[]{:S(2)}, u32[]{:S(2)}) collective-permute-start(bf16[2,272,128]{2,1,0:T(8,128)(2,1)S(1)} %get-tuple-element.32), channel_id=1, source_target_pairs={{0,8},{1,3},{2,10},{3,5},{4,12},{5,7},{6,14},{7,1},{8,16},{9,11},{... | collective-permute-start | bytes 417800 | tf_op jit(solution)/shard_map/ppermute | solution.py:637
  50.6 5.6 %collective-permute-start.9 = (bf16[2,272,128]{2,1,0:T(8,128)(2,1)S(1)}, bf16[2,272,128]{2,1,0:T(8,128)(2,1)S(1)}, u32[]{:S(2)}, u32[]{:S(2)}) collective-permute-start(bf16[2,272,128]{2,1,0:T(8,128)(2,1)S(1)} %get-tuple-element.33), channel_id=1, source_target_pairs={{0,24},{1,7},{2,26},{3,1},{4,28},{5,3},{6,30},{7,5},{8,0},{9,15},{... | collective-permute-start | bytes 417800 | tf_op jit(solution)/shard_map/ppermute | solution.py:637
  56.9 1.4 %collective-permute-start.10 = (f32[272,128]{1,0:T(8,128)S(1)}, f32[272,128]{1,0:T(8,128)S(1)}, u32[]{:S(2)}, u32[]{:S(2)}) collective-permute-start(f32[272,128]{1,0:T(8,128)S(1)} %get-tuple-element.35), channel_id=1, source_target_pairs={{0,1},{1,0},{2,3},{3,2},{4,5},{5,4},{6,7},{7,6},{8,9},{9,8},{10,11... | collective-permute-start | bytes 417800 | tf_op jit(solution)/shard_map/ppermute | solution.py:646
  59.7 6.3 %collective-permute-start.11 = (bf16[20,1024]{1,0:T(8,128)(2,1)S(1)}, bf16[20,1024]{1,0:T(8,128)(2,1)S(1)}, u32[]{:S(2)}, u32[]{:S(2)}) collective-permute-start(bf16[20,1024]{1,0:T(8,128)(2,1)S(1)} %get-tuple-element.39), channel_id=1, source_target_pairs={{0,32},{64,96},{32,0},{96,64},{1,33},{65,97},{33,1},{97,65},{2,34}... | collective-permute-start | bytes 122888 | tf_op jit(solution)/shard_map/ppermute | solution.py:593
  60.1 6.0 %collective-permute-start.12 = (bf16[20,1024]{1,0:T(8,128)(2,1)S(1)}, bf16[20,1024]{1,0:T(8,128)(2,1)S(1)}, u32[]{:S(2)}, u32[]{:S(2)}) collective-permute-start(bf16[20,1024]{1,0:T(8,128)(2,1)S(1)} %get-tuple-element.40), channel_id=1, source_target_pairs={{32,64},{64,32},{33,65},{65,33},{34,66},{66,34},{35,67},{67,35},{3... | collective-permute-start | bytes 122888 | tf_op jit(solution)/shard_map/ppermute | solution.py:593

commit v8 on v7

--- a/solution.py
+++ b/solution.py
@@ -120,12 +120,11 @@
                 lhs[at : at + 16, t * lanes : (t + 1) * lanes] = jnp.concatenate(pair, axis=0).astype(bf16)
 
 
-def edge_scratch(taps, tiles, width):
+def edge_scratch(taps, tiles):
     spans = edge_spans(taps)
     return [
         pltpu.VMEM((2, 2, tiles, 48, lanes), f32),
         pltpu.VMEM((2, 128, spans * lanes), bf16),
-        pltpu.VMEM((2, spans * lanes, width), bf16),
     ]
 
 
@@ -330,40 +329,45 @@
 
         def patch(i, _):
             u = (place[1] + chunk) % size
-            v = (place[2] + i // 2) % size
-            p = jnp.where(core == 0, v * size + u, u * size + v) * 2 + i % 2
+            v = (place[2] + i) % size
+            p = jnp.where(core == 0, v * size + u, u * size + v) * 2
 
             def some(used):
                 entries = []
-                for s in range(used):
-                    word = table[patches + p * slots + s]
-                    plane = word // 256
+                for c in range(2):
+                    words = [table[patches + (p + c) * slots + s] for s in range(used)]
                     entries.append(
-                        (plane % (2 * number), word % 256, (plane // (2 * number)).astype(f32))
+                        [
+                            ((word >> 8) & (2 * number - 1), word & 255, (word >> 12).astype(f32))
+                            for word in words
+                        ]
                     )
-                for c in range(rows // 16):
-                    total = [jnp.zeros((16, lanes), f32)] * tiles
-                    for e, o, weight in entries:
-                        early = lane < o
-                        before = None
-                        for k in range(tiles + 1):
-                            piece = planes[e, c * 16 : c * 16 + 16, k * lanes : (k + 1) * lanes]
-                            turned = pltpu.roll(piece, o, 1).astype(f32)
-                            if k:
-                                part = jnp.where(early, before, turned)
-                                total[k - 1] = total[k - 1] + weight * part
-                            before = turned
-                    for k in range(tiles):
-                        at = k * rows + c * 16
-                        out[i, at : at + 16, :] = total[k].astype(out.dtype)
-                cover = jnp.zeros((16, lanes), f32)
-                whole = jnp.zeros((16, lanes), f32)
-                for e, o, weight in entries:
-                    cover = cover + jnp.where(lane < o, 0.0, weight)
-                    whole = whole + weight
-                out[i, tiles * rows :, :] = jnp.where(tail == 0, cover, whole).astype(out.dtype)
-
-            used = table[p]
+                for r in range(rows // 16):
+                    for c in range(2):
+                        total = [jnp.zeros((16, lanes), f32)] * tiles
+                        for e, o, weight in entries[c]:
+                            early = lane < o
+                            before = None
+                            for k in range(tiles + 1):
+                                piece = planes[e, r * 16 : r * 16 + 16, k * lanes : (k + 1) * lanes]
+                                turned = pltpu.roll(piece, o, 1).astype(f32)
+                                if k:
+                                    part = jnp.where(early, before, turned)
+                                    total[k - 1] = total[k - 1] + weight * part
+                                before = turned
+                        for k in range(tiles):
+                            at = k * rows + r * 16
+                            out[2 * i + c, at : at + 16, :] = total[k].astype(out.dtype)
+                for c in range(2):
+                    cover = jnp.zeros((16, lanes), f32)
+                    whole = jnp.zeros((16, lanes), f32)
+                    for e, o, weight in entries[c]:
+                        cover = cover + jnp.where(lane < o, 0.0, weight)
+                        whole = whole + weight
+                    last = jnp.where(tail == 0, cover, whole)
+                    out[2 * i + c, tiles * rows :, :] = last.astype(out.dtype)
+
+            used = jnp.maximum(table[p], table[p + 1])
             for top in range(2, slots + 1, 2):
                 low = top - 2 if top > 2 else -1
 
@@ -373,7 +377,7 @@
 
             return 0
 
-        lax.fori_loop(0, 2 * size, patch, 0)
+        lax.fori_loop(0, size, patch, 0)
 
 
 def pile(chunks, kinds, size, place, table, mine, other):
@@ -490,70 +494,77 @@
     )(odd, place, mine, other)
 
 
-def detect_own_body(taps, psf, x, acc, profile, frame, lhs, w):
+def bands_body(taps, psf, w):
+    spans = taps + 3
+    mask = band_mask(112, taps)
+    clear_band(w, taps, 112, 0, spans)
+    for s in range(psf.shape[0]):
+        total = 0.0
+        for rows_at, cols_at in zip(row_places(48, taps), lane_places(taps)):
+            moved = jnp.dot(rows_at.astype(bf16), psf[s], preferred_element_type=f32)
+            total = total + jnp.dot(
+                moved.astype(bf16), cols_at.astype(bf16), preferred_element_type=f32
+            )
+        put_band(w, total, taps, mask, 0, spans, 256 * s)
+
+
+def detect_bands(psf):
+    scales, _, taps = psf.shape
+    return pl.pallas_call(
+        functools.partial(bands_body, taps),
+        out_shape=jax.ShapeDtypeStruct(((taps + 3) * lanes, scales * 256), bf16),
+        compiler_params=pltpu.CompilerParams(vmem_limit_bytes=12 * mib),
+        name="bands",
+    )(psf)
+
+
+def detect_own_body(taps, w, x, acc, frame, lhs):
     reach = taps // 2
     rows, cols = x.shape
     spans = taps + 3
-    mask = band_mask(112, taps)
     for row in (0, 24 + rows):
         frame[:, :, row : row + 24, :] = jnp.zeros((2, cols // lanes, 24, lanes), f32)
     put_frame(frame, columns(x[...]), 24, reach)
     put_lhs(lhs, frame, spans, 24 - reach)
-    clear_band(w, taps, 112, 0, spans)
-    for s in range(psf.shape[0]):
-        total = 0.0
-        for rows_at, cols_at in zip(row_places(profile.shape[1], taps), lane_places(taps)):
-            moved = jnp.dot(rows_at.astype(bf16), psf[s], preferred_element_type=f32)
-            total = total + jnp.dot(
-                moved.astype(bf16), cols_at.astype(bf16), preferred_element_type=f32
-            )
-        profile[s] = total
-        put_band(w, total, taps, mask, 0, spans, 256 * s)
-        cut = slice(256 * s, 256 * s + 256)
+    for at in range(0, w.shape[1], 256):
+        cut = slice(at, at + 256)
         acc[:, cut] = jnp.dot(lhs[...], w[:, cut], preferred_element_type=f32)
 
 
-def detect_own(psf, x):
+def detect_own(w, x, taps):
     rows, cols = x.shape
-    scales, _, taps = psf.shape
     spans = taps + 3
     return pl.pallas_call(
         functools.partial(detect_own_body, taps),
-        out_shape=(
-            jax.ShapeDtypeStruct((256, scales * 256), f32),
-            jax.ShapeDtypeStruct((scales, 48, lanes), f32),
-        ),
+        out_shape=jax.ShapeDtypeStruct((256, w.shape[1]), f32),
         scratch_shapes=[
             pltpu.VMEM((2, cols // lanes, 24 + rows + 24, lanes), f32),
             pltpu.VMEM((256, spans * lanes), bf16),
-            pltpu.VMEM((spans * lanes, scales * 256), bf16),
         ],
-        compiler_params=pltpu.CompilerParams(vmem_limit_bytes=20 * mib),
+        compiler_params=pltpu.CompilerParams(vmem_limit_bytes=16 * mib),
         cost_estimate=pl.CostEstimate(
-            flops=scales * 2 * 256 * 256 * spans * lanes, bytes_accessed=4 * x.size, transcendentals=0
+            flops=2 * 256 * w.size, bytes_accessed=2 * w.size, transcendentals=0
         ),
         name="detect_own",
-    )(psf, x)
-
-
-def detect_halo_body(taps, odd, profile, first, second, acc, out, frame, lhs, w, stage):
+    )(w, x)
+
+
+def detect_halo_body(taps, odd, w, first, second, acc, out, frame, lhs, stage):
     scales, rows, cols = out.shape
     count = cols // lanes
     spans = edge_spans(taps)
     frame[...] = jnp.zeros_like(frame)
-    clear_band(w.at[0], taps, 112, 0, spans)
-    clear_band(w.at[1], taps, 112, taps + 3 - spans, taps + 3)
-    mask = band_mask(112, taps)
+    ends_at = (0, (taps + 3 - spans) * lanes)
     lane = lane_ids(16)
     lo, hi = halo_pair(odd[0] == 1, first[...], second[...])
     put_edges(taps, frame, lhs, lo, hi)
     for s in range(scales):
         at = 256 * s
-        put_band(w.at[0], profile[s], taps, mask, 0, spans, at)
-        put_band(w.at[1], profile[s], taps, mask, taps + 3 - spans, taps + 3, at)
         ends = [
-            jnp.dot(lhs[side], w[side, :, at : at + 256], preferred_element_type=f32)
-            for side in range(2)
+            jnp.dot(
+                lhs[side], w[row : row + spans * lanes, at : at + 256], preferred_element_type=f32
+            )
+            for side, row in enumerate(ends_at)
         ]
         for m in range(count):
             for h in range(2):
@@ -568,9 +579,9 @@
             out[s, :, m * lanes : (m + 1) * lanes] = stage[s, m]
 
 
-def detect_halo(odd, profile, first, second, acc, rows, taps):
+def detect_halo(odd, w, first, second, acc, rows, taps):
     cols = first.shape[1]
-    scales = profile.shape[0]
+    scales = w.shape[1] // 256
     smem = pl.BlockSpec(memory_space=pltpu.SMEM)
     vmem = pl.BlockSpec(memory_space=pltpu.VMEM)
     return pl.pallas_call(
@@ -578,11 +589,11 @@
         in_specs=[smem, vmem, vmem, vmem, vmem],
         out_specs=vmem,
         out_shape=jax.ShapeDtypeStruct((scales, rows, cols), f32),
-        scratch_shapes=edge_scratch(taps, cols // lanes, scales * 256)
+        scratch_shapes=edge_scratch(taps, cols // lanes)
         + [pltpu.VMEM((scales, cols // lanes, rows, lanes), f32)],
-        compiler_params=pltpu.CompilerParams(vmem_limit_bytes=20 * mib),
+        compiler_params=pltpu.CompilerParams(vmem_limit_bytes=16 * mib),
         name="detect_halo",
-    )(odd, profile, first, second, acc)
+    )(odd, w, first, second, acc)
 
 
 def trade(first, second):
@@ -633,21 +644,26 @@
     mine, send = match(odd, place, profile, exposures, first, second)
     other = lax.ppermute(send, "core", swap)
 
-    steps = (2, 1, 3)
+    steps = (2, 3, 1)
     move = lambda rows, step, by: lax.ppermute(rows, sky, role_pairs(step, size, by))
     (far,) = pile((2,), (bf16,), size, place, table, mine, other)
     came = [move(far, 0, 2)]
     far, table = lax.optimization_barrier((far, table))
-    ahead, behind, own = pile((1, 3, 0), (bf16, bf16, f32), size, place, table, mine, other)
-    came += [move(ahead, 0, 1), move(behind, 0, 3)]
+    behind, ahead = pile((3, 1), (bf16, bf16), size, place, table, mine, other)
+    came += [move(behind, 0, 3), move(ahead, 0, 1)]
+    ahead, table = lax.optimization_barrier((ahead, table))
+    (own,) = pile((0,), (f32,), size, place, table, mine, other)
+    own, psf_kernels = lax.optimization_barrier((own, psf_kernels))
+    bands = detect_bands(psf_kernels)
+    own, bands = lax.optimization_barrier((own, bands))
     keep, *sends = fold(own, came)
     came = [move(sends[by - 1], 1, by) for by in steps]
     mine, send = meet(place, keep, came)
     other = lax.ppermute(send, "core", swap)
     coadd, rounded, first, second = coadd_of(odd, place, mine, other, rows, cols, wide_reach)
     first, second = trade(first, second)
-    acc, profile = detect_own(psf_kernels, rounded)
-    detect = detect_halo(odd, profile, first, second, acc, rows, wide)
+    acc = detect_own(bands, rounded, wide)
+    detect = detect_halo(odd, bands, first, second, acc, rows, wide)
     return (coadd[None], detect[None])
 
 

time: 70.5 us -> 71.7 us (1.017)
  local copies, waits for them, and re-layouts: 0.76 us -> 4.78 us
  Pallas kernels: 30.2 us -> 28.2 us
    unnamed x12, local copies, waits for them, and re-layouts: 0.02 us -> 4.04 us
    ppermute x6, starting transfers between devices: 12.9 us -> 10.4 us  [on_device(): lax.ppermute(rows, sky, role_pairs(step, size, by))]
    pallas_call x2 -> x3, Pallas kernels: 8.79 us -> 7.29 us  [pile(): pl.pallas_call(functools.partial(pile_body, chunks, size), in_specs=[smem...]
    ppermute x6, waiting for transfers between devices: 10.5 us -> 11.9 us  [on_device(): lax.ppermute(rows, sky, role_pairs(step, size, by))]
    ppermute x4, starting transfers between devices: 6.66 us -> 7.93 us  [trade(): lax.ppermute(rows, 'section', pairs + [(b, a) for a, b in pairs])]
    pallas_call x1, Pallas kernels: 3.31 us -> 2.48 us  [detect_halo(): pl.pallas_call(functools.partial(detect_halo_body, taps), in_specs=[smem,...]
    pallas_call x1 -> x2, Pallas kernels: 3.57 us -> 3.87 us  [the longest x1 2.53 us: detect_own(): pl.pallas_call(functools.partial(detect_own_body, taps), out_shape=jax.Sh...]
  transfers between devices with their start and end apart: 13 -> 13, of which waited for: 6 -> 8; matrix products, arithmetic and copies ran while one was open for 2% -> 2% of each run, Pallas kernels for 20% -> 19%
where the time goes in v8:
time: 71.7 us; the launch traced here: 71.2 us
  Pallas kernels  28.2 us (39%)
  starting transfers between devices  19 us (26%)
  waiting for transfers between devices  16.4 us (23%)
  local copies, waits for them, and re-layouts  4.78 us (7%)
  other arithmetic  1.97 us (3%)
  between operations  0.84 us (1%)
    ppermute x6, waiting for transfers between devices, on_device(): lax.ppermute(rows, sky, role_pairs(step, size, by))  11.9 us
    ppermute x6, starting transfers between devices, on_device(): lax.ppermute(rows, sky, role_pairs(step, size, by))  10.4 us
    pallas_call x1, Pallas kernels, match(): pl.pallas_call(functools.partial(match_body, taps), in_specs=[smem, smem,...  8.09 us
    ppermute x4, starting transfers between devices, trade(): lax.ppermute(rows, 'section', pairs + [(b, a) for a, b in pairs])  7.93 us
    pallas_call x3, Pallas kernels, pile(): pl.pallas_call(functools.partial(pile_body, chunks, size), in_specs=[smem...  7.29 us
    unnamed x12, local copies, waits for them, and re-layouts  4.04 us
    ppermute x2, waiting for transfers between devices, on_device(): other = lax.ppermute(send, 'core', swap)  3.07 us
    pallas_call x1, Pallas kernels, detect_own(): pl.pallas_call(functools.partial(detect_own_body, taps), out_shape=jax.Sh...  2.53 us
  transfers between devices with their start and end apart: 13, of which 8 were waited for; matrix products, arithmetic and copies ran while one was open for 2% of the time, Pallas kernels for 19%

profile of v8, /device:TPU:32, one launch (start us, length us, event | category | flops | bytes accessed | tf_op | source)
XLA Modules:
  0.0 71.2 jit_solution(9164614430713072393)
XLA Ops:
  0.6 1.1 %broadcast_select_fusion = (bf16[8,11,1024]{2,1,0:T(8,128)(2,1)S(1)}, bf16[8,11,1024]{2,1,0:T(8,128)(2,1)S(1)}) fusion(pred[]{:T(512)S(6)} %eq.11, bf16[8,64,1024]{2,1,0:T(8,128)(2,1)} %far.1), kind=kLoop, calls=%fused_computation | loop fusion | flops 180224 | bytes 720897 | tf_op jit(solution)/shard_map/jit(_where)/select_n | solution.py:632
  1.8 3.8 %collective-permute-start.2 = (bf16[8,11,1024]{2,1,0:T(8,128)(2,1)S(1)}, bf16[8,11,1024]{2,1,0:T(8,128)(2,1)S(1)}, u32[]{:S(2)}, u32[]{:S(2)}) collective-permute-start(bf16[8,11,1024]{2,1,0:T(8,128)(2,1)S(1)} %get-tuple-element.46), channel_id=1, source_target_pairs={{32,64},{64,32},{33,65},{65,33},{34,66},{66,34},{35,67},{67,35},{3... | collective-permute-start | bytes 540680 | tf_op jit(solution)/shard_map/ppermute | solution.py:604
  5.6 0.1 collective-permute-start.1
  5.7 0.7 %copy.11 = s32[8,1]{1,0:T(8,128)S(1)} copy(s32[8,1]{0,1:T(1,128)} %bitcast.12) | data formatting | bytes 64 | tf_op jit(solution)/shard_map/broadcast_in_dim | solution.py:636
  6.4 0.8 %pad_add_fusion.mine = s32[8,17]{1,0:T(8,128)S(1)} fusion(s32[8,8]{1,0:T(8,128)} %param.16, s32[8,8]{1,0:T(8,128)} %param.15, s32[8,1]{1,0:T(8,128)S(1)} %copy.11), kind=kLoop, calls=%fused_computation.2 | loop fusion | flops 272 | bytes 1088 | tf_op jit(solution)/shard_map/concatenate | solution.py:635
  7.2 0.0 collective-permute-start
  7.2 0.1 pad_add_fusion.1.place
  7.3 0.7 %copy-done.2 = f32[27,64]{1,0:T(8,128)S(1)} copy-done((f32[27,64]{1,0:T(8,128)S(1)}, f32[27,64]{1,0:T(8,128)}, u32[]{:S(2)}) %copy-start.2) | copy-done | bytes 6936
  8.0 0.7 copy-done.3
  8.7 0.7 copy-done.4
  9.4 0.7 copy-done.5
  10.1 1.9 %profiles.1.profile = f32[8,24,128]{2,1,0:T(8,128)S(1)} custom-call(s32[8,27]{1,0:T(8,128)S(1)} %copy-done.5, f32[27,64]{1,0:T(8,128)S(1)} %copy-done.2, f32[23,27]{1,0:T(8,128)S(1)} %bitcast.9, f32[23,27]{1,0:T(8,128)S(1)} %bitcast.10), custom_call_target="tpu_custom_call" | custom-call | tf_op jit(solution)/shard_map/profiles/pallas_call | solution.py:179
  12.0 0.0 collective-permute-done.other
  12.0 2.4 %slot_table.1.table = s32[288]{0:T(512)S(1)} custom-call(s32[8,17]{1,0:T(8,128)S(1)} %pad_add_fusion.mine, s32[8,17]{1,0:T(8,128)S(1)} %collective-permute-done.other), custom_call_target="tpu_custom_call" | custom-call | tf_op jit(solution)/shard_map/slot_table/pallas_call | solution.py:296
  14.5 0.0 collective-permute-done.2.second
  14.5 0.0 collective-permute-done.1.first
  14.5 0.0 copy-start
  14.5 1.2 %copy-done = bf16[8,64,1024]{2,1,0:T(8,128)(2,1)S(1)} copy-done((bf16[8,64,1024]{2,1,0:T(8,128)(2,1)S(1)}, bf16[8,64,1024]{2,1,0:T(8,128)(2,1)}, u32[]{:S(2)}) %copy-start) | copy-done | bytes 1048600
  15.7 8.1 %match.1 = (bf16[8,64,640]{2,1,0:T(8,128)(2,1)S(1)}, bf16[8,64,640]{2,1,0:T(8,128)(2,1)S(1)}) custom-call(s32[1]{0:T(128)} %bitcast.odd, s32[3]{0:T(128)S(1)} %pad_add_fusion.1.place, f32[8,24,128]{2,1,0:T(8,128)S(1)} %profiles.1.profile, bf16[8,64,1024]{2,1,0:T(8,128)(2,1)S(1)} %copy-done, bf16[8,11,1024]{2,1,0:T(8,128)(2,1)S(1)} %collective-permute-done.1.first, ...), custom_call_target="tpu_custom_call" | custom-call | flops 3489660928 | bytes 2097152 | tf_op jit(solution)/shard_map/match/pallas_call | solution.py:245
  23.8 0.0 copy-start.1
  23.8 0.6 collective-permute-start.3
  24.4 1.7 %collective-permute-done.3.other = bf16[8,64,640]{2,1,0:T(8,128)(2,1)S(1)} collective-permute-done((bf16[8,64,640]{2,1,0:T(8,128)(2,1)S(1)}, bf16[8,64,640]{2,1,0:T(8,128)(2,1)S(1)}, u32[]{:S(2)}, u32[]{:S(2)}) %collective-permute-start.3) | collective-permute-done | bytes 655392 | tf_op jit(solution)/shard_map/ppermute | solution.py:645
  26.1 2.0 %pile_2.1 = bf16[8,272,128]{2,1,0:T(8,128)(2,1)S(1)} custom-call(s32[3]{0:T(128)S(1)} %pad_add_fusion.1.place, s32[288]{0:T(512)S(1)} %slot_table.1.table, bf16[8,64,640]{2,1,0:T(8,128)(2,1)S(1)} %get-tuple-element.26.mine, bf16[8,64,640]{2,1,0:T(8,128)(2,1)S(1)} %collective-permute-done.3.other), custom_call_target="tpu_custom_call" | custom-call | flops 1000000000 | bytes 1310720 | tf_op jit(solution)/shard_map/pile_2/pallas_call | solution.py:388
  28.1 2.9 %collective-permute-start.4 = (bf16[8,272,128]{2,1,0:T(8,128)(2,1)S(1)}, bf16[8,272,128]{2,1,0:T(8,128)(2,1)S(1)}, u32[]{:S(2)}, u32[]{:S(2)}) collective-permute-start(bf16[8,272,128]{2,1,0:T(8,128)(2,1)S(1)} %pile_2.1), channel_id=1, source_target_pairs={{0,4},{1,17},{2,6},{3,19},{4,0},{5,21},{6,2},{7,23},{8,12},{9,25},... | collective-permute-start | bytes 1671176 | tf_op jit(solution)/shard_map/ppermute | solution.py:648
  31.1 3.4 %pile_3_1.1 = (bf16[8,272,128]{2,1,0:T(8,128)(2,1)S(1)}, bf16[8,272,128]{2,1,0:T(8,128)(2,1)S(1)}) custom-call(s32[3]{0:T(128)S(1)} %pad_add_fusion.1.place, s32[288]{0:T(512)S(1)} %slot_table.1.table, bf16[8,64,640]{2,1,0:T(8,128)(2,1)S(1)} %get-tuple-element.26.mine, bf16[8,64,640]{2,1,0:T(8,128)(2,1)S(1)} %collective-permute-done.3.other), custom_call_target="tpu_custom_call" | custom-call | flops 2000000000 | bytes 1310720 | tf_op jit(solution)/shard_map/pile_3_1/pallas_call | solution.py:388
  34.5 1.3 %collective-permute-start.5 = (bf16[8,272,128]{2,1,0:T(8,128)(2,1)S(1)}, bf16[8,272,128]{2,1,0:T(8,128)(2,1)S(1)}, u32[]{:S(2)}, u32[]{:S(2)}) collective-permute-start(bf16[8,272,128]{2,1,0:T(8,128)(2,1)S(1)} %get-tuple-element.34), channel_id=1, source_target_pairs={{0,6},{1,25},{2,0},{3,27},{4,2},{5,29},{6,4},{7,31},{8,14},{9,1},{... | collective-permute-start | bytes 1671176 | tf_op jit(solution)/shard_map/ppermute | solution.py:648
  35.8 0.8 %collective-permute-start.6 = (bf16[8,272,128]{2,1,0:T(8,128)(2,1)S(1)}, bf16[8,272,128]{2,1,0:T(8,128)(2,1)S(1)}, u32[]{:S(2)}, u32[]{:S(2)}) collective-permute-start(bf16[8,272,128]{2,1,0:T(8,128)(2,1)S(1)} %get-tuple-element.29), channel_id=1, source_target_pairs={{0,2},{1,9},{2,4},{3,11},{4,6},{5,13},{6,0},{7,15},{8,10},{9,17},{... | collective-permute-start | bytes 1671176 | tf_op jit(solution)/shard_map/ppermute | solution.py:648
  36.6 1.8 %pile_0.1.own = f32[8,272,128]{2,1,0:T(8,128)S(1)} custom-call(s32[3]{0:T(128)S(1)} %pad_add_fusion.1.place, s32[288]{0:T(512)S(1)} %slot_table.1.table, bf16[8,64,640]{2,1,0:T(8,128)(2,1)S(1)} %get-tuple-element.26.mine, bf16[8,64,640]{2,1,0:T(8,128)(2,1)S(1)} %collective-permute-done.3.other), custom_call_target="tpu_custom_call" | custom-call | flops 1000000000 | bytes 1310720 | tf_op jit(solution)/shard_map/pile_0/pallas_call | solution.py:388
  38.5 1.3 %bands.1.w = bf16[5632,768]{1,0:T(8,128)(2,1)S(1)} custom-call(bf16[3,41,41]{2,1,0:T(8,128)(2,1)S(1)} %copy-done.1), custom_call_target="tpu_custom_call" | custom-call | tf_op jit(solution)/shard_map/bands/pallas_call | solution.py:513
  39.8 0.0 collective-permute-done.4.rest_0_
  39.8 5.4 %collective-permute-done.5.rest_1_ = bf16[8,272,128]{2,1,0:T(8,128)(2,1)S(1)} collective-permute-done((bf16[8,272,128]{2,1,0:T(8,128)(2,1)S(1)}, bf16[8,272,128]{2,1,0:T(8,128)(2,1)S(1)}, u32[]{:S(2)}, u32[]{:S(2)}) %collective-permute-start.5) | collective-permute-done | bytes 557088 | tf_op jit(solution)/shard_map/ppermute | solution.py:648
  45.2 1.3 %collective-permute-done.6.rest_2_ = bf16[8,272,128]{2,1,0:T(8,128)(2,1)S(1)} collective-permute-done((bf16[8,272,128]{2,1,0:T(8,128)(2,1)S(1)}, bf16[8,272,128]{2,1,0:T(8,128)(2,1)S(1)}, u32[]{:S(2)}, u32[]{:S(2)}) %collective-permute-start.6) | collective-permute-done | bytes 557088 | tf_op jit(solution)/shard_map/ppermute | solution.py:648
  46.6 0.2 fold.1
  46.8 3.4 %collective-permute-start.7 = (bf16[2,272,128]{2,1,0:T(8,128)(2,1)S(1)}, bf16[2,272,128]{2,1,0:T(8,128)(2,1)S(1)}, u32[]{:S(2)}, u32[]{:S(2)}) collective-permute-start(bf16[2,272,128]{2,1,0:T(8,128)(2,1)S(1)} %get-tuple-element.36), channel_id=1, source_target_pairs={{0,16},{1,5},{2,18},{3,7},{4,20},{5,1},{6,22},{7,3},{8,24},{9,13},... | collective-permute-start | bytes 417800 | tf_op jit(solution)/shard_map/ppermute | solution.py:648
  50.2 1.0 %collective-permute-start.8 = (bf16[2,272,128]{2,1,0:T(8,128)(2,1)S(1)}, bf16[2,272,128]{2,1,0:T(8,128)(2,1)S(1)}, u32[]{:S(2)}, u32[]{:S(2)}) collective-permute-start(bf16[2,272,128]{2,1,0:T(8,128)(2,1)S(1)} %get-tuple-element.37), channel_id=1, source_target_pairs={{0,24},{1,7},{2,26},{3,1},{4,28},{5,3},{6,30},{7,5},{8,0},{9,15},{... | collective-permute-start | bytes 417800 | tf_op jit(solution)/shard_map/ppermute | solution.py:648
  51.1 1.1 %collective-permute-start.9 = (bf16[2,272,128]{2,1,0:T(8,128)(2,1)S(1)}, bf16[2,272,128]{2,1,0:T(8,128)(2,1)S(1)}, u32[]{:S(2)}, u32[]{:S(2)}) collective-permute-start(bf16[2,272,128]{2,1,0:T(8,128)(2,1)S(1)} %get-tuple-element.38), channel_id=1, source_target_pairs={{0,8},{1,3},{2,10},{3,5},{4,12},{5,7},{6,14},{7,1},{8,16},{9,11},{... | collective-permute-start | bytes 417800 | tf_op jit(solution)/shard_map/ppermute | solution.py:648
  52.2 1.2 %collective-permute-done.7.rest_0_ = bf16[2,272,128]{2,1,0:T(8,128)(2,1)S(1)} collective-permute-done((bf16[2,272,128]{2,1,0:T(8,128)(2,1)S(1)}, bf16[2,272,128]{2,1,0:T(8,128)(2,1)S(1)}, u32[]{:S(2)}, u32[]{:S(2)}) %collective-permute-start.7) | collective-permute-done | bytes 139296 | tf_op jit(solution)/shard_map/ppermute | solution.py:648
  53.4 1.8 %collective-permute-done.8.rest_1_ = bf16[2,272,128]{2,1,0:T(8,128)(2,1)S(1)} collective-permute-done((bf16[2,272,128]{2,1,0:T(8,128)(2,1)S(1)}, bf16[2,272,128]{2,1,0:T(8,128)(2,1)S(1)}, u32[]{:S(2)}, u32[]{:S(2)}) %collective-permute-start.8) | collective-permute-done | bytes 139296 | tf_op jit(solution)/shard_map/ppermute | solution.py:648
  55.3 2.1 %collective-permute-done.9.rest_2_ = bf16[2,272,128]{2,1,0:T(8,128)(2,1)S(1)} collective-permute-done((bf16[2,272,128]{2,1,0:T(8,128)(2,1)S(1)}, bf16[2,272,128]{2,1,0:T(8,128)(2,1)S(1)}, u32[]{:S(2)}, u32[]{:S(2)}) %collective-permute-start.9) | collective-permute-done | bytes 139296 | tf_op jit(solution)/shard_map/ppermute | solution.py:648
  57.4 0.6 meet.1
  58.0 0.1 collective-permute-start.10
  58.1 1.3 %collective-permute-done.10.other = f32[272,128]{1,0:T(8,128)S(1)} collective-permute-done((f32[272,128]{1,0:T(8,128)S(1)}, f32[272,128]{1,0:T(8,128)S(1)}, u32[]{:S(2)}, u32[]{:S(2)}) %collective-permute-start.10) | collective-permute-done | bytes 139296 | tf_op jit(solution)/shard_map/ppermute | solution.py:662
  59.4 1.3 %coadd.1 = (f32[64,1024]{1,0:T(8,128)}, bf16[64,1024]{1,0:T(8,128)(2,1)S(1)}, bf16[20,1024]{1,0:T(8,128)(2,1)S(1)}, bf16[20,1024]{1,0:T(8,128)(2,1)S(1)}) custom-call(s32[1]{0:T(128)} %bitcast.odd, s32[3]{0:T(128)S(1)} %pad_add_fusion.1.place, f32[272,128]{1,0:T(8,128)S(1)} %get-tuple-element.39.mine, f32[272,128]{1,0:T(8,128)S(1)} %collective-permute-done.10.other), custom_call_target="tpu_custom_call" | custom-call | tf_op jit(solution)/shard_map/coadd/pallas_call | solution.py:481
  60.8 2.0 %collective-permute-start.11 = (bf16[20,1024]{1,0:T(8,128)(2,1)S(1)}, bf16[20,1024]{1,0:T(8,128)(2,1)S(1)}, u32[]{:S(2)}, u32[]{:S(2)}) collective-permute-start(bf16[20,1024]{1,0:T(8,128)(2,1)S(1)} %get-tuple-element.43), channel_id=1, source_target_pairs={{0,32},{64,96},{32,0},{96,64},{1,33},{65,97},{33,1},{97,65},{2,34}... | collective-permute-start | bytes 122888 | tf_op jit(solution)/shard_map/ppermute | solution.py:604
  62.8 2.0 %collective-permute-start.12 = (bf16[20,1024]{1,0:T(8,128)(2,1)S(1)}, bf16[20,1024]{1,0:T(8,128)(2,1)S(1)}, u32[]{:S(2)}, u32[]{:S(2)}) collective-permute-start(bf16[20,1024]{1,0:T(8,128)(2,1)S(1)} %get-tuple-element.44), channel_id=1, source_target_pairs={{32,64},{64,32},{33,65},{65,33},{34,66},{66,34},{35,67},{67,35},{3... | collective-permute-start | bytes 122888 | tf_op jit(solution)/shard_map/ppermute | solution.py:604
  64.8 2.5 %detect_own.1.acc = f32[256,768]{1,0:T(8,128)S(1)} custom-call(bf16[5632,768]{1,0:T(8,128)(2,1)S(1)} %bands.1.w, bf16[64,1024]{1,0:T(8,128)(2,1)S(1)} %get-tuple-element.45.x), custom_call_target="tpu_custom_call" | custom-call | flops 2214592512 | bytes 8650752 | tf_op jit(solution)/shard_map/detect_own/pallas_call | solution.py:537
  67.4 1.4 %collective-permute-done.12.second = bf16[20,1024]{1,0:T(8,128)(2,1)S(1)} collective-permute-done((bf16[20,1024]{1,0:T(8,128)(2,1)S(1)}, bf16[20,1024]{1,0:T(8,128)(2,1)S(1)}, u32[]{:S(2)}, u32[]{:S(2)}) %collective-permute-start.12) | collective-permute-done | bytes 40992 | tf_op jit(solution)/shard_map/ppermute | solution.py:604
  68.8 2.5 %detect_halo.1 = f32[3,64,1024]{2,1,0:T(8,128)} custom-call(s32[1]{0:T(128)} %bitcast.odd, bf16[5632,768]{1,0:T(8,128)(2,1)S(1)} %bands.1.w, bf16[20,1024]{1,0:T(8,128)(2,1)S(1)} %collective-permute-done.11.first, bf16[20,1024]{1,0:T(8,128)(2,1)S(1)} %collective-permute-done.12.second, f32[256,768]{1,0:T(8,128)S(1)} %detect_own.1.acc), custom_call_target="tpu_custom_call" | custom-call | tf_op jit(solution)/shard_map/detect_halo/pallas_call | solution.py:587
  (6 shorter events, 0.0 us)
Async XLA Ops:
  1.8 12.7 %collective-permute-start.2 = (bf16[8,11,1024]{2,1,0:T(8,128)(2,1)S(1)}, bf16[8,11,1024]{2,1,0:T(8,128)(2,1)S(1)}, u32[]{:S(2)}, u32[]{:S(2)}) collective-permute-start(bf16[8,11,1024]{2,1,0:T(8,128)(2,1)S(1)} %get-tuple-element.46), channel_id=1, source_target_pairs={{32,64},{64,32},{33,65},{65,33},{34,66},{66,34},{35,67},{67,35},{3... | collective-permute-start | bytes 540680 | tf_op jit(solution)/shard_map/ppermute | solution.py:604
  5.6 8.9 %collective-permute-start.1 = (bf16[8,11,1024]{2,1,0:T(8,128)(2,1)S(1)}, bf16[8,11,1024]{2,1,0:T(8,128)(2,1)S(1)}, u32[]{:S(2)}, u32[]{:S(2)}) collective-permute-start(bf16[8,11,1024]{2,1,0:T(8,128)(2,1)S(1)} %get-tuple-element.47), channel_id=1, source_target_pairs={{0,32},{64,96},{32,0},{96,64},{1,33},{65,97},{33,1},{97,65},{2,34}... | collective-permute-start | bytes 540680 | tf_op jit(solution)/shard_map/ppermute | solution.py:604
  7.2 4.8 %collective-permute-start = (s32[8,17]{1,0:T(8,128)S(1)}, s32[8,17]{1,0:T(8,128)S(1)}, u32[]{:S(2)}, u32[]{:S(2)}) collective-permute-start(s32[8,17]{1,0:T(8,128)S(1)} %pad_add_fusion.mine), channel_id=1, source_target_pairs={{0,1},{1,0},{2,3},{3,2},{4,5},{5,4},{6,7},{7,6},{8,9},{9,8},{10,11... | collective-permute-start | bytes 1640 | tf_op jit(solution)/shard_map/ppermute | solution.py:639
  7.3 0.7 %copy-start.2 = (f32[27,64]{1,0:T(8,128)S(1)}, f32[27,64]{1,0:T(8,128)}, u32[]{:S(2)}) copy-start(f32[27,64]{1,0:T(8,128)} %table.1) | copy-start | bytes 20740
  8.0 0.7 copy-start.3
  8.7 0.7 copy-start.4
  9.4 0.7 copy-start.5
  14.5 1.2 %copy-start = (bf16[8,64,1024]{2,1,0:T(8,128)(2,1)S(1)}, bf16[8,64,1024]{2,1,0:T(8,128)(2,1)}, u32[]{:S(2)}) copy-start(bf16[8,64,1024]{2,1,0:T(8,128)(2,1)} %far.1) | copy-start | bytes 3145732
  23.8 14.6 %copy-start.1 = (bf16[3,41,41]{2,1,0:T(8,128)(2,1)S(1)}, bf16[3,41,41]{2,1,0:T(8,128)(2,1)}, u32[]{:S(2)}) copy-start(bf16[3,41,41]{2,1,0:T(8,128)(2,1)} %psf) | copy-start | bytes 30262
  23.8 2.3 %collective-permute-start.3 = (bf16[8,64,640]{2,1,0:T(8,128)(2,1)S(1)}, bf16[8,64,640]{2,1,0:T(8,128)(2,1)S(1)}, u32[]{:S(2)}, u32[]{:S(2)}) collective-permute-start(bf16[8,64,640]{2,1,0:T(8,128)(2,1)S(1)} %get-tuple-element.27), channel_id=1, source_target_pairs={{0,1},{1,0},{2,3},{3,2},{4,5},{5,4},{6,7},{7,6},{8,9},{9,8},{10,11... | collective-permute-start | bytes 1966088 | tf_op jit(solution)/shard_map/ppermute | solution.py:645
  28.1 11.7 %collective-permute-start.4 = (bf16[8,272,128]{2,1,0:T(8,128)(2,1)S(1)}, bf16[8,272,128]{2,1,0:T(8,128)(2,1)S(1)}, u32[]{:S(2)}, u32[]{:S(2)}) collective-permute-start(bf16[8,272,128]{2,1,0:T(8,128)(2,1)S(1)} %pile_2.1), channel_id=1, source_target_pairs={{0,4},{1,17},{2,6},{3,19},{4,0},{5,21},{6,2},{7,23},{8,12},{9,25},... | collective-permute-start | bytes 1671176 | tf_op jit(solution)/shard_map/ppermute | solution.py:648
  34.5 10.7 %collective-permute-start.5 = (bf16[8,272,128]{2,1,0:T(8,128)(2,1)S(1)}, bf16[8,272,128]{2,1,0:T(8,128)(2,1)S(1)}, u32[]{:S(2)}, u32[]{:S(2)}) collective-permute-start(bf16[8,272,128]{2,1,0:T(8,128)(2,1)S(1)} %get-tuple-element.34), channel_id=1, source_target_pairs={{0,6},{1,25},{2,0},{3,27},{4,2},{5,29},{6,4},{7,31},{8,14},{9,1},{... | collective-permute-start | bytes 1671176 | tf_op jit(solution)/shard_map/ppermute | solution.py:648
  35.8 10.7 %collective-permute-start.6 = (bf16[8,272,128]{2,1,0:T(8,128)(2,1)S(1)}, bf16[8,272,128]{2,1,0:T(8,128)(2,1)S(1)}, u32[]{:S(2)}, u32[]{:S(2)}) collective-permute-start(bf16[8,272,128]{2,1,0:T(8,128)(2,1)S(1)} %get-tuple-element.29), channel_id=1, source_target_pairs={{0,2},{1,9},{2,4},{3,11},{4,6},{5,13},{6,0},{7,15},{8,10},{9,17},{... | collective-permute-start | bytes 1671176 | tf_op jit(solution)/shard_map/ppermute | solution.py:648
  46.8 6.6 %collective-permute-start.7 = (bf16[2,272,128]{2,1,0:T(8,128)(2,1)S(1)}, bf16[2,272,128]{2,1,0:T(8,128)(2,1)S(1)}, u32[]{:S(2)}, u32[]{:S(2)}) collective-permute-start(bf16[2,272,128]{2,1,0:T(8,128)(2,1)S(1)} %get-tuple-element.36), channel_id=1, source_target_pairs={{0,16},{1,5},{2,18},{3,7},{4,20},{5,1},{6,22},{7,3},{8,24},{9,13},... | collective-permute-start | bytes 417800 | tf_op jit(solution)/shard_map/ppermute | solution.py:648
  50.2 5.1 %collective-permute-start.8 = (bf16[2,272,128]{2,1,0:T(8,128)(2,1)S(1)}, bf16[2,272,128]{2,1,0:T(8,128)(2,1)S(1)}, u32[]{:S(2)}, u32[]{:S(2)}) collective-permute-start(bf16[2,272,128]{2,1,0:T(8,128)(2,1)S(1)} %get-tuple-element.37), channel_id=1, source_target_pairs={{0,24},{1,7},{2,26},{3,1},{4,28},{5,3},{6,30},{7,5},{8,0},{9,15},{... | collective-permute-start | bytes 417800 | tf_op jit(solution)/shard_map/ppermute | solution.py:648
  51.1 6.3 %collective-permute-start.9 = (bf16[2,272,128]{2,1,0:T(8,128)(2,1)S(1)}, bf16[2,272,128]{2,1,0:T(8,128)(2,1)S(1)}, u32[]{:S(2)}, u32[]{:S(2)}) collective-permute-start(bf16[2,272,128]{2,1,0:T(8,128)(2,1)S(1)} %get-tuple-element.38), channel_id=1, source_target_pairs={{0,8},{1,3},{2,10},{3,5},{4,12},{5,7},{6,14},{7,1},{8,16},{9,11},{... | collective-permute-start | bytes 417800 | tf_op jit(solution)/shard_map/ppermute | solution.py:648
  58.0 1.4 %collective-permute-start.10 = (f32[272,128]{1,0:T(8,128)S(1)}, f32[272,128]{1,0:T(8,128)S(1)}, u32[]{:S(2)}, u32[]{:S(2)}) collective-permute-start(f32[272,128]{1,0:T(8,128)S(1)} %get-tuple-element.40), channel_id=1, source_target_pairs={{0,1},{1,0},{2,3},{3,2},{4,5},{5,4},{6,7},{7,6},{8,9},{9,8},{10,11... | collective-permute-start | bytes 417800 | tf_op jit(solution)/shard_map/ppermute | solution.py:662
  60.8 6.6 %collective-permute-start.11 = (bf16[20,1024]{1,0:T(8,128)(2,1)S(1)}, bf16[20,1024]{1,0:T(8,128)(2,1)S(1)}, u32[]{:S(2)}, u32[]{:S(2)}) collective-permute-start(bf16[20,1024]{1,0:T(8,128)(2,1)S(1)} %get-tuple-element.43), channel_id=1, source_target_pairs={{0,32},{64,96},{32,0},{96,64},{1,33},{65,97},{33,1},{97,65},{2,34}... | collective-permute-start | bytes 122888 | tf_op jit(solution)/shard_map/ppermute | solution.py:604
  62.8 6.0 %collective-permute-start.12 = (bf16[20,1024]{1,0:T(8,128)(2,1)S(1)}, bf16[20,1024]{1,0:T(8,128)(2,1)S(1)}, u32[]{:S(2)}, u32[]{:S(2)}) collective-permute-start(bf16[20,1024]{1,0:T(8,128)(2,1)S(1)} %get-tuple-element.44), channel_id=1, source_target_pairs={{32,64},{64,32},{33,65},{65,33},{34,66},{66,34},{35,67},{67,35},{3... | collective-permute-start | bytes 122888 | tf_op jit(solution)/shard_map/ppermute | solution.py:604

commit v9 on v7

--- a/solution.py
+++ b/solution.py
@@ -330,40 +330,45 @@
 
         def patch(i, _):
             u = (place[1] + chunk) % size
-            v = (place[2] + i // 2) % size
-            p = jnp.where(core == 0, v * size + u, u * size + v) * 2 + i % 2
+            v = (place[2] + i) % size
+            p = jnp.where(core == 0, v * size + u, u * size + v) * 2
 
             def some(used):
                 entries = []
-                for s in range(used):
-                    word = table[patches + p * slots + s]
-                    plane = word // 256
+                for c in range(2):
+                    words = [table[patches + (p + c) * slots + s] for s in range(used)]
                     entries.append(
-                        (plane % (2 * number), word % 256, (plane // (2 * number)).astype(f32))
+                        [
+                            ((word >> 8) & (2 * number - 1), word & 255, (word >> 12).astype(f32))
+                            for word in words
+                        ]
                     )
-                for c in range(rows // 16):
-                    total = [jnp.zeros((16, lanes), f32)] * tiles
-                    for e, o, weight in entries:
-                        early = lane < o
-                        before = None
-                        for k in range(tiles + 1):
-                            piece = planes[e, c * 16 : c * 16 + 16, k * lanes : (k + 1) * lanes]
-                            turned = pltpu.roll(piece, o, 1).astype(f32)
-                            if k:
-                                part = jnp.where(early, before, turned)
-                                total[k - 1] = total[k - 1] + weight * part
-                            before = turned
-                    for k in range(tiles):
-                        at = k * rows + c * 16
-                        out[i, at : at + 16, :] = total[k].astype(out.dtype)
-                cover = jnp.zeros((16, lanes), f32)
-                whole = jnp.zeros((16, lanes), f32)
-                for e, o, weight in entries:
-                    cover = cover + jnp.where(lane < o, 0.0, weight)
-                    whole = whole + weight
-                out[i, tiles * rows :, :] = jnp.where(tail == 0, cover, whole).astype(out.dtype)
-
-            used = table[p]
+                for r in range(rows // 16):
+                    for c in range(2):
+                        total = [jnp.zeros((16, lanes), f32)] * tiles
+                        for e, o, weight in entries[c]:
+                            early = lane < o
+                            before = None
+                            for k in range(tiles + 1):
+                                piece = planes[e, r * 16 : r * 16 + 16, k * lanes : (k + 1) * lanes]
+                                turned = pltpu.roll(piece, o, 1).astype(f32)
+                                if k:
+                                    part = jnp.where(early, before, turned)
+                                    total[k - 1] = total[k - 1] + weight * part
+                                before = turned
+                        for k in range(tiles):
+                            at = k * rows + r * 16
+                            out[2 * i + c, at : at + 16, :] = total[k].astype(out.dtype)
+                for c in range(2):
+                    cover = jnp.zeros((16, lanes), f32)
+                    whole = jnp.zeros((16, lanes), f32)
+                    for e, o, weight in entries[c]:
+                        cover = cover + jnp.where(lane < o, 0.0, weight)
+                        whole = whole + weight
+                    last = jnp.where(tail == 0, cover, whole)
+                    out[2 * i + c, tiles * rows :, :] = last.astype(out.dtype)
+
+            used = jnp.maximum(table[p], table[p + 1])
             for top in range(2, slots + 1, 2):
                 low = top - 2 if top > 2 else -1
 
@@ -373,7 +378,7 @@
 
             return 0
 
-        lax.fori_loop(0, 2 * size, patch, 0)
+        lax.fori_loop(0, size, patch, 0)
 
 
 def pile(chunks, kinds, size, place, table, mine, other):
@@ -633,13 +638,15 @@
     mine, send = match(odd, place, profile, exposures, first, second)
     other = lax.ppermute(send, "core", swap)
 
-    steps = (2, 1, 3)
+    steps = (2, 3, 1)
     move = lambda rows, step, by: lax.ppermute(rows, sky, role_pairs(step, size, by))
     (far,) = pile((2,), (bf16,), size, place, table, mine, other)
     came = [move(far, 0, 2)]
     far, table = lax.optimization_barrier((far, table))
-    ahead, behind, own = pile((1, 3, 0), (bf16, bf16, f32), size, place, table, mine, other)
-    came += [move(ahead, 0, 1), move(behind, 0, 3)]
+    behind, ahead = pile((3, 1), (bf16, bf16), size, place, table, mine, other)
+    came += [move(behind, 0, 3), move(ahead, 0, 1)]
+    ahead, table = lax.optimization_barrier((ahead, table))
+    (own,) = pile((0,), (f32,), size, place, table, mine, other)
     keep, *sends = fold(own, came)
     came = [move(sends[by - 1], 1, by) for by in steps]
     mine, send = meet(place, keep, came)

time: 70.5 us -> 68.9 us (0.977)
  waiting for transfers between devices: 15.8 us -> 18.5 us
  starting transfers between devices: 19.7 us -> 17.1 us
  Pallas kernels: 30.2 us -> 28.9 us
    ppermute x6, waiting for transfers between devices: 10.5 us -> 13.1 us  [on_device(): lax.ppermute(rows, sky, role_pairs(step, size, by))]
    ppermute x6, starting transfers between devices: 12.9 us -> 10.4 us  [on_device(): lax.ppermute(rows, sky, role_pairs(step, size, by))]
    pallas_call x2 -> x3, Pallas kernels: 8.79 us -> 7.47 us  [pile(): pl.pallas_call(functools.partial(pile_body, chunks, size), in_specs=[smem...]
  transfers between devices with their start and end apart: 13 -> 13, of which waited for: 6 -> 11; matrix products, arithmetic and copies ran while one was open for 2% -> 2% of each run, Pallas kernels for 20% -> 20%
where the time goes in v9:
time: 68.9 us; the launch traced here: 68.2 us
  Pallas kernels  28.9 us (42%)
  waiting for transfers between devices  18.5 us (27%)
  starting transfers between devices  17.1 us (25%)
  other arithmetic  2.05 us (3%)
  between operations  0.86 us (1%)
  local copies, waits for them, and re-layouts  0.76 us (1%)
    ppermute x6, waiting for transfers between devices, on_device(): lax.ppermute(rows, sky, role_pairs(step, size, by))  13.1 us
    ppermute x6, starting transfers between devices, on_device(): lax.ppermute(rows, sky, role_pairs(step, size, by))  10.4 us
    pallas_call x1, Pallas kernels, match(): pl.pallas_call(functools.partial(match_body, taps), in_specs=[smem, smem,...  8.09 us
    pallas_call x3, Pallas kernels, pile(): pl.pallas_call(functools.partial(pile_body, chunks, size), in_specs=[smem...  7.47 us
    ppermute x4, starting transfers between devices, trade(): lax.ppermute(rows, 'section', pairs + [(b, a) for a, b in pairs])  6.48 us
    pallas_call x1, Pallas kernels, detect_own(): pl.pallas_call(functools.partial(detect_own_body, taps), out_shape=(jax.S...  3.57 us
    ppermute x2, waiting for transfers between devices, on_device(): other = lax.ppermute(send, 'core', swap)  3.43 us
    pallas_call x1, Pallas kernels, detect_halo(): pl.pallas_call(functools.partial(detect_halo_body, taps), in_specs=[smem,...  3.3 us
  transfers between devices with their start and end apart: 13, of which 11 were waited for; matrix products, arithmetic and copies ran while one was open for 2% of the time, Pallas kernels for 20%

profile of v9, /device:TPU:32, one launch (start us, length us, event | category | flops | bytes accessed | tf_op | source)
XLA Modules:
  0.0 68.2 jit_solution(16260033746195335668)
XLA Ops:
  0.6 0.0 copy-start
  0.6 0.0 copy-start.3
  0.7 0.0 copy-start.2
  0.7 0.0 copy-start.1
  0.7 1.2 %broadcast_select_fusion = (bf16[8,11,1024]{2,1,0:T(8,128)(2,1)S(1)}, bf16[8,11,1024]{2,1,0:T(8,128)(2,1)S(1)}) fusion(pred[]{:T(512)S(6)} %eq.11, bf16[8,64,1024]{2,1,0:T(8,128)(2,1)} %far.1), kind=kLoop, calls=%fused_computation | loop fusion | flops 180224 | bytes 720897 | tf_op jit(solution)/shard_map/jit(_where)/select_n | solution.py:626
  1.9 3.8 %collective-permute-start.2 = (bf16[8,11,1024]{2,1,0:T(8,128)(2,1)S(1)}, bf16[8,11,1024]{2,1,0:T(8,128)(2,1)S(1)}, u32[]{:S(2)}, u32[]{:S(2)}) collective-permute-start(bf16[8,11,1024]{2,1,0:T(8,128)(2,1)S(1)} %get-tuple-element.42), channel_id=1, source_target_pairs={{32,64},{64,32},{33,65},{65,33},{34,66},{66,34},{35,67},{67,35},{3... | collective-permute-start | bytes 540680 | tf_op jit(solution)/shard_map/ppermute | solution.py:598
  5.7 0.1 collective-permute-start.1
  5.8 0.7 %copy.11 = s32[8,1]{1,0:T(8,128)S(1)} copy(s32[8,1]{0,1:T(1,128)} %bitcast.12) | data formatting | bytes 64 | tf_op jit(solution)/shard_map/broadcast_in_dim | solution.py:630
  6.5 0.8 %pad_add_fusion.mine = s32[8,17]{1,0:T(8,128)S(1)} fusion(s32[8,8]{1,0:T(8,128)} %param.16, s32[8,8]{1,0:T(8,128)} %param.15, s32[8,1]{1,0:T(8,128)S(1)} %copy.11), kind=kLoop, calls=%fused_computation.2 | loop fusion | flops 272 | bytes 1088 | tf_op jit(solution)/shard_map/concatenate | solution.py:629
  7.3 0.0 collective-permute-start
  7.4 0.1 pad_add_fusion.1.place
  7.4 0.0 copy-done.2
  7.5 0.0 copy-done.4
  7.5 1.9 %profiles.1.profile = f32[8,24,128]{2,1,0:T(8,128)S(1)} custom-call(s32[8,27]{1,0:T(8,128)S(1)} %copy-done.4, f32[27,64]{1,0:T(8,128)S(1)} %copy-done.1, f32[23,27]{1,0:T(8,128)S(1)} %bitcast.9, f32[23,27]{1,0:T(8,128)S(1)} %bitcast.10), custom_call_target="tpu_custom_call" | custom-call | tf_op jit(solution)/shard_map/profiles/pallas_call | solution.py:180
  9.3 0.0 collective-permute-done.other
  9.3 2.4 %slot_table.1.table = s32[288]{0:T(512)S(1)} custom-call(s32[8,17]{1,0:T(8,128)S(1)} %pad_add_fusion.mine, s32[8,17]{1,0:T(8,128)S(1)} %collective-permute-done.other), custom_call_target="tpu_custom_call" | custom-call | tf_op jit(solution)/shard_map/slot_table/pallas_call | solution.py:297
  11.8 0.2 collective-permute-done.2.second
  12.0 1.6 %collective-permute-done.1.first = bf16[8,11,1024]{2,1,0:T(8,128)(2,1)S(1)} collective-permute-done((bf16[8,11,1024]{2,1,0:T(8,128)(2,1)S(1)}, bf16[8,11,1024]{2,1,0:T(8,128)(2,1)S(1)}, u32[]{:S(2)}, u32[]{:S(2)}) %collective-permute-start.1) | collective-permute-done | bytes 180256 | tf_op jit(solution)/shard_map/ppermute | solution.py:598
  13.6 8.1 %match.1 = (bf16[8,64,640]{2,1,0:T(8,128)(2,1)S(1)}, bf16[8,64,640]{2,1,0:T(8,128)(2,1)S(1)}) custom-call(s32[1]{0:T(128)} %bitcast.odd, s32[3]{0:T(128)S(1)} %pad_add_fusion.1.place, f32[8,24,128]{2,1,0:T(8,128)S(1)} %profiles.1.profile, bf16[8,64,1024]{2,1,0:T(8,128)(2,1)S(1)} %copy-done, bf16[8,11,1024]{2,1,0:T(8,128)(2,1)S(1)} %collective-permute-done.1.first, ...), custom_call_target="tpu_custom_call" | custom-call | flops 3489660928 | bytes 2097152 | tf_op jit(solution)/shard_map/match/pallas_call | solution.py:246
  21.7 0.1 collective-permute-start.3
  21.8 2.1 %collective-permute-done.3.other = bf16[8,64,640]{2,1,0:T(8,128)(2,1)S(1)} collective-permute-done((bf16[8,64,640]{2,1,0:T(8,128)(2,1)S(1)}, bf16[8,64,640]{2,1,0:T(8,128)(2,1)S(1)}, u32[]{:S(2)}, u32[]{:S(2)}) %collective-permute-start.3) | collective-permute-done | bytes 655392 | tf_op jit(solution)/shard_map/ppermute | solution.py:639
  23.8 2.0 %pile_2.1 = bf16[8,272,128]{2,1,0:T(8,128)(2,1)S(1)} custom-call(s32[3]{0:T(128)S(1)} %pad_add_fusion.1.place, s32[288]{0:T(512)S(1)} %slot_table.1.table, bf16[8,64,640]{2,1,0:T(8,128)(2,1)S(1)} %get-tuple-element.24.mine, bf16[8,64,640]{2,1,0:T(8,128)(2,1)S(1)} %collective-permute-done.3.other), custom_call_target="tpu_custom_call" | custom-call | flops 1000000000 | bytes 1310720 | tf_op jit(solution)/shard_map/pile_2/pallas_call | solution.py:389
  25.9 3.1 %collective-permute-start.4 = (bf16[8,272,128]{2,1,0:T(8,128)(2,1)S(1)}, bf16[8,272,128]{2,1,0:T(8,128)(2,1)S(1)}, u32[]{:S(2)}, u32[]{:S(2)}) collective-permute-start(bf16[8,272,128]{2,1,0:T(8,128)(2,1)S(1)} %pile_2.1), channel_id=1, source_target_pairs={{0,4},{1,17},{2,6},{3,19},{4,0},{5,21},{6,2},{7,23},{8,12},{9,25},... | collective-permute-start | bytes 1671176 | tf_op jit(solution)/shard_map/ppermute | solution.py:642
  29.0 3.5 %pile_3_1.1 = (bf16[8,272,128]{2,1,0:T(8,128)(2,1)S(1)}, bf16[8,272,128]{2,1,0:T(8,128)(2,1)S(1)}) custom-call(s32[3]{0:T(128)S(1)} %pad_add_fusion.1.place, s32[288]{0:T(512)S(1)} %slot_table.1.table, bf16[8,64,640]{2,1,0:T(8,128)(2,1)S(1)} %get-tuple-element.24.mine, bf16[8,64,640]{2,1,0:T(8,128)(2,1)S(1)} %collective-permute-done.3.other), custom_call_target="tpu_custom_call" | custom-call | flops 2000000000 | bytes 1310720 | tf_op jit(solution)/shard_map/pile_3_1/pallas_call | solution.py:389
  32.4 1.1 %collective-permute-start.5 = (bf16[8,272,128]{2,1,0:T(8,128)(2,1)S(1)}, bf16[8,272,128]{2,1,0:T(8,128)(2,1)S(1)}, u32[]{:S(2)}, u32[]{:S(2)}) collective-permute-start(bf16[8,272,128]{2,1,0:T(8,128)(2,1)S(1)} %get-tuple-element.29), channel_id=1, source_target_pairs={{0,6},{1,25},{2,0},{3,27},{4,2},{5,29},{6,4},{7,31},{8,14},{9,1},{... | collective-permute-start | bytes 1671176 | tf_op jit(solution)/shard_map/ppermute | solution.py:642
  33.6 1.0 %collective-permute-start.6 = (bf16[8,272,128]{2,1,0:T(8,128)(2,1)S(1)}, bf16[8,272,128]{2,1,0:T(8,128)(2,1)S(1)}, u32[]{:S(2)}, u32[]{:S(2)}) collective-permute-start(bf16[8,272,128]{2,1,0:T(8,128)(2,1)S(1)} %get-tuple-element.27), channel_id=1, source_target_pairs={{0,2},{1,9},{2,4},{3,11},{4,6},{5,13},{6,0},{7,15},{8,10},{9,17},{... | collective-permute-start | bytes 1671176 | tf_op jit(solution)/shard_map/ppermute | solution.py:642
  34.5 2.0 %pile_0.1.own = f32[8,272,128]{2,1,0:T(8,128)S(1)} custom-call(s32[3]{0:T(128)S(1)} %pad_add_fusion.1.place, s32[288]{0:T(512)S(1)} %slot_table.1.table, bf16[8,64,640]{2,1,0:T(8,128)(2,1)S(1)} %get-tuple-element.24.mine, bf16[8,64,640]{2,1,0:T(8,128)(2,1)S(1)} %collective-permute-done.3.other), custom_call_target="tpu_custom_call" | custom-call | flops 1000000000 | bytes 1310720 | tf_op jit(solution)/shard_map/pile_0/pallas_call | solution.py:389
  36.5 0.0 copy-start.5
  36.5 0.4 collective-permute-done.4.rest_0_
  37.0 6.1 %collective-permute-done.5.rest_1_ = bf16[8,272,128]{2,1,0:T(8,128)(2,1)S(1)} collective-permute-done((bf16[8,272,128]{2,1,0:T(8,128)(2,1)S(1)}, bf16[8,272,128]{2,1,0:T(8,128)(2,1)S(1)}, u32[]{:S(2)}, u32[]{:S(2)}) %collective-permute-start.5) | collective-permute-done | bytes 557088 | tf_op jit(solution)/shard_map/ppermute | solution.py:642
  43.0 1.3 %collective-permute-done.6.rest_2_ = bf16[8,272,128]{2,1,0:T(8,128)(2,1)S(1)} collective-permute-done((bf16[8,272,128]{2,1,0:T(8,128)(2,1)S(1)}, bf16[8,272,128]{2,1,0:T(8,128)(2,1)S(1)}, u32[]{:S(2)}, u32[]{:S(2)}) %collective-permute-start.6) | collective-permute-done | bytes 557088 | tf_op jit(solution)/shard_map/ppermute | solution.py:642
  44.3 0.2 fold.1
  44.5 3.2 %collective-permute-start.7 = (bf16[2,272,128]{2,1,0:T(8,128)(2,1)S(1)}, bf16[2,272,128]{2,1,0:T(8,128)(2,1)S(1)}, u32[]{:S(2)}, u32[]{:S(2)}) collective-permute-start(bf16[2,272,128]{2,1,0:T(8,128)(2,1)S(1)} %get-tuple-element.31), channel_id=1, source_target_pairs={{0,16},{1,5},{2,18},{3,7},{4,20},{5,1},{6,22},{7,3},{8,24},{9,13},... | collective-permute-start | bytes 417800 | tf_op jit(solution)/shard_map/ppermute | solution.py:642
  47.7 1.1 %collective-permute-start.8 = (bf16[2,272,128]{2,1,0:T(8,128)(2,1)S(1)}, bf16[2,272,128]{2,1,0:T(8,128)(2,1)S(1)}, u32[]{:S(2)}, u32[]{:S(2)}) collective-permute-start(bf16[2,272,128]{2,1,0:T(8,128)(2,1)S(1)} %get-tuple-element.32), channel_id=1, source_target_pairs={{0,24},{1,7},{2,26},{3,1},{4,28},{5,3},{6,30},{7,5},{8,0},{9,15},{... | collective-permute-start | bytes 417800 | tf_op jit(solution)/shard_map/ppermute | solution.py:642
  48.9 0.9 %collective-permute-start.9 = (bf16[2,272,128]{2,1,0:T(8,128)(2,1)S(1)}, bf16[2,272,128]{2,1,0:T(8,128)(2,1)S(1)}, u32[]{:S(2)}, u32[]{:S(2)}) collective-permute-start(bf16[2,272,128]{2,1,0:T(8,128)(2,1)S(1)} %get-tuple-element.33), channel_id=1, source_target_pairs={{0,8},{1,3},{2,10},{3,5},{4,12},{5,7},{6,14},{7,1},{8,16},{9,11},{... | collective-permute-start | bytes 417800 | tf_op jit(solution)/shard_map/ppermute | solution.py:642
  49.7 1.4 %collective-permute-done.7.rest_0_ = bf16[2,272,128]{2,1,0:T(8,128)(2,1)S(1)} collective-permute-done((bf16[2,272,128]{2,1,0:T(8,128)(2,1)S(1)}, bf16[2,272,128]{2,1,0:T(8,128)(2,1)S(1)}, u32[]{:S(2)}, u32[]{:S(2)}) %collective-permute-start.7) | collective-permute-done | bytes 139296 | tf_op jit(solution)/shard_map/ppermute | solution.py:642
  51.2 1.8 %collective-permute-done.8.rest_1_ = bf16[2,272,128]{2,1,0:T(8,128)(2,1)S(1)} collective-permute-done((bf16[2,272,128]{2,1,0:T(8,128)(2,1)S(1)}, bf16[2,272,128]{2,1,0:T(8,128)(2,1)S(1)}, u32[]{:S(2)}, u32[]{:S(2)}) %collective-permute-start.8) | collective-permute-done | bytes 139296 | tf_op jit(solution)/shard_map/ppermute | solution.py:642
  53.0 2.1 %collective-permute-done.9.rest_2_ = bf16[2,272,128]{2,1,0:T(8,128)(2,1)S(1)} collective-permute-done((bf16[2,272,128]{2,1,0:T(8,128)(2,1)S(1)}, bf16[2,272,128]{2,1,0:T(8,128)(2,1)S(1)}, u32[]{:S(2)}, u32[]{:S(2)}) %collective-permute-start.9) | collective-permute-done | bytes 139296 | tf_op jit(solution)/shard_map/ppermute | solution.py:642
  55.1 0.6 meet.1
  55.7 0.1 collective-permute-start.10
  55.8 1.3 %collective-permute-done.10.other = f32[272,128]{1,0:T(8,128)S(1)} collective-permute-done((f32[272,128]{1,0:T(8,128)S(1)}, f32[272,128]{1,0:T(8,128)S(1)}, u32[]{:S(2)}, u32[]{:S(2)}) %collective-permute-start.10) | collective-permute-done | bytes 139296 | tf_op jit(solution)/shard_map/ppermute | solution.py:653
  57.2 1.3 %coadd.1 = (f32[64,1024]{1,0:T(8,128)}, bf16[64,1024]{1,0:T(8,128)(2,1)S(1)}, bf16[20,1024]{1,0:T(8,128)(2,1)S(1)}, bf16[20,1024]{1,0:T(8,128)(2,1)S(1)}) custom-call(s32[1]{0:T(128)} %bitcast.odd, s32[3]{0:T(128)S(1)} %pad_add_fusion.1.place, f32[272,128]{1,0:T(8,128)S(1)} %get-tuple-element.34.mine, f32[272,128]{1,0:T(8,128)S(1)} %collective-permute-done.10.other), custom_call_target="tpu_custom_call" | custom-call | tf_op jit(solution)/shard_map/coadd/pallas_call | solution.py:482
  58.5 0.4 collective-permute-start.11
  58.9 2.2 %collective-permute-start.12 = (bf16[20,1024]{1,0:T(8,128)(2,1)S(1)}, bf16[20,1024]{1,0:T(8,128)(2,1)S(1)}, u32[]{:S(2)}, u32[]{:S(2)}) collective-permute-start(bf16[20,1024]{1,0:T(8,128)(2,1)S(1)} %get-tuple-element.40), channel_id=1, source_target_pairs={{32,64},{64,32},{33,65},{65,33},{34,66},{66,34},{35,67},{67,35},{3... | collective-permute-start | bytes 122888 | tf_op jit(solution)/shard_map/ppermute | solution.py:598
  61.1 3.6 %detect_own.1 = (f32[256,768]{1,0:T(8,128)S(1)}, f32[3,48,128]{2,1,0:T(8,128)S(1)}) custom-call(bf16[3,41,41]{2,1,0:T(8,128)(2,1)S(1)} %copy-done.5, bf16[64,1024]{1,0:T(8,128)(2,1)S(1)} %get-tuple-element.37.x), custom_call_target="tpu_custom_call" | custom-call | flops 2214592512 | bytes 262144 | tf_op jit(solution)/shard_map/detect_own/pallas_call | solution.py:525
  64.7 0.0 collective-permute-done.11.first
  64.7 0.2 collective-permute-done.12.second
  64.9 3.3 %detect_halo.1 = f32[3,64,1024]{2,1,0:T(8,128)} custom-call(s32[1]{0:T(128)} %bitcast.odd, f32[3,48,128]{2,1,0:T(8,128)S(1)} %get-tuple-element.38.profile, bf16[20,1024]{1,0:T(8,128)(2,1)S(1)} %collective-permute-done.11.first, bf16[20,1024]{1,0:T(8,128)(2,1)S(1)} %collective-permute-done.12.second, f32[256,768]{1,0:T(8,128)S(1)} %get-tuple-element.41.acc), custom_call_target="tpu_custom_call" | custom-call | tf_op jit(solution)/shard_map/detect_halo/pallas_call | solution.py:581
  (5 shorter events, 0.0 us)
Async XLA Ops:
  0.6 12.9 %copy-start = (bf16[8,64,1024]{2,1,0:T(8,128)(2,1)S(1)}, bf16[8,64,1024]{2,1,0:T(8,128)(2,1)}, u32[]{:S(2)}) copy-start(bf16[8,64,1024]{2,1,0:T(8,128)(2,1)} %far.1) | copy-start | bytes 3145732
  0.6 6.8 %copy-start.3 = (f32[27,23]{0,1:T(8,128)S(1)}, f32[27,23]{0,1:T(8,128)}, u32[]{:S(2)}) copy-start(f32[27,23]{0,1:T(8,128)} %param.13) | copy-start | bytes 7456
  0.7 6.8 %copy-start.2 = (f32[27,23]{0,1:T(8,128)S(1)}, f32[27,23]{0,1:T(8,128)}, u32[]{:S(2)}) copy-start(f32[27,23]{0,1:T(8,128)} %param.12) | copy-start | bytes 7456
  0.7 6.8 %copy-start.1 = (f32[27,64]{1,0:T(8,128)S(1)}, f32[27,64]{1,0:T(8,128)}, u32[]{:S(2)}) copy-start(f32[27,64]{1,0:T(8,128)} %table.1) | copy-start | bytes 20740
  0.7 6.8 %copy-start.4 = (s32[8,27]{1,0:T(8,128)S(1)}, s32[8,27]{1,0:T(8,128)}, u32[]{:S(2)}) copy-start(s32[8,27]{1,0:T(8,128)} %code.1) | copy-start | bytes 2596
  1.9 10.1 %collective-permute-start.2 = (bf16[8,11,1024]{2,1,0:T(8,128)(2,1)S(1)}, bf16[8,11,1024]{2,1,0:T(8,128)(2,1)S(1)}, u32[]{:S(2)}, u32[]{:S(2)}) collective-permute-start(bf16[8,11,1024]{2,1,0:T(8,128)(2,1)S(1)} %get-tuple-element.42), channel_id=1, source_target_pairs={{32,64},{64,32},{33,65},{65,33},{34,66},{66,34},{35,67},{67,35},{3... | collective-permute-start | bytes 540680 | tf_op jit(solution)/shard_map/ppermute | solution.py:598
  5.7 7.8 %collective-permute-start.1 = (bf16[8,11,1024]{2,1,0:T(8,128)(2,1)S(1)}, bf16[8,11,1024]{2,1,0:T(8,128)(2,1)S(1)}, u32[]{:S(2)}, u32[]{:S(2)}) collective-permute-start(bf16[8,11,1024]{2,1,0:T(8,128)(2,1)S(1)} %get-tuple-element.43), channel_id=1, source_target_pairs={{0,32},{64,96},{32,0},{96,64},{1,33},{65,97},{33,1},{97,65},{2,34}... | collective-permute-start | bytes 540680 | tf_op jit(solution)/shard_map/ppermute | solution.py:598
  7.3 2.0 %collective-permute-start = (s32[8,17]{1,0:T(8,128)S(1)}, s32[8,17]{1,0:T(8,128)S(1)}, u32[]{:S(2)}, u32[]{:S(2)}) collective-permute-start(s32[8,17]{1,0:T(8,128)S(1)} %pad_add_fusion.mine), channel_id=1, source_target_pairs={{0,1},{1,0},{2,3},{3,2},{4,5},{5,4},{6,7},{7,6},{8,9},{9,8},{10,11... | collective-permute-start | bytes 1640 | tf_op jit(solution)/shard_map/ppermute | solution.py:633
  21.7 2.2 %collective-permute-start.3 = (bf16[8,64,640]{2,1,0:T(8,128)(2,1)S(1)}, bf16[8,64,640]{2,1,0:T(8,128)(2,1)S(1)}, u32[]{:S(2)}, u32[]{:S(2)}) collective-permute-start(bf16[8,64,640]{2,1,0:T(8,128)(2,1)S(1)} %get-tuple-element.25), channel_id=1, source_target_pairs={{0,1},{1,0},{2,3},{3,2},{4,5},{5,4},{6,7},{7,6},{8,9},{9,8},{10,11... | collective-permute-start | bytes 1966088 | tf_op jit(solution)/shard_map/ppermute | solution.py:639
  25.9 11.1 %collective-permute-start.4 = (bf16[8,272,128]{2,1,0:T(8,128)(2,1)S(1)}, bf16[8,272,128]{2,1,0:T(8,128)(2,1)S(1)}, u32[]{:S(2)}, u32[]{:S(2)}) collective-permute-start(bf16[8,272,128]{2,1,0:T(8,128)(2,1)S(1)} %pile_2.1), channel_id=1, source_target_pairs={{0,4},{1,17},{2,6},{3,19},{4,0},{5,21},{6,2},{7,23},{8,12},{9,25},... | collective-permute-start | bytes 1671176 | tf_op jit(solution)/shard_map/ppermute | solution.py:642
  32.4 10.6 %collective-permute-start.5 = (bf16[8,272,128]{2,1,0:T(8,128)(2,1)S(1)}, bf16[8,272,128]{2,1,0:T(8,128)(2,1)S(1)}, u32[]{:S(2)}, u32[]{:S(2)}) collective-permute-start(bf16[8,272,128]{2,1,0:T(8,128)(2,1)S(1)} %get-tuple-element.29), channel_id=1, source_target_pairs={{0,6},{1,25},{2,0},{3,27},{4,2},{5,29},{6,4},{7,31},{8,14},{9,1},{... | collective-permute-start | bytes 1671176 | tf_op jit(solution)/shard_map/ppermute | solution.py:642
  33.6 10.7 %collective-permute-start.6 = (bf16[8,272,128]{2,1,0:T(8,128)(2,1)S(1)}, bf16[8,272,128]{2,1,0:T(8,128)(2,1)S(1)}, u32[]{:S(2)}, u32[]{:S(2)}) collective-permute-start(bf16[8,272,128]{2,1,0:T(8,128)(2,1)S(1)} %get-tuple-element.27), channel_id=1, source_target_pairs={{0,2},{1,9},{2,4},{3,11},{4,6},{5,13},{6,0},{7,15},{8,10},{9,17},{... | collective-permute-start | bytes 1671176 | tf_op jit(solution)/shard_map/ppermute | solution.py:642
  36.5 24.6 %copy-start.5 = (bf16[3,41,41]{2,1,0:T(8,128)(2,1)S(1)}, bf16[3,41,41]{2,1,0:T(8,128)(2,1)}, u32[]{:S(2)}) copy-start(bf16[3,41,41]{2,1,0:T(8,128)(2,1)} %psf.1) | copy-start | bytes 30262
  44.5 6.6 %collective-permute-start.7 = (bf16[2,272,128]{2,1,0:T(8,128)(2,1)S(1)}, bf16[2,272,128]{2,1,0:T(8,128)(2,1)S(1)}, u32[]{:S(2)}, u32[]{:S(2)}) collective-permute-start(bf16[2,272,128]{2,1,0:T(8,128)(2,1)S(1)} %get-tuple-element.31), channel_id=1, source_target_pairs={{0,16},{1,5},{2,18},{3,7},{4,20},{5,1},{6,22},{7,3},{8,24},{9,13},... | collective-permute-start | bytes 417800 | tf_op jit(solution)/shard_map/ppermute | solution.py:642
  47.7 5.3 %collective-permute-start.8 = (bf16[2,272,128]{2,1,0:T(8,128)(2,1)S(1)}, bf16[2,272,128]{2,1,0:T(8,128)(2,1)S(1)}, u32[]{:S(2)}, u32[]{:S(2)}) collective-permute-start(bf16[2,272,128]{2,1,0:T(8,128)(2,1)S(1)} %get-tuple-element.32), channel_id=1, source_target_pairs={{0,24},{1,7},{2,26},{3,1},{4,28},{5,3},{6,30},{7,5},{8,0},{9,15},{... | collective-permute-start | bytes 417800 | tf_op jit(solution)/shard_map/ppermute | solution.py:642
  48.9 6.3 %collective-permute-start.9 = (bf16[2,272,128]{2,1,0:T(8,128)(2,1)S(1)}, bf16[2,272,128]{2,1,0:T(8,128)(2,1)S(1)}, u32[]{:S(2)}, u32[]{:S(2)}) collective-permute-start(bf16[2,272,128]{2,1,0:T(8,128)(2,1)S(1)} %get-tuple-element.33), channel_id=1, source_target_pairs={{0,8},{1,3},{2,10},{3,5},{4,12},{5,7},{6,14},{7,1},{8,16},{9,11},{... | collective-permute-start | bytes 417800 | tf_op jit(solution)/shard_map/ppermute | solution.py:642
  55.7 1.4 %collective-permute-start.10 = (f32[272,128]{1,0:T(8,128)S(1)}, f32[272,128]{1,0:T(8,128)S(1)}, u32[]{:S(2)}, u32[]{:S(2)}) collective-permute-start(f32[272,128]{1,0:T(8,128)S(1)} %get-tuple-element.35), channel_id=1, source_target_pairs={{0,1},{1,0},{2,3},{3,2},{4,5},{5,4},{6,7},{7,6},{8,9},{9,8},{10,11... | collective-permute-start | bytes 417800 | tf_op jit(solution)/shard_map/ppermute | solution.py:653
  58.5 6.2 %collective-permute-start.11 = (bf16[20,1024]{1,0:T(8,128)(2,1)S(1)}, bf16[20,1024]{1,0:T(8,128)(2,1)S(1)}, u32[]{:S(2)}, u32[]{:S(2)}) collective-permute-start(bf16[20,1024]{1,0:T(8,128)(2,1)S(1)} %get-tuple-element.39), channel_id=1, source_target_pairs={{0,32},{64,96},{32,0},{96,64},{1,33},{65,97},{33,1},{97,65},{2,34}... | collective-permute-start | bytes 122888 | tf_op jit(solution)/shard_map/ppermute | solution.py:598
  58.9 6.0 %collective-permute-start.12 = (bf16[20,1024]{1,0:T(8,128)(2,1)S(1)}, bf16[20,1024]{1,0:T(8,128)(2,1)S(1)}, u32[]{:S(2)}, u32[]{:S(2)}) collective-permute-start(bf16[20,1024]{1,0:T(8,128)(2,1)S(1)} %get-tuple-element.40), channel_id=1, source_target_pairs={{32,64},{64,32},{33,65},{65,33},{34,66},{66,34},{35,67},{67,35},{3... | collective-permute-start | bytes 122888 | tf_op jit(solution)/shard_map/ppermute | solution.py:598

commit v10 on v9

--- a/solution.py
+++ b/solution.py
@@ -142,7 +142,7 @@
     return jnp.where(odd, first, second), jnp.where(odd, second, first)
 
 
-ways = 4
+ways = 8
 
 
 def profile_body(code, table, base_rows, base_cols, out, g):
@@ -188,15 +188,12 @@
     )(code, table, base_rows, base_cols)
 
 
-def match_body(taps, odd, place, profile, far, first, second, keep, send, x, frame, lhs, w, arrive):
+def match_body(taps, odd, place, profile, x, first, second, keep, send, frame, lhs, w):
     number, _, cols = x.shape
     reach = taps // 2
     spans = taps + 3
     count = cols // lanes
     depth = 96
-    come = [pltpu.make_async_copy(far.at[e], x.at[e], arrive.at[e]) for e in range(number)]
-    for copy in come:
-        copy.start()
     mask = band_mask(depth, taps)
     lane = lane_ids(16)
     for way in range(ways):
@@ -225,9 +222,6 @@
                     keep[e, rows, at] = jnp.where(place[0] == 0, low[k], high[k])
                     send[e, rows, at] = jnp.where(place[0] == 0, high[k], low[k])
 
-    for copy in come:
-        copy.wait()
-
     def some(i, _):
         for way in range(ways):
             one(ways * i + way, way)
@@ -241,21 +235,18 @@
     taps = profile.shape[1] - 1
     smem = pl.BlockSpec(memory_space=pltpu.SMEM)
     vmem = pl.BlockSpec(memory_space=pltpu.VMEM)
-    far = pl.BlockSpec(memory_space=pltpu.HBM)
     spans = taps + 3
     return pl.pallas_call(
         functools.partial(match_body, taps),
-        in_specs=[smem, smem, vmem, far, vmem, vmem],
+        in_specs=[smem, smem] + [vmem] * 4,
         out_specs=(vmem, vmem),
         out_shape=(jax.ShapeDtypeStruct((number, rows, cols // 2 + lanes), bf16),) * 2,
         scratch_shapes=[
-            pltpu.VMEM(x.shape, bf16),
             pltpu.VMEM((ways, 2, cols // lanes, 96, lanes), f32),
             pltpu.VMEM((ways, 256, spans * lanes), bf16),
             pltpu.VMEM((ways, spans * lanes, 256), bf16),
-            pltpu.SemaphoreType.DMA((number,)),
         ],
-        compiler_params=pltpu.CompilerParams(vmem_limit_bytes=24 * mib),
+        compiler_params=pltpu.CompilerParams(vmem_limit_bytes=40 * mib),
         cost_estimate=pl.CostEstimate(
             flops=number * 2 * 256 * 256 * spans * lanes, bytes_accessed=4 * x.size, transcendentals=0
         ),

time: 68.9 us -> 67.1 us (0.974)
  Pallas kernels: 28.9 us -> 26.8 us
    pallas_call x1, Pallas kernels: 8.09 us -> 6.22 us  [match(): pl.pallas_call(functools.partial(match_body, taps), in_specs=[smem, smem]...]
where the time goes in v10:
time: 67.1 us; the launch traced here: 66.2 us
  Pallas kernels  26.8 us (40%)
  waiting for transfers between devices  18.8 us (28%)
  starting transfers between devices  17 us (25%)
  other arithmetic  2.05 us (3%)
  between operations  0.86 us (1%)
  local copies, waits for them, and re-layouts  0.76 us (1%)
    ppermute x6, waiting for transfers between devices, on_device(): lax.ppermute(rows, sky, role_pairs(step, size, by))  13.4 us
    ppermute x6, starting transfers between devices, on_device(): lax.ppermute(rows, sky, role_pairs(step, size, by))  10.3 us
    pallas_call x3, Pallas kernels, pile(): pl.pallas_call(functools.partial(pile_body, chunks, size), in_specs=[smem...  7.2 us
    ppermute x4, starting transfers between devices, trade(): lax.ppermute(rows, 'section', pairs + [(b, a) for a, b in pairs])  6.48 us
    pallas_call x1, Pallas kernels, match(): pl.pallas_call(functools.partial(match_body, taps), in_specs=[smem, smem]...  6.22 us
    pallas_call x1, Pallas kernels, detect_own(): pl.pallas_call(functools.partial(detect_own_body, taps), out_shape=(jax.S...  3.57 us
    ppermute x2, waiting for transfers between devices, on_device(): other = lax.ppermute(send, 'core', swap)  3.43 us
    pallas_call x1, Pallas kernels, detect_halo(): pl.pallas_call(functools.partial(detect_halo_body, taps), in_specs=[smem,...  3.3 us
  transfers between devices with their start and end apart: 13, of which 11 were waited for; matrix products, arithmetic and copies ran while one was open for 2% of the time, Pallas kernels for 20%

profile of v10, /device:TPU:32, one launch (start us, length us, event | category | flops | bytes accessed | tf_op | source)
XLA Modules:
  0.0 66.2 jit_solution(16736120526515821663)
XLA Ops:
  0.6 0.0 copy-start
  0.6 0.0 copy-start.3
  0.7 0.0 copy-start.2
  0.7 0.0 copy-start.1
  0.7 0.0 copy-start.4
  0.7 1.2 %broadcast_select_fusion = (bf16[8,11,1024]{2,1,0:T(8,128)(2,1)S(1)}, bf16[8,11,1024]{2,1,0:T(8,128)(2,1)S(1)}) fusion(pred[]{:T(512)S(6)} %eq.11, bf16[8,64,1024]{2,1,0:T(8,128)(2,1)} %x.1), kind=kLoop, calls=%fused_computation | loop fusion | flops 180224 | bytes 720897 | tf_op jit(solution)/shard_map/jit(_where)/select_n | solution.py:617
  1.9 3.8 %collective-permute-start.2 = (bf16[8,11,1024]{2,1,0:T(8,128)(2,1)S(1)}, bf16[8,11,1024]{2,1,0:T(8,128)(2,1)S(1)}, u32[]{:S(2)}, u32[]{:S(2)}) collective-permute-start(bf16[8,11,1024]{2,1,0:T(8,128)(2,1)S(1)} %get-tuple-element.42), channel_id=1, source_target_pairs={{32,64},{64,32},{33,65},{65,33},{34,66},{66,34},{35,67},{67,35},{3... | collective-permute-start | bytes 540680 | tf_op jit(solution)/shard_map/ppermute | solution.py:589
  5.7 0.1 collective-permute-start.1
  5.8 0.7 %copy.11 = s32[8,1]{1,0:T(8,128)S(1)} copy(s32[8,1]{0,1:T(1,128)} %bitcast.12) | data formatting | bytes 64 | tf_op jit(solution)/shard_map/broadcast_in_dim | solution.py:621
  6.5 0.8 %pad_add_fusion.mine = s32[8,17]{1,0:T(8,128)S(1)} fusion(s32[8,8]{1,0:T(8,128)} %param.16, s32[8,8]{1,0:T(8,128)} %param.15, s32[8,1]{1,0:T(8,128)S(1)} %copy.11), kind=kLoop, calls=%fused_computation.2 | loop fusion | flops 272 | bytes 1088 | tf_op jit(solution)/shard_map/concatenate | solution.py:620
  7.3 0.0 collective-permute-start
  7.4 0.1 pad_add_fusion.1.place
  7.4 0.0 copy-done.3
  7.5 1.9 %profiles.1.profile = f32[8,24,128]{2,1,0:T(8,128)S(1)} custom-call(s32[8,27]{1,0:T(8,128)S(1)} %copy-done.4, f32[27,64]{1,0:T(8,128)S(1)} %copy-done.1, f32[23,27]{1,0:T(8,128)S(1)} %bitcast.9, f32[23,27]{1,0:T(8,128)S(1)} %bitcast.10), custom_call_target="tpu_custom_call" | custom-call | tf_op jit(solution)/shard_map/profiles/pallas_call | solution.py:180
  9.3 0.0 collective-permute-done.other
  9.3 2.4 %slot_table.1.table = s32[288]{0:T(512)S(1)} custom-call(s32[8,17]{1,0:T(8,128)S(1)} %pad_add_fusion.mine, s32[8,17]{1,0:T(8,128)S(1)} %collective-permute-done.other), custom_call_target="tpu_custom_call" | custom-call | tf_op jit(solution)/shard_map/slot_table/pallas_call | solution.py:288
  11.8 0.2 collective-permute-done.2.second
  12.0 1.6 %collective-permute-done.1.first = bf16[8,11,1024]{2,1,0:T(8,128)(2,1)S(1)} collective-permute-done((bf16[8,11,1024]{2,1,0:T(8,128)(2,1)S(1)}, bf16[8,11,1024]{2,1,0:T(8,128)(2,1)S(1)}, u32[]{:S(2)}, u32[]{:S(2)}) %collective-permute-start.1) | collective-permute-done | bytes 180256 | tf_op jit(solution)/shard_map/ppermute | solution.py:589
  13.6 6.2 %match.1 = (bf16[8,64,640]{2,1,0:T(8,128)(2,1)S(1)}, bf16[8,64,640]{2,1,0:T(8,128)(2,1)S(1)}) custom-call(s32[1]{0:T(128)} %bitcast.odd, s32[3]{0:T(128)S(1)} %pad_add_fusion.1.place, f32[8,24,128]{2,1,0:T(8,128)S(1)} %profiles.1.profile, bf16[8,64,1024]{2,1,0:T(8,128)(2,1)S(1)} %copy-done, bf16[8,11,1024]{2,1,0:T(8,128)(2,1)S(1)} %collective-permute-done.1.first, ...), custom_call_target="tpu_custom_call" | custom-call | flops 3489660928 | bytes 2097152 | tf_op jit(solution)/shard_map/match/pallas_call | solution.py:239
  19.8 0.1 collective-permute-start.3
  19.9 2.1 %collective-permute-done.3.other = bf16[8,64,640]{2,1,0:T(8,128)(2,1)S(1)} collective-permute-done((bf16[8,64,640]{2,1,0:T(8,128)(2,1)S(1)}, bf16[8,64,640]{2,1,0:T(8,128)(2,1)S(1)}, u32[]{:S(2)}, u32[]{:S(2)}) %collective-permute-start.3) | collective-permute-done | bytes 655392 | tf_op jit(solution)/shard_map/ppermute | solution.py:630
  22.0 2.0 %pile_2.1 = bf16[8,272,128]{2,1,0:T(8,128)(2,1)S(1)} custom-call(s32[3]{0:T(128)S(1)} %pad_add_fusion.1.place, s32[288]{0:T(512)S(1)} %slot_table.1.table, bf16[8,64,640]{2,1,0:T(8,128)(2,1)S(1)} %get-tuple-element.24.mine, bf16[8,64,640]{2,1,0:T(8,128)(2,1)S(1)} %collective-permute-done.3.other), custom_call_target="tpu_custom_call" | custom-call | flops 1000000000 | bytes 1310720 | tf_op jit(solution)/shard_map/pile_2/pallas_call | solution.py:380
  24.0 2.9 %collective-permute-start.4 = (bf16[8,272,128]{2,1,0:T(8,128)(2,1)S(1)}, bf16[8,272,128]{2,1,0:T(8,128)(2,1)S(1)}, u32[]{:S(2)}, u32[]{:S(2)}) collective-permute-start(bf16[8,272,128]{2,1,0:T(8,128)(2,1)S(1)} %pile_2.1), channel_id=1, source_target_pairs={{0,4},{1,17},{2,6},{3,19},{4,0},{5,21},{6,2},{7,23},{8,12},{9,25},... | collective-permute-start | bytes 1671176 | tf_op jit(solution)/shard_map/ppermute | solution.py:633
  26.9 3.4 %pile_3_1.1 = (bf16[8,272,128]{2,1,0:T(8,128)(2,1)S(1)}, bf16[8,272,128]{2,1,0:T(8,128)(2,1)S(1)}) custom-call(s32[3]{0:T(128)S(1)} %pad_add_fusion.1.place, s32[288]{0:T(512)S(1)} %slot_table.1.table, bf16[8,64,640]{2,1,0:T(8,128)(2,1)S(1)} %get-tuple-element.24.mine, bf16[8,64,640]{2,1,0:T(8,128)(2,1)S(1)} %collective-permute-done.3.other), custom_call_target="tpu_custom_call" | custom-call | flops 2000000000 | bytes 1310720 | tf_op jit(solution)/shard_map/pile_3_1/pallas_call | solution.py:380
  30.3 1.3 %collective-permute-start.5 = (bf16[8,272,128]{2,1,0:T(8,128)(2,1)S(1)}, bf16[8,272,128]{2,1,0:T(8,128)(2,1)S(1)}, u32[]{:S(2)}, u32[]{:S(2)}) collective-permute-start(bf16[8,272,128]{2,1,0:T(8,128)(2,1)S(1)} %get-tuple-element.29), channel_id=1, source_target_pairs={{0,6},{1,25},{2,0},{3,27},{4,2},{5,29},{6,4},{7,31},{8,14},{9,1},{... | collective-permute-start | bytes 1671176 | tf_op jit(solution)/shard_map/ppermute | solution.py:633
  31.6 0.8 %collective-permute-start.6 = (bf16[8,272,128]{2,1,0:T(8,128)(2,1)S(1)}, bf16[8,272,128]{2,1,0:T(8,128)(2,1)S(1)}, u32[]{:S(2)}, u32[]{:S(2)}) collective-permute-start(bf16[8,272,128]{2,1,0:T(8,128)(2,1)S(1)} %get-tuple-element.27), channel_id=1, source_target_pairs={{0,2},{1,9},{2,4},{3,11},{4,6},{5,13},{6,0},{7,15},{8,10},{9,17},{... | collective-permute-start | bytes 1671176 | tf_op jit(solution)/shard_map/ppermute | solution.py:633
  32.4 1.8 %pile_0.1.own = f32[8,272,128]{2,1,0:T(8,128)S(1)} custom-call(s32[3]{0:T(128)S(1)} %pad_add_fusion.1.place, s32[288]{0:T(512)S(1)} %slot_table.1.table, bf16[8,64,640]{2,1,0:T(8,128)(2,1)S(1)} %get-tuple-element.24.mine, bf16[8,64,640]{2,1,0:T(8,128)(2,1)S(1)} %collective-permute-done.3.other), custom_call_target="tpu_custom_call" | custom-call | flops 1000000000 | bytes 1310720 | tf_op jit(solution)/shard_map/pile_0/pallas_call | solution.py:380
  34.2 0.0 copy-start.5
  34.3 0.9 %collective-permute-done.4.rest_0_ = bf16[8,272,128]{2,1,0:T(8,128)(2,1)S(1)} collective-permute-done((bf16[8,272,128]{2,1,0:T(8,128)(2,1)S(1)}, bf16[8,272,128]{2,1,0:T(8,128)(2,1)S(1)}, u32[]{:S(2)}, u32[]{:S(2)}) %collective-permute-start.4) | collective-permute-done | bytes 557088 | tf_op jit(solution)/shard_map/ppermute | solution.py:633
  35.1 6.1 %collective-permute-done.5.rest_1_ = bf16[8,272,128]{2,1,0:T(8,128)(2,1)S(1)} collective-permute-done((bf16[8,272,128]{2,1,0:T(8,128)(2,1)S(1)}, bf16[8,272,128]{2,1,0:T(8,128)(2,1)S(1)}, u32[]{:S(2)}, u32[]{:S(2)}) %collective-permute-start.5) | collective-permute-done | bytes 557088 | tf_op jit(solution)/shard_map/ppermute | solution.py:633
  41.2 1.2 %collective-permute-done.6.rest_2_ = bf16[8,272,128]{2,1,0:T(8,128)(2,1)S(1)} collective-permute-done((bf16[8,272,128]{2,1,0:T(8,128)(2,1)S(1)}, bf16[8,272,128]{2,1,0:T(8,128)(2,1)S(1)}, u32[]{:S(2)}, u32[]{:S(2)}) %collective-permute-start.6) | collective-permute-done | bytes 557088 | tf_op jit(solution)/shard_map/ppermute | solution.py:633
  42.3 0.2 fold.1
  42.6 3.3 %collective-permute-start.7 = (bf16[2,272,128]{2,1,0:T(8,128)(2,1)S(1)}, bf16[2,272,128]{2,1,0:T(8,128)(2,1)S(1)}, u32[]{:S(2)}, u32[]{:S(2)}) collective-permute-start(bf16[2,272,128]{2,1,0:T(8,128)(2,1)S(1)} %get-tuple-element.31), channel_id=1, source_target_pairs={{0,16},{1,5},{2,18},{3,7},{4,20},{5,1},{6,22},{7,3},{8,24},{9,13},... | collective-permute-start | bytes 417800 | tf_op jit(solution)/shard_map/ppermute | solution.py:633
  45.8 1.1 %collective-permute-start.8 = (bf16[2,272,128]{2,1,0:T(8,128)(2,1)S(1)}, bf16[2,272,128]{2,1,0:T(8,128)(2,1)S(1)}, u32[]{:S(2)}, u32[]{:S(2)}) collective-permute-start(bf16[2,272,128]{2,1,0:T(8,128)(2,1)S(1)} %get-tuple-element.32), channel_id=1, source_target_pairs={{0,24},{1,7},{2,26},{3,1},{4,28},{5,3},{6,30},{7,5},{8,0},{9,15},{... | collective-permute-start | bytes 417800 | tf_op jit(solution)/shard_map/ppermute | solution.py:633
  46.9 1.0 %collective-permute-start.9 = (bf16[2,272,128]{2,1,0:T(8,128)(2,1)S(1)}, bf16[2,272,128]{2,1,0:T(8,128)(2,1)S(1)}, u32[]{:S(2)}, u32[]{:S(2)}) collective-permute-start(bf16[2,272,128]{2,1,0:T(8,128)(2,1)S(1)} %get-tuple-element.33), channel_id=1, source_target_pairs={{0,8},{1,3},{2,10},{3,5},{4,12},{5,7},{6,14},{7,1},{8,16},{9,11},{... | collective-permute-start | bytes 417800 | tf_op jit(solution)/shard_map/ppermute | solution.py:633
  47.9 1.3 %collective-permute-done.7.rest_0_ = bf16[2,272,128]{2,1,0:T(8,128)(2,1)S(1)} collective-permute-done((bf16[2,272,128]{2,1,0:T(8,128)(2,1)S(1)}, bf16[2,272,128]{2,1,0:T(8,128)(2,1)S(1)}, u32[]{:S(2)}, u32[]{:S(2)}) %collective-permute-start.7) | collective-permute-done | bytes 139296 | tf_op jit(solution)/shard_map/ppermute | solution.py:633
  49.2 1.7 %collective-permute-done.8.rest_1_ = bf16[2,272,128]{2,1,0:T(8,128)(2,1)S(1)} collective-permute-done((bf16[2,272,128]{2,1,0:T(8,128)(2,1)S(1)}, bf16[2,272,128]{2,1,0:T(8,128)(2,1)S(1)}, u32[]{:S(2)}, u32[]{:S(2)}) %collective-permute-start.8) | collective-permute-done | bytes 139296 | tf_op jit(solution)/shard_map/ppermute | solution.py:633
  51.0 2.2 %collective-permute-done.9.rest_2_ = bf16[2,272,128]{2,1,0:T(8,128)(2,1)S(1)} collective-permute-done((bf16[2,272,128]{2,1,0:T(8,128)(2,1)S(1)}, bf16[2,272,128]{2,1,0:T(8,128)(2,1)S(1)}, u32[]{:S(2)}, u32[]{:S(2)}) %collective-permute-start.9) | collective-permute-done | bytes 139296 | tf_op jit(solution)/shard_map/ppermute | solution.py:633
  53.2 0.6 meet.1
  53.8 0.1 collective-permute-start.10
  53.9 1.3 %collective-permute-done.10.other = f32[272,128]{1,0:T(8,128)S(1)} collective-permute-done((f32[272,128]{1,0:T(8,128)S(1)}, f32[272,128]{1,0:T(8,128)S(1)}, u32[]{:S(2)}, u32[]{:S(2)}) %collective-permute-start.10) | collective-permute-done | bytes 139296 | tf_op jit(solution)/shard_map/ppermute | solution.py:644
  55.2 1.3 %coadd.1 = (f32[64,1024]{1,0:T(8,128)}, bf16[64,1024]{1,0:T(8,128)(2,1)S(1)}, bf16[20,1024]{1,0:T(8,128)(2,1)S(1)}, bf16[20,1024]{1,0:T(8,128)(2,1)S(1)}) custom-call(s32[1]{0:T(128)} %bitcast.odd, s32[3]{0:T(128)S(1)} %pad_add_fusion.1.place, f32[272,128]{1,0:T(8,128)S(1)} %get-tuple-element.34.mine, f32[272,128]{1,0:T(8,128)S(1)} %collective-permute-done.10.other), custom_call_target="tpu_custom_call" | custom-call | tf_op jit(solution)/shard_map/coadd/pallas_call | solution.py:473
  56.6 0.4 collective-permute-start.11
  56.9 2.2 %collective-permute-start.12 = (bf16[20,1024]{1,0:T(8,128)(2,1)S(1)}, bf16[20,1024]{1,0:T(8,128)(2,1)S(1)}, u32[]{:S(2)}, u32[]{:S(2)}) collective-permute-start(bf16[20,1024]{1,0:T(8,128)(2,1)S(1)} %get-tuple-element.40), channel_id=1, source_target_pairs={{32,64},{64,32},{33,65},{65,33},{34,66},{66,34},{35,67},{67,35},{3... | collective-permute-start | bytes 122888 | tf_op jit(solution)/shard_map/ppermute | solution.py:589
  59.2 3.6 %detect_own.1 = (f32[256,768]{1,0:T(8,128)S(1)}, f32[3,48,128]{2,1,0:T(8,128)S(1)}) custom-call(bf16[3,41,41]{2,1,0:T(8,128)(2,1)S(1)} %copy-done.5, bf16[64,1024]{1,0:T(8,128)(2,1)S(1)} %get-tuple-element.37.x), custom_call_target="tpu_custom_call" | custom-call | flops 2214592512 | bytes 262144 | tf_op jit(solution)/shard_map/detect_own/pallas_call | solution.py:516
  62.7 0.0 collective-permute-done.11.first
  62.8 0.2 collective-permute-done.12.second
  62.9 3.3 %detect_halo.1 = f32[3,64,1024]{2,1,0:T(8,128)} custom-call(s32[1]{0:T(128)} %bitcast.odd, f32[3,48,128]{2,1,0:T(8,128)S(1)} %get-tuple-element.38.profile, bf16[20,1024]{1,0:T(8,128)(2,1)S(1)} %collective-permute-done.11.first, bf16[20,1024]{1,0:T(8,128)(2,1)S(1)} %collective-permute-done.12.second, f32[256,768]{1,0:T(8,128)S(1)} %get-tuple-element.41.acc), custom_call_target="tpu_custom_call" | custom-call | tf_op jit(solution)/shard_map/detect_halo/pallas_call | solution.py:572
  (5 shorter events, 0.0 us)
Async XLA Ops:
  0.6 12.9 %copy-start = (bf16[8,64,1024]{2,1,0:T(8,128)(2,1)S(1)}, bf16[8,64,1024]{2,1,0:T(8,128)(2,1)}, u32[]{:S(2)}) copy-start(bf16[8,64,1024]{2,1,0:T(8,128)(2,1)} %x.1) | copy-start | bytes 3145732
  0.6 6.8 %copy-start.3 = (f32[27,23]{0,1:T(8,128)S(1)}, f32[27,23]{0,1:T(8,128)}, u32[]{:S(2)}) copy-start(f32[27,23]{0,1:T(8,128)} %param.13) | copy-start | bytes 7456
  0.7 6.8 %copy-start.2 = (f32[27,23]{0,1:T(8,128)S(1)}, f32[27,23]{0,1:T(8,128)}, u32[]{:S(2)}) copy-start(f32[27,23]{0,1:T(8,128)} %param.12) | copy-start | bytes 7456
  0.7 6.8 %copy-start.1 = (f32[27,64]{1,0:T(8,128)S(1)}, f32[27,64]{1,0:T(8,128)}, u32[]{:S(2)}) copy-start(f32[27,64]{1,0:T(8,128)} %table.1) | copy-start | bytes 20740
  0.7 6.8 %copy-start.4 = (s32[8,27]{1,0:T(8,128)S(1)}, s32[8,27]{1,0:T(8,128)}, u32[]{:S(2)}) copy-start(s32[8,27]{1,0:T(8,128)} %code.1) | copy-start | bytes 2596
  1.9 10.1 %collective-permute-start.2 = (bf16[8,11,1024]{2,1,0:T(8,128)(2,1)S(1)}, bf16[8,11,1024]{2,1,0:T(8,128)(2,1)S(1)}, u32[]{:S(2)}, u32[]{:S(2)}) collective-permute-start(bf16[8,11,1024]{2,1,0:T(8,128)(2,1)S(1)} %get-tuple-element.42), channel_id=1, source_target_pairs={{32,64},{64,32},{33,65},{65,33},{34,66},{66,34},{35,67},{67,35},{3... | collective-permute-start | bytes 540680 | tf_op jit(solution)/shard_map/ppermute | solution.py:589
  5.7 7.8 %collective-permute-start.1 = (bf16[8,11,1024]{2,1,0:T(8,128)(2,1)S(1)}, bf16[8,11,1024]{2,1,0:T(8,128)(2,1)S(1)}, u32[]{:S(2)}, u32[]{:S(2)}) collective-permute-start(bf16[8,11,1024]{2,1,0:T(8,128)(2,1)S(1)} %get-tuple-element.43), channel_id=1, source_target_pairs={{0,32},{64,96},{32,0},{96,64},{1,33},{65,97},{33,1},{97,65},{2,34}... | collective-permute-start | bytes 540680 | tf_op jit(solution)/shard_map/ppermute | solution.py:589
  7.3 2.0 %collective-permute-start = (s32[8,17]{1,0:T(8,128)S(1)}, s32[8,17]{1,0:T(8,128)S(1)}, u32[]{:S(2)}, u32[]{:S(2)}) collective-permute-start(s32[8,17]{1,0:T(8,128)S(1)} %pad_add_fusion.mine), channel_id=1, source_target_pairs={{0,1},{1,0},{2,3},{3,2},{4,5},{5,4},{6,7},{7,6},{8,9},{9,8},{10,11... | collective-permute-start | bytes 1640 | tf_op jit(solution)/shard_map/ppermute | solution.py:624
  19.8 2.2 %collective-permute-start.3 = (bf16[8,64,640]{2,1,0:T(8,128)(2,1)S(1)}, bf16[8,64,640]{2,1,0:T(8,128)(2,1)S(1)}, u32[]{:S(2)}, u32[]{:S(2)}) collective-permute-start(bf16[8,64,640]{2,1,0:T(8,128)(2,1)S(1)} %get-tuple-element.25), channel_id=1, source_target_pairs={{0,1},{1,0},{2,3},{3,2},{4,5},{5,4},{6,7},{7,6},{8,9},{9,8},{10,11... | collective-permute-start | bytes 1966088 | tf_op jit(solution)/shard_map/ppermute | solution.py:630
  24.0 11.1 %collective-permute-start.4 = (bf16[8,272,128]{2,1,0:T(8,128)(2,1)S(1)}, bf16[8,272,128]{2,1,0:T(8,128)(2,1)S(1)}, u32[]{:S(2)}, u32[]{:S(2)}) collective-permute-start(bf16[8,272,128]{2,1,0:T(8,128)(2,1)S(1)} %pile_2.1), channel_id=1, source_target_pairs={{0,4},{1,17},{2,6},{3,19},{4,0},{5,21},{6,2},{7,23},{8,12},{9,25},... | collective-permute-start | bytes 1671176 | tf_op jit(solution)/shard_map/ppermute | solution.py:633
  30.3 10.9 %collective-permute-start.5 = (bf16[8,272,128]{2,1,0:T(8,128)(2,1)S(1)}, bf16[8,272,128]{2,1,0:T(8,128)(2,1)S(1)}, u32[]{:S(2)}, u32[]{:S(2)}) collective-permute-start(bf16[8,272,128]{2,1,0:T(8,128)(2,1)S(1)} %get-tuple-element.29), channel_id=1, source_target_pairs={{0,6},{1,25},{2,0},{3,27},{4,2},{5,29},{6,4},{7,31},{8,14},{9,1},{... | collective-permute-start | bytes 1671176 | tf_op jit(solution)/shard_map/ppermute | solution.py:633
  31.6 10.7 %collective-permute-start.6 = (bf16[8,272,128]{2,1,0:T(8,128)(2,1)S(1)}, bf16[8,272,128]{2,1,0:T(8,128)(2,1)S(1)}, u32[]{:S(2)}, u32[]{:S(2)}) collective-permute-start(bf16[8,272,128]{2,1,0:T(8,128)(2,1)S(1)} %get-tuple-element.27), channel_id=1, source_target_pairs={{0,2},{1,9},{2,4},{3,11},{4,6},{5,13},{6,0},{7,15},{8,10},{9,17},{... | collective-permute-start | bytes 1671176 | tf_op jit(solution)/shard_map/ppermute | solution.py:633
  34.2 24.9 %copy-start.5 = (bf16[3,41,41]{2,1,0:T(8,128)(2,1)S(1)}, bf16[3,41,41]{2,1,0:T(8,128)(2,1)}, u32[]{:S(2)}) copy-start(bf16[3,41,41]{2,1,0:T(8,128)(2,1)} %psf.1) | copy-start | bytes 30262
  42.6 6.6 %collective-permute-start.7 = (bf16[2,272,128]{2,1,0:T(8,128)(2,1)S(1)}, bf16[2,272,128]{2,1,0:T(8,128)(2,1)S(1)}, u32[]{:S(2)}, u32[]{:S(2)}) collective-permute-start(bf16[2,272,128]{2,1,0:T(8,128)(2,1)S(1)} %get-tuple-element.31), channel_id=1, source_target_pairs={{0,16},{1,5},{2,18},{3,7},{4,20},{5,1},{6,22},{7,3},{8,24},{9,13},... | collective-permute-start | bytes 417800 | tf_op jit(solution)/shard_map/ppermute | solution.py:633
  45.8 5.1 %collective-permute-start.8 = (bf16[2,272,128]{2,1,0:T(8,128)(2,1)S(1)}, bf16[2,272,128]{2,1,0:T(8,128)(2,1)S(1)}, u32[]{:S(2)}, u32[]{:S(2)}) collective-permute-start(bf16[2,272,128]{2,1,0:T(8,128)(2,1)S(1)} %get-tuple-element.32), channel_id=1, source_target_pairs={{0,24},{1,7},{2,26},{3,1},{4,28},{5,3},{6,30},{7,5},{8,0},{9,15},{... | collective-permute-start | bytes 417800 | tf_op jit(solution)/shard_map/ppermute | solution.py:633
  46.9 6.3 %collective-permute-start.9 = (bf16[2,272,128]{2,1,0:T(8,128)(2,1)S(1)}, bf16[2,272,128]{2,1,0:T(8,128)(2,1)S(1)}, u32[]{:S(2)}, u32[]{:S(2)}) collective-permute-start(bf16[2,272,128]{2,1,0:T(8,128)(2,1)S(1)} %get-tuple-element.33), channel_id=1, source_target_pairs={{0,8},{1,3},{2,10},{3,5},{4,12},{5,7},{6,14},{7,1},{8,16},{9,11},{... | collective-permute-start | bytes 417800 | tf_op jit(solution)/shard_map/ppermute | solution.py:633
  53.8 1.4 %collective-permute-start.10 = (f32[272,128]{1,0:T(8,128)S(1)}, f32[272,128]{1,0:T(8,128)S(1)}, u32[]{:S(2)}, u32[]{:S(2)}) collective-permute-start(f32[272,128]{1,0:T(8,128)S(1)} %get-tuple-element.35), channel_id=1, source_target_pairs={{0,1},{1,0},{2,3},{3,2},{4,5},{5,4},{6,7},{7,6},{8,9},{9,8},{10,11... | collective-permute-start | bytes 417800 | tf_op jit(solution)/shard_map/ppermute | solution.py:644
  56.6 6.2 %collective-permute-start.11 = (bf16[20,1024]{1,0:T(8,128)(2,1)S(1)}, bf16[20,1024]{1,0:T(8,128)(2,1)S(1)}, u32[]{:S(2)}, u32[]{:S(2)}) collective-permute-start(bf16[20,1024]{1,0:T(8,128)(2,1)S(1)} %get-tuple-element.39), channel_id=1, source_target_pairs={{0,32},{64,96},{32,0},{96,64},{1,33},{65,97},{33,1},{97,65},{2,34}... | collective-permute-start | bytes 122888 | tf_op jit(solution)/shard_map/ppermute | solution.py:589
  56.9 6.0 %collective-permute-start.12 = (bf16[20,1024]{1,0:T(8,128)(2,1)S(1)}, bf16[20,1024]{1,0:T(8,128)(2,1)S(1)}, u32[]{:S(2)}, u32[]{:S(2)}) collective-permute-start(bf16[20,1024]{1,0:T(8,128)(2,1)S(1)} %get-tuple-element.40), channel_id=1, source_target_pairs={{32,64},{64,32},{33,65},{65,33},{34,66},{66,34},{35,67},{67,35},{3... | collective-permute-start | bytes 122888 | tf_op jit(solution)/shard_map/ppermute | solution.py:589

commit v11 on v10

--- a/solution.py
+++ b/solution.py
@@ -532,8 +532,13 @@
     )(psf, x)
 
 
-def detect_halo_body(taps, odd, profile, first, second, acc, out, frame, lhs, w, stage):
+def detect_halo_body(
+    taps, odd, profile, first, second, acc, coadd, out, again, frame, lhs, w, stage, ready, leave
+):
     scales, rows, cols = out.shape
+    go = [pltpu.make_async_copy(ready.at[s], out.at[s], leave.at[s]) for s in range(scales)]
+    go.append(pltpu.make_async_copy(coadd, again, leave.at[scales]))
+    go[scales].start()
     count = cols // lanes
     spans = edge_spans(taps)
     frame[...] = jnp.zeros_like(frame)
@@ -561,24 +566,34 @@
                     blocks.append(own + more)
                 for b, part in enumerate(split_rows(*blocks, lane)):
                     stage[s, m, pl.ds(2 * h + b, 16, stride=group), :] = part
-            out[s, :, m * lanes : (m + 1) * lanes] = stage[s, m]
-
-
-def detect_halo(odd, profile, first, second, acc, rows, taps):
+            ready[s, :, m * lanes : (m + 1) * lanes] = stage[s, m]
+        go[s].start()
+    for copy in go:
+        copy.wait()
+
+
+def detect_halo(odd, profile, first, second, acc, coadd, rows, taps):
     cols = first.shape[1]
     scales = profile.shape[0]
     smem = pl.BlockSpec(memory_space=pltpu.SMEM)
     vmem = pl.BlockSpec(memory_space=pltpu.VMEM)
     return pl.pallas_call(
         functools.partial(detect_halo_body, taps),
-        in_specs=[smem, vmem, vmem, vmem, vmem],
-        out_specs=vmem,
-        out_shape=jax.ShapeDtypeStruct((scales, rows, cols), f32),
+        in_specs=[smem] + [vmem] * 5,
+        out_specs=(pl.BlockSpec(memory_space=pl.ANY),) * 2,
+        out_shape=(
+            jax.ShapeDtypeStruct((scales, rows, cols), f32),
+            jax.ShapeDtypeStruct((rows, cols), f32),
+        ),
         scratch_shapes=edge_scratch(taps, cols // lanes, scales * 256)
-        + [pltpu.VMEM((scales, cols // lanes, rows, lanes), f32)],
+        + [
+            pltpu.VMEM((scales, cols // lanes, rows, lanes), f32),
+            pltpu.VMEM((scales, rows, cols), f32),
+            pltpu.SemaphoreType.DMA((scales + 1,)),
+        ],
         compiler_params=pltpu.CompilerParams(vmem_limit_bytes=20 * mib),
         name="detect_halo",
-    )(odd, profile, first, second, acc)
+    )(odd, profile, first, second, acc, coadd)
 
 
 def trade(first, second):
@@ -645,7 +660,7 @@
     coadd, rounded, first, second = coadd_of(odd, place, mine, other, rows, cols, wide_reach)
     first, second = trade(first, second)
     acc, profile = detect_own(psf_kernels, rounded)
-    detect = detect_halo(odd, profile, first, second, acc, rows, wide)
+    detect, coadd = detect_halo(odd, profile, first, second, acc, coadd, rows, wide)
     return (coadd[None], detect[None])
 
 

time: 67.1 us -> 66.5 us (level)
  waiting for transfers between devices: 18.8 us -> 18.1 us
    pallas_call x1, Pallas kernels: 1.33 us -> 0.63 us  [coadd_of(): pl.pallas_call(functools.partial(coadd_body, reach), in_specs=[smem, smem...]
    ppermute x6, waiting for transfers between devices: 13.4 us -> 12.7 us  [on_device(): lax.ppermute(rows, sky, role_pairs(step, size, by))]
  transfers between devices with their start and end apart: 13 -> 13, of which waited for: 11 -> 10; matrix products, arithmetic and copies ran while one was open for 2% -> 2% of each run, Pallas kernels for 20% -> 20%
where the time goes in v11:
time: 66.5 us; the launch traced here: 65.6 us
  Pallas kernels  26.2 us (39%)
  waiting for transfers between devices  18.1 us (27%)
  starting transfers between devices  17.5 us (26%)
  other arithmetic  2.05 us (3%)
  between operations  1.04 us (2%)
  local copies, waits for them, and re-layouts  0.76 us (1%)
    ppermute x6, waiting for transfers between devices, on_device(): lax.ppermute(rows, sky, role_pairs(step, size, by))  12.7 us
    ppermute x6, starting transfers between devices, on_device(): lax.ppermute(rows, sky, role_pairs(step, size, by))  10.8 us
    pallas_call x3, Pallas kernels, pile(): pl.pallas_call(functools.partial(pile_body, chunks, size), in_specs=[smem...  7.47 us
    ppermute x4, starting transfers between devices, trade(): lax.ppermute(rows, 'section', pairs + [(b, a) for a, b in pairs])  6.56 us
    pallas_call x1, Pallas kernels, match(): pl.pallas_call(functools.partial(match_body, taps), in_specs=[smem, smem]...  6.22 us
    pallas_call x1, Pallas kernels, detect_own(): pl.pallas_call(functools.partial(detect_own_body, taps), out_shape=(jax.S...  3.57 us
    ppermute x2, waiting for transfers between devices, on_device(): other = lax.ppermute(send, 'core', swap)  3.43 us
    pallas_call x1, Pallas kernels, detect_halo(): pl.pallas_call(functools.partial(detect_halo_body, taps), in_specs=[smem]...  3.16 us
  transfers between devices with their start and end apart: 13, of which 10 were waited for; matrix products, arithmetic and copies ran while one was open for 2% of the time, Pallas kernels for 20%

profile of v11, /device:TPU:32, one launch (start us, length us, event | category | flops | bytes accessed | tf_op | source)
XLA Modules:
  0.0 65.6 jit_solution(14536425582295312840)
XLA Ops:
  0.6 0.0 copy-start
  0.6 0.0 copy-start.3
  0.7 0.0 copy-start.2
  0.7 0.0 copy-start.1
  0.7 0.0 copy-start.4
  0.7 1.2 %broadcast_select_fusion = (bf16[8,11,1024]{2,1,0:T(8,128)(2,1)S(1)}, bf16[8,11,1024]{2,1,0:T(8,128)(2,1)S(1)}) fusion(pred[]{:T(512)S(6)} %eq.11, bf16[8,64,1024]{2,1,0:T(8,128)(2,1)} %x.1), kind=kLoop, calls=%fused_computation | loop fusion | flops 180224 | bytes 720897 | tf_op jit(solution)/shard_map/jit(_where)/select_n | solution.py:632
  1.9 3.8 %collective-permute-start.2 = (bf16[8,11,1024]{2,1,0:T(8,128)(2,1)S(1)}, bf16[8,11,1024]{2,1,0:T(8,128)(2,1)S(1)}, u32[]{:S(2)}, u32[]{:S(2)}) collective-permute-start(bf16[8,11,1024]{2,1,0:T(8,128)(2,1)S(1)} %get-tuple-element.46), channel_id=1, source_target_pairs={{32,64},{64,32},{33,65},{65,33},{34,66},{66,34},{35,67},{67,35},{3... | collective-permute-start | bytes 540680 | tf_op jit(solution)/shard_map/ppermute | solution.py:604
  5.7 0.1 collective-permute-start.1
  5.8 0.7 %copy.11 = s32[8,1]{1,0:T(8,128)S(1)} copy(s32[8,1]{0,1:T(1,128)} %bitcast.11) | data formatting | bytes 64 | tf_op jit(solution)/shard_map/broadcast_in_dim | solution.py:636
  6.5 0.8 %pad_add_fusion.mine = s32[8,17]{1,0:T(8,128)S(1)} fusion(s32[8,8]{1,0:T(8,128)} %param.16, s32[8,8]{1,0:T(8,128)} %param.15, s32[8,1]{1,0:T(8,128)S(1)} %copy.11), kind=kLoop, calls=%fused_computation.2 | loop fusion | flops 272 | bytes 1088 | tf_op jit(solution)/shard_map/concatenate | solution.py:635
  7.3 0.0 collective-permute-start
  7.4 0.1 pad_add_fusion.1.place
  7.4 0.0 copy-done.3
  7.5 1.9 %profiles.1.profile = f32[8,24,128]{2,1,0:T(8,128)S(1)} custom-call(s32[8,27]{1,0:T(8,128)S(1)} %copy-done.4, f32[27,64]{1,0:T(8,128)S(1)} %copy-done.1, f32[23,27]{1,0:T(8,128)S(1)} %bitcast.9, f32[23,27]{1,0:T(8,128)S(1)} %bitcast.10), custom_call_target="tpu_custom_call" | custom-call | tf_op jit(solution)/shard_map/profiles/pallas_call | solution.py:180
  9.3 0.0 collective-permute-done.other
  9.3 2.4 %slot_table.1.table = s32[288]{0:T(512)S(1)} custom-call(s32[8,17]{1,0:T(8,128)S(1)} %pad_add_fusion.mine, s32[8,17]{1,0:T(8,128)S(1)} %collective-permute-done.other), custom_call_target="tpu_custom_call" | custom-call | tf_op jit(solution)/shard_map/slot_table/pallas_call | solution.py:288
  11.8 0.2 collective-permute-done.2.second
  12.0 1.6 %collective-permute-done.1.first = bf16[8,11,1024]{2,1,0:T(8,128)(2,1)S(1)} collective-permute-done((bf16[8,11,1024]{2,1,0:T(8,128)(2,1)S(1)}, bf16[8,11,1024]{2,1,0:T(8,128)(2,1)S(1)}, u32[]{:S(2)}, u32[]{:S(2)}) %collective-permute-start.1) | collective-permute-done | bytes 180256 | tf_op jit(solution)/shard_map/ppermute | solution.py:604
  13.6 6.2 %match.1 = (bf16[8,64,640]{2,1,0:T(8,128)(2,1)S(1)}, bf16[8,64,640]{2,1,0:T(8,128)(2,1)S(1)}) custom-call(s32[1]{0:T(128)} %bitcast.odd, s32[3]{0:T(128)S(1)} %pad_add_fusion.1.place, f32[8,24,128]{2,1,0:T(8,128)S(1)} %profiles.1.profile, bf16[8,64,1024]{2,1,0:T(8,128)(2,1)S(1)} %copy-done, bf16[8,11,1024]{2,1,0:T(8,128)(2,1)S(1)} %collective-permute-done.1.first, ...), custom_call_target="tpu_custom_call" | custom-call | flops 3489660928 | bytes 2097152 | tf_op jit(solution)/shard_map/match/pallas_call | solution.py:239
  19.8 0.1 collective-permute-start.3
  19.9 2.1 %collective-permute-done.3.other = bf16[8,64,640]{2,1,0:T(8,128)(2,1)S(1)} collective-permute-done((bf16[8,64,640]{2,1,0:T(8,128)(2,1)S(1)}, bf16[8,64,640]{2,1,0:T(8,128)(2,1)S(1)}, u32[]{:S(2)}, u32[]{:S(2)}) %collective-permute-start.3) | collective-permute-done | bytes 655392 | tf_op jit(solution)/shard_map/ppermute | solution.py:645
  22.0 1.9 %pile_2.1 = bf16[8,272,128]{2,1,0:T(8,128)(2,1)S(1)} custom-call(s32[3]{0:T(128)S(1)} %pad_add_fusion.1.place, s32[288]{0:T(512)S(1)} %slot_table.1.table, bf16[8,64,640]{2,1,0:T(8,128)(2,1)S(1)} %get-tuple-element.26.mine, bf16[8,64,640]{2,1,0:T(8,128)(2,1)S(1)} %collective-permute-done.3.other), custom_call_target="tpu_custom_call" | custom-call | flops 1000000000 | bytes 1310720 | tf_op jit(solution)/shard_map/pile_2/pallas_call | solution.py:380
  23.9 3.4 %collective-permute-start.4 = (bf16[8,272,128]{2,1,0:T(8,128)(2,1)S(1)}, bf16[8,272,128]{2,1,0:T(8,128)(2,1)S(1)}, u32[]{:S(2)}, u32[]{:S(2)}) collective-permute-start(bf16[8,272,128]{2,1,0:T(8,128)(2,1)S(1)} %pile_2.1), channel_id=1, source_target_pairs={{0,4},{1,17},{2,6},{3,19},{4,0},{5,21},{6,2},{7,23},{8,12},{9,25},... | collective-permute-start | bytes 1671176 | tf_op jit(solution)/shard_map/ppermute | solution.py:648
  27.4 3.3 %pile_3_1.1 = (bf16[8,272,128]{2,1,0:T(8,128)(2,1)S(1)}, bf16[8,272,128]{2,1,0:T(8,128)(2,1)S(1)}) custom-call(s32[3]{0:T(128)S(1)} %pad_add_fusion.1.place, s32[288]{0:T(512)S(1)} %slot_table.1.table, bf16[8,64,640]{2,1,0:T(8,128)(2,1)S(1)} %get-tuple-element.26.mine, bf16[8,64,640]{2,1,0:T(8,128)(2,1)S(1)} %collective-permute-done.3.other), custom_call_target="tpu_custom_call" | custom-call | flops 2000000000 | bytes 1310720 | tf_op jit(solution)/shard_map/pile_3_1/pallas_call | solution.py:380
  30.6 1.0 %collective-permute-start.5 = (bf16[8,272,128]{2,1,0:T(8,128)(2,1)S(1)}, bf16[8,272,128]{2,1,0:T(8,128)(2,1)S(1)}, u32[]{:S(2)}, u32[]{:S(2)}) collective-permute-start(bf16[8,272,128]{2,1,0:T(8,128)(2,1)S(1)} %get-tuple-element.31), channel_id=1, source_target_pairs={{0,6},{1,25},{2,0},{3,27},{4,2},{5,29},{6,4},{7,31},{8,14},{9,1},{... | collective-permute-start | bytes 1671176 | tf_op jit(solution)/shard_map/ppermute | solution.py:648
  31.7 1.1 %collective-permute-start.6 = (bf16[8,272,128]{2,1,0:T(8,128)(2,1)S(1)}, bf16[8,272,128]{2,1,0:T(8,128)(2,1)S(1)}, u32[]{:S(2)}, u32[]{:S(2)}) collective-permute-start(bf16[8,272,128]{2,1,0:T(8,128)(2,1)S(1)} %get-tuple-element.29), channel_id=1, source_target_pairs={{0,2},{1,9},{2,4},{3,11},{4,6},{5,13},{6,0},{7,15},{8,10},{9,17},{... | collective-permute-start | bytes 1671176 | tf_op jit(solution)/shard_map/ppermute | solution.py:648
  32.7 2.3 %pile_0.1.own = f32[8,272,128]{2,1,0:T(8,128)S(1)} custom-call(s32[3]{0:T(128)S(1)} %pad_add_fusion.1.place, s32[288]{0:T(512)S(1)} %slot_table.1.table, bf16[8,64,640]{2,1,0:T(8,128)(2,1)S(1)} %get-tuple-element.26.mine, bf16[8,64,640]{2,1,0:T(8,128)(2,1)S(1)} %collective-permute-done.3.other), custom_call_target="tpu_custom_call" | custom-call | flops 1000000000 | bytes 1310720 | tf_op jit(solution)/shard_map/pile_0/pallas_call | solution.py:380
  35.0 0.0 copy-start.5
  35.0 0.0 collective-permute-done.4.rest_0_
  35.0 6.1 %collective-permute-done.5.rest_1_ = bf16[8,272,128]{2,1,0:T(8,128)(2,1)S(1)} collective-permute-done((bf16[8,272,128]{2,1,0:T(8,128)(2,1)S(1)}, bf16[8,272,128]{2,1,0:T(8,128)(2,1)S(1)}, u32[]{:S(2)}, u32[]{:S(2)}) %collective-permute-start.5) | collective-permute-done | bytes 557088 | tf_op jit(solution)/shard_map/ppermute | solution.py:648
  41.2 1.3 %collective-permute-done.6.rest_2_ = bf16[8,272,128]{2,1,0:T(8,128)(2,1)S(1)} collective-permute-done((bf16[8,272,128]{2,1,0:T(8,128)(2,1)S(1)}, bf16[8,272,128]{2,1,0:T(8,128)(2,1)S(1)}, u32[]{:S(2)}, u32[]{:S(2)}) %collective-permute-start.6) | collective-permute-done | bytes 557088 | tf_op jit(solution)/shard_map/ppermute | solution.py:648
  42.4 0.2 fold.1
  42.7 3.2 %collective-permute-start.7 = (bf16[2,272,128]{2,1,0:T(8,128)(2,1)S(1)}, bf16[2,272,128]{2,1,0:T(8,128)(2,1)S(1)}, u32[]{:S(2)}, u32[]{:S(2)}) collective-permute-start(bf16[2,272,128]{2,1,0:T(8,128)(2,1)S(1)} %get-tuple-element.33), channel_id=1, source_target_pairs={{0,16},{1,5},{2,18},{3,7},{4,20},{5,1},{6,22},{7,3},{8,24},{9,13},... | collective-permute-start | bytes 417800 | tf_op jit(solution)/shard_map/ppermute | solution.py:648
  45.8 1.1 %collective-permute-start.8 = (bf16[2,272,128]{2,1,0:T(8,128)(2,1)S(1)}, bf16[2,272,128]{2,1,0:T(8,128)(2,1)S(1)}, u32[]{:S(2)}, u32[]{:S(2)}) collective-permute-start(bf16[2,272,128]{2,1,0:T(8,128)(2,1)S(1)} %get-tuple-element.34), channel_id=1, source_target_pairs={{0,24},{1,7},{2,26},{3,1},{4,28},{5,3},{6,30},{7,5},{8,0},{9,15},{... | collective-permute-start | bytes 417800 | tf_op jit(solution)/shard_map/ppermute | solution.py:648
  46.9 1.0 %collective-permute-start.9 = (bf16[2,272,128]{2,1,0:T(8,128)(2,1)S(1)}, bf16[2,272,128]{2,1,0:T(8,128)(2,1)S(1)}, u32[]{:S(2)}, u32[]{:S(2)}) collective-permute-start(bf16[2,272,128]{2,1,0:T(8,128)(2,1)S(1)} %get-tuple-element.35), channel_id=1, source_target_pairs={{0,8},{1,3},{2,10},{3,5},{4,12},{5,7},{6,14},{7,1},{8,16},{9,11},{... | collective-permute-start | bytes 417800 | tf_op jit(solution)/shard_map/ppermute | solution.py:648
  47.9 1.4 %collective-permute-done.7.rest_0_ = bf16[2,272,128]{2,1,0:T(8,128)(2,1)S(1)} collective-permute-done((bf16[2,272,128]{2,1,0:T(8,128)(2,1)S(1)}, bf16[2,272,128]{2,1,0:T(8,128)(2,1)S(1)}, u32[]{:S(2)}, u32[]{:S(2)}) %collective-permute-start.7) | collective-permute-done | bytes 139296 | tf_op jit(solution)/shard_map/ppermute | solution.py:648
  49.3 1.9 %collective-permute-done.8.rest_1_ = bf16[2,272,128]{2,1,0:T(8,128)(2,1)S(1)} collective-permute-done((bf16[2,272,128]{2,1,0:T(8,128)(2,1)S(1)}, bf16[2,272,128]{2,1,0:T(8,128)(2,1)S(1)}, u32[]{:S(2)}, u32[]{:S(2)}) %collective-permute-start.8) | collective-permute-done | bytes 139296 | tf_op jit(solution)/shard_map/ppermute | solution.py:648
  51.2 2.0 %collective-permute-done.9.rest_2_ = bf16[2,272,128]{2,1,0:T(8,128)(2,1)S(1)} collective-permute-done((bf16[2,272,128]{2,1,0:T(8,128)(2,1)S(1)}, bf16[2,272,128]{2,1,0:T(8,128)(2,1)S(1)}, u32[]{:S(2)}, u32[]{:S(2)}) %collective-permute-start.9) | collective-permute-done | bytes 139296 | tf_op jit(solution)/shard_map/ppermute | solution.py:648
  53.2 0.6 meet.1
  53.8 0.1 collective-permute-start.10
  53.9 1.3 %collective-permute-done.10.other = f32[272,128]{1,0:T(8,128)S(1)} collective-permute-done((f32[272,128]{1,0:T(8,128)S(1)}, f32[272,128]{1,0:T(8,128)S(1)}, u32[]{:S(2)}, u32[]{:S(2)}) %collective-permute-start.10) | collective-permute-done | bytes 139296 | tf_op jit(solution)/shard_map/ppermute | solution.py:659
  55.2 0.6 coadd.1
  55.9 0.4 collective-permute-start.11
  56.3 2.2 %collective-permute-start.12 = (bf16[20,1024]{1,0:T(8,128)(2,1)S(1)}, bf16[20,1024]{1,0:T(8,128)(2,1)S(1)}, u32[]{:S(2)}, u32[]{:S(2)}) collective-permute-start(bf16[20,1024]{1,0:T(8,128)(2,1)S(1)} %get-tuple-element.41), channel_id=1, source_target_pairs={{32,64},{64,32},{33,65},{65,33},{34,66},{66,34},{35,67},{67,35},{3... | collective-permute-start | bytes 122888 | tf_op jit(solution)/shard_map/ppermute | solution.py:604
  58.5 3.6 %detect_own.1 = (f32[256,768]{1,0:T(8,128)S(1)}, f32[3,48,128]{2,1,0:T(8,128)S(1)}) custom-call(bf16[3,41,41]{2,1,0:T(8,128)(2,1)S(1)} %copy-done.5, bf16[64,1024]{1,0:T(8,128)(2,1)S(1)} %get-tuple-element.38.x), custom_call_target="tpu_custom_call" | custom-call | flops 2214592512 | bytes 262144 | tf_op jit(solution)/shard_map/detect_own/pallas_call | solution.py:516
  62.1 0.0 collective-permute-done.11.first
  62.1 0.2 collective-permute-done.12.second
  62.3 3.2 %detect_halo.1 = (f32[3,64,1024]{2,1,0:T(8,128)}, f32[64,1024]{1,0:T(8,128)}) custom-call(s32[1]{0:T(128)} %bitcast.odd, f32[3,48,128]{2,1,0:T(8,128)S(1)} %get-tuple-element.39.profile, bf16[20,1024]{1,0:T(8,128)(2,1)S(1)} %collective-permute-done.11.first, bf16[20,1024]{1,0:T(8,128)(2,1)S(1)} %collective-permute-done.12.second, ...), custom_call_target="tpu_custom_call" | custom-call | tf_op jit(solution)/shard_map/detect_halo/pallas_call | solution.py:580
  (5 shorter events, 0.0 us)
Async XLA Ops:
  0.6 12.9 %copy-start = (bf16[8,64,1024]{2,1,0:T(8,128)(2,1)S(1)}, bf16[8,64,1024]{2,1,0:T(8,128)(2,1)}, u32[]{:S(2)}) copy-start(bf16[8,64,1024]{2,1,0:T(8,128)(2,1)} %x.1) | copy-start | bytes 3145732
  0.6 6.8 %copy-start.3 = (f32[27,23]{0,1:T(8,128)S(1)}, f32[27,23]{0,1:T(8,128)}, u32[]{:S(2)}) copy-start(f32[27,23]{0,1:T(8,128)} %param.13) | copy-start | bytes 7456
  0.7 6.8 %copy-start.2 = (f32[27,23]{0,1:T(8,128)S(1)}, f32[27,23]{0,1:T(8,128)}, u32[]{:S(2)}) copy-start(f32[27,23]{0,1:T(8,128)} %param.12) | copy-start | bytes 7456
  0.7 6.8 %copy-start.1 = (f32[27,64]{1,0:T(8,128)S(1)}, f32[27,64]{1,0:T(8,128)}, u32[]{:S(2)}) copy-start(f32[27,64]{1,0:T(8,128)} %table.1) | copy-start | bytes 20740
  0.7 6.8 %copy-start.4 = (s32[8,27]{1,0:T(8,128)S(1)}, s32[8,27]{1,0:T(8,128)}, u32[]{:S(2)}) copy-start(s32[8,27]{1,0:T(8,128)} %code.1) | copy-start | bytes 2596
  1.9 10.1 %collective-permute-start.2 = (bf16[8,11,1024]{2,1,0:T(8,128)(2,1)S(1)}, bf16[8,11,1024]{2,1,0:T(8,128)(2,1)S(1)}, u32[]{:S(2)}, u32[]{:S(2)}) collective-permute-start(bf16[8,11,1024]{2,1,0:T(8,128)(2,1)S(1)} %get-tuple-element.46), channel_id=1, source_target_pairs={{32,64},{64,32},{33,65},{65,33},{34,66},{66,34},{35,67},{67,35},{3... | collective-permute-start | bytes 540680 | tf_op jit(solution)/shard_map/ppermute | solution.py:604
  5.7 7.8 %collective-permute-start.1 = (bf16[8,11,1024]{2,1,0:T(8,128)(2,1)S(1)}, bf16[8,11,1024]{2,1,0:T(8,128)(2,1)S(1)}, u32[]{:S(2)}, u32[]{:S(2)}) collective-permute-start(bf16[8,11,1024]{2,1,0:T(8,128)(2,1)S(1)} %get-tuple-element.47), channel_id=1, source_target_pairs={{0,32},{64,96},{32,0},{96,64},{1,33},{65,97},{33,1},{97,65},{2,34}... | collective-permute-start | bytes 540680 | tf_op jit(solution)/shard_map/ppermute | solution.py:604
  7.3 2.0 %collective-permute-start = (s32[8,17]{1,0:T(8,128)S(1)}, s32[8,17]{1,0:T(8,128)S(1)}, u32[]{:S(2)}, u32[]{:S(2)}) collective-permute-start(s32[8,17]{1,0:T(8,128)S(1)} %pad_add_fusion.mine), channel_id=1, source_target_pairs={{0,1},{1,0},{2,3},{3,2},{4,5},{5,4},{6,7},{7,6},{8,9},{9,8},{10,11... | collective-permute-start | bytes 1640 | tf_op jit(solution)/shard_map/ppermute | solution.py:639
  19.8 2.2 %collective-permute-start.3 = (bf16[8,64,640]{2,1,0:T(8,128)(2,1)S(1)}, bf16[8,64,640]{2,1,0:T(8,128)(2,1)S(1)}, u32[]{:S(2)}, u32[]{:S(2)}) collective-permute-start(bf16[8,64,640]{2,1,0:T(8,128)(2,1)S(1)} %get-tuple-element.27), channel_id=1, source_target_pairs={{0,1},{1,0},{2,3},{3,2},{4,5},{5,4},{6,7},{7,6},{8,9},{9,8},{10,11... | collective-permute-start | bytes 1966088 | tf_op jit(solution)/shard_map/ppermute | solution.py:645
  23.9 11.1 %collective-permute-start.4 = (bf16[8,272,128]{2,1,0:T(8,128)(2,1)S(1)}, bf16[8,272,128]{2,1,0:T(8,128)(2,1)S(1)}, u32[]{:S(2)}, u32[]{:S(2)}) collective-permute-start(bf16[8,272,128]{2,1,0:T(8,128)(2,1)S(1)} %pile_2.1), channel_id=1, source_target_pairs={{0,4},{1,17},{2,6},{3,19},{4,0},{5,21},{6,2},{7,23},{8,12},{9,25},... | collective-permute-start | bytes 1671176 | tf_op jit(solution)/shard_map/ppermute | solution.py:648
  30.6 10.5 %collective-permute-start.5 = (bf16[8,272,128]{2,1,0:T(8,128)(2,1)S(1)}, bf16[8,272,128]{2,1,0:T(8,128)(2,1)S(1)}, u32[]{:S(2)}, u32[]{:S(2)}) collective-permute-start(bf16[8,272,128]{2,1,0:T(8,128)(2,1)S(1)} %get-tuple-element.31), channel_id=1, source_target_pairs={{0,6},{1,25},{2,0},{3,27},{4,2},{5,29},{6,4},{7,31},{8,14},{9,1},{... | collective-permute-start | bytes 1671176 | tf_op jit(solution)/shard_map/ppermute | solution.py:648
  31.7 10.7 %collective-permute-start.6 = (bf16[8,272,128]{2,1,0:T(8,128)(2,1)S(1)}, bf16[8,272,128]{2,1,0:T(8,128)(2,1)S(1)}, u32[]{:S(2)}, u32[]{:S(2)}) collective-permute-start(bf16[8,272,128]{2,1,0:T(8,128)(2,1)S(1)} %get-tuple-element.29), channel_id=1, source_target_pairs={{0,2},{1,9},{2,4},{3,11},{4,6},{5,13},{6,0},{7,15},{8,10},{9,17},{... | collective-permute-start | bytes 1671176 | tf_op jit(solution)/shard_map/ppermute | solution.py:648
  35.0 23.5 %copy-start.5 = (bf16[3,41,41]{2,1,0:T(8,128)(2,1)S(1)}, bf16[3,41,41]{2,1,0:T(8,128)(2,1)}, u32[]{:S(2)}) copy-start(bf16[3,41,41]{2,1,0:T(8,128)(2,1)} %psf.1) | copy-start | bytes 30262
  42.7 6.6 %collective-permute-start.7 = (bf16[2,272,128]{2,1,0:T(8,128)(2,1)S(1)}, bf16[2,272,128]{2,1,0:T(8,128)(2,1)S(1)}, u32[]{:S(2)}, u32[]{:S(2)}) collective-permute-start(bf16[2,272,128]{2,1,0:T(8,128)(2,1)S(1)} %get-tuple-element.33), channel_id=1, source_target_pairs={{0,16},{1,5},{2,18},{3,7},{4,20},{5,1},{6,22},{7,3},{8,24},{9,13},... | collective-permute-start | bytes 417800 | tf_op jit(solution)/shard_map/ppermute | solution.py:648
  45.8 5.4 %collective-permute-start.8 = (bf16[2,272,128]{2,1,0:T(8,128)(2,1)S(1)}, bf16[2,272,128]{2,1,0:T(8,128)(2,1)S(1)}, u32[]{:S(2)}, u32[]{:S(2)}) collective-permute-start(bf16[2,272,128]{2,1,0:T(8,128)(2,1)S(1)} %get-tuple-element.34), channel_id=1, source_target_pairs={{0,24},{1,7},{2,26},{3,1},{4,28},{5,3},{6,30},{7,5},{8,0},{9,15},{... | collective-permute-start | bytes 417800 | tf_op jit(solution)/shard_map/ppermute | solution.py:648
  46.9 6.3 %collective-permute-start.9 = (bf16[2,272,128]{2,1,0:T(8,128)(2,1)S(1)}, bf16[2,272,128]{2,1,0:T(8,128)(2,1)S(1)}, u32[]{:S(2)}, u32[]{:S(2)}) collective-permute-start(bf16[2,272,128]{2,1,0:T(8,128)(2,1)S(1)} %get-tuple-element.35), channel_id=1, source_target_pairs={{0,8},{1,3},{2,10},{3,5},{4,12},{5,7},{6,14},{7,1},{8,16},{9,11},{... | collective-permute-start | bytes 417800 | tf_op jit(solution)/shard_map/ppermute | solution.py:648
  53.8 1.4 %collective-permute-start.10 = (f32[272,128]{1,0:T(8,128)S(1)}, f32[272,128]{1,0:T(8,128)S(1)}, u32[]{:S(2)}, u32[]{:S(2)}) collective-permute-start(f32[272,128]{1,0:T(8,128)S(1)} %get-tuple-element.37), channel_id=1, source_target_pairs={{0,1},{1,0},{2,3},{3,2},{4,5},{5,4},{6,7},{7,6},{8,9},{9,8},{10,11... | collective-permute-start | bytes 417800 | tf_op jit(solution)/shard_map/ppermute | solution.py:659
  55.9 6.2 %collective-permute-start.11 = (bf16[20,1024]{1,0:T(8,128)(2,1)S(1)}, bf16[20,1024]{1,0:T(8,128)(2,1)S(1)}, u32[]{:S(2)}, u32[]{:S(2)}) collective-permute-start(bf16[20,1024]{1,0:T(8,128)(2,1)S(1)} %get-tuple-element.40), channel_id=1, source_target_pairs={{0,32},{64,96},{32,0},{96,64},{1,33},{65,97},{33,1},{97,65},{2,34}... | collective-permute-start | bytes 122888 | tf_op jit(solution)/shard_map/ppermute | solution.py:604
  56.3 6.0 %collective-permute-start.12 = (bf16[20,1024]{1,0:T(8,128)(2,1)S(1)}, bf16[20,1024]{1,0:T(8,128)(2,1)S(1)}, u32[]{:S(2)}, u32[]{:S(2)}) collective-permute-start(bf16[20,1024]{1,0:T(8,128)(2,1)S(1)} %get-tuple-element.41), channel_id=1, source_target_pairs={{32,64},{64,32},{33,65},{65,33},{34,66},{66,34},{35,67},{67,35},{3... | collective-permute-start | bytes 122888 | tf_op jit(solution)/shard_map/ppermute | solution.py:604

commit v12 on v11

--- a/solution.py
+++ b/solution.py
@@ -505,8 +505,7 @@
             )
         profile[s] = total
         put_band(w, total, taps, mask, 0, spans, 256 * s)
-        cut = slice(256 * s, 256 * s + 256)
-        acc[:, cut] = jnp.dot(lhs[...], w[:, cut], preferred_element_type=f32)
+    acc[...] = jnp.dot(lhs[...], w[...], preferred_element_type=f32)
 
 
 def detect_own(psf, x):
@@ -549,9 +548,10 @@
     lo, hi = halo_pair(odd[0] == 1, first[...], second[...])
     put_edges(taps, frame, lhs, lo, hi)
     for s in range(scales):
+        put_band(w.at[0], profile[s], taps, mask, 0, spans, 256 * s)
+        put_band(w.at[1], profile[s], taps, mask, taps + 3 - spans, taps + 3, 256 * s)
+    for s in range(scales):
         at = 256 * s
-        put_band(w.at[0], profile[s], taps, mask, 0, spans, at)
-        put_band(w.at[1], profile[s], taps, mask, taps + 3 - spans, taps + 3, at)
         ends = [
             jnp.dot(lhs[side], w[side, :, at : at + 256], preferred_element_type=f32)
             for side in range(2)

time: 66.5 us -> 66 us (level)
  waiting for transfers between devices: 18.1 us -> 19.6 us
  Pallas kernels: 26.2 us -> 25.3 us
    ppermute x6, waiting for transfers between devices: 12.7 us -> 13.7 us  [on_device(): lax.ppermute(rows, sky, role_pairs(step, size, by))]
  transfers between devices with their start and end apart: 13 -> 13, of which waited for: 10 -> 11; matrix products, arithmetic and copies ran while one was open for 2% -> 2% of each run, Pallas kernels for 20% -> 19%
where the time goes in v12:
time: 66 us; the launch traced here: 65.6 us
  Pallas kernels  25.3 us (38%)
  waiting for transfers between devices  19.6 us (30%)
  starting transfers between devices  16.9 us (26%)
  other arithmetic  2.05 us (3%)
  between operations  1.03 us (2%)
  local copies, waits for them, and re-layouts  0.76 us (1%)
    ppermute x6, waiting for transfers between devices, on_device(): lax.ppermute(rows, sky, role_pairs(step, size, by))  13.7 us
    ppermute x6, starting transfers between devices, on_device(): lax.ppermute(rows, sky, role_pairs(step, size, by))  10.2 us
    pallas_call x3, Pallas kernels, pile(): pl.pallas_call(functools.partial(pile_body, chunks, size), in_specs=[smem...  7.29 us
    ppermute x4, starting transfers between devices, trade(): lax.ppermute(rows, 'section', pairs + [(b, a) for a, b in pairs])  6.56 us
    pallas_call x1, Pallas kernels, match(): pl.pallas_call(functools.partial(match_body, taps), in_specs=[smem, smem]...  6.22 us
    ppermute x2, waiting for transfers between devices, on_device(): other = lax.ppermute(send, 'core', swap)  3.43 us
    pallas_call x1, Pallas kernels, detect_own(): pl.pallas_call(functools.partial(detect_own_body, taps), out_shape=(jax.S...  3.12 us
    pallas_call x1, Pallas kernels, detect_halo(): pl.pallas_call(functools.partial(detect_halo_body, taps), in_specs=[smem]...  2.91 us
  transfers between devices with their start and end apart: 13, of which 11 were waited for; matrix products, arithmetic and copies ran while one was open for 2% of the time, Pallas kernels for 19%

profile of v12, /device:TPU:32, one launch (start us, length us, event | category | flops | bytes accessed | tf_op | source)
XLA Modules:
  0.0 65.6 jit_solution(13816810863073794554)
XLA Ops:
  0.6 0.0 copy-start
  0.6 0.0 copy-start.3
  0.7 0.0 copy-start.2
  0.7 0.0 copy-start.1
  0.7 0.0 copy-start.4
  0.7 1.2 %broadcast_select_fusion = (bf16[8,11,1024]{2,1,0:T(8,128)(2,1)S(1)}, bf16[8,11,1024]{2,1,0:T(8,128)(2,1)S(1)}) fusion(pred[]{:T(512)S(6)} %eq.11, bf16[8,64,1024]{2,1,0:T(8,128)(2,1)} %x.1), kind=kLoop, calls=%fused_computation | loop fusion | flops 180224 | bytes 720897 | tf_op jit(solution)/shard_map/jit(_where)/select_n | solution.py:632
  1.9 3.8 %collective-permute-start.2 = (bf16[8,11,1024]{2,1,0:T(8,128)(2,1)S(1)}, bf16[8,11,1024]{2,1,0:T(8,128)(2,1)S(1)}, u32[]{:S(2)}, u32[]{:S(2)}) collective-permute-start(bf16[8,11,1024]{2,1,0:T(8,128)(2,1)S(1)} %get-tuple-element.46), channel_id=1, source_target_pairs={{32,64},{64,32},{33,65},{65,33},{34,66},{66,34},{35,67},{67,35},{3... | collective-permute-start | bytes 540680 | tf_op jit(solution)/shard_map/ppermute | solution.py:604
  5.7 0.1 collective-permute-start.1
  5.8 0.7 %copy.11 = s32[8,1]{1,0:T(8,128)S(1)} copy(s32[8,1]{0,1:T(1,128)} %bitcast.11) | data formatting | bytes 64 | tf_op jit(solution)/shard_map/broadcast_in_dim | solution.py:636
  6.5 0.8 %pad_add_fusion.mine = s32[8,17]{1,0:T(8,128)S(1)} fusion(s32[8,8]{1,0:T(8,128)} %param.16, s32[8,8]{1,0:T(8,128)} %param.15, s32[8,1]{1,0:T(8,128)S(1)} %copy.11), kind=kLoop, calls=%fused_computation.2 | loop fusion | flops 272 | bytes 1088 | tf_op jit(solution)/shard_map/concatenate | solution.py:635
  7.3 0.0 collective-permute-start
  7.4 0.1 pad_add_fusion.1.place
  7.4 0.0 copy-done.2
  7.5 1.9 %profiles.1.profile = f32[8,24,128]{2,1,0:T(8,128)S(1)} custom-call(s32[8,27]{1,0:T(8,128)S(1)} %copy-done.4, f32[27,64]{1,0:T(8,128)S(1)} %copy-done.1, f32[23,27]{1,0:T(8,128)S(1)} %bitcast.9, f32[23,27]{1,0:T(8,128)S(1)} %bitcast.10), custom_call_target="tpu_custom_call" | custom-call | tf_op jit(solution)/shard_map/profiles/pallas_call | solution.py:180
  9.3 0.0 collective-permute-done.other
  9.3 2.4 %slot_table.1.table = s32[288]{0:T(512)S(1)} custom-call(s32[8,17]{1,0:T(8,128)S(1)} %pad_add_fusion.mine, s32[8,17]{1,0:T(8,128)S(1)} %collective-permute-done.other), custom_call_target="tpu_custom_call" | custom-call | tf_op jit(solution)/shard_map/slot_table/pallas_call | solution.py:288
  11.8 0.2 collective-permute-done.2.second
  12.0 1.6 %collective-permute-done.1.first = bf16[8,11,1024]{2,1,0:T(8,128)(2,1)S(1)} collective-permute-done((bf16[8,11,1024]{2,1,0:T(8,128)(2,1)S(1)}, bf16[8,11,1024]{2,1,0:T(8,128)(2,1)S(1)}, u32[]{:S(2)}, u32[]{:S(2)}) %collective-permute-start.1) | collective-permute-done | bytes 180256 | tf_op jit(solution)/shard_map/ppermute | solution.py:604
  13.6 6.2 %match.1 = (bf16[8,64,640]{2,1,0:T(8,128)(2,1)S(1)}, bf16[8,64,640]{2,1,0:T(8,128)(2,1)S(1)}) custom-call(s32[1]{0:T(128)} %bitcast.odd, s32[3]{0:T(128)S(1)} %pad_add_fusion.1.place, f32[8,24,128]{2,1,0:T(8,128)S(1)} %profiles.1.profile, bf16[8,64,1024]{2,1,0:T(8,128)(2,1)S(1)} %copy-done, bf16[8,11,1024]{2,1,0:T(8,128)(2,1)S(1)} %collective-permute-done.1.first, ...), custom_call_target="tpu_custom_call" | custom-call | flops 3489660928 | bytes 2097152 | tf_op jit(solution)/shard_map/match/pallas_call | solution.py:239
  19.8 0.1 collective-permute-start.3
  19.9 2.1 %collective-permute-done.3.other = bf16[8,64,640]{2,1,0:T(8,128)(2,1)S(1)} collective-permute-done((bf16[8,64,640]{2,1,0:T(8,128)(2,1)S(1)}, bf16[8,64,640]{2,1,0:T(8,128)(2,1)S(1)}, u32[]{:S(2)}, u32[]{:S(2)}) %collective-permute-start.3) | collective-permute-done | bytes 655392 | tf_op jit(solution)/shard_map/ppermute | solution.py:645
  22.0 2.1 %pile_2.1 = bf16[8,272,128]{2,1,0:T(8,128)(2,1)S(1)} custom-call(s32[3]{0:T(128)S(1)} %pad_add_fusion.1.place, s32[288]{0:T(512)S(1)} %slot_table.1.table, bf16[8,64,640]{2,1,0:T(8,128)(2,1)S(1)} %get-tuple-element.26.mine, bf16[8,64,640]{2,1,0:T(8,128)(2,1)S(1)} %collective-permute-done.3.other), custom_call_target="tpu_custom_call" | custom-call | flops 1000000000 | bytes 1310720 | tf_op jit(solution)/shard_map/pile_2/pallas_call | solution.py:380
  24.1 2.8 %collective-permute-start.4 = (bf16[8,272,128]{2,1,0:T(8,128)(2,1)S(1)}, bf16[8,272,128]{2,1,0:T(8,128)(2,1)S(1)}, u32[]{:S(2)}, u32[]{:S(2)}) collective-permute-start(bf16[8,272,128]{2,1,0:T(8,128)(2,1)S(1)} %pile_2.1), channel_id=1, source_target_pairs={{0,4},{1,17},{2,6},{3,19},{4,0},{5,21},{6,2},{7,23},{8,12},{9,25},... | collective-permute-start | bytes 1671176 | tf_op jit(solution)/shard_map/ppermute | solution.py:648
  26.9 3.4 %pile_3_1.1 = (bf16[8,272,128]{2,1,0:T(8,128)(2,1)S(1)}, bf16[8,272,128]{2,1,0:T(8,128)(2,1)S(1)}) custom-call(s32[3]{0:T(128)S(1)} %pad_add_fusion.1.place, s32[288]{0:T(512)S(1)} %slot_table.1.table, bf16[8,64,640]{2,1,0:T(8,128)(2,1)S(1)} %get-tuple-element.26.mine, bf16[8,64,640]{2,1,0:T(8,128)(2,1)S(1)} %collective-permute-done.3.other), custom_call_target="tpu_custom_call" | custom-call | flops 2000000000 | bytes 1310720 | tf_op jit(solution)/shard_map/pile_3_1/pallas_call | solution.py:380
  30.3 1.6 %collective-permute-start.5 = (bf16[8,272,128]{2,1,0:T(8,128)(2,1)S(1)}, bf16[8,272,128]{2,1,0:T(8,128)(2,1)S(1)}, u32[]{:S(2)}, u32[]{:S(2)}) collective-permute-start(bf16[8,272,128]{2,1,0:T(8,128)(2,1)S(1)} %get-tuple-element.31), channel_id=1, source_target_pairs={{0,6},{1,25},{2,0},{3,27},{4,2},{5,29},{6,4},{7,31},{8,14},{9,1},{... | collective-permute-start | bytes 1671176 | tf_op jit(solution)/shard_map/ppermute | solution.py:648
  31.9 0.5 collective-permute-start.6
  32.4 1.8 %pile_0.1.own = f32[8,272,128]{2,1,0:T(8,128)S(1)} custom-call(s32[3]{0:T(128)S(1)} %pad_add_fusion.1.place, s32[288]{0:T(512)S(1)} %slot_table.1.table, bf16[8,64,640]{2,1,0:T(8,128)(2,1)S(1)} %get-tuple-element.26.mine, bf16[8,64,640]{2,1,0:T(8,128)(2,1)S(1)} %collective-permute-done.3.other), custom_call_target="tpu_custom_call" | custom-call | flops 1000000000 | bytes 1310720 | tf_op jit(solution)/shard_map/pile_0/pallas_call | solution.py:380
  34.2 0.0 copy-start.5
  34.3 0.9 %collective-permute-done.4.rest_0_ = bf16[8,272,128]{2,1,0:T(8,128)(2,1)S(1)} collective-permute-done((bf16[8,272,128]{2,1,0:T(8,128)(2,1)S(1)}, bf16[8,272,128]{2,1,0:T(8,128)(2,1)S(1)}, u32[]{:S(2)}, u32[]{:S(2)}) %collective-permute-start.4) | collective-permute-done | bytes 557088 | tf_op jit(solution)/shard_map/ppermute | solution.py:648
  35.2 5.8 %collective-permute-done.5.rest_1_ = bf16[8,272,128]{2,1,0:T(8,128)(2,1)S(1)} collective-permute-done((bf16[8,272,128]{2,1,0:T(8,128)(2,1)S(1)}, bf16[8,272,128]{2,1,0:T(8,128)(2,1)S(1)}, u32[]{:S(2)}, u32[]{:S(2)}) %collective-permute-start.5) | collective-permute-done | bytes 557088 | tf_op jit(solution)/shard_map/ppermute | solution.py:648
  41.0 1.6 %collective-permute-done.6.rest_2_ = bf16[8,272,128]{2,1,0:T(8,128)(2,1)S(1)} collective-permute-done((bf16[8,272,128]{2,1,0:T(8,128)(2,1)S(1)}, bf16[8,272,128]{2,1,0:T(8,128)(2,1)S(1)}, u32[]{:S(2)}, u32[]{:S(2)}) %collective-permute-start.6) | collective-permute-done | bytes 557088 | tf_op jit(solution)/shard_map/ppermute | solution.py:648
  42.6 0.2 fold.1
  42.8 3.2 %collective-permute-start.7 = (bf16[2,272,128]{2,1,0:T(8,128)(2,1)S(1)}, bf16[2,272,128]{2,1,0:T(8,128)(2,1)S(1)}, u32[]{:S(2)}, u32[]{:S(2)}) collective-permute-start(bf16[2,272,128]{2,1,0:T(8,128)(2,1)S(1)} %get-tuple-element.33), channel_id=1, source_target_pairs={{0,16},{1,5},{2,18},{3,7},{4,20},{5,1},{6,22},{7,3},{8,24},{9,13},... | collective-permute-start | bytes 417800 | tf_op jit(solution)/shard_map/ppermute | solution.py:648
  46.0 1.1 %collective-permute-start.8 = (bf16[2,272,128]{2,1,0:T(8,128)(2,1)S(1)}, bf16[2,272,128]{2,1,0:T(8,128)(2,1)S(1)}, u32[]{:S(2)}, u32[]{:S(2)}) collective-permute-start(bf16[2,272,128]{2,1,0:T(8,128)(2,1)S(1)} %get-tuple-element.34), channel_id=1, source_target_pairs={{0,24},{1,7},{2,26},{3,1},{4,28},{5,3},{6,30},{7,5},{8,0},{9,15},{... | collective-permute-start | bytes 417800 | tf_op jit(solution)/shard_map/ppermute | solution.py:648
  47.2 0.9 %collective-permute-start.9 = (bf16[2,272,128]{2,1,0:T(8,128)(2,1)S(1)}, bf16[2,272,128]{2,1,0:T(8,128)(2,1)S(1)}, u32[]{:S(2)}, u32[]{:S(2)}) collective-permute-start(bf16[2,272,128]{2,1,0:T(8,128)(2,1)S(1)} %get-tuple-element.35), channel_id=1, source_target_pairs={{0,8},{1,3},{2,10},{3,5},{4,12},{5,7},{6,14},{7,1},{8,16},{9,11},{... | collective-permute-start | bytes 417800 | tf_op jit(solution)/shard_map/ppermute | solution.py:648
  48.0 1.4 %collective-permute-done.7.rest_0_ = bf16[2,272,128]{2,1,0:T(8,128)(2,1)S(1)} collective-permute-done((bf16[2,272,128]{2,1,0:T(8,128)(2,1)S(1)}, bf16[2,272,128]{2,1,0:T(8,128)(2,1)S(1)}, u32[]{:S(2)}, u32[]{:S(2)}) %collective-permute-start.7) | collective-permute-done | bytes 139296 | tf_op jit(solution)/shard_map/ppermute | solution.py:648
  49.5 1.7 %collective-permute-done.8.rest_1_ = bf16[2,272,128]{2,1,0:T(8,128)(2,1)S(1)} collective-permute-done((bf16[2,272,128]{2,1,0:T(8,128)(2,1)S(1)}, bf16[2,272,128]{2,1,0:T(8,128)(2,1)S(1)}, u32[]{:S(2)}, u32[]{:S(2)}) %collective-permute-start.8) | collective-permute-done | bytes 139296 | tf_op jit(solution)/shard_map/ppermute | solution.py:648
  51.2 2.2 %collective-permute-done.9.rest_2_ = bf16[2,272,128]{2,1,0:T(8,128)(2,1)S(1)} collective-permute-done((bf16[2,272,128]{2,1,0:T(8,128)(2,1)S(1)}, bf16[2,272,128]{2,1,0:T(8,128)(2,1)S(1)}, u32[]{:S(2)}, u32[]{:S(2)}) %collective-permute-start.9) | collective-permute-done | bytes 139296 | tf_op jit(solution)/shard_map/ppermute | solution.py:648
  53.4 0.6 meet.1
  54.1 0.1 collective-permute-start.10
  54.1 1.3 %collective-permute-done.10.other = f32[272,128]{1,0:T(8,128)S(1)} collective-permute-done((f32[272,128]{1,0:T(8,128)S(1)}, f32[272,128]{1,0:T(8,128)S(1)}, u32[]{:S(2)}, u32[]{:S(2)}) %collective-permute-start.10) | collective-permute-done | bytes 139296 | tf_op jit(solution)/shard_map/ppermute | solution.py:659
  55.5 0.6 coadd.1
  56.1 0.4 collective-permute-start.11
  56.6 2.2 %collective-permute-start.12 = (bf16[20,1024]{1,0:T(8,128)(2,1)S(1)}, bf16[20,1024]{1,0:T(8,128)(2,1)S(1)}, u32[]{:S(2)}, u32[]{:S(2)}) collective-permute-start(bf16[20,1024]{1,0:T(8,128)(2,1)S(1)} %get-tuple-element.41), channel_id=1, source_target_pairs={{32,64},{64,32},{33,65},{65,33},{34,66},{66,34},{35,67},{67,35},{3... | collective-permute-start | bytes 122888 | tf_op jit(solution)/shard_map/ppermute | solution.py:604
  58.8 3.1 %detect_own.1 = (f32[256,768]{1,0:T(8,128)S(1)}, f32[3,48,128]{2,1,0:T(8,128)S(1)}) custom-call(bf16[3,41,41]{2,1,0:T(8,128)(2,1)S(1)} %copy-done.5, bf16[64,1024]{1,0:T(8,128)(2,1)S(1)} %get-tuple-element.38.x), custom_call_target="tpu_custom_call" | custom-call | flops 2214592512 | bytes 262144 | tf_op jit(solution)/shard_map/detect_own/pallas_call | solution.py:515
  61.9 0.0 collective-permute-done.11.first
  61.9 0.6 collective-permute-done.12.second
  62.5 2.9 %detect_halo.1 = (f32[3,64,1024]{2,1,0:T(8,128)}, f32[64,1024]{1,0:T(8,128)}) custom-call(s32[1]{0:T(128)} %bitcast.odd, f32[3,48,128]{2,1,0:T(8,128)S(1)} %get-tuple-element.39.profile, bf16[20,1024]{1,0:T(8,128)(2,1)S(1)} %collective-permute-done.11.first, bf16[20,1024]{1,0:T(8,128)(2,1)S(1)} %collective-permute-done.12.second, ...), custom_call_target="tpu_custom_call" | custom-call | tf_op jit(solution)/shard_map/detect_halo/pallas_call | solution.py:580
  (5 shorter events, 0.0 us)
Async XLA Ops:
  0.6 12.9 %copy-start = (bf16[8,64,1024]{2,1,0:T(8,128)(2,1)S(1)}, bf16[8,64,1024]{2,1,0:T(8,128)(2,1)}, u32[]{:S(2)}) copy-start(bf16[8,64,1024]{2,1,0:T(8,128)(2,1)} %x.1) | copy-start | bytes 3145732
  0.6 6.8 %copy-start.3 = (f32[27,23]{0,1:T(8,128)S(1)}, f32[27,23]{0,1:T(8,128)}, u32[]{:S(2)}) copy-start(f32[27,23]{0,1:T(8,128)} %param.13) | copy-start | bytes 7456
  0.7 6.8 %copy-start.2 = (f32[27,23]{0,1:T(8,128)S(1)}, f32[27,23]{0,1:T(8,128)}, u32[]{:S(2)}) copy-start(f32[27,23]{0,1:T(8,128)} %param.12) | copy-start | bytes 7456
  0.7 6.8 %copy-start.1 = (f32[27,64]{1,0:T(8,128)S(1)}, f32[27,64]{1,0:T(8,128)}, u32[]{:S(2)}) copy-start(f32[27,64]{1,0:T(8,128)} %table.1) | copy-start | bytes 20740
  0.7 6.8 %copy-start.4 = (s32[8,27]{1,0:T(8,128)S(1)}, s32[8,27]{1,0:T(8,128)}, u32[]{:S(2)}) copy-start(s32[8,27]{1,0:T(8,128)} %code.1) | copy-start | bytes 2596
  1.9 10.1 %collective-permute-start.2 = (bf16[8,11,1024]{2,1,0:T(8,128)(2,1)S(1)}, bf16[8,11,1024]{2,1,0:T(8,128)(2,1)S(1)}, u32[]{:S(2)}, u32[]{:S(2)}) collective-permute-start(bf16[8,11,1024]{2,1,0:T(8,128)(2,1)S(1)} %get-tuple-element.46), channel_id=1, source_target_pairs={{32,64},{64,32},{33,65},{65,33},{34,66},{66,34},{35,67},{67,35},{3... | collective-permute-start | bytes 540680 | tf_op jit(solution)/shard_map/ppermute | solution.py:604
  5.7 7.8 %collective-permute-start.1 = (bf16[8,11,1024]{2,1,0:T(8,128)(2,1)S(1)}, bf16[8,11,1024]{2,1,0:T(8,128)(2,1)S(1)}, u32[]{:S(2)}, u32[]{:S(2)}) collective-permute-start(bf16[8,11,1024]{2,1,0:T(8,128)(2,1)S(1)} %get-tuple-element.47), channel_id=1, source_target_pairs={{0,32},{64,96},{32,0},{96,64},{1,33},{65,97},{33,1},{97,65},{2,34}... | collective-permute-start | bytes 540680 | tf_op jit(solution)/shard_map/ppermute | solution.py:604
  7.3 2.0 %collective-permute-start = (s32[8,17]{1,0:T(8,128)S(1)}, s32[8,17]{1,0:T(8,128)S(1)}, u32[]{:S(2)}, u32[]{:S(2)}) collective-permute-start(s32[8,17]{1,0:T(8,128)S(1)} %pad_add_fusion.mine), channel_id=1, source_target_pairs={{0,1},{1,0},{2,3},{3,2},{4,5},{5,4},{6,7},{7,6},{8,9},{9,8},{10,11... | collective-permute-start | bytes 1640 | tf_op jit(solution)/shard_map/ppermute | solution.py:639
  19.8 2.2 %collective-permute-start.3 = (bf16[8,64,640]{2,1,0:T(8,128)(2,1)S(1)}, bf16[8,64,640]{2,1,0:T(8,128)(2,1)S(1)}, u32[]{:S(2)}, u32[]{:S(2)}) collective-permute-start(bf16[8,64,640]{2,1,0:T(8,128)(2,1)S(1)} %get-tuple-element.27), channel_id=1, source_target_pairs={{0,1},{1,0},{2,3},{3,2},{4,5},{5,4},{6,7},{7,6},{8,9},{9,8},{10,11... | collective-permute-start | bytes 1966088 | tf_op jit(solution)/shard_map/ppermute | solution.py:645
  24.1 11.1 %collective-permute-start.4 = (bf16[8,272,128]{2,1,0:T(8,128)(2,1)S(1)}, bf16[8,272,128]{2,1,0:T(8,128)(2,1)S(1)}, u32[]{:S(2)}, u32[]{:S(2)}) collective-permute-start(bf16[8,272,128]{2,1,0:T(8,128)(2,1)S(1)} %pile_2.1), channel_id=1, source_target_pairs={{0,4},{1,17},{2,6},{3,19},{4,0},{5,21},{6,2},{7,23},{8,12},{9,25},... | collective-permute-start | bytes 1671176 | tf_op jit(solution)/shard_map/ppermute | solution.py:648
  30.3 10.7 %collective-permute-start.5 = (bf16[8,272,128]{2,1,0:T(8,128)(2,1)S(1)}, bf16[8,272,128]{2,1,0:T(8,128)(2,1)S(1)}, u32[]{:S(2)}, u32[]{:S(2)}) collective-permute-start(bf16[8,272,128]{2,1,0:T(8,128)(2,1)S(1)} %get-tuple-element.31), channel_id=1, source_target_pairs={{0,6},{1,25},{2,0},{3,27},{4,2},{5,29},{6,4},{7,31},{8,14},{9,1},{... | collective-permute-start | bytes 1671176 | tf_op jit(solution)/shard_map/ppermute | solution.py:648
  31.9 10.7 %collective-permute-start.6 = (bf16[8,272,128]{2,1,0:T(8,128)(2,1)S(1)}, bf16[8,272,128]{2,1,0:T(8,128)(2,1)S(1)}, u32[]{:S(2)}, u32[]{:S(2)}) collective-permute-start(bf16[8,272,128]{2,1,0:T(8,128)(2,1)S(1)} %get-tuple-element.29), channel_id=1, source_target_pairs={{0,2},{1,9},{2,4},{3,11},{4,6},{5,13},{6,0},{7,15},{8,10},{9,17},{... | collective-permute-start | bytes 1671176 | tf_op jit(solution)/shard_map/ppermute | solution.py:648
  34.2 24.6 %copy-start.5 = (bf16[3,41,41]{2,1,0:T(8,128)(2,1)S(1)}, bf16[3,41,41]{2,1,0:T(8,128)(2,1)}, u32[]{:S(2)}) copy-start(bf16[3,41,41]{2,1,0:T(8,128)(2,1)} %psf.1) | copy-start | bytes 30262
  42.8 6.6 %collective-permute-start.7 = (bf16[2,272,128]{2,1,0:T(8,128)(2,1)S(1)}, bf16[2,272,128]{2,1,0:T(8,128)(2,1)S(1)}, u32[]{:S(2)}, u32[]{:S(2)}) collective-permute-start(bf16[2,272,128]{2,1,0:T(8,128)(2,1)S(1)} %get-tuple-element.33), channel_id=1, source_target_pairs={{0,16},{1,5},{2,18},{3,7},{4,20},{5,1},{6,22},{7,3},{8,24},{9,13},... | collective-permute-start | bytes 417800 | tf_op jit(solution)/shard_map/ppermute | solution.py:648
  46.0 5.2 %collective-permute-start.8 = (bf16[2,272,128]{2,1,0:T(8,128)(2,1)S(1)}, bf16[2,272,128]{2,1,0:T(8,128)(2,1)S(1)}, u32[]{:S(2)}, u32[]{:S(2)}) collective-permute-start(bf16[2,272,128]{2,1,0:T(8,128)(2,1)S(1)} %get-tuple-element.34), channel_id=1, source_target_pairs={{0,24},{1,7},{2,26},{3,1},{4,28},{5,3},{6,30},{7,5},{8,0},{9,15},{... | collective-permute-start | bytes 417800 | tf_op jit(solution)/shard_map/ppermute | solution.py:648
  47.2 6.3 %collective-permute-start.9 = (bf16[2,272,128]{2,1,0:T(8,128)(2,1)S(1)}, bf16[2,272,128]{2,1,0:T(8,128)(2,1)S(1)}, u32[]{:S(2)}, u32[]{:S(2)}) collective-permute-start(bf16[2,272,128]{2,1,0:T(8,128)(2,1)S(1)} %get-tuple-element.35), channel_id=1, source_target_pairs={{0,8},{1,3},{2,10},{3,5},{4,12},{5,7},{6,14},{7,1},{8,16},{9,11},{... | collective-permute-start | bytes 417800 | tf_op jit(solution)/shard_map/ppermute | solution.py:648
  54.1 1.4 %collective-permute-start.10 = (f32[272,128]{1,0:T(8,128)S(1)}, f32[272,128]{1,0:T(8,128)S(1)}, u32[]{:S(2)}, u32[]{:S(2)}) collective-permute-start(f32[272,128]{1,0:T(8,128)S(1)} %get-tuple-element.37), channel_id=1, source_target_pairs={{0,1},{1,0},{2,3},{3,2},{4,5},{5,4},{6,7},{7,6},{8,9},{9,8},{10,11... | collective-permute-start | bytes 417800 | tf_op jit(solution)/shard_map/ppermute | solution.py:659
  56.1 5.8 %collective-permute-start.11 = (bf16[20,1024]{1,0:T(8,128)(2,1)S(1)}, bf16[20,1024]{1,0:T(8,128)(2,1)S(1)}, u32[]{:S(2)}, u32[]{:S(2)}) collective-permute-start(bf16[20,1024]{1,0:T(8,128)(2,1)S(1)} %get-tuple-element.40), channel_id=1, source_target_pairs={{0,32},{64,96},{32,0},{96,64},{1,33},{65,97},{33,1},{97,65},{2,34}... | collective-permute-start | bytes 122888 | tf_op jit(solution)/shard_map/ppermute | solution.py:604
  56.6 6.0 %collective-permute-start.12 = (bf16[20,1024]{1,0:T(8,128)(2,1)S(1)}, bf16[20,1024]{1,0:T(8,128)(2,1)S(1)}, u32[]{:S(2)}, u32[]{:S(2)}) collective-permute-start(bf16[20,1024]{1,0:T(8,128)(2,1)S(1)} %get-tuple-element.41), channel_id=1, source_target_pairs={{32,64},{64,32},{33,65},{65,33},{34,66},{66,34},{35,67},{67,35},{3... | collective-permute-start | bytes 122888 | tf_op jit(solution)/shard_map/ppermute | solution.py:604
